TPU v7x, 128 devices: a whole 4x4x4 slice. The times are simulated.
128 devices in a mesh: dp: 8 (over x, core), ctx: 4 (over y), head: 4 (over z).
Axes of the slice: x: 4, y: 4, z: 4, core: 2. Of those that a mesh axis runs over, the one named last changes fastest.
Arguments:
- tokens: bfloat16 [8, 1024, 2048], P('dp', 'ctx'), may hold values from -6 to 6
- proj_weights: bfloat16 [3, 2048, 1024], P(None, None, 'head'), may hold values from -0.125 to 0.125
- init_weight: float32 [8, 128, 128], P('head'), may hold values from -0.5 to 0.5
- base_rates: float32 [8], P('head'), may hold values from 0.005 to 1
- gate_values: float32 [8, 8, 1024], P('dp', 'head', 'ctx'), may hold values from 0.3 to 480
- out_gain: float32 [8, 128], P('head'), may hold values from 0.5 to 1.5
- cotangent: bfloat16 [8, 1024, 1024], P('dp', 'ctx', 'head'), may hold values from -6 to 6
Outputs:
- grad_tokens: bfloat16 [8, 1024, 2048], P('dp', 'ctx', 'head')
- grad_proj: float32 [3, 2048, 1024], P(None, None, 'head')
- grad_init: float32 [8, 128, 128], P('head')
- grad_gain: float32 [8, 128], P('head')
- grad_rates: float32 [8], P('head')
- grad_gates: float32 [8, 8, 1024], P('dp', 'head', 'ctx')
All inputs are finite; a program needn't handle non-finite values.
Results may differ from a plain program's by a relative error of at most 0.0072.
Values sent between devices are 32-bit elements; how exact they have to be, the bound alone decides.
No kernel may reach another device: no remote copies, remote signals or barrier semaphores. Data moves between devices by JAX's collectives and lax.ppermute only.
A program may use at most 64 MiB of HBM per device.

v0:
```python
import functools

import jax
import jax.numpy as jnp
from jax import lax
from jax.experimental import pallas as pl
from jax.experimental.pallas import tpu as pltpu
from jax.sharding import PartitionSpec as P

MB = 16
HS = 128
F32 = jnp.float32
BF = jnp.bfloat16
NN = (((1,), (0,)), ((), ()))
NT = (((1,), (1,)), ((), ()))
TN = (((0,), (0,)), ((), ()))


def dot(a, b, dims, passes):
    ah = a.astype(BF)
    bh = b.astype(BF)
    result = lax.dot_general(ah, bh, dims, preferred_element_type=F32)
    if passes == 3:
        al = (a - ah.astype(F32)).astype(BF)
        bl = (b - bh.astype(F32)).astype(BF)
        result = result + (
            lax.dot_general(ah, bl, dims, preferred_element_type=F32)
            + lax.dot_general(al, bh, dims, preferred_element_type=F32)
        )
    return result


def places(n):
    return (
        lax.broadcasted_iota(jnp.int32, (n, n), 0),
        lax.broadcasted_iota(jnp.int32, (n, n), 1),
    )


def to_col(row):
    i, j = places(row.shape[1])
    return jnp.sum(jnp.where(i == j, row, 0.0), axis=1, keepdims=True)


def to_row(col):
    i, j = places(col.shape[0])
    return jnp.sum(jnp.where(i == j, col, 0.0), axis=0, keepdims=True)


def unit_lower_inverses(lowers):
    n = lowers[0].shape[0]
    i, j = places(n)
    size = 2 * MB
    same = (i // size) == (j // size)
    inverses = [jnp.where(i == j, 1.0, 0.0) - jnp.where(same, low, 0.0) for low in lowers]
    while size < n:
        pair = ((i // (2 * size)) == (j // (2 * size))) & ((i // size) != (j // size))
        corners = [jnp.where(pair, low, 0.0) for low in lowers]
        halves = [dot(inv, corner, NN, 3) for inv, corner in zip(inverses, corners)]
        inverses = [inv - dot(half, inv, NN, 3) for inv, half in zip(inverses, halves)]
        size *= 2
    return inverses


def span(h):
    return slice(h * HS, (h + 1) * HS)


def rates_of(base_ref, gate_ref, h):
    boost = base_ref[h] * gate_ref[0, h : h + 1, :]
    return boost, boost / (1.0 + boost)


def maps_kernel(
    ctx_ref, base_ref, tok_ref, wk_ref, wv_ref, gate_ref, init_ref,
    k_ref, v_ref, ninv_ref, gram_ref, inv_ref, bt_ref, d_ref, send_ref, o_ref,
):
    tok = tok_ref[0]
    kraw_all = jnp.dot(tok, wk_ref[0], preferred_element_type=F32).astype(BF).astype(F32)
    v_all = jnp.dot(tok, wv_ref[0], preferred_element_type=F32).astype(BF).astype(F32)
    n = kraw_all.shape[0]
    i, j = places(n)
    strict = (i // MB) > (j // MB)
    heads = range(init_ref.shape[0])
    ks, kts, es, lows = [], [], [], []
    for h in heads:
        kraw = kraw_all[:, span(h)]
        ninv = lax.rsqrt(jnp.sum(kraw * kraw, -1, keepdims=True) + 1e-06)
        k = kraw * ninv
        kt = k.T
        _, e = rates_of(base_ref, gate_ref, h)
        gram = dot(k, kt, NN, 3)
        ninv_ref[h] = jnp.broadcast_to(ninv, (n, HS))
        k_ref[:, span(h)] = k
        gram_ref[h] = gram
        ks.append(k)
        kts.append(kt)
        es.append(e)
        lows.append(jnp.where(strict, gram * e, 0.0))
    v_ref[...] = v_all
    inverses = unit_lower_inverses(lows)
    a, b = places(HS)
    for h in heads:
        bt = dot(kts[h] * es[h], inverses[h], NN, 3)
        inv_ref[h] = inverses[h]
        bt_ref[h] = bt
        decay = jnp.where(a == b, 1.0, 0.0) - dot(bt, ks[h], NN, 3)
        offset = dot(bt, v_all[:, span(h)], NN, 3)
        d_ref[h] = decay
        o_ref[h] = offset
        first = dot(decay, init_ref[h], NN, 3) + offset
        send_ref[h] = jnp.where(ctx_ref[0] == 0, first, offset)


def reach_kernel(base_ref, tok_ref, wq_ref, gate_ref, k_ref, v_ref, inv_ref,
                 q_ref, score_ref, rv_ref, y_ref, qt_ref, zv_ref):
    q_all = jnp.dot(tok_ref[0], wq_ref[0], preferred_element_type=F32).astype(BF).astype(F32)
    n = q_all.shape[0]
    i, j = places(n)
    q_ref[...] = q_all
    for h in range(inv_ref.shape[0]):
        q = q_all[:, span(h)]
        k = k_ref[:, span(h)]
        _, e = rates_of(base_ref, gate_ref, h)
        score = dot(q, k, NT, 3)
        mix = jnp.where(i >= j, score * e, 0.0)
        inv = inv_ref[h]
        rv = dot(inv, v_ref[:, span(h)], NN, 3)
        y = dot(inv, k, NN, 3)
        score_ref[h] = score
        rv_ref[:, span(h)] = rv
        y_ref[:, span(h)] = y
        qt_ref[:, span(h)] = q - dot(mix, y, NN, 3)
        zv_ref[:, span(h)] = dot(mix, rv, NN, 3)


def step_kernel(d_ref, w_ref, o_ref, out_ref, *, transposed):
    for h in range(d_ref.shape[0]):
        out_ref[h] = o_ref[h] + dot(d_ref[h], w_ref[h], TN if transposed else NN, 3)


def norm_kernel(
    ctx_ref, init_ref, near_ref, mid_ref, far_ref, rd_ref, qt_ref, zv_ref, up_ref, gain_ref,
    w_ref, h_ref, p_ref, dgain_ref,
):
    ctx = ctx_ref[0]
    for h in range(init_ref.shape[0]):
        last = dot(rd_ref[h], far_ref[h], NN, 3) + near_ref[h]
        start = jnp.where(
            ctx == 0, init_ref[h], jnp.where(ctx == 1, near_ref[h], jnp.where(ctx == 2, mid_ref[h], last))
        )
        w_ref[h] = start
        qt = qt_ref[:, span(h)]
        z = dot(qt, start, NN, 3) + zv_ref[:, span(h)]
        up = up_ref[0, :, span(h)].astype(F32)
        centred = z - jnp.mean(z, -1, keepdims=True)
        inv_std = lax.rsqrt(jnp.mean(centred * centred, -1, keepdims=True) + 1e-05)
        normed = centred * inv_std
        weighted = up * gain_ref[h : h + 1, :]
        back = inv_std * (
            weighted
            - jnp.mean(weighted, -1, keepdims=True)
            - normed * jnp.mean(weighted * normed, -1, keepdims=True)
        )
        h_ref[:, span(h)] = back
        p_ref[h] = dot(qt, back, TN, 3)
        dgain_ref[h : h + 1, :] = jnp.sum(up * normed, axis=0, keepdims=True)


def query_kernel(
    base_ref, gate_ref, w_ref, h_ref, up_ref, q_ref, score_ref, rv_ref, y_ref, k_ref, inv_ref,
    dq_ref, r_ref, x_ref, dk_ref, de_ref,
):
    n = h_ref.shape[0]
    i, j = places(n)
    for h in range(w_ref.shape[0]):
        w = w_ref[h]
        back = h_ref[:, span(h)]
        k = k_ref[:, span(h)]
        q = q_ref[:, span(h)]
        score = score_ref[h]
        _, e = rates_of(base_ref, gate_ref, h)
        mix = jnp.where(i >= j, score * e, 0.0)
        r = rv_ref[:, span(h)] - dot(y_ref[:, span(h)], w, NN, 3)
        r_ref[:, span(h)] = r
        d_mix = jnp.where(i >= j, dot(back, r, NT, 3), 0.0)
        d_score = d_mix * e
        dq = up_ref[0, :, span(h)].astype(F32) + dot(back, w, NT, 3) + dot(d_score, k, NN, 3)
        dq_ref[:, span(h)] = dq.astype(BF)
        x_ref[:, span(h)] = dot(inv_ref[h], dot(mix, back, TN, 3), TN, 3)
        dk_ref[:, span(h)] = dot(d_score, q, TN, 3)
        de_ref[h : h + 1, :] = jnp.sum(d_mix * score, axis=0, keepdims=True)


def keys_kernel(
    ctx_ref, base_ref, gate_ref, rp_ref, mid_ref, far_ref, rd_ref, p_ref, d_ref, w_ref, k_ref, ninv_ref,
    gram_ref, bt_ref, r_ref, x_ref, dk_ref, de_ref, dgain_ref,
    dkraw_ref, dv_ref, gates_ref, extra_ref,
):
    ctx = ctx_ref[0]
    n = k_ref.shape[0]
    i, j = places(n)
    strict = (i // MB) > (j // MB)
    extra_ref[...] = jnp.zeros_like(extra_ref)
    for h in range(w_ref.shape[0]):
        first = rp_ref[h] + dot(rd_ref[h], far_ref[h], TN, 3)
        end = jnp.where(
            ctx == 0, first, jnp.where(ctx == 1, mid_ref[h], jnp.where(ctx == 2, rp_ref[h], 0.0))
        )
        extra_ref[h, 0:HS, :] = jnp.where(ctx == 0, p_ref[h] + dot(d_ref[h], end, TN, 3), 0.0)
        w = w_ref[h]
        k = k_ref[:, span(h)]
        r = r_ref[:, span(h)]
        boost, e = rates_of(base_ref, gate_ref, h)
        x = x_ref[:, span(h)] + dot(bt_ref[h], end, TN, 3)
        dv_ref[:, span(h)] = x.astype(BF)
        d_low = jnp.where(strict, -dot(x, r, NT, 3), 0.0)
        d_gram = d_low * e
        dk = (
            dk_ref[:, span(h)]
            - dot(x, w, NT, 3)
            + to_col(e) * dot(r, end, NT, 3)
            + dot(d_gram + d_gram.T, k, NN, 3)
        )
        pull = to_row(jnp.sum(r * dot(k, end, NN, 3), axis=1, keepdims=True))
        de = de_ref[h : h + 1, :] + jnp.sum(d_low * gram_ref[h], axis=0, keepdims=True) + pull
        draw = ninv_ref[h] * (dk - k * jnp.sum(k * dk, -1, keepdims=True))
        dkraw_ref[:, span(h)] = draw.astype(BF)
        d_boost = de / ((1.0 + boost) * (1.0 + boost))
        gates_ref[0, h : h + 1, :] = d_boost * base_ref[h]
        extra_ref[h, HS : HS + 1, :] = dgain_ref[h : h + 1, :]
        extra_ref[h, HS + 1 : HS + 2, :] = jnp.broadcast_to(
            jnp.sum(d_boost * gate_ref[0, h : h + 1, :], axis=1, keepdims=True), (1, HS)
        )


VM = pl.BlockSpec(memory_space=pltpu.VMEM)
SM = pl.BlockSpec(memory_space=pltpu.SMEM)
PARAMS = pltpu.CompilerParams(vmem_limit_bytes=48 * 1024 * 1024)


def shape(*dims, dtype=F32):
    return jax.ShapeDtypeStruct(dims, dtype)


def whole(kernel, outs, specs):
    return pl.pallas_call(
        kernel,
        out_shape=outs,
        in_specs=specs,
        out_specs=jax.tree.map(lambda _: VM, outs),
        compiler_params=PARAMS,
    )


def part(which, dims):
    return pl.BlockSpec((1,) + dims, lambda i: (which, 0, 0))


def full(*dims):
    return pl.BlockSpec(dims, lambda i: (0,) * len(dims))


def body(tokens, proj_weights, init_weight, base_rates, gate_values, out_gain, cotangent):
    n = tokens.shape[1]
    model = tokens.shape[2]
    heads = init_weight.shape[0]
    wide = heads * HS
    ctx = lax.axis_index("ctx")
    ctx_arr = ctx.astype(jnp.int32).reshape(1)

    wide_f32 = shape(n, wide)
    square = shape(heads, n, n)
    small = shape(heads, HS, HS)
    wspec = functools.partial(part, dims=(model, wide))

    k, v, ninv, gram, inv, bt, decay, send, offset = pl.pallas_call(
        maps_kernel,
        grid=(1,),
        out_shape=(wide_f32, wide_f32, shape(heads, n, HS), square, square, shape(heads, HS, n), small, small, small),
        in_specs=[SM, SM, full(1, n, model), wspec(1), wspec(2), full(1, heads, n), full(heads, HS, HS)],
        out_specs=(
            full(n, wide), full(n, wide), full(heads, n, HS), full(heads, n, n), full(heads, n, n),
            full(heads, HS, n), full(heads, HS, HS), full(heads, HS, HS), full(heads, HS, HS),
        ),
        compiler_params=PARAMS,
    )(ctx_arr, base_rates, tokens, proj_weights, proj_weights, gate_values, init_weight)

    near = lax.ppermute(send, "ctx", [(0, 1), (2, 3)])
    moved = lax.ppermute(decay, "ctx", [(2, 3), (1, 0)])

    q, score, rv, y, qt, zv = pl.pallas_call(
        reach_kernel,
        grid=(1,),
        out_shape=(wide_f32, square, wide_f32, wide_f32, wide_f32, wide_f32),
        in_specs=[SM, full(1, n, model), wspec(0), full(1, heads, n), full(n, wide), full(n, wide), full(heads, n, n)],
        out_specs=(full(n, wide), full(heads, n, n), full(n, wide), full(n, wide), full(n, wide), full(n, wide)),
        compiler_params=PARAMS,
    )(base_rates, tokens, proj_weights, gate_values, k, v, inv)

    second = whole(functools.partial(step_kernel, transposed=False), small, [VM] * 3)(decay, near, offset)
    mid = lax.ppermute(second, "ctx", [(1, 2)])
    far = lax.ppermute(second, "ctx", [(1, 3)])

    w, back, pulled, dgain = whole(
        norm_kernel, (small, wide_f32, small, shape(heads, HS)), [SM] + [VM] * 9
    )(ctx_arr, init_weight, near, mid, far, moved, qt, zv, cotangent, out_gain)

    back_near = lax.ppermute(pulled, "ctx", [(3, 2), (1, 0)])

    dq, r, x, dk, de = whole(
        query_kernel,
        (shape(n, wide, dtype=BF), wide_f32, wide_f32, wide_f32, shape(heads, n)),
        [SM] + [VM] * 10,
    )(base_rates, gate_values, w, back, cotangent, q, score, rv, y, k, inv)

    back_second = whole(functools.partial(step_kernel, transposed=True), small, [VM] * 3)(decay, back_near, pulled)
    back_mid = lax.ppermute(back_second, "ctx", [(2, 1)])
    back_far = lax.ppermute(back_second, "ctx", [(2, 0)])

    dkraw, dv, grad_gates, extra = whole(
        keys_kernel,
        (shape(n, wide, dtype=BF), shape(n, wide, dtype=BF), shape(1, heads, n), shape(heads, HS + 8, HS)),
        [SM, SM] + [VM] * 17,
    )(ctx_arr, base_rates, gate_values, back_near, back_mid, back_far, moved, pulled, decay, w, k, ninv, gram, bt, r, x,
      dk, de, dgain)

    flat = tokens[0]
    local = jnp.concatenate([dq, dkraw, dv], axis=1)
    proj_terms = jnp.stack(
        [
            lax.dot_general(flat, d, (((0,), (0,)), ((), ())), preferred_element_type=F32)
            for d in (dq, dkraw, dv)
        ]
    )
    grad_proj, extra = lax.psum((proj_terms, extra), ("dp", "ctx"))
    weights = jnp.concatenate([proj_weights[0], proj_weights[1], proj_weights[2]], axis=1)
    summed = lax.dot_general(weights, local, (((1,), (1,)), ((), ())), preferred_element_type=F32)
    token_rows = lax.psum_scatter(summed, "head", scatter_dimension=0, tiled=True)
    grad_tokens = token_rows.T.astype(BF).reshape(1, n, -1)
    return (grad_tokens, grad_proj, extra[:, :HS], extra[:, HS], extra[:, HS + 1, 0], grad_gates)


def solution(mesh):
    in_specs = (
        P("dp", "ctx", None),
        P(None, None, "head"),
        P("head", None, None),
        P("head"),
        P("dp", "head", "ctx"),
        P("head", None),
        P("dp", "ctx", "head"),
    )
    out_specs = (
        P("dp", "ctx", "head"),
        P(None, None, "head"),
        P("head", None, None),
        P("head", None),
        P("head"),
        P("dp", "head", "ctx"),
    )
    return jax.shard_map(body, mesh=mesh, in_specs=in_specs, out_specs=out_specs, check_vma=False)
```

profile of v0, /device:TPU:1, one launch (start us, length us, event | category | flops | bytes accessed | tf_op | source)
XLA Modules:
  0.0 196.0 jit_solution(2915914068232719658)
XLA Ops:
  8.0 0.0 all-reduce.3.cloned.1.call-start
  8.0 0.0 copy-start
  8.1 1.2 copy-done
  9.3 0.9 copy-done.2
  10.2 0.7 copy-done.5
  10.9 0.7 copy-done.6
  11.5 5.4 %shard_map.118 = (f32[256,256]{1,0:T(8,128)S(1)}, f32[256,256]{1,0:T(8,128)S(1)}, f32[2,256,128]{2,1,0:T(8,128)S(1)}, f32[2,256,256]{2,1,0:T(8,128)S(1)}, f32[2,...) custom-call(s32[1]{0:T(128)} %bitcast.3.ctx_ref, ...), custom_call_target="tpu_custom_call" | custom-call | tf_op jit(solution)/shard_map/pallas_call | solution.py:277
  16.9 0.0 copy-start.3
  17.0 0.0 copy-start.4
  17.0 0.0 copy-start.8
  17.0 4.2 %collective-permute-start = (f32[2,128,128]{2,1,0:T(8,128)S(1)}, f32[2,128,128]{2,1,0:T(8,128)S(1)}, u32[]{:S(2)}, u32[]{:S(2)}) collective-permute-start(f32[2,128,128]{2,1,0:T(8,128)S(1)} %get-tuple-element.34), channel_id=1, source_target_pairs={{0,4},{8,12},{1,5},{9,13},{2,6},{10,14},{3,7},{11,15},{16,20},{24,... | collective-permute-start | bytes 393224 | tf_op jit(solution)/shard_map/ppermute | solution.py:289
  21.2 1.3 collective-permute-start.3
  22.5 0.9 collective-permute-done.w_ref.near_ref
  23.3 0.2 shard_map.119
  23.5 0.7 collective-permute-start.1
  24.2 0.7 collective-permute-start.2
  24.9 0.0 copy-done.1
  24.9 3.6 %shard_map.120 = (f32[256,256]{1,0:T(8,128)S(1)}, f32[2,256,256]{2,1,0:T(8,128)S(1)}, f32[256,256]{1,0:T(8,128)S(1)}, f32[256,256]{1,0:T(8,128)S(1)}, f32[256,256]{1,0:T(8,128)S(1)}, /*index=5*/f32[256,256]{1,0:T(8,128)S(1)}) custom-call(f32[2]{0:T(128)S(1)} %copy-done.7, bf16[1,256,2048]{2,1,0:T(8,128)(2,1)S(1)} %copy-done.1, bf16[3,2048,256]{2,1,0:T(8,128)(2,1)} %wq_ref.1, ...), custom_call_target="tpu_custom_call" | custom-call | tf_op jit(solution)/shard_map/pallas_call | solution.py:292
  28.5 0.0 collective-permute-done.3.rd_ref
  28.5 0.0 collective-permute-done.1.mid_ref
  28.5 0.0 collective-permute-done.2.far_ref
  28.5 1.6 shard_map.121
  30.1 1.3 collective-permute-start.4
  31.4 2.9 %shard_map.122 = (bf16[256,256]{1,0:T(8,128)(2,1)S(1)}, f32[256,256]{1,0:T(8,128)S(1)}, f32[256,256]{1,0:T(8,128)S(1)}, f32[256,256]{1,0:T(8,128)S(1)}, f32[2,256]{1,0:T(2,128)S(1)}) custom-call(f32[2]{0:T(128)S(1)} %copy-done.7, f32[1,2,256]{2,1,0:T(2,128)S(1)} %copy-done.5, f32[2,128,128]{2,1,0:T(8,128)S(1)} %get-tuple-element.42.w_ref, ...), custom_call_target="tpu_custom_call" | custom-call | tf_op jit(solution)/shard_map/pallas_call | solution.py:311
  34.3 4.9 %collective-permute-done.4.w_ref.rp_ref = f32[2,128,128]{2,1,0:T(8,128)S(1)} collective-permute-done((f32[2,128,128]{2,1,0:T(8,128)S(1)}, f32[2,128,128]{2,1,0:T(8,128)S(1)}, u32[]{:S(2)}, u32[]{:S(2)}) %collective-permute-start.4) | collective-permute-done | bytes 131104 | tf_op jit(solution)/shard_map/ppermute | solution.py:309
  39.2 0.2 shard_map.123
  39.4 0.7 collective-permute-start.5
  40.1 1.3 collective-permute-start.6
  41.4 0.5 convolution_bitcast_fusion.2
  41.9 0.0 collective-permute-done.5.mid_ref
  41.9 5.4 %collective-permute-done.6.far_ref = f32[2,128,128]{2,1,0:T(8,128)S(1)} collective-permute-done((f32[2,128,128]{2,1,0:T(8,128)S(1)}, f32[2,128,128]{2,1,0:T(8,128)S(1)}, u32[]{:S(2)}, u32[]{:S(2)}) %collective-permute-start.6) | collective-permute-done | bytes 131104 | tf_op jit(solution)/shard_map/ppermute | solution.py:319
  47.3 3.5 %shard_map.124 = (bf16[256,256]{1,0:T(8,128)(2,1)S(1)}, bf16[256,256]{1,0:T(8,128)(2,1)S(1)}, f32[1,2,256]{2,1,0:T(2,128)}, f32[2,136,128]{2,1,0:T(8,128)}) custom-call(s32[1]{0:T(128)} %bitcast.3.ctx_ref, f32[2]{0:T(128)S(1)} %copy-done.7, f32[1,2,256]{2,1,0:T(2,128)S(1)} %copy-done.5, f32[2,128,128]{2,1,0:T(8,128)S(1)} %collective-permute-done.4.w_ref.rp_ref, ...), custom_call_target="tpu_custom_call" | custom-call | tf_op jit(solution)/shard_map/pallas_call | solution.py:321
  50.9 0.5 convolution_bitcast_fusion
  51.3 0.5 convolution_bitcast_fusion.1
  51.8 3.1 %pad_maximum_fusion = f32[3,2048,256]{1,2,0:T(8,128)} fusion(f32[1,2048,256]{1,2,0:T(8,128)S(1)} %convolution_bitcast_fusion, f32[1,2048,256]{1,2,0:T(8,128)S(1)} %convolution_bitcast_fusion.1, f32[1,2048,256]{1,2,0:T(8,128)S(1)} %convolution_bitcast_fusion.2), kind=kLoop, calls=%fused_computation | loop fusion | flops 3145728 | bytes 12582912 | tf_op jit(solution)/shard_map/stack | solution.py:330
  54.9 0.0 all-reduce.3.cloned.1.call-update
  54.9 0.0 reduce-scatter.2.cloned.1.call-start
  55.0 1.8 copy-done.9
  56.8 0.2 slice_bitcast_fusion.2
  57.0 2.4 %fusion = f32[2048,256]{1,0:T(8,128)} fusion(bf16[2048,256]{1,0:T(8,128)(2,1)S(1)} %get-tuple-element.77, bf16[2048,256]{1,0:T(8,128)(2,1)S(1)} %get-tuple-element.78, bf16[2048,256]{1,0:T(8,128)(2,1)S(1)} %get-tuple-element.76, bf16[256,256]{1,0:T(8,128)(2,1)S(1)} %get-tuple-element.59, bf16[256,256]{1,0:T(8,128)(2,1)S(1)} %get-tuple-element.58, ...), kind=kOutput, calls=%fused_computation.1 | convolution fusion | flops 815923200 | bytes 5636096 | tf_op jit(solution)/shard_map/dot_general | solution.py:338
  59.4 0.0 reduce-scatter.2.cloned.1.call-update
  59.4 116.5 %all-reduce.3.cloned.1.call-done = (f32[3,2048,256]{1,2,0:T(8,128)}, f32[2,136,128]{2,1,0:T(8,128)}) async-done(((f32[3,2048,256]{1,2,0:T(8,128)}, f32[2,136,128]{2,1,0:T(8,128)}), (f32[3,2048,256]{1,2,0:T(8,128)}, f32[2,136,128]{2,1,0:T(8,128)})) %all-reduce.3.cloned.1.call-update) | async-done | bytes 6430736 | tf_op jit(solution)/shard_map/psum | solution.py:336
  175.9 1.6 slice.24
  177.5 1.3 slice.25
  178.8 6.6 %copy.16 = f32[3,2048,256]{2,1,0:T(8,128)} copy(f32[3,2048,256]{1,2,0:T(8,128)} %get-tuple-element.74) | data formatting | bytes 12582912
  185.3 1.3 slice_reduce_fusion
  186.6 1.1 convert_bitcast_fusion
  187.7 0.8 copy.15
  (11 shorter events, 0.0 us)
Async XLA Ops:
  8.0 167.9 %all-reduce.3.cloned.1.call-start = ((), (), s32[]{:S(2)}) async-start(), calls=%async_computation.2 | async-start | bytes 12861440 | tf_op jit(solution)/shard_map/psum | solution.py:336
  8.0 1.2 copy-start
  9.3 0.9 copy-start.2
  10.2 0.7 copy-start.5
  10.9 0.7 copy-start.6
  11.5 13.4 %copy-start.1 = (bf16[1,256,2048]{2,1,0:T(8,128)(2,1)S(1)}, bf16[1,256,2048]{2,1,0:T(8,128)(2,1)}, u32[]{:S(2)}) copy-start(bf16[1,256,2048]{2,1,0:T(8,128)(2,1)} %tok_ref.3) | copy-start | bytes 3145732
  11.5 13.4 %copy-start.7 = (f32[2]{0:T(128)S(1)}, f32[2]{0:T(128)}, u32[]{:S(2)}) copy-start(f32[2]{0:T(128)} %base_ref.7) | copy-start | bytes 28
  16.9 11.6 %copy-start.3 = (f32[2,128,128]{2,1,0:T(8,128)S(1)}, f32[2,128,128]{2,1,0:T(8,128)}, u32[]{:S(2)}) copy-start(f32[2,128,128]{2,1,0:T(8,128)} %init_ref.3) | copy-start | bytes 393220
  17.0 11.6 %copy-start.4 = (bf16[1,256,256]{2,1,0:T(8,128)(2,1)S(1)}, bf16[1,256,256]{2,1,0:T(8,128)(2,1)}, u32[]{:S(2)}) copy-start(bf16[1,256,256]{2,1,0:T(8,128)(2,1)} %up_ref.3) | copy-start | bytes 393220
  17.0 11.6 %copy-start.8 = (f32[2,128]{1,0:T(2,128)S(1)}, f32[2,128]{1,0:T(2,128)}, u32[]{:S(2)}) copy-start(f32[2,128]{1,0:T(2,128)} %gain_ref.1) | copy-start | bytes 3076
  17.0 6.3 %collective-permute-start = (f32[2,128,128]{2,1,0:T(8,128)S(1)}, f32[2,128,128]{2,1,0:T(8,128)S(1)}, u32[]{:S(2)}, u32[]{:S(2)}) collective-permute-start(f32[2,128,128]{2,1,0:T(8,128)S(1)} %get-tuple-element.34), channel_id=1, source_target_pairs={{0,4},{8,12},{1,5},{9,13},{2,6},{10,14},{3,7},{11,15},{16,20},{24,... | collective-permute-start | bytes 393224 | tf_op jit(solution)/shard_map/ppermute | solution.py:289
  21.2 7.3 %collective-permute-start.3 = (f32[2,128,128]{2,1,0:T(8,128)S(1)}, f32[2,128,128]{2,1,0:T(8,128)S(1)}, u32[]{:S(2)}, u32[]{:S(2)}) collective-permute-start(f32[2,128,128]{2,1,0:T(8,128)S(1)} %get-tuple-element.35.d_ref), channel_id=1, source_target_pairs={{8,12},{4,0},{9,13},{5,1},{10,14},{6,2},{11,15},{7,3},{24,28},{20,... | collective-permute-start | bytes 393224 | tf_op jit(solution)/shard_map/ppermute | solution.py:290
  23.5 5.0 %collective-permute-start.1 = (f32[2,128,128]{2,1,0:T(8,128)S(1)}, f32[2,128,128]{2,1,0:T(8,128)S(1)}, u32[]{:S(2)}, u32[]{:S(2)}) collective-permute-start(f32[2,128,128]{2,1,0:T(8,128)S(1)} %shard_map.119), channel_id=1, source_target_pairs={{4,8},{5,9},{6,10},{7,11},{20,24},{21,25},{22,26},{23,27},{36,40},... | collective-permute-start | bytes 393224 | tf_op jit(solution)/shard_map/ppermute | solution.py:302
  24.2 4.3 %collective-permute-start.2 = (f32[2,128,128]{2,1,0:T(8,128)S(1)}, f32[2,128,128]{2,1,0:T(8,128)S(1)}, u32[]{:S(2)}, u32[]{:S(2)}) collective-permute-start(f32[2,128,128]{2,1,0:T(8,128)S(1)} %shard_map.119), channel_id=1, source_target_pairs={{4,12},{5,13},{6,14},{7,15},{20,28},{21,29},{22,30},{23,31},{36,44... | collective-permute-start | bytes 393224 | tf_op jit(solution)/shard_map/ppermute | solution.py:303
  30.1 9.0 %collective-permute-start.4 = (f32[2,128,128]{2,1,0:T(8,128)S(1)}, f32[2,128,128]{2,1,0:T(8,128)S(1)}, u32[]{:S(2)}, u32[]{:S(2)}) collective-permute-start(f32[2,128,128]{2,1,0:T(8,128)S(1)} %get-tuple-element.49.o_ref.p_ref), channel_id=1, source_target_pairs={{12,8},{4,0},{13,9},{5,1},{14,10},{6,2},{15,11},{7,3},{28,24},{20,... | collective-permute-start | bytes 393224 | tf_op jit(solution)/shard_map/ppermute | solution.py:309
  39.4 2.4 %collective-permute-start.5 = (f32[2,128,128]{2,1,0:T(8,128)S(1)}, f32[2,128,128]{2,1,0:T(8,128)S(1)}, u32[]{:S(2)}, u32[]{:S(2)}) collective-permute-start(f32[2,128,128]{2,1,0:T(8,128)S(1)} %shard_map.123), channel_id=1, source_target_pairs={{8,4},{9,5},{10,6},{11,7},{24,20},{25,21},{26,22},{27,23},{40,36},... | collective-permute-start | bytes 393224 | tf_op jit(solution)/shard_map/ppermute | solution.py:318
  40.1 7.2 %collective-permute-start.6 = (f32[2,128,128]{2,1,0:T(8,128)S(1)}, f32[2,128,128]{2,1,0:T(8,128)S(1)}, u32[]{:S(2)}, u32[]{:S(2)}) collective-permute-start(f32[2,128,128]{2,1,0:T(8,128)S(1)} %shard_map.123), channel_id=1, source_target_pairs={{8,0},{9,1},{10,2},{11,3},{24,16},{25,17},{26,18},{27,19},{40,32},... | collective-permute-start | bytes 393224 | tf_op jit(solution)/shard_map/ppermute | solution.py:319
  54.9 1.9 copy-start.9
  54.9 131.7 %reduce-scatter.2.cloned.1.call-start = ((), (), s32[]{:S(2)}) async-start(), calls=%async_computation.1 | async-start | bytes 2621440 | tf_op jit(solution)/shard_map/reduce_scatter | solution.py:339
Sparse Core Ops, SparseCore 0:
  55.1 120.8 all-reduce.2
Sparse Core Ops, SparseCore 1:
  59.5 33.8 reduce-scatter.1
where the time goes:
time: 197 us; the launch traced here: 196 us
  waiting for transfers between devices  128 us (65%)
  Pallas kernels  17.4 us (9%)
  local copies, waits for them, and re-layouts  17 us (9%)
  between operations  15.7 us (8%)
  starting transfers between devices  10.1 us (5%)
  other arithmetic  4.2 us (2%)
  matrix products  3.78 us (2%)
    psum x1, waiting for transfers between devices, body(): grad_proj, extra = lax.psum((proj_terms, extra), ('dp', 'ctx'))  117 us
    unnamed x22, local copies, waits for them, and re-layouts  12.7 us
    ppermute x1, waiting for transfers between devices, body(): back_far = lax.ppermute(back_second, 'ctx', [(2, 0)])  5.45 us
    pallas_call x1, Pallas kernels, body(): pl.pallas_call(maps_kernel, grid=(1,), out_shape=(wide_f32, wide_f32, sha...  5.41 us
    ppermute x1, waiting for transfers between devices, body(): back_near = lax.ppermute(pulled, 'ctx', [(3, 2), (1, 0)])  4.87 us
    ppermute x1, starting transfers between devices, body(): near = lax.ppermute(send, 'ctx', [(0, 1), (2, 3)])  4.18 us
  transfers between devices with their start and end apart: 9, of which 4 were waited for; matrix products, arithmetic and copies ran while one was open for 7% of the time, Pallas kernels for 3%

commit v1 on v0

--- a/solution.py
+++ b/solution.py
@@ -9,6 +9,11 @@
 
 MB = 16
 HS = 128
+RING = 4
+TURNS = (0, 1, 3, 2)
+CHUNK = 256
+PIECE = 24
+EXTRA = 2 * RING * PIECE
 F32 = jnp.float32
 BF = jnp.bfloat16
 NN = (((1,), (0,)), ((), ()))
@@ -186,7 +191,7 @@
         d_mix = jnp.where(i >= j, dot(back, r, NT, 3), 0.0)
         d_score = d_mix * e
         dq = up_ref[0, :, span(h)].astype(F32) + dot(back, w, NT, 3) + dot(d_score, k, NN, 3)
-        dq_ref[:, span(h)] = dq.astype(BF)
+        dq_ref[:, span(h)] = dq.astype(BF).astype(F32)
         x_ref[:, span(h)] = dot(inv_ref[h], dot(mix, back, TN, 3), TN, 3)
         dk_ref[:, span(h)] = dot(d_score, q, TN, 3)
         de_ref[h : h + 1, :] = jnp.sum(d_mix * score, axis=0, keepdims=True)
@@ -195,25 +200,25 @@
 def keys_kernel(
     ctx_ref, base_ref, gate_ref, rp_ref, mid_ref, far_ref, rd_ref, p_ref, d_ref, w_ref, k_ref, ninv_ref,
     gram_ref, bt_ref, r_ref, x_ref, dk_ref, de_ref, dgain_ref,
-    dkraw_ref, dv_ref, gates_ref, extra_ref,
+    dkraw_ref, dv_ref, gates_ref,
 ):
     ctx = ctx_ref[0]
     n = k_ref.shape[0]
     i, j = places(n)
     strict = (i // MB) > (j // MB)
-    extra_ref[...] = jnp.zeros_like(extra_ref)
+    dkraw_ref[n + HS : n + EXTRA, :] = jnp.zeros((EXTRA - HS, dkraw_ref.shape[1]), F32)
     for h in range(w_ref.shape[0]):
         first = rp_ref[h] + dot(rd_ref[h], far_ref[h], TN, 3)
         end = jnp.where(
             ctx == 0, first, jnp.where(ctx == 1, mid_ref[h], jnp.where(ctx == 2, rp_ref[h], 0.0))
         )
-        extra_ref[h, 0:HS, :] = jnp.where(ctx == 0, p_ref[h] + dot(d_ref[h], end, TN, 3), 0.0)
+        dkraw_ref[n : n + HS, span(h)] = jnp.where(ctx == 0, p_ref[h] + dot(d_ref[h], end, TN, 3), 0.0)
         w = w_ref[h]
         k = k_ref[:, span(h)]
         r = r_ref[:, span(h)]
         boost, e = rates_of(base_ref, gate_ref, h)
         x = x_ref[:, span(h)] + dot(bt_ref[h], end, TN, 3)
-        dv_ref[:, span(h)] = x.astype(BF)
+        dv_ref[:, span(h)] = x.astype(BF).astype(F32)
         d_low = jnp.where(strict, -dot(x, r, NT, 3), 0.0)
         d_gram = d_low * e
         dk = (
@@ -225,18 +230,114 @@
         pull = to_row(jnp.sum(r * dot(k, end, NN, 3), axis=1, keepdims=True))
         de = de_ref[h : h + 1, :] + jnp.sum(d_low * gram_ref[h], axis=0, keepdims=True) + pull
         draw = ninv_ref[h] * (dk - k * jnp.sum(k * dk, -1, keepdims=True))
-        dkraw_ref[:, span(h)] = draw.astype(BF)
+        dkraw_ref[0:n, span(h)] = draw.astype(BF).astype(F32)
         d_boost = de / ((1.0 + boost) * (1.0 + boost))
         gates_ref[0, h : h + 1, :] = d_boost * base_ref[h]
-        extra_ref[h, HS : HS + 1, :] = dgain_ref[h : h + 1, :]
-        extra_ref[h, HS + 1 : HS + 2, :] = jnp.broadcast_to(
+        dkraw_ref[n + HS : n + HS + 1, span(h)] = dgain_ref[h : h + 1, :]
+        dkraw_ref[n + HS + 1 : n + HS + 2, span(h)] = jnp.broadcast_to(
             jnp.sum(d_boost * gate_ref[0, h : h + 1, :], axis=1, keepdims=True), (1, HS)
         )
+
+
+def turn_kernel(own_ref, other_ref, out_ref):
+    n = own_ref.shape[0]
+    out_ref[:, 0:n] = own_ref[...].T.astype(BF)
+    out_ref[:, n : 2 * n] = other_ref[...].T.astype(BF)
+
+
+def product_kernel(pos_ref, tokt_ref, own_ref, other_ref, *out_refs):
+    n = tokt_ref.shape[1] // 2
+    d = jnp.concatenate([own_ref[0:n, :], other_ref[0:n, :]], axis=0).astype(BF)
+    for turn, out_ref in zip(TURNS, out_refs):
+        at = (pos_ref[1] + turn) & (RING - 1)
+        rows = pl.ds(pl.multiple_of(at * CHUNK, CHUNK), CHUNK)
+        out_ref[0:CHUNK, :] = jnp.dot(tokt_ref[rows, :], d, preferred_element_type=F32)
+        if own_ref.shape[0] > n:
+            extra = pl.ds(pl.multiple_of(n + (pos_ref[0] * RING + at) * PIECE, 8), PIECE)
+            out_ref[CHUNK : CHUNK + PIECE, :] = own_ref[extra, :] + other_ref[extra, :]
+
+
+def token_kernel(pos_ref, w_ref, dq_ref, dk_ref, dv_ref, *out_refs):
+    n = dq_ref.shape[0]
+    ds = [dq_ref[...].astype(BF), dk_ref[0:n, :].astype(BF), dv_ref[...].astype(BF)]
+    span_rows = w_ref.shape[1] // RING
+    for turn, out_ref in zip(TURNS, out_refs):
+        at = (pos_ref[3] + turn) & (RING - 1)
+        rows = pl.ds(pl.multiple_of(at * span_rows, span_rows), span_rows)
+        total = lax.dot_general(ds[0], w_ref[0, rows, :], NT, preferred_element_type=F32)
+        total = total + lax.dot_general(ds[1], w_ref[1, rows, :], NT, preferred_element_type=F32)
+        out_ref[...] = total + lax.dot_general(ds[2], w_ref[2, rows, :], NT, preferred_element_type=F32)
+
+
+def place_kernel(pos_ref, *refs):
+    pieces = [refs[8 * s : 8 * s + 8] for s in range(3)]
+    out_ref, init_ref, gain_ref, rates_ref, extra_ref, sem, extra_sem = refs[24:]
+    copies = []
+    for s in range(3):
+        for m in range(8):
+            half, turn = m // RING, TURNS[m % RING]
+            core = pos_ref[0] if half == 0 else 1 - pos_ref[0]
+            at = core * RING + ((pos_ref[1 + half] + turn) & (RING - 1))
+            rows = pl.ds(pl.multiple_of(at * CHUNK, CHUNK), CHUNK)
+            copies.append(
+                pltpu.make_async_copy(pieces[s][m].at[pl.ds(0, CHUNK), :], out_ref.at[s, rows, :], sem.at[s, m])
+            )
+            if s == 1:
+                rows = pl.ds(pl.multiple_of(at * PIECE, 8), PIECE)
+                copies.append(
+                    pltpu.make_async_copy(
+                        pieces[s][m].at[pl.ds(CHUNK, PIECE), :], extra_ref.at[rows, :], extra_sem.at[m]
+                    )
+                )
+    for copy in copies:
+        copy.start()
+    for copy in copies:
+        copy.wait()
+    for h in range(init_ref.shape[0]):
+        init_ref[h] = extra_ref[0:HS, span(h)]
+        gain_ref[h : h + 1, :] = extra_ref[HS : HS + 1, span(h)]
+        rates_ref[h : h + 1, :] = extra_ref[HS + 1 : HS + 2, span(h)]
+
+
+def moves(first, by):
+    pairs = []
+    for x in range(RING):
+        for core in range(2):
+            for y in range(RING):
+                along_x = (core == 0) == first
+                to_x = (x + by) % RING if along_x else x
+                to_y = y if along_x else (y + by) % RING
+                pairs.append(((x * 2 + core) * RING + y, (to_x * 2 + core) * RING + to_y))
+    return pairs
+
+
+def round_turn(chunks, first):
+    return [
+        lax.ppermute(chunk, ("dp", "ctx"), moves(first, turn)) for chunk, turn in zip(chunks, TURNS[1:])
+    ]
+
+
+def swap(value):
+    return lax.ppermute(value, "dp", [(i, i ^ 1) for i in range(2 * RING)])
+
+
+def reduce_stream(pos, tokt, d):
+    other = swap(d)
+    rows = CHUNK + (PIECE if d.shape[0] > CHUNK else 0)
+    piece = shape(rows, d.shape[1])
+    own, *away = whole(product_kernel, (piece,) * RING, [SM] + [VM] * 3)(pos, tokt, d, other)
+    from_back, from_ahead, from_far = round_turn(away, True)
+    part_sum = (own + from_far) + (from_back + from_ahead)
+    from_back, from_ahead, from_far = round_turn([part_sum] * 3, False)
+    total = (part_sum + from_far) + (from_back + from_ahead)
+    from_back, from_ahead, from_far = round_turn([total] * 3, True)
+    mine = [total, from_ahead, from_back, from_far]
+    return mine + [swap(piece) for piece in mine]
 
 
 VM = pl.BlockSpec(memory_space=pltpu.VMEM)
 SM = pl.BlockSpec(memory_space=pltpu.SMEM)
-PARAMS = pltpu.CompilerParams(vmem_limit_bytes=48 * 1024 * 1024)
+PARAMS = pltpu.CompilerParams(vmem_limit_bytes=32 * 1024 * 1024)
 
 
 def shape(*dims, dtype=F32):
@@ -268,6 +369,15 @@
     wide = heads * HS
     ctx = lax.axis_index("ctx")
     ctx_arr = ctx.astype(jnp.int32).reshape(1)
+    dp = lax.axis_index("dp")
+    core, x_at = dp % 2, dp // 2
+    pos = jnp.stack(
+        [core, jnp.where(core == 0, x_at, ctx), jnp.where(core == 0, ctx, x_at), lax.axis_index("head")]
+    ).astype(jnp.int32)
+    half = model // 2
+    own_half = lax.dynamic_slice_in_dim(tokens[0], core * half, half, 1).astype(F32)
+    other_half = lax.dynamic_slice_in_dim(tokens[0], (1 - core) * half, half, 1).astype(F32)
+    got_half = swap(other_half)
 
     wide_f32 = shape(n, wide)
     square = shape(heads, n, n)
@@ -310,7 +420,7 @@
 
     dq, r, x, dk, de = whole(
         query_kernel,
-        (shape(n, wide, dtype=BF), wide_f32, wide_f32, wide_f32, shape(heads, n)),
+        (wide_f32, wide_f32, wide_f32, wide_f32, shape(heads, n)),
         [SM] + [VM] * 10,
     )(base_rates, gate_values, w, back, cotangent, q, score, rv, y, k, inv)
 
@@ -318,27 +428,38 @@
     back_mid = lax.ppermute(back_second, "ctx", [(2, 1)])
     back_far = lax.ppermute(back_second, "ctx", [(2, 0)])
 
-    dkraw, dv, grad_gates, extra = whole(
+    dkraw, dv, grad_gates = whole(
         keys_kernel,
-        (shape(n, wide, dtype=BF), shape(n, wide, dtype=BF), shape(1, heads, n), shape(heads, HS + 8, HS)),
+        (shape(n + EXTRA, wide), wide_f32, shape(1, heads, n)),
         [SM, SM] + [VM] * 17,
     )(ctx_arr, base_rates, gate_values, back_near, back_mid, back_far, moved, pulled, decay, w, k, ninv, gram, bt, r, x,
       dk, de, dgain)
 
-    flat = tokens[0]
-    local = jnp.concatenate([dq, dkraw, dv], axis=1)
-    proj_terms = jnp.stack(
-        [
-            lax.dot_general(flat, d, (((0,), (0,)), ((), ())), preferred_element_type=F32)
-            for d in (dq, dkraw, dv)
-        ]
-    )
-    grad_proj, extra = lax.psum((proj_terms, extra), ("dp", "ctx"))
-    weights = jnp.concatenate([proj_weights[0], proj_weights[1], proj_weights[2]], axis=1)
-    summed = lax.dot_general(weights, local, (((1,), (1,)), ((), ())), preferred_element_type=F32)
-    token_rows = lax.psum_scatter(summed, "head", scatter_dimension=0, tiled=True)
-    grad_tokens = token_rows.T.astype(BF).reshape(1, n, -1)
-    return (grad_tokens, grad_proj, extra[:, :HS], extra[:, HS], extra[:, HS + 1, 0], grad_gates)
+    tokt = whole(turn_kernel, shape(half, 2 * n, dtype=BF), [VM] * 2)(own_half, got_half)
+    query_pieces = reduce_stream(pos, tokt, dq)
+    value_pieces = reduce_stream(pos, tokt, dv)
+    key_pieces = reduce_stream(pos, tokt, dkraw)
+
+    quarter = shape(n, model // RING)
+    own, *away = whole(token_kernel, (quarter,) * RING, [SM] + [VM] * 4)(pos, proj_weights, dq, dkraw, dv)
+    from_back, from_ahead, from_far = [
+        lax.ppermute(chunk, "head", [(i, (i + turn) % RING) for i in range(RING)])
+        for chunk, turn in zip(away, TURNS[1:])
+    ]
+    grad_tokens = ((own + from_far) + (from_back + from_ahead)).astype(BF).reshape(1, n, -1)
+
+    anywhere = pl.BlockSpec(memory_space=pl.ANY)
+    grad_proj, grad_init, grad_gain, rates = pl.pallas_call(
+        place_kernel,
+        out_shape=(shape(3, model, wide), small, shape(heads, HS), shape(heads, HS)),
+        in_specs=[SM] + [anywhere] * 24,
+        out_specs=(anywhere, VM, VM, VM),
+        scratch_shapes=[
+            pltpu.VMEM((EXTRA, wide), F32), pltpu.SemaphoreType.DMA((3, 8)), pltpu.SemaphoreType.DMA((8,))
+        ],
+        compiler_params=PARAMS,
+    )(pos, *query_pieces, *key_pieces, *value_pieces)
+    return (grad_tokens, grad_proj, grad_init, grad_gain, rates[:, 0], grad_gates)
 
 
 def solution(mesh):

time: 197 us -> 169 us (0.86)
  waiting for transfers between devices: 128 us -> 29.8 us
  starting transfers between devices: 10.1 us -> 83.3 us
  between operations: 15.7 us -> 1.14 us
  Pallas kernels: 17.4 us -> 26.6 us
  local copies, waits for them, and re-layouts: 17 us -> 23 us
  matrix products: 3.78 us -> 0 us
    psum x1 -> x0, waiting for transfers between devices: 117 us -> none  [body(): grad_proj, extra = lax.psum((proj_terms, extra), ('dp', 'ctx'))]
    ppermute x0 -> x46, starting transfers between devices: none -> 73.5 us  [the longest x27 35.9 us: round_turn(): lax.ppermute(chunk, ('dp', 'ctx'), moves(first, turn))]
    ppermute x0 -> x46, waiting for transfers between devices: none -> 20.4 us  [the longest x3 11 us: body(): lax.ppermute(chunk, 'head', [(i, (i + turn) % RING) for i in range(RING)])]
    pallas_call x2 -> x8, Pallas kernels: 6.4 us -> 16.8 us  [the longest x1 4.15 us: body(): pl.pallas_call(place_kernel, out_shape=(shape(3, model, wide), small, sha...]
    unnamed x22 -> x80, local copies, waits for them, and re-layouts: 12.7 us -> 22.4 us
    ppermute x1, waiting for transfers between devices: 5.45 us -> 0.01 us  [body(): back_far = lax.ppermute(back_second, 'ctx', [(2, 0)])]
    dot_general x4 -> x0, matrix products: 3.78 us -> none  [the longest x1 2.4 us: body(): lax.dot_general(weights, local, (((1,), (1,)), ((), ())), preferred_eleme...]
    slice x3 -> x1, local copies, waits for them, and re-layouts: 4.13 us -> 0.63 us  [body(): rates[:, 0]]
  transfers between devices with their start and end apart: 9 -> 53, of which waited for: 4 -> 12; matrix products, arithmetic and copies ran while one was open for 7% -> 1% of each run, Pallas kernels for 3% -> 13%
where the time goes in v1:
time: 169 us; the launch traced here: 168 us
  starting transfers between devices  83.3 us (49%)
  waiting for transfers between devices  29.8 us (18%)
  Pallas kernels  26.6 us (16%)
  local copies, waits for them, and re-layouts  23 us (14%)
  other arithmetic  4.33 us (3%)
    ppermute x27, starting transfers between devices, round_turn(): lax.ppermute(chunk, ('dp', 'ctx'), moves(first, turn))  35.9 us
    ppermute x16, starting transfers between devices, swap(): return lax.ppermute(value, 'dp', [(i, i ^ 1) for i in range(2 * RING)])  34.5 us
    unnamed x80, local copies, waits for them, and re-layouts  22.4 us
    ppermute x3, waiting for transfers between devices, body(): lax.ppermute(chunk, 'head', [(i, (i + turn) % RING) for i in range(RING)])  11 us
    ppermute x27, waiting for transfers between devices, round_turn(): lax.ppermute(chunk, ('dp', 'ctx'), moves(first, turn))  8.47 us
    ppermute x1, waiting for transfers between devices, body(): back_near = lax.ppermute(pulled, 'ctx', [(3, 2), (1, 0)])  7.81 us
    pallas_call x1, Pallas kernels, body(): pl.pallas_call(maps_kernel, grid=(1,), out_shape=(wide_f32, wide_f32, sha...  4.29 us
    pallas_call x1, Pallas kernels, body(): pl.pallas_call(place_kernel, out_shape=(shape(3, model, wide), small, sha...  4.15 us
  transfers between devices with their start and end apart: 53, of which 12 were waited for; matrix products, arithmetic and copies ran while one was open for 1% of the time, Pallas kernels for 13%

profile of v1, /device:TPU:1, one launch (start us, length us, event | category | flops | bytes accessed | tf_op | source)
XLA Modules:
  0.0 168.2 jit_solution(5146254822073178340)
XLA Ops:
  0.7 2.9 %bitcast_convert_fusion = (f32[256,1024]{1,0:T(8,128)}, f32[256,1024]{1,0:T(8,128)}) fusion(bf16[1,256,2048]{2,1,0:T(8,128)(2,1)} %tok_ref.3, s32[]{:T(128)S(6)} %select_n.28, s32[]{:T(128)S(6)} %select_n.27), kind=kLoop, calls=%fused_computation | loop fusion | flops 524288 | bytes 3145736 | tf_op jit(solution)/shard_map/convert_element_type | solution.py:379
  3.6 1.4 collective-permute-start.10
  5.0 1.9 %copy-done = bf16[3,2048,256]{2,1,0:T(8,128)(2,1)S(1)} copy-done((bf16[3,2048,256]{2,1,0:T(8,128)(2,1)S(1)}, bf16[3,2048,256]{2,1,0:T(8,128)(2,1)}, u32[]{:S(2)}) %copy-start) | copy-done | bytes 3145752
  6.9 1.2 copy-done.2
  10.4 4.3 %shard_map.118 = (f32[256,256]{1,0:T(8,128)S(1)}, f32[256,256]{1,0:T(8,128)S(1)}, f32[2,256,128]{2,1,0:T(8,128)S(1)}, f32[2,256,256]{2,1,0:T(8,128)S(1)}, f32[2,...) custom-call(s32[1]{0:T(128)} %bitcast.4.ctx_ref, ...), custom_call_target="tpu_custom_call" | custom-call | tf_op jit(solution)/shard_map/pallas_call | solution.py:387
  15.4 3.3 %collective-permute-start = (f32[2,128,128]{2,1,0:T(8,128)S(1)}, f32[2,128,128]{2,1,0:T(8,128)S(1)}, u32[]{:S(2)}, u32[]{:S(2)}) collective-permute-start(f32[2,128,128]{2,1,0:T(8,128)S(1)} %get-tuple-element.53), channel_id=1, source_target_pairs={{0,4},{8,12},{1,5},{9,13},{2,6},{10,14},{3,7},{11,15},{16,20},{24,... | collective-permute-start | bytes 393224 | tf_op jit(solution)/shard_map/ppermute | solution.py:399
  18.7 1.3 collective-permute-start.3
  20.0 1.6 collective-permute-done.w_ref.near_ref
  23.1 2.9 %shard_map.120 = (f32[256,256]{1,0:T(8,128)S(1)}, f32[2,256,256]{2,1,0:T(8,128)S(1)}, f32[256,256]{1,0:T(8,128)S(1)}, f32[256,256]{1,0:T(8,128)S(1)}, f32[256,256]{1,0:T(8,128)S(1)}, /*index=5*/f32[256,256]{1,0:T(8,128)S(1)}) custom-call(f32[2]{0:T(128)S(1)} %copy-done.37, bf16[1,256,2048]{2,1,0:T(8,128)(2,1)S(1)} %copy-done.3, ...), custom_call_target="tpu_custom_call" | custom-call | tf_op jit(solution)/shard_map/pallas_call | solution.py:402
  26.8 1.6 shard_map.121
  29.1 1.3 collective-permute-start.4
  30.3 7.8 %collective-permute-done.4.w_ref.rp_ref = f32[2,128,128]{2,1,0:T(8,128)S(1)} collective-permute-done((f32[2,128,128]{2,1,0:T(8,128)S(1)}, f32[2,128,128]{2,1,0:T(8,128)S(1)}, u32[]{:S(2)}, u32[]{:S(2)}) %collective-permute-start.4) | collective-permute-done | bytes 131104 | tf_op jit(solution)/shard_map/ppermute | solution.py:419
  39.7 1.3 collective-permute-start.5
  41.0 1.3 collective-permute-start.6
  42.5 1.1 copy-done.6
  50.2 2.8 %shard_map.122 = (f32[256,256]{1,0:T(8,128)S(1)}, f32[256,256]{1,0:T(8,128)S(1)}, f32[256,256]{1,0:T(8,128)S(1)}, f32[256,256]{1,0:T(8,128)S(1)}, f32[2,256]{1,0:T(2,128)S(1)}) custom-call(f32[2]{0:T(128)S(1)} %copy-done.38, f32[1,2,256]{2,1,0:T(2,128)S(1)} %copy-done.36, f32[2,128,128]{2,1,0:T(8,128)S(1)} %copy-done.13, f32[256,256]{1,0:T(8,128)S(1)} %copy-done.34, ...), custom_call_target="tpu_custom_call" | custom-call | tf_op jit(solution)/shard_map/pallas_call | solution.py:421
  53.1 2.6 %collective-permute-start.11 = (f32[256,256]{1,0:T(8,128)S(1)}, f32[256,256]{1,0:T(8,128)S(1)}, u32[]{:S(2)}, u32[]{:S(2)}) collective-permute-start(f32[256,256]{1,0:T(8,128)S(1)} %get-tuple-element.67.dq_ref.own_ref), channel_id=1, source_target_pairs={{0,16},{16,0},{32,48},{48,32},{64,80},{80,64},{96,112},{112,96},{1... | collective-permute-start | bytes 786440 | tf_op jit(solution)/shard_map/ppermute | solution.py:321
  62.2 3.7 %shard_map.124 = (f32[448,256]{1,0:T(8,128)S(1)}, f32[256,256]{1,0:T(8,128)S(1)}, f32[1,2,256]{2,1,0:T(2,128)}) custom-call(s32[1]{0:T(128)} %bitcast.4.ctx_ref, f32[2]{0:T(128)S(1)} %copy-done.38, f32[1,2,256]{2,1,0:T(2,128)S(1)} %copy-done.36, f32[2,128,128]{2,1,0:T(8,128)S(1)} %copy-done.18, f32[2,128,128]{2,1,0:T(8,128)} %collective-permute-done.5.mid_ref, ...), custom_call_target="tpu_custom_call" | custom-call | tf_op jit(solution)/shard_map/pallas_call | solution.py:431
  66.0 1.6 shard_map.125
  67.5 1.7 %collective-permute-start.8 = (f32[256,512]{1,0:T(8,128)S(1)}, f32[256,512]{1,0:T(8,128)S(1)}, u32[]{:S(2)}, u32[]{:S(2)}) collective-permute-start(f32[256,512]{1,0:T(8,128)S(1)} %get-tuple-element.81), channel_id=1, source_target_pairs={{0,1},{1,2},{2,3},{3,0},{4,5},{5,6},{6,7},{7,4},{8,9},{9,10},{10,1... | collective-permute-start | bytes 1572872 | tf_op jit(solution)/shard_map/ppermute | solution.py:446
  69.7 1.6 shard_map.126.tokt_ref
  72.4 2.7 %collective-permute-start.14 = (f32[256,256]{1,0:T(8,128)S(1)}, f32[256,256]{1,0:T(8,128)S(1)}, u32[]{:S(2)}, u32[]{:S(2)}) collective-permute-start(f32[256,256]{1,0:T(8,128)S(1)} %get-tuple-element.86), channel_id=1, source_target_pairs={{0,96},{4,100},{8,104},{12,108},{16,28},{20,16},{24,20},{28,24},{3... | collective-permute-start | bytes 786440 | tf_op jit(solution)/shard_map/ppermute | solution.py:316
  75.1 3.3 %collective-permute-start.12 = (f32[256,256]{1,0:T(8,128)S(1)}, f32[256,256]{1,0:T(8,128)S(1)}, u32[]{:S(2)}, u32[]{:S(2)}) collective-permute-start(f32[256,256]{1,0:T(8,128)S(1)} %get-tuple-element.84), channel_id=1, source_target_pairs={{0,64},{4,68},{8,72},{12,76},{16,24},{20,28},{24,16},{28,20},{32,9... | collective-permute-start | bytes 786440 | tf_op jit(solution)/shard_map/ppermute | solution.py:316
  79.4 4.2 %collective-permute-done.8 = f32[256,512]{1,0:T(8,128)S(1)} collective-permute-done((f32[256,512]{1,0:T(8,128)S(1)}, f32[256,512]{1,0:T(8,128)S(1)}, u32[]{:S(2)}, u32[]{:S(2)}) %collective-permute-start.8) | collective-permute-done | bytes 524320 | tf_op jit(solution)/shard_map/ppermute | solution.py:446
  83.6 1.2 collective-permute-start.42
  84.8 3.3 %collective-permute-start.40 = (f32[256,256]{1,0:T(8,128)S(1)}, f32[256,256]{1,0:T(8,128)S(1)}, u32[]{:S(2)}, u32[]{:S(2)}) collective-permute-start(f32[256,256]{1,0:T(8,128)S(1)} %get-tuple-element.92), channel_id=1, source_target_pairs={{0,64},{4,68},{8,72},{12,76},{16,24},{20,28},{24,16},{28,20},{32,9... | collective-permute-start | bytes 786440 | tf_op jit(solution)/shard_map/ppermute | solution.py:316
  88.1 1.3 collective-permute-start.9
  91.4 1.8 %collective-permute-start.28 = (f32[280,256]{1,0:T(8,128)S(1)}, f32[280,256]{1,0:T(8,128)S(1)}, u32[]{:S(2)}, u32[]{:S(2)}) collective-permute-start(f32[280,256]{1,0:T(8,128)S(1)} %get-tuple-element.90), channel_id=1, source_target_pairs={{0,96},{4,100},{8,104},{12,108},{16,28},{20,16},{24,20},{28,24},{3... | collective-permute-start | bytes 860168 | tf_op jit(solution)/shard_map/ppermute | solution.py:316
  93.2 1.7 %collective-permute-start.26 = (f32[280,256]{1,0:T(8,128)S(1)}, f32[280,256]{1,0:T(8,128)S(1)}, u32[]{:S(2)}, u32[]{:S(2)}) collective-permute-start(f32[280,256]{1,0:T(8,128)S(1)} %get-tuple-element.88), channel_id=1, source_target_pairs={{0,64},{4,68},{8,72},{12,76},{16,24},{20,28},{24,16},{28,20},{32,9... | collective-permute-start | bytes 860168 | tf_op jit(solution)/shard_map/ppermute | solution.py:316
  95.1 6.8 %collective-permute-done.9 = f32[256,512]{1,0:T(8,128)S(1)} collective-permute-done((f32[256,512]{1,0:T(8,128)S(1)}, f32[256,512]{1,0:T(8,128)S(1)}, u32[]{:S(2)}, u32[]{:S(2)}) %collective-permute-start.9) | collective-permute-done | bytes 524320 | tf_op jit(solution)/shard_map/ppermute | solution.py:446
  101.9 1.3 collective-permute-start.16
  103.2 1.4 collective-permute-start.17
  104.6 1.6 collective-permute-start.15
  107.4 1.2 collective-permute-done.16
  108.7 1.5 collective-permute-start.45
  110.1 1.2 collective-permute-start.43
  111.3 1.1 collective-permute-done.15
  112.4 1.4 collective-permute-start.31
  113.9 1.3 collective-permute-done.44
  116.7 4.4 %collective-permute-done.43 = f32[256,256]{1,0:T(8,128)S(1)} collective-permute-done((f32[256,256]{1,0:T(8,128)S(1)}, f32[256,256]{1,0:T(8,128)S(1)}, u32[]{:S(2)}, u32[]{:S(2)}) %collective-permute-start.43) | collective-permute-done | bytes 262176 | tf_op jit(solution)/shard_map/ppermute | solution.py:316
  122.6 16.6 %collective-permute-start.21 = (f32[256,256]{1,0:T(8,128)S(1)}, f32[256,256]{1,0:T(8,128)S(1)}, u32[]{:S(2)}, u32[]{:S(2)}) collective-permute-start(f32[256,256]{1,0:T(8,128)S(1)} %add_add_fusion.4.refs_0_), channel_id=1, source_target_pairs={{0,16},{16,0},{32,48},{48,32},{64,80},{80,64},{96,112},{112,96},{1... | collective-permute-start | bytes 786440 | tf_op jit(solution)/shard_map/ppermute | solution.py:321
  139.2 1.5 collective-permute-start.47
  140.7 3.2 %collective-permute-start.48 = (f32[256,256]{1,0:T(8,128)S(1)}, f32[256,256]{1,0:T(8,128)S(1)}, u32[]{:S(2)}, u32[]{:S(2)}) collective-permute-start(f32[256,256]{1,0:T(8,128)S(1)} %add_add_fusion.2.refs_16_), channel_id=1, source_target_pairs={{0,64},{4,68},{8,72},{12,76},{16,24},{20,28},{24,16},{28,20},{32,9... | collective-permute-start | bytes 786440 | tf_op jit(solution)/shard_map/ppermute | solution.py:316
  145.5 2.4 %collective-permute-start.34 = (f32[280,256]{1,0:T(8,128)S(1)}, f32[280,256]{1,0:T(8,128)S(1)}, u32[]{:S(2)}, u32[]{:S(2)}) collective-permute-start(f32[280,256]{1,0:T(8,128)S(1)} %add_add_fusion.refs_8_), channel_id=1, source_target_pairs={{0,64},{4,68},{8,72},{12,76},{16,24},{20,28},{24,16},{28,20},{32,9... | collective-permute-start | bytes 860168 | tf_op jit(solution)/shard_map/ppermute | solution.py:316
  147.9 2.5 %collective-permute-start.49 = (f32[256,256]{1,0:T(8,128)S(1)}, f32[256,256]{1,0:T(8,128)S(1)}, u32[]{:S(2)}, u32[]{:S(2)}) collective-permute-start(f32[256,256]{1,0:T(8,128)S(1)} %add_add_fusion.2.refs_16_), channel_id=1, source_target_pairs={{0,16},{16,0},{32,48},{48,32},{64,80},{80,64},{96,112},{112,96},{1... | collective-permute-start | bytes 786440 | tf_op jit(solution)/shard_map/ppermute | solution.py:321
  152.0 2.9 %collective-permute-start.23 = (f32[256,256]{1,0:T(8,128)S(1)}, f32[256,256]{1,0:T(8,128)S(1)}, u32[]{:S(2)}, u32[]{:S(2)}) collective-permute-start(f32[256,256]{1,0:T(8,128)S(1)} %collective-permute-done.19.refs_2_), channel_id=1, source_target_pairs={{0,16},{16,0},{32,48},{48,32},{64,80},{80,64},{96,112},{112,96},{1... | collective-permute-start | bytes 786440 | tf_op jit(solution)/shard_map/ppermute | solution.py:321
  154.9 5.0 %collective-permute-start.24 = (f32[256,256]{1,0:T(8,128)S(1)}, f32[256,256]{1,0:T(8,128)S(1)}, u32[]{:S(2)}, u32[]{:S(2)}) collective-permute-start(f32[256,256]{1,0:T(8,128)S(1)} %collective-permute-done.20.refs_3_), channel_id=1, source_target_pairs={{0,16},{16,0},{32,48},{48,32},{64,80},{80,64},{96,112},{112,96},{1... | collective-permute-start | bytes 786440 | tf_op jit(solution)/shard_map/ppermute | solution.py:321
  163.4 4.2 %shard_map.130 = (f32[3,2048,256]{2,1,0:T(8,128)}, f32[2,128,128]{2,1,0:T(8,128)}, f32[2,128]{1,0:T(2,128)}, f32[2,128]{1,0:T(2,128)S(1)}) custom-call(s32[4]{0:T(128)S(1)} %pad_add_fusion.pos_ref, f32[256,256]{1,0:T(8,128)S(1)} %add_add_fusion.4.refs_0_, f32[256,256]{1,0:T(8,128)S(1)} %collective-permute-done.18.refs_1_, ...), custom_call_target="tpu_custom_call" | custom-call | tf_op jit(solution)/shard_map/pallas_call | solution.py:452
  (161 shorter events, 37.0 us)
Async XLA Ops:
  3.6 66.2 %collective-permute-start.10 = (f32[256,1024]{1,0:T(8,128)}, f32[256,1024]{1,0:T(8,128)}, u32[]{:S(2)}, u32[]{:S(2)}) collective-permute-start(f32[256,1024]{1,0:T(8,128)} %get-tuple-element.100), channel_id=1, source_target_pairs={{0,16},{16,0},{32,48},{48,32},{64,80},{80,64},{96,112},{112,96},{1... | collective-permute-start | bytes 3145736 | tf_op jit(solution)/shard_map/ppermute | solution.py:321
  15.4 6.2 %collective-permute-start = (f32[2,128,128]{2,1,0:T(8,128)S(1)}, f32[2,128,128]{2,1,0:T(8,128)S(1)}, u32[]{:S(2)}, u32[]{:S(2)}) collective-permute-start(f32[2,128,128]{2,1,0:T(8,128)S(1)} %get-tuple-element.53), channel_id=1, source_target_pairs={{0,4},{8,12},{1,5},{9,13},{2,6},{10,14},{3,7},{11,15},{16,20},{24,... | collective-permute-start | bytes 393224 | tf_op jit(solution)/shard_map/ppermute | solution.py:399
  18.7 8.1 %collective-permute-start.3 = (f32[2,128,128]{2,1,0:T(8,128)S(1)}, f32[2,128,128]{2,1,0:T(8,128)S(1)}, u32[]{:S(2)}, u32[]{:S(2)}) collective-permute-start(f32[2,128,128]{2,1,0:T(8,128)S(1)} %get-tuple-element.54.d_ref), channel_id=1, source_target_pairs={{8,12},{4,0},{9,13},{5,1},{10,14},{6,2},{11,15},{7,3},{24,28},{20,... | collective-permute-start | bytes 393224 | tf_op jit(solution)/shard_map/ppermute | solution.py:400
  21.8 5.0 %collective-permute-start.1 = (f32[2,128,128]{2,1,0:T(8,128)S(1)}, f32[2,128,128]{2,1,0:T(8,128)S(1)}, u32[]{:S(2)}, u32[]{:S(2)}) collective-permute-start(f32[2,128,128]{2,1,0:T(8,128)S(1)} %shard_map.119), channel_id=1, source_target_pairs={{4,8},{5,9},{6,10},{7,11},{20,24},{21,25},{22,26},{23,27},{36,40},... | collective-permute-start | bytes 393224 | tf_op jit(solution)/shard_map/ppermute | solution.py:412
  22.4 4.3 %collective-permute-start.2 = (f32[2,128,128]{2,1,0:T(8,128)S(1)}, f32[2,128,128]{2,1,0:T(8,128)S(1)}, u32[]{:S(2)}, u32[]{:S(2)}) collective-permute-start(f32[2,128,128]{2,1,0:T(8,128)S(1)} %shard_map.119), channel_id=1, source_target_pairs={{4,12},{5,13},{6,14},{7,15},{20,28},{21,29},{22,30},{23,31},{36,44... | collective-permute-start | bytes 393224 | tf_op jit(solution)/shard_map/ppermute | solution.py:413
  29.1 9.1 %collective-permute-start.4 = (f32[2,128,128]{2,1,0:T(8,128)S(1)}, f32[2,128,128]{2,1,0:T(8,128)S(1)}, u32[]{:S(2)}, u32[]{:S(2)}) collective-permute-start(f32[2,128,128]{2,1,0:T(8,128)S(1)} %get-tuple-element.68.o_ref.p_ref), channel_id=1, source_target_pairs={{12,8},{4,0},{13,9},{5,1},{14,10},{6,2},{15,11},{7,3},{28,24},{20,... | collective-permute-start | bytes 393224 | tf_op jit(solution)/shard_map/ppermute | solution.py:419
  39.7 15.9 %collective-permute-start.5 = (f32[2,128,128]{2,1,0:T(8,128)}, f32[2,128,128]{2,1,0:T(8,128)}, u32[]{:S(2)}, u32[]{:S(2)}) collective-permute-start(f32[2,128,128]{2,1,0:T(8,128)} %shard_map.123), channel_id=1, source_target_pairs={{8,4},{9,5},{10,6},{11,7},{24,20},{25,21},{26,22},{27,23},{40,36},... | collective-permute-start | bytes 393224 | tf_op jit(solution)/shard_map/ppermute | solution.py:428
  41.0 14.6 %collective-permute-start.6 = (f32[2,128,128]{2,1,0:T(8,128)}, f32[2,128,128]{2,1,0:T(8,128)}, u32[]{:S(2)}, u32[]{:S(2)}) collective-permute-start(f32[2,128,128]{2,1,0:T(8,128)} %shard_map.123), channel_id=1, source_target_pairs={{8,0},{9,1},{10,2},{11,3},{24,16},{25,17},{26,18},{27,19},{40,32},... | collective-permute-start | bytes 393224 | tf_op jit(solution)/shard_map/ppermute | solution.py:429
  53.1 18.3 %collective-permute-start.11 = (f32[256,256]{1,0:T(8,128)S(1)}, f32[256,256]{1,0:T(8,128)S(1)}, u32[]{:S(2)}, u32[]{:S(2)}) collective-permute-start(f32[256,256]{1,0:T(8,128)S(1)} %get-tuple-element.67.dq_ref.own_ref), channel_id=1, source_target_pairs={{0,16},{16,0},{32,48},{48,32},{64,80},{80,64},{96,112},{112,96},{1... | collective-permute-start | bytes 786440 | tf_op jit(solution)/shard_map/ppermute | solution.py:321
  67.5 16.1 %collective-permute-start.8 = (f32[256,512]{1,0:T(8,128)S(1)}, f32[256,512]{1,0:T(8,128)S(1)}, u32[]{:S(2)}, u32[]{:S(2)}) collective-permute-start(f32[256,512]{1,0:T(8,128)S(1)} %get-tuple-element.81), channel_id=1, source_target_pairs={{0,1},{1,2},{2,3},{3,0},{4,5},{5,6},{6,7},{7,4},{8,9},{9,10},{10,1... | collective-permute-start | bytes 1572872 | tf_op jit(solution)/shard_map/ppermute | solution.py:446
  69.2 10.1 %collective-permute-start.25 = (f32[448,256]{1,0:T(8,128)S(1)}, f32[448,256]{1,0:T(8,128)S(1)}, u32[]{:S(2)}, u32[]{:S(2)}) collective-permute-start(f32[448,256]{1,0:T(8,128)S(1)} %get-tuple-element.77.dk_ref.own_ref), channel_id=1, source_target_pairs={{0,16},{16,0},{32,48},{48,32},{64,80},{80,64},{96,112},{112,96},{1... | collective-permute-start | bytes 1376264 | tf_op jit(solution)/shard_map/ppermute | solution.py:321
  69.5 5.5 %collective-permute-start.39 = (f32[256,256]{1,0:T(8,128)S(1)}, f32[256,256]{1,0:T(8,128)S(1)}, u32[]{:S(2)}, u32[]{:S(2)}) collective-permute-start(f32[256,256]{1,0:T(8,128)S(1)} %get-tuple-element.78.dv_ref.own_ref), channel_id=1, source_target_pairs={{0,16},{16,0},{32,48},{48,32},{64,80},{80,64},{96,112},{112,96},{1... | collective-permute-start | bytes 786440 | tf_op jit(solution)/shard_map/ppermute | solution.py:321
  72.3 12.5 %collective-permute-start.13 = (f32[256,256]{1,0:T(8,128)S(1)}, f32[256,256]{1,0:T(8,128)S(1)}, u32[]{:S(2)}, u32[]{:S(2)}) collective-permute-start(f32[256,256]{1,0:T(8,128)S(1)} %get-tuple-element.85), channel_id=1, source_target_pairs={{0,32},{4,36},{8,40},{12,44},{16,20},{20,24},{24,28},{28,16},{32,6... | collective-permute-start | bytes 786440 | tf_op jit(solution)/shard_map/ppermute | solution.py:316
  72.4 15.7 %collective-permute-start.14 = (f32[256,256]{1,0:T(8,128)S(1)}, f32[256,256]{1,0:T(8,128)S(1)}, u32[]{:S(2)}, u32[]{:S(2)}) collective-permute-start(f32[256,256]{1,0:T(8,128)S(1)} %get-tuple-element.86), channel_id=1, source_target_pairs={{0,96},{4,100},{8,104},{12,108},{16,28},{20,16},{24,20},{28,24},{3... | collective-permute-start | bytes 786440 | tf_op jit(solution)/shard_map/ppermute | solution.py:316
  75.1 15.3 %collective-permute-start.12 = (f32[256,256]{1,0:T(8,128)S(1)}, f32[256,256]{1,0:T(8,128)S(1)}, u32[]{:S(2)}, u32[]{:S(2)}) collective-permute-start(f32[256,256]{1,0:T(8,128)S(1)} %get-tuple-element.84), channel_id=1, source_target_pairs={{0,64},{4,68},{8,72},{12,76},{16,24},{20,28},{24,16},{28,20},{32,9... | collective-permute-start | bytes 786440 | tf_op jit(solution)/shard_map/ppermute | solution.py:316
  79.3 11.1 %collective-permute-start.41 = (f32[256,256]{1,0:T(8,128)S(1)}, f32[256,256]{1,0:T(8,128)S(1)}, u32[]{:S(2)}, u32[]{:S(2)}) collective-permute-start(f32[256,256]{1,0:T(8,128)S(1)} %get-tuple-element.93), channel_id=1, source_target_pairs={{0,32},{4,36},{8,40},{12,44},{16,20},{20,24},{24,28},{28,16},{32,6... | collective-permute-start | bytes 786440 | tf_op jit(solution)/shard_map/ppermute | solution.py:316
  83.6 7.8 %collective-permute-start.42 = (f32[256,256]{1,0:T(8,128)S(1)}, f32[256,256]{1,0:T(8,128)S(1)}, u32[]{:S(2)}, u32[]{:S(2)}) collective-permute-start(f32[256,256]{1,0:T(8,128)S(1)} %get-tuple-element.94), channel_id=1, source_target_pairs={{0,96},{4,100},{8,104},{12,108},{16,28},{20,16},{24,20},{28,24},{3... | collective-permute-start | bytes 786440 | tf_op jit(solution)/shard_map/ppermute | solution.py:316
  84.8 8.4 %collective-permute-start.40 = (f32[256,256]{1,0:T(8,128)S(1)}, f32[256,256]{1,0:T(8,128)S(1)}, u32[]{:S(2)}, u32[]{:S(2)}) collective-permute-start(f32[256,256]{1,0:T(8,128)S(1)} %get-tuple-element.92), channel_id=1, source_target_pairs={{0,64},{4,68},{8,72},{12,76},{16,24},{20,28},{24,16},{28,20},{32,9... | collective-permute-start | bytes 786440 | tf_op jit(solution)/shard_map/ppermute | solution.py:316
  88.1 13.8 %collective-permute-start.9 = (f32[256,512]{1,0:T(8,128)S(1)}, f32[256,512]{1,0:T(8,128)S(1)}, u32[]{:S(2)}, u32[]{:S(2)}) collective-permute-start(f32[256,512]{1,0:T(8,128)S(1)} %get-tuple-element.82), channel_id=1, source_target_pairs={{0,3},{1,0},{2,1},{3,2},{4,7},{5,4},{6,5},{7,6},{8,11},{9,8},{10,9... | collective-permute-start | bytes 1572872 | tf_op jit(solution)/shard_map/ppermute | solution.py:446
  90.3 16.4 %collective-permute-start.7 = (f32[256,512]{1,0:T(8,128)S(1)}, f32[256,512]{1,0:T(8,128)S(1)}, u32[]{:S(2)}, u32[]{:S(2)}) collective-permute-start(f32[256,512]{1,0:T(8,128)S(1)} %get-tuple-element.80), channel_id=1, source_target_pairs={{0,2},{1,3},{2,0},{3,1},{4,6},{5,7},{6,4},{7,5},{8,10},{9,11},{10,... | collective-permute-start | bytes 1572872 | tf_op jit(solution)/shard_map/ppermute | solution.py:446
  90.4 12.7 %collective-permute-start.27 = (f32[280,256]{1,0:T(8,128)S(1)}, f32[280,256]{1,0:T(8,128)S(1)}, u32[]{:S(2)}, u32[]{:S(2)}) collective-permute-start(f32[280,256]{1,0:T(8,128)S(1)} %get-tuple-element.89), channel_id=1, source_target_pairs={{0,32},{4,36},{8,40},{12,44},{16,20},{20,24},{24,28},{28,16},{32,6... | collective-permute-start | bytes 860168 | tf_op jit(solution)/shard_map/ppermute | solution.py:316
  91.4 13.2 %collective-permute-start.28 = (f32[280,256]{1,0:T(8,128)S(1)}, f32[280,256]{1,0:T(8,128)S(1)}, u32[]{:S(2)}, u32[]{:S(2)}) collective-permute-start(f32[280,256]{1,0:T(8,128)S(1)} %get-tuple-element.90), channel_id=1, source_target_pairs={{0,96},{4,100},{8,104},{12,108},{16,28},{20,16},{24,20},{28,24},{3... | collective-permute-start | bytes 860168 | tf_op jit(solution)/shard_map/ppermute | solution.py:316
  93.2 13.1 %collective-permute-start.26 = (f32[280,256]{1,0:T(8,128)S(1)}, f32[280,256]{1,0:T(8,128)S(1)}, u32[]{:S(2)}, u32[]{:S(2)}) collective-permute-start(f32[280,256]{1,0:T(8,128)S(1)} %get-tuple-element.88), channel_id=1, source_target_pairs={{0,64},{4,68},{8,72},{12,76},{16,24},{20,28},{24,16},{28,20},{32,9... | collective-permute-start | bytes 860168 | tf_op jit(solution)/shard_map/ppermute | solution.py:316
  101.9 6.8 %collective-permute-start.16 = (f32[256,256]{1,0:T(8,128)S(1)}, f32[256,256]{1,0:T(8,128)S(1)}, u32[]{:S(2)}, u32[]{:S(2)}) collective-permute-start(f32[256,256]{1,0:T(8,128)S(1)} %add_add_fusion.5), channel_id=1, source_target_pairs={{0,4},{4,8},{8,12},{12,0},{16,48},{20,52},{24,56},{28,60},{32,36},... | collective-permute-start | bytes 786440 | tf_op jit(solution)/shard_map/ppermute | solution.py:316
  103.2 6.9 %collective-permute-start.17 = (f32[256,256]{1,0:T(8,128)S(1)}, f32[256,256]{1,0:T(8,128)S(1)}, u32[]{:S(2)}, u32[]{:S(2)}) collective-permute-start(f32[256,256]{1,0:T(8,128)S(1)} %add_add_fusion.5), channel_id=1, source_target_pairs={{0,12},{4,0},{8,4},{12,8},{16,112},{20,116},{24,120},{28,124},{32,... | collective-permute-start | bytes 786440 | tf_op jit(solution)/shard_map/ppermute | solution.py:316
  104.6 7.8 %collective-permute-start.15 = (f32[256,256]{1,0:T(8,128)S(1)}, f32[256,256]{1,0:T(8,128)S(1)}, u32[]{:S(2)}, u32[]{:S(2)}) collective-permute-start(f32[256,256]{1,0:T(8,128)S(1)} %add_add_fusion.5), channel_id=1, source_target_pairs={{0,8},{4,12},{8,0},{12,4},{16,80},{20,84},{24,88},{28,92},{32,40},... | collective-permute-start | bytes 786440 | tf_op jit(solution)/shard_map/ppermute | solution.py:316
  106.3 8.9 %collective-permute-start.44 = (f32[256,256]{1,0:T(8,128)S(1)}, f32[256,256]{1,0:T(8,128)S(1)}, u32[]{:S(2)}, u32[]{:S(2)}) collective-permute-start(f32[256,256]{1,0:T(8,128)S(1)} %add_add_fusion.3), channel_id=1, source_target_pairs={{0,4},{4,8},{8,12},{12,0},{16,48},{20,52},{24,56},{28,60},{32,36},... | collective-permute-start | bytes 786440 | tf_op jit(solution)/shard_map/ppermute | solution.py:316
  106.7 15.2 %collective-permute-start.30 = (f32[280,256]{1,0:T(8,128)S(1)}, f32[280,256]{1,0:T(8,128)S(1)}, u32[]{:S(2)}, u32[]{:S(2)}) collective-permute-start(f32[280,256]{1,0:T(8,128)S(1)} %add_add_fusion.1), channel_id=1, source_target_pairs={{0,4},{4,8},{8,12},{12,0},{16,48},{20,52},{24,56},{28,60},{32,36},... | collective-permute-start | bytes 860168 | tf_op jit(solution)/shard_map/ppermute | solution.py:316
  108.7 7.7 %collective-permute-start.45 = (f32[256,256]{1,0:T(8,128)S(1)}, f32[256,256]{1,0:T(8,128)S(1)}, u32[]{:S(2)}, u32[]{:S(2)}) collective-permute-start(f32[256,256]{1,0:T(8,128)S(1)} %add_add_fusion.3), channel_id=1, source_target_pairs={{0,12},{4,0},{8,4},{12,8},{16,112},{20,116},{24,120},{28,124},{32,... | collective-permute-start | bytes 786440 | tf_op jit(solution)/shard_map/ppermute | solution.py:316
  110.1 11.0 %collective-permute-start.43 = (f32[256,256]{1,0:T(8,128)S(1)}, f32[256,256]{1,0:T(8,128)S(1)}, u32[]{:S(2)}, u32[]{:S(2)}) collective-permute-start(f32[256,256]{1,0:T(8,128)S(1)} %add_add_fusion.3), channel_id=1, source_target_pairs={{0,8},{4,12},{8,0},{12,4},{16,80},{20,84},{24,88},{28,92},{32,40},... | collective-permute-start | bytes 786440 | tf_op jit(solution)/shard_map/ppermute | solution.py:316
  112.4 10.1 %collective-permute-start.31 = (f32[280,256]{1,0:T(8,128)S(1)}, f32[280,256]{1,0:T(8,128)S(1)}, u32[]{:S(2)}, u32[]{:S(2)}) collective-permute-start(f32[280,256]{1,0:T(8,128)S(1)} %add_add_fusion.1), channel_id=1, source_target_pairs={{0,12},{4,0},{8,4},{12,8},{16,112},{20,116},{24,120},{28,124},{32,... | collective-permute-start | bytes 860168 | tf_op jit(solution)/shard_map/ppermute | solution.py:316
  115.2 24.1 %collective-permute-start.29 = (f32[280,256]{1,0:T(8,128)S(1)}, f32[280,256]{1,0:T(8,128)S(1)}, u32[]{:S(2)}, u32[]{:S(2)}) collective-permute-start(f32[280,256]{1,0:T(8,128)S(1)} %add_add_fusion.1), channel_id=1, source_target_pairs={{0,8},{4,12},{8,0},{12,4},{16,80},{20,84},{24,88},{28,92},{32,40},... | collective-permute-start | bytes 860168 | tf_op jit(solution)/shard_map/ppermute | solution.py:316
  116.3 22.9 %collective-permute-start.18 = (f32[256,256]{1,0:T(8,128)S(1)}, f32[256,256]{1,0:T(8,128)S(1)}, u32[]{:S(2)}, u32[]{:S(2)}) collective-permute-start(f32[256,256]{1,0:T(8,128)S(1)} %add_add_fusion.4.refs_0_), channel_id=1, source_target_pairs={{0,96},{4,100},{8,104},{12,108},{16,28},{20,16},{24,20},{28,24},{3... | collective-permute-start | bytes 786440 | tf_op jit(solution)/shard_map/ppermute | solution.py:316
  121.1 19.6 %collective-permute-start.19 = (f32[256,256]{1,0:T(8,128)S(1)}, f32[256,256]{1,0:T(8,128)S(1)}, u32[]{:S(2)}, u32[]{:S(2)}) collective-permute-start(f32[256,256]{1,0:T(8,128)S(1)} %add_add_fusion.4.refs_0_), channel_id=1, source_target_pairs={{0,32},{4,36},{8,40},{12,44},{16,20},{20,24},{24,28},{28,16},{32,6... | collective-permute-start | bytes 786440 | tf_op jit(solution)/shard_map/ppermute | solution.py:316
  121.9 22.0 %collective-permute-start.20 = (f32[256,256]{1,0:T(8,128)S(1)}, f32[256,256]{1,0:T(8,128)S(1)}, u32[]{:S(2)}, u32[]{:S(2)}) collective-permute-start(f32[256,256]{1,0:T(8,128)S(1)} %add_add_fusion.4.refs_0_), channel_id=1, source_target_pairs={{0,64},{4,68},{8,72},{12,76},{16,24},{20,28},{24,16},{28,20},{32,9... | collective-permute-start | bytes 786440 | tf_op jit(solution)/shard_map/ppermute | solution.py:316
  122.6 22.2 %collective-permute-start.21 = (f32[256,256]{1,0:T(8,128)S(1)}, f32[256,256]{1,0:T(8,128)S(1)}, u32[]{:S(2)}, u32[]{:S(2)}) collective-permute-start(f32[256,256]{1,0:T(8,128)S(1)} %add_add_fusion.4.refs_0_), channel_id=1, source_target_pairs={{0,16},{16,0},{32,48},{48,32},{64,80},{80,64},{96,112},{112,96},{1... | collective-permute-start | bytes 786440 | tf_op jit(solution)/shard_map/ppermute | solution.py:321
  139.2 6.3 %collective-permute-start.46 = (f32[256,256]{1,0:T(8,128)S(1)}, f32[256,256]{1,0:T(8,128)S(1)}, u32[]{:S(2)}, u32[]{:S(2)}) collective-permute-start(f32[256,256]{1,0:T(8,128)S(1)} %add_add_fusion.2.refs_16_), channel_id=1, source_target_pairs={{0,96},{4,100},{8,104},{12,108},{16,28},{20,16},{24,20},{28,24},{3... | collective-permute-start | bytes 786440 | tf_op jit(solution)/shard_map/ppermute | solution.py:316
  139.2 8.7 %collective-permute-start.47 = (f32[256,256]{1,0:T(8,128)S(1)}, f32[256,256]{1,0:T(8,128)S(1)}, u32[]{:S(2)}, u32[]{:S(2)}) collective-permute-start(f32[256,256]{1,0:T(8,128)S(1)} %add_add_fusion.2.refs_16_), channel_id=1, source_target_pairs={{0,32},{4,36},{8,40},{12,44},{16,20},{20,24},{24,28},{28,16},{32,6... | collective-permute-start | bytes 786440 | tf_op jit(solution)/shard_map/ppermute | solution.py:316
  140.7 10.1 %collective-permute-start.48 = (f32[256,256]{1,0:T(8,128)S(1)}, f32[256,256]{1,0:T(8,128)S(1)}, u32[]{:S(2)}, u32[]{:S(2)}) collective-permute-start(f32[256,256]{1,0:T(8,128)S(1)} %add_add_fusion.2.refs_16_), channel_id=1, source_target_pairs={{0,64},{4,68},{8,72},{12,76},{16,24},{20,28},{24,16},{28,20},{32,9... | collective-permute-start | bytes 786440 | tf_op jit(solution)/shard_map/ppermute | solution.py:316
  144.0 8.0 %collective-permute-start.32 = (f32[280,256]{1,0:T(8,128)S(1)}, f32[280,256]{1,0:T(8,128)S(1)}, u32[]{:S(2)}, u32[]{:S(2)}) collective-permute-start(f32[280,256]{1,0:T(8,128)S(1)} %add_add_fusion.refs_8_), channel_id=1, source_target_pairs={{0,96},{4,100},{8,104},{12,108},{16,28},{20,16},{24,20},{28,24},{3... | collective-permute-start | bytes 860168 | tf_op jit(solution)/shard_map/ppermute | solution.py:316
  144.7 10.2 %collective-permute-start.33 = (f32[280,256]{1,0:T(8,128)S(1)}, f32[280,256]{1,0:T(8,128)S(1)}, u32[]{:S(2)}, u32[]{:S(2)}) collective-permute-start(f32[280,256]{1,0:T(8,128)S(1)} %add_add_fusion.refs_8_), channel_id=1, source_target_pairs={{0,32},{4,36},{8,40},{12,44},{16,20},{20,24},{24,28},{28,16},{32,6... | collective-permute-start | bytes 860168 | tf_op jit(solution)/shard_map/ppermute | solution.py:316
  145.5 14.4 %collective-permute-start.34 = (f32[280,256]{1,0:T(8,128)S(1)}, f32[280,256]{1,0:T(8,128)S(1)}, u32[]{:S(2)}, u32[]{:S(2)}) collective-permute-start(f32[280,256]{1,0:T(8,128)S(1)} %add_add_fusion.refs_8_), channel_id=1, source_target_pairs={{0,64},{4,68},{8,72},{12,76},{16,24},{20,28},{24,16},{28,20},{32,9... | collective-permute-start | bytes 860168 | tf_op jit(solution)/shard_map/ppermute | solution.py:316
  147.9 3.9 %collective-permute-start.49 = (f32[256,256]{1,0:T(8,128)S(1)}, f32[256,256]{1,0:T(8,128)S(1)}, u32[]{:S(2)}, u32[]{:S(2)}) collective-permute-start(f32[256,256]{1,0:T(8,128)S(1)} %add_add_fusion.2.refs_16_), channel_id=1, source_target_pairs={{0,16},{16,0},{32,48},{48,32},{64,80},{80,64},{96,112},{112,96},{1... | collective-permute-start | bytes 786440 | tf_op jit(solution)/shard_map/ppermute | solution.py:321
  150.8 9.1 %collective-permute-start.35 = (f32[280,256]{1,0:T(8,128)S(1)}, f32[280,256]{1,0:T(8,128)S(1)}, u32[]{:S(2)}, u32[]{:S(2)}) collective-permute-start(f32[280,256]{1,0:T(8,128)S(1)} %add_add_fusion.refs_8_), channel_id=1, source_target_pairs={{0,16},{16,0},{32,48},{48,32},{64,80},{80,64},{96,112},{112,96},{1... | collective-permute-start | bytes 860168 | tf_op jit(solution)/shard_map/ppermute | solution.py:321
  151.8 8.6 %collective-permute-start.22 = (f32[256,256]{1,0:T(8,128)S(1)}, f32[256,256]{1,0:T(8,128)S(1)}, u32[]{:S(2)}, u32[]{:S(2)}) collective-permute-start(f32[256,256]{1,0:T(8,128)S(1)} %collective-permute-done.18.refs_1_), channel_id=1, source_target_pairs={{0,16},{16,0},{32,48},{48,32},{64,80},{80,64},{96,112},{112,96},{1... | collective-permute-start | bytes 786440 | tf_op jit(solution)/shard_map/ppermute | solution.py:321
  152.0 8.5 %collective-permute-start.23 = (f32[256,256]{1,0:T(8,128)S(1)}, f32[256,256]{1,0:T(8,128)S(1)}, u32[]{:S(2)}, u32[]{:S(2)}) collective-permute-start(f32[256,256]{1,0:T(8,128)S(1)} %collective-permute-done.19.refs_2_), channel_id=1, source_target_pairs={{0,16},{16,0},{32,48},{48,32},{64,80},{80,64},{96,112},{112,96},{1... | collective-permute-start | bytes 786440 | tf_op jit(solution)/shard_map/ppermute | solution.py:321
  154.9 6.1 %collective-permute-start.24 = (f32[256,256]{1,0:T(8,128)S(1)}, f32[256,256]{1,0:T(8,128)S(1)}, u32[]{:S(2)}, u32[]{:S(2)}) collective-permute-start(f32[256,256]{1,0:T(8,128)S(1)} %collective-permute-done.20.refs_3_), channel_id=1, source_target_pairs={{0,16},{16,0},{32,48},{48,32},{64,80},{80,64},{96,112},{112,96},{1... | collective-permute-start | bytes 786440 | tf_op jit(solution)/shard_map/ppermute | solution.py:321
  159.9 3.5 %collective-permute-start.36 = (f32[280,256]{1,0:T(8,128)S(1)}, f32[280,256]{1,0:T(8,128)S(1)}, u32[]{:S(2)}, u32[]{:S(2)}) collective-permute-start(f32[280,256]{1,0:T(8,128)S(1)} %collective-permute-done.32.refs_9_), channel_id=1, source_target_pairs={{0,16},{16,0},{32,48},{48,32},{64,80},{80,64},{96,112},{112,96},{1... | collective-permute-start | bytes 860168 | tf_op jit(solution)/shard_map/ppermute | solution.py:321
  (45 other events, 300.7 us)

commit v2 on v1

--- a/solution.py
+++ b/solution.py
@@ -77,9 +77,12 @@
 
 
 def maps_kernel(
-    ctx_ref, base_ref, tok_ref, wk_ref, wv_ref, gate_ref, init_ref,
-    k_ref, v_ref, ninv_ref, gram_ref, inv_ref, bt_ref, d_ref, send_ref, o_ref,
+    pos_ref, base_ref, tok_ref, wk_ref, wv_ref, gate_ref, init_ref,
+    k_ref, v_ref, ninv_ref, gram_ref, inv_ref, bt_ref, d_ref, send_ref, o_ref, half_ref,
 ):
+    half = tok_ref.shape[2] // 2
+    columns = pl.ds(pl.multiple_of((1 - pos_ref[0]) * half, half), half)
+    half_ref[...] = tok_ref[0, :, columns].astype(F32)
     tok = tok_ref[0]
     kraw_all = jnp.dot(tok, wk_ref[0], preferred_element_type=F32).astype(BF).astype(F32)
     v_all = jnp.dot(tok, wv_ref[0], preferred_element_type=F32).astype(BF).astype(F32)
@@ -114,11 +117,16 @@
         d_ref[h] = decay
         o_ref[h] = offset
         first = dot(decay, init_ref[h], NN, 3) + offset
-        send_ref[h] = jnp.where(ctx_ref[0] == 0, first, offset)
-
-
-def reach_kernel(base_ref, tok_ref, wq_ref, gate_ref, k_ref, v_ref, inv_ref,
-                 q_ref, score_ref, rv_ref, y_ref, qt_ref, zv_ref):
+        send_ref[h] = jnp.where(pos_ref[4] == 0, first, offset)
+
+
+def reach_kernel(
+    pos_ref, base_ref, tok_ref, wq_ref, gate_ref, k_ref, v_ref, inv_ref,
+    q_ref, score_ref, rv_ref, y_ref, qt_ref, zv_ref, tokt_ref,
+):
+    half = tok_ref.shape[2] // 2
+    columns = pl.ds(pl.multiple_of(pos_ref[0] * half, half), half)
+    tokt_ref[...] = tok_ref[0, :, columns].astype(F32).T.astype(BF)
     q_all = jnp.dot(tok_ref[0], wq_ref[0], preferred_element_type=F32).astype(BF).astype(F32)
     n = q_all.shape[0]
     i, j = places(n)
@@ -139,16 +147,18 @@
         zv_ref[:, span(h)] = dot(mix, rv, NN, 3)
 
 
-def step_kernel(d_ref, w_ref, o_ref, out_ref, *, transposed):
+def step_kernel(d_ref, w_ref, o_ref, after_ref, out_ref, *, transposed):
+    del after_ref
     for h in range(d_ref.shape[0]):
         out_ref[h] = o_ref[h] + dot(d_ref[h], w_ref[h], TN if transposed else NN, 3)
 
 
 def norm_kernel(
-    ctx_ref, init_ref, near_ref, mid_ref, far_ref, rd_ref, qt_ref, zv_ref, up_ref, gain_ref,
+    pos_ref, init_ref, near_ref, mid_ref, far_ref, rd_ref, qt_ref, zv_ref, up_ref, gain_ref, after_ref,
     w_ref, h_ref, p_ref, dgain_ref,
 ):
-    ctx = ctx_ref[0]
+    del after_ref
+    ctx = pos_ref[4]
     for h in range(init_ref.shape[0]):
         last = dot(rd_ref[h], far_ref[h], NN, 3) + near_ref[h]
         start = jnp.where(
@@ -198,27 +208,28 @@
 
 
 def keys_kernel(
-    ctx_ref, base_ref, gate_ref, rp_ref, mid_ref, far_ref, rd_ref, p_ref, d_ref, w_ref, k_ref, ninv_ref,
-    gram_ref, bt_ref, r_ref, x_ref, dk_ref, de_ref, dgain_ref,
-    dkraw_ref, dv_ref, gates_ref,
+    pos_ref, base_ref, gate_ref, rp_ref, mid_ref, far_ref, rd_ref, p_ref, d_ref, w_ref, k_ref, ninv_ref,
+    gram_ref, bt_ref, r_ref, x_ref, dk_ref, de_ref, dgain_ref, after_ref,
+    both_ref, gates_ref,
 ):
-    ctx = ctx_ref[0]
+    del after_ref
+    ctx = pos_ref[4]
     n = k_ref.shape[0]
     i, j = places(n)
     strict = (i // MB) > (j // MB)
-    dkraw_ref[n + HS : n + EXTRA, :] = jnp.zeros((EXTRA - HS, dkraw_ref.shape[1]), F32)
+    both_ref[2 * n + HS : 2 * n + EXTRA, :] = jnp.zeros((EXTRA - HS, both_ref.shape[1]), F32)
     for h in range(w_ref.shape[0]):
         first = rp_ref[h] + dot(rd_ref[h], far_ref[h], TN, 3)
         end = jnp.where(
             ctx == 0, first, jnp.where(ctx == 1, mid_ref[h], jnp.where(ctx == 2, rp_ref[h], 0.0))
         )
-        dkraw_ref[n : n + HS, span(h)] = jnp.where(ctx == 0, p_ref[h] + dot(d_ref[h], end, TN, 3), 0.0)
+        both_ref[2 * n : 2 * n + HS, span(h)] = jnp.where(ctx == 0, p_ref[h] + dot(d_ref[h], end, TN, 3), 0.0)
         w = w_ref[h]
         k = k_ref[:, span(h)]
         r = r_ref[:, span(h)]
         boost, e = rates_of(base_ref, gate_ref, h)
         x = x_ref[:, span(h)] + dot(bt_ref[h], end, TN, 3)
-        dv_ref[:, span(h)] = x.astype(BF).astype(F32)
+        both_ref[n : 2 * n, span(h)] = x.astype(BF).astype(F32)
         d_low = jnp.where(strict, -dot(x, r, NT, 3), 0.0)
         d_gram = d_low * e
         dk = (
@@ -230,36 +241,41 @@
         pull = to_row(jnp.sum(r * dot(k, end, NN, 3), axis=1, keepdims=True))
         de = de_ref[h : h + 1, :] + jnp.sum(d_low * gram_ref[h], axis=0, keepdims=True) + pull
         draw = ninv_ref[h] * (dk - k * jnp.sum(k * dk, -1, keepdims=True))
-        dkraw_ref[0:n, span(h)] = draw.astype(BF).astype(F32)
+        both_ref[0:n, span(h)] = draw.astype(BF).astype(F32)
         d_boost = de / ((1.0 + boost) * (1.0 + boost))
         gates_ref[0, h : h + 1, :] = d_boost * base_ref[h]
-        dkraw_ref[n + HS : n + HS + 1, span(h)] = dgain_ref[h : h + 1, :]
-        dkraw_ref[n + HS + 1 : n + HS + 2, span(h)] = jnp.broadcast_to(
+        both_ref[2 * n + HS : 2 * n + HS + 1, span(h)] = dgain_ref[h : h + 1, :]
+        both_ref[2 * n + HS + 1 : 2 * n + HS + 2, span(h)] = jnp.broadcast_to(
             jnp.sum(d_boost * gate_ref[0, h : h + 1, :], axis=1, keepdims=True), (1, HS)
         )
 
 
-def turn_kernel(own_ref, other_ref, out_ref):
-    n = own_ref.shape[0]
-    out_ref[:, 0:n] = own_ref[...].T.astype(BF)
-    out_ref[:, n : 2 * n] = other_ref[...].T.astype(BF)
-
-
-def product_kernel(pos_ref, tokt_ref, own_ref, other_ref, *out_refs):
-    n = tokt_ref.shape[1] // 2
-    d = jnp.concatenate([own_ref[0:n, :], other_ref[0:n, :]], axis=0).astype(BF)
+def turn_kernel(other_ref, out_ref):
+    out_ref[...] = other_ref[...].T.astype(BF)
+
+
+def product_kernel(pos_ref, tokt_ref, other_tokt_ref, own_ref, other_ref, *out_refs):
+    n = tokt_ref.shape[1]
+    count = own_ref.shape[0] // n
+    if count > 1:
+        count = (own_ref.shape[0] - EXTRA) // n
     for turn, out_ref in zip(TURNS, out_refs):
         at = (pos_ref[1] + turn) & (RING - 1)
         rows = pl.ds(pl.multiple_of(at * CHUNK, CHUNK), CHUNK)
-        out_ref[0:CHUNK, :] = jnp.dot(tokt_ref[rows, :], d, preferred_element_type=F32)
-        if own_ref.shape[0] > n:
-            extra = pl.ds(pl.multiple_of(n + (pos_ref[0] * RING + at) * PIECE, 8), PIECE)
-            out_ref[CHUNK : CHUNK + PIECE, :] = own_ref[extra, :] + other_ref[extra, :]
-
-
-def token_kernel(pos_ref, w_ref, dq_ref, dk_ref, dv_ref, *out_refs):
+        for m in range(count):
+            out_ref[m * CHUNK : (m + 1) * CHUNK, :] = jnp.dot(
+                tokt_ref[rows, :], own_ref[m * n : (m + 1) * n, :].astype(BF), preferred_element_type=F32
+            ) + jnp.dot(
+                other_tokt_ref[rows, :], other_ref[m * n : (m + 1) * n, :].astype(BF), preferred_element_type=F32
+            )
+        if count > 1:
+            extra = pl.ds(pl.multiple_of(count * n + (pos_ref[0] * RING + at) * PIECE, 8), PIECE)
+            out_ref[count * CHUNK : count * CHUNK + PIECE, :] = own_ref[extra, :] + other_ref[extra, :]
+
+
+def token_kernel(pos_ref, w_ref, dq_ref, both_ref, *out_refs):
     n = dq_ref.shape[0]
-    ds = [dq_ref[...].astype(BF), dk_ref[0:n, :].astype(BF), dv_ref[...].astype(BF)]
+    ds = [dq_ref[...].astype(BF), both_ref[0:n, :].astype(BF), both_ref[n : 2 * n, :].astype(BF)]
     span_rows = w_ref.shape[1] // RING
     for turn, out_ref in zip(TURNS, out_refs):
         at = (pos_ref[3] + turn) & (RING - 1)
@@ -270,25 +286,25 @@
 
 
 def place_kernel(pos_ref, *refs):
-    pieces = [refs[8 * s : 8 * s + 8] for s in range(3)]
-    out_ref, init_ref, gain_ref, rates_ref, extra_ref, sem, extra_sem = refs[24:]
+    out_ref, init_ref, gain_ref, rates_ref, extra_ref, sem, extra_sem = refs[16:]
     copies = []
-    for s in range(3):
-        for m in range(8):
-            half, turn = m // RING, TURNS[m % RING]
-            core = pos_ref[0] if half == 0 else 1 - pos_ref[0]
-            at = core * RING + ((pos_ref[1 + half] + turn) & (RING - 1))
-            rows = pl.ds(pl.multiple_of(at * CHUNK, CHUNK), CHUNK)
+    for m in range(8):
+        half, turn = m // RING, TURNS[m % RING]
+        core = pos_ref[0] if half == 0 else 1 - pos_ref[0]
+        at = core * RING + ((pos_ref[1 + half] + turn) & (RING - 1))
+        rows = pl.ds(pl.multiple_of(at * CHUNK, CHUNK), CHUNK)
+        for s in range(3):
+            piece = refs[m] if s == 0 else refs[8 + m]
+            start = 0 if s == 0 else (s - 1) * CHUNK
             copies.append(
-                pltpu.make_async_copy(pieces[s][m].at[pl.ds(0, CHUNK), :], out_ref.at[s, rows, :], sem.at[s, m])
+                pltpu.make_async_copy(piece.at[pl.ds(start, CHUNK), :], out_ref.at[s, rows, :], sem.at[s, m])
             )
-            if s == 1:
-                rows = pl.ds(pl.multiple_of(at * PIECE, 8), PIECE)
-                copies.append(
-                    pltpu.make_async_copy(
-                        pieces[s][m].at[pl.ds(CHUNK, PIECE), :], extra_ref.at[rows, :], extra_sem.at[m]
-                    )
-                )
+        rows = pl.ds(pl.multiple_of(at * PIECE, 8), PIECE)
+        copies.append(
+            pltpu.make_async_copy(
+                refs[8 + m].at[pl.ds(2 * CHUNK, PIECE), :], extra_ref.at[rows, :], extra_sem.at[m]
+            )
+        )
     for copy in copies:
         copy.start()
     for copy in copies:
@@ -321,11 +337,16 @@
     return lax.ppermute(value, "dp", [(i, i ^ 1) for i in range(2 * RING)])
 
 
-def reduce_stream(pos, tokt, d):
+def reduce_products(pos, tokt, other_tokt, d):
     other = swap(d)
-    rows = CHUNK + (PIECE if d.shape[0] > CHUNK else 0)
-    piece = shape(rows, d.shape[1])
-    own, *away = whole(product_kernel, (piece,) * RING, [SM] + [VM] * 3)(pos, tokt, d, other)
+    rows = d.shape[0] if d.shape[0] == CHUNK else 2 * CHUNK + PIECE
+    return whole(product_kernel, (vmem(rows, d.shape[1]),) * RING, [SM] + [VM] * 4)(
+        pos, tokt, other_tokt, d, other
+    )
+
+
+def reduce_stream(products):
+    own, *away = products
     from_back, from_ahead, from_far = round_turn(away, True)
     part_sum = (own + from_far) + (from_back + from_ahead)
     from_back, from_ahead, from_far = round_turn([part_sum] * 3, False)
@@ -337,11 +358,19 @@
 
 VM = pl.BlockSpec(memory_space=pltpu.VMEM)
 SM = pl.BlockSpec(memory_space=pltpu.SMEM)
-PARAMS = pltpu.CompilerParams(vmem_limit_bytes=32 * 1024 * 1024)
+PARAMS = pltpu.CompilerParams(vmem_limit_bytes=20 * 1024 * 1024)
 
 
 def shape(*dims, dtype=F32):
     return jax.ShapeDtypeStruct(dims, dtype)
+
+
+def vmem(*dims, dtype=F32):
+    return pltpu.VMEM(dims, dtype)
+
+
+def hbm(value):
+    return pltpu.with_memory_space_constraint(value, pltpu.HBM)
 
 
 def whole(kernel, outs, specs):
@@ -349,7 +378,7 @@
         kernel,
         out_shape=outs,
         in_specs=specs,
-        out_specs=jax.tree.map(lambda _: VM, outs),
+        out_specs=tuple(VM for _ in outs) if isinstance(outs, tuple) else VM,
         compiler_params=PARAMS,
     )
 
@@ -368,97 +397,104 @@
     heads = init_weight.shape[0]
     wide = heads * HS
     ctx = lax.axis_index("ctx")
-    ctx_arr = ctx.astype(jnp.int32).reshape(1)
     dp = lax.axis_index("dp")
     core, x_at = dp % 2, dp // 2
     pos = jnp.stack(
-        [core, jnp.where(core == 0, x_at, ctx), jnp.where(core == 0, ctx, x_at), lax.axis_index("head")]
+        [core, jnp.where(core == 0, x_at, ctx), jnp.where(core == 0, ctx, x_at), lax.axis_index("head"), ctx]
     ).astype(jnp.int32)
     half = model // 2
-    own_half = lax.dynamic_slice_in_dim(tokens[0], core * half, half, 1).astype(F32)
-    other_half = lax.dynamic_slice_in_dim(tokens[0], (1 - core) * half, half, 1).astype(F32)
-    got_half = swap(other_half)
-
-    wide_f32 = shape(n, wide)
-    square = shape(heads, n, n)
-    small = shape(heads, HS, HS)
+
+    wide_f32 = vmem(n, wide)
+    square = vmem(heads, n, n)
+    small = vmem(heads, HS, HS)
     wspec = functools.partial(part, dims=(model, wide))
-
-    k, v, ninv, gram, inv, bt, decay, send, offset = pl.pallas_call(
+    tokens = hbm(tokens)
+    proj_weights = hbm(proj_weights)
+    anywhere = pl.BlockSpec(memory_space=pl.ANY)
+
+    k, v, ninv, gram, inv, bt, decay, send, offset, other_half = pl.pallas_call(
         maps_kernel,
         grid=(1,),
-        out_shape=(wide_f32, wide_f32, shape(heads, n, HS), square, square, shape(heads, HS, n), small, small, small),
+        out_shape=(
+            wide_f32, wide_f32, vmem(heads, n, HS), square, square, vmem(heads, HS, n), small, small, small,
+            vmem(n, half),
+        ),
         in_specs=[SM, SM, full(1, n, model), wspec(1), wspec(2), full(1, heads, n), full(heads, HS, HS)],
-        out_specs=(
-            full(n, wide), full(n, wide), full(heads, n, HS), full(heads, n, n), full(heads, n, n),
-            full(heads, HS, n), full(heads, HS, HS), full(heads, HS, HS), full(heads, HS, HS),
-        ),
+        out_specs=(VM,) * 10,
         compiler_params=PARAMS,
-    )(ctx_arr, base_rates, tokens, proj_weights, proj_weights, gate_values, init_weight)
+    )(pos, hbm(base_rates), tokens, proj_weights, proj_weights, hbm(gate_values), hbm(init_weight))
 
     near = lax.ppermute(send, "ctx", [(0, 1), (2, 3)])
     moved = lax.ppermute(decay, "ctx", [(2, 3), (1, 0)])
-
-    q, score, rv, y, qt, zv = pl.pallas_call(
+    got_half = swap(other_half)
+
+    q, score, rv, y, qt, zv, tokt = pl.pallas_call(
         reach_kernel,
         grid=(1,),
-        out_shape=(wide_f32, square, wide_f32, wide_f32, wide_f32, wide_f32),
-        in_specs=[SM, full(1, n, model), wspec(0), full(1, heads, n), full(n, wide), full(n, wide), full(heads, n, n)],
-        out_specs=(full(n, wide), full(heads, n, n), full(n, wide), full(n, wide), full(n, wide), full(n, wide)),
+        out_shape=(wide_f32, square, wide_f32, wide_f32, wide_f32, wide_f32, vmem(half, n, dtype=BF)),
+        in_specs=[SM, SM, full(1, n, model), wspec(0), full(1, heads, n), VM, VM, VM],
+        out_specs=(VM,) * 7,
         compiler_params=PARAMS,
-    )(base_rates, tokens, proj_weights, gate_values, k, v, inv)
-
-    second = whole(functools.partial(step_kernel, transposed=False), small, [VM] * 3)(decay, near, offset)
+    )(pos, base_rates, tokens, proj_weights, gate_values, k, v, inv)
+
+    second = whole(functools.partial(step_kernel, transposed=False), small, [VM] * 3 + [anywhere])(
+        decay, near, offset, qt
+    )
     mid = lax.ppermute(second, "ctx", [(1, 2)])
     far = lax.ppermute(second, "ctx", [(1, 3)])
+    other_tokt = whole(turn_kernel, vmem(half, n, dtype=BF), [VM])(got_half)
 
     w, back, pulled, dgain = whole(
-        norm_kernel, (small, wide_f32, small, shape(heads, HS)), [SM] + [VM] * 9
-    )(ctx_arr, init_weight, near, mid, far, moved, qt, zv, cotangent, out_gain)
+        norm_kernel, (small, wide_f32, small, vmem(heads, HS)), [SM] + [VM] * 9 + [anywhere]
+    )(pos, init_weight, near, mid, far, moved, qt, zv, cotangent, out_gain, other_tokt)
 
     back_near = lax.ppermute(pulled, "ctx", [(3, 2), (1, 0)])
 
     dq, r, x, dk, de = whole(
-        query_kernel,
-        (wide_f32, wide_f32, wide_f32, wide_f32, shape(heads, n)),
-        [SM] + [VM] * 10,
+        query_kernel, (wide_f32, wide_f32, wide_f32, wide_f32, vmem(heads, n)), [SM] + [VM] * 10
     )(base_rates, gate_values, w, back, cotangent, q, score, rv, y, k, inv)
 
-    back_second = whole(functools.partial(step_kernel, transposed=True), small, [VM] * 3)(decay, back_near, pulled)
+    back_second = whole(functools.partial(step_kernel, transposed=True), small, [VM] * 3 + [anywhere])(
+        decay, back_near, pulled, de
+    )
     back_mid = lax.ppermute(back_second, "ctx", [(2, 1)])
     back_far = lax.ppermute(back_second, "ctx", [(2, 0)])
-
-    dkraw, dv, grad_gates = whole(
-        keys_kernel,
-        (shape(n + EXTRA, wide), wide_f32, shape(1, heads, n)),
-        [SM, SM] + [VM] * 17,
-    )(ctx_arr, base_rates, gate_values, back_near, back_mid, back_far, moved, pulled, decay, w, k, ninv, gram, bt, r, x,
-      dk, de, dgain)
-
-    tokt = whole(turn_kernel, shape(half, 2 * n, dtype=BF), [VM] * 2)(own_half, got_half)
-    query_pieces = reduce_stream(pos, tokt, dq)
-    value_pieces = reduce_stream(pos, tokt, dv)
-    key_pieces = reduce_stream(pos, tokt, dkraw)
-
-    quarter = shape(n, model // RING)
-    own, *away = whole(token_kernel, (quarter,) * RING, [SM] + [VM] * 4)(pos, proj_weights, dq, dkraw, dv)
+    query_products = reduce_products(pos, tokt, other_tokt, dq)
+
+    both, grad_gates = whole(
+        keys_kernel, (vmem(2 * n + EXTRA, wide), shape(1, heads, n)), [SM, SM] + [VM] * 17 + [anywhere]
+    )(pos, base_rates, gate_values, back_near, back_mid, back_far, moved, pulled, decay, w, k, ninv, gram, bt, r, x,
+      dk, de, dgain, query_products[0])
+
+    both_products = reduce_products(pos, tokt, other_tokt, both)
+    query_pieces = reduce_stream(query_products)
+    both_pieces = reduce_stream(both_products)
+
+    quarter = vmem(n, model // RING)
+    own, *away = pl.pallas_call(
+        token_kernel,
+        grid=(1,),
+        out_shape=(quarter,) * RING,
+        in_specs=[SM, full(3, model, wide), VM, VM],
+        out_specs=(VM,) * RING,
+        compiler_params=PARAMS,
+    )(pos, proj_weights, dq, both)
     from_back, from_ahead, from_far = [
         lax.ppermute(chunk, "head", [(i, (i + turn) % RING) for i in range(RING)])
         for chunk, turn in zip(away, TURNS[1:])
     ]
     grad_tokens = ((own + from_far) + (from_back + from_ahead)).astype(BF).reshape(1, n, -1)
 
-    anywhere = pl.BlockSpec(memory_space=pl.ANY)
     grad_proj, grad_init, grad_gain, rates = pl.pallas_call(
         place_kernel,
-        out_shape=(shape(3, model, wide), small, shape(heads, HS), shape(heads, HS)),
-        in_specs=[SM] + [anywhere] * 24,
+        out_shape=(shape(3, model, wide), shape(heads, HS, HS), shape(heads, HS), shape(heads, HS)),
+        in_specs=[SM] + [anywhere] * 16,
         out_specs=(anywhere, VM, VM, VM),
         scratch_shapes=[
             pltpu.VMEM((EXTRA, wide), F32), pltpu.SemaphoreType.DMA((3, 8)), pltpu.SemaphoreType.DMA((8,))
         ],
         compiler_params=PARAMS,
-    )(pos, *query_pieces, *key_pieces, *value_pieces)
+    )(pos, *query_pieces, *both_pieces)
     return (grad_tokens, grad_proj, grad_init, grad_gain, rates[:, 0], grad_gates)
 
 

time: 169 us -> 155 us (0.917)
  the two profiles are of different devices: /device:TPU:1 before, /device:TPU:65 now
where the time goes in v2:
time: 155 us
  waiting for transfers between devices  79 us (51%)
  starting transfers between devices  44.9 us (29%)
  Pallas kernels  27.9 us (18%)
    ppermute x18, waiting for transfers between devices, round_turn(): lax.ppermute(chunk, ('dp', 'ctx'), moves(first, turn))  41.6 us
    ppermute x11, starting transfers between devices, swap(): return lax.ppermute(value, 'dp', [(i, i ^ 1) for i in range(2 * RING)])  20.1 us
    ppermute x3, waiting for transfers between devices, body(): lax.ppermute(chunk, 'head', [(i, (i + turn) % RING) for i in range(RING)])  19.1 us
    ppermute x18, starting transfers between devices, round_turn(): lax.ppermute(chunk, ('dp', 'ctx'), moves(first, turn))  12.5 us
    ppermute x11, waiting for transfers between devices, swap(): return lax.ppermute(value, 'dp', [(i, i ^ 1) for i in range(2 * RING)])  6.52 us
    ppermute x1, waiting for transfers between devices, body(): back_far = lax.ppermute(back_second, 'ctx', [(2, 0)])  6.27 us
    pallas_call x1, Pallas kernels, body(): pl.pallas_call(maps_kernel, grid=(1,), out_shape=(wide_f32, wide_f32, vme...  5.71 us
    ppermute x1, waiting for transfers between devices, body(): back_near = lax.ppermute(pulled, 'ctx', [(3, 2), (1, 0)])  5.43 us
  transfers between devices with their start and end apart: 39, of which 16 were waited for; matrix products, arithmetic and copies ran while one was open for 1% of the time, Pallas kernels for 7%

profile of v2, /device:TPU:65, one launch (start us, length us, event | category | flops | bytes accessed | tf_op | source)
XLA Modules:
  0.0 154.8 jit_solution(7873385377984813525)
XLA Ops:
  0.8 5.7 %shard_map.118 = (f32[256,256]{1,0:T(8,128)S(1)}, f32[256,256]{1,0:T(8,128)S(1)}, f32[2,256,128]{2,1,0:T(8,128)S(1)}, f32[2,256,256]{2,1,0:T(8,128)S(1)}, f32[2,...) custom-call(s32[5]{0:T(128)S(1)} %stack.23.pos_ref, ...), custom_call_target="tpu_custom_call" | custom-call | tf_op jit(solution)/shard_map/pallas_call | solution.py:415
  6.5 0.8 collective-permute-start.4
  7.2 3.2 %collective-permute-start = (f32[2,128,128]{2,1,0:T(8,128)S(1)}, f32[2,128,128]{2,1,0:T(8,128)S(1)}, u32[]{:S(2)}, u32[]{:S(2)}) collective-permute-start(f32[2,128,128]{2,1,0:T(8,128)S(1)} %get-tuple-element.50), channel_id=1, source_target_pairs={{0,4},{8,12},{1,5},{9,13},{2,6},{10,14},{3,7},{11,15},{16,20},{24,... | collective-permute-start | bytes 393224 | tf_op jit(solution)/shard_map/ppermute | solution.py:427
  10.5 1.3 collective-permute-start.3
  11.8 3.9 %shard_map.119 = (f32[256,256]{1,0:T(8,128)S(1)}, f32[2,256,256]{2,1,0:T(8,128)S(1)}, f32[256,256]{1,0:T(8,128)S(1)}, f32[256,256]{1,0:T(8,128)S(1)}, f32[256,25...) custom-call(s32[5]{0:T(128)S(1)} %stack.23.pos_ref, f32[2]{0:T(128)S(1)} %copy-done.3, ...), custom_call_target="tpu_custom_call" | custom-call | tf_op jit(solution)/shard_map/pallas_call | solution.py:431
  15.9 0.7 collective-permute-start.1
  16.6 0.7 collective-permute-start.2
  17.5 2.1 %shard_map.122 = (f32[2,128,128]{2,1,0:T(8,128)S(1)}, f32[256,256]{1,0:T(8,128)S(1)}, f32[2,128,128]{2,1,0:T(8,128)S(1)}, f32[2,128]{1,0:T(2,128)S(1)}) custom-call(s32[5]{0:T(128)S(1)} %stack.23.pos_ref, f32[2,128,128]{2,1,0:T(8,128)S(1)} %copy-done, f32[2,128,128]{2,1,0:T(8,128)S(1)} %collective-permute-done.w_ref.near_ref, ...), custom_call_target="tpu_custom_call" | custom-call | tf_op jit(solution)/shard_map/pallas_call | solution.py:447
  19.7 1.3 collective-permute-start.5
  21.0 2.9 %shard_map.123 = (f32[256,256]{1,0:T(8,128)S(1)}, f32[256,256]{1,0:T(8,128)S(1)}, f32[256,256]{1,0:T(8,128)S(1)}, f32[256,256]{1,0:T(8,128)S(1)}, f32[2,256]{1,0:T(2,128)S(1)}) custom-call(f32[2]{0:T(128)S(1)} %copy-done.3, f32[1,2,256]{2,1,0:T(2,128)S(1)} %copy-done.2, f32[2,128,128]{2,1,0:T(8,128)S(1)} %get-tuple-element.59.w_ref, ...), custom_call_target="tpu_custom_call" | custom-call | tf_op jit(solution)/shard_map/pallas_call | solution.py:453
  23.8 0.9 collective-permute-start.8
  24.7 5.4 %collective-permute-done.5.w_ref.rp_ref = f32[2,128,128]{2,1,0:T(8,128)S(1)} collective-permute-done((f32[2,128,128]{2,1,0:T(8,128)S(1)}, f32[2,128,128]{2,1,0:T(8,128)S(1)}, u32[]{:S(2)}, u32[]{:S(2)}) %collective-permute-start.5) | collective-permute-done | bytes 131104 | tf_op jit(solution)/shard_map/ppermute | solution.py:451
  30.3 0.7 collective-permute-start.6
  31.0 1.3 collective-permute-start.7
  32.3 1.0 shard_map.125
  33.3 6.3 %collective-permute-done.7.far_ref = f32[2,128,128]{2,1,0:T(8,128)S(1)} collective-permute-done((f32[2,128,128]{2,1,0:T(8,128)S(1)}, f32[2,128,128]{2,1,0:T(8,128)S(1)}, u32[]{:S(2)}, u32[]{:S(2)}) %collective-permute-start.7) | collective-permute-done | bytes 131104 | tf_op jit(solution)/shard_map/ppermute | solution.py:461
  39.6 3.3 %shard_map.126 = (f32[704,256]{1,0:T(8,128)S(1)}, f32[1,2,256]{2,1,0:T(2,128)}) custom-call(s32[5]{0:T(128)S(1)} %stack.23.pos_ref, f32[2]{0:T(128)S(1)} %copy-done.3, f32[1,2,256]{2,1,0:T(2,128)S(1)} %copy-done.2, f32[2,128,128]{2,1,0:T(8,128)S(1)} %collective-permute-done.5.w_ref.rp_ref, f32[2,128,128]{2,1,0:T(8,128)S(1)} %collective-permute-done.6.mid_ref, ...), custom_call_target="tpu_custom_call" | custom-call | tf_op jit(solution)/shard_map/pallas_call | solution.py:464
  42.9 2.6 %collective-permute-start.25 = (f32[704,256]{1,0:T(8,128)S(1)}, f32[704,256]{1,0:T(8,128)S(1)}, u32[]{:S(2)}, u32[]{:S(2)}) collective-permute-start(f32[704,256]{1,0:T(8,128)S(1)} %get-tuple-element.77.both_ref.own_ref), channel_id=1, source_target_pairs={{0,16},{16,0},{32,48},{48,32},{64,80},{80,64},{96,112},{112,96},{1... | collective-permute-start | bytes 2162696 | tf_op jit(solution)/shard_map/ppermute | solution.py:337
  45.6 1.8 %collective-permute-done.25.other_ref = f32[704,256]{1,0:T(8,128)S(1)} collective-permute-done((f32[704,256]{1,0:T(8,128)S(1)}, f32[704,256]{1,0:T(8,128)S(1)}, u32[]{:S(2)}, u32[]{:S(2)}) %collective-permute-start.25) | collective-permute-done | bytes 720928 | tf_op jit(solution)/shard_map/ppermute | solution.py:337
  47.4 1.3 shard_map.128
  48.7 2.7 %collective-permute-start.28 = (f32[536,256]{1,0:T(8,128)S(1)}, f32[536,256]{1,0:T(8,128)S(1)}, u32[]{:S(2)}, u32[]{:S(2)}) collective-permute-start(f32[536,256]{1,0:T(8,128)S(1)} %get-tuple-element.88), channel_id=1, source_target_pairs={{0,96},{4,100},{8,104},{12,108},{16,28},{20,16},{24,20},{28,24},{3... | collective-permute-start | bytes 1646600 | tf_op jit(solution)/shard_map/ppermute | solution.py:332
  51.4 0.6 collective-permute-start.13
  52.0 2.1 %collective-permute-start.14 = (f32[256,256]{1,0:T(8,128)S(1)}, f32[256,256]{1,0:T(8,128)S(1)}, u32[]{:S(2)}, u32[]{:S(2)}) collective-permute-start(f32[256,256]{1,0:T(8,128)S(1)} %get-tuple-element.84), channel_id=1, source_target_pairs={{0,96},{4,100},{8,104},{12,108},{16,28},{20,16},{24,20},{28,24},{3... | collective-permute-start | bytes 786440 | tf_op jit(solution)/shard_map/ppermute | solution.py:332
  54.1 10.3 %collective-permute-done.27 = f32[536,256]{1,0:T(8,128)S(1)} collective-permute-done((f32[536,256]{1,0:T(8,128)S(1)}, f32[536,256]{1,0:T(8,128)S(1)}, u32[]{:S(2)}, u32[]{:S(2)}) %collective-permute-start.27) | collective-permute-done | bytes 548896 | tf_op jit(solution)/shard_map/ppermute | solution.py:332
  64.6 1.1 collective-permute-start.30
  65.7 1.5 collective-permute-done.13
  67.2 2.1 %collective-permute-done.14 = f32[256,256]{1,0:T(8,128)S(1)} collective-permute-done((f32[256,256]{1,0:T(8,128)S(1)}, f32[256,256]{1,0:T(8,128)S(1)}, u32[]{:S(2)}, u32[]{:S(2)}) %collective-permute-start.14) | collective-permute-done | bytes 262176 | tf_op jit(solution)/shard_map/ppermute | solution.py:332
  69.3 4.9 %collective-permute-done.12 = f32[256,256]{1,0:T(8,128)S(1)} collective-permute-done((f32[256,256]{1,0:T(8,128)S(1)}, f32[256,256]{1,0:T(8,128)S(1)}, u32[]{:S(2)}, u32[]{:S(2)}) %collective-permute-start.12) | collective-permute-done | bytes 262176 | tf_op jit(solution)/shard_map/ppermute | solution.py:332
  74.2 0.9 collective-permute-start.16
  75.1 1.9 %collective-permute-start.31 = (f32[536,256]{1,0:T(8,128)S(1)}, f32[536,256]{1,0:T(8,128)S(1)}, u32[]{:S(2)}, u32[]{:S(2)}) collective-permute-start(f32[536,256]{1,0:T(8,128)S(1)} %add_add_fusion.1), channel_id=1, source_target_pairs={{0,12},{4,0},{8,4},{12,8},{16,112},{20,116},{24,120},{28,124},{32,... | collective-permute-start | bytes 1646600 | tf_op jit(solution)/shard_map/ppermute | solution.py:332
  77.0 1.1 collective-permute-start.29
  78.1 0.9 collective-permute-start.17
  79.0 2.1 %collective-permute-done.16 = f32[256,256]{1,0:T(8,128)S(1)} collective-permute-done((f32[256,256]{1,0:T(8,128)S(1)}, f32[256,256]{1,0:T(8,128)S(1)}, u32[]{:S(2)}, u32[]{:S(2)}) %collective-permute-start.16) | collective-permute-done | bytes 262176 | tf_op jit(solution)/shard_map/ppermute | solution.py:332
  81.0 1.1 collective-permute-start.15
  82.1 2.9 %shard_map.127 = (f32[256,512]{1,0:T(8,128)S(1)}, f32[256,512]{1,0:T(8,128)S(1)}, f32[256,512]{1,0:T(8,128)S(1)}, f32[256,512]{1,0:T(8,128)S(1)}) custom-call(s32[5]{0:T(128)S(1)} %stack.23.pos_ref, bf16[3,2048,256]{2,1,0:T(8,128)(2,1)} %w_ref.1, f32[256,256]{1,0:T(8,128)S(1)} %get-tuple-element.65.own_ref.dq_ref, ...), custom_call_target="tpu_custom_call" | custom-call | tf_op jit(solution)/shard_map/pallas_call | solution.py:474
  85.1 9.8 %collective-permute-done.17 = f32[256,256]{1,0:T(8,128)S(1)} collective-permute-done((f32[256,256]{1,0:T(8,128)S(1)}, f32[256,256]{1,0:T(8,128)S(1)}, u32[]{:S(2)}, u32[]{:S(2)}) %collective-permute-start.17) | collective-permute-done | bytes 262176 | tf_op jit(solution)/shard_map/ppermute | solution.py:332
  94.9 1.4 collective-permute-start.10
  96.3 1.7 %collective-permute-start.9 = (f32[256,512]{1,0:T(8,128)S(1)}, f32[256,512]{1,0:T(8,128)S(1)}, u32[]{:S(2)}, u32[]{:S(2)}) collective-permute-start(f32[256,512]{1,0:T(8,128)S(1)} %get-tuple-element.79), channel_id=1, source_target_pairs={{0,2},{1,3},{2,0},{3,1},{4,6},{5,7},{6,4},{7,5},{8,10},{9,11},{10,... | collective-permute-start | bytes 1572872 | tf_op jit(solution)/shard_map/ppermute | solution.py:483
  98.4 8.8 %collective-permute-done.10 = f32[256,512]{1,0:T(8,128)S(1)} collective-permute-done((f32[256,512]{1,0:T(8,128)S(1)}, f32[256,512]{1,0:T(8,128)S(1)}, u32[]{:S(2)}, u32[]{:S(2)}) %collective-permute-start.10) | collective-permute-done | bytes 524320 | tf_op jit(solution)/shard_map/ppermute | solution.py:483
  107.2 0.6 collective-permute-done.11
  107.8 9.7 %collective-permute-done.9 = f32[256,512]{1,0:T(8,128)S(1)} collective-permute-done((f32[256,512]{1,0:T(8,128)S(1)}, f32[256,512]{1,0:T(8,128)S(1)}, u32[]{:S(2)}, u32[]{:S(2)}) %collective-permute-start.9) | collective-permute-done | bytes 524320 | tf_op jit(solution)/shard_map/ppermute | solution.py:483
  117.6 10.9 %collective-permute-done.19.refs_2_ = f32[256,256]{1,0:T(8,128)S(1)} collective-permute-done((f32[256,256]{1,0:T(8,128)S(1)}, f32[256,256]{1,0:T(8,128)S(1)}, u32[]{:S(2)}, u32[]{:S(2)}) %collective-permute-start.19) | collective-permute-done | bytes 262176 | tf_op jit(solution)/shard_map/ppermute | solution.py:332
  128.5 14.1 %collective-permute-start.21 = (f32[256,256]{1,0:T(8,128)S(1)}, f32[256,256]{1,0:T(8,128)S(1)}, u32[]{:S(2)}, u32[]{:S(2)}) collective-permute-start(f32[256,256]{1,0:T(8,128)S(1)} %add_add_fusion.2.refs_0_), channel_id=1, source_target_pairs={{0,16},{16,0},{32,48},{48,32},{64,80},{80,64},{96,112},{112,96},{1... | collective-permute-start | bytes 786440 | tf_op jit(solution)/shard_map/ppermute | solution.py:337
  142.6 1.2 collective-permute-done.21.refs_4_
  145.2 3.3 %collective-permute-done.23.refs_6_ = f32[256,256]{1,0:T(8,128)S(1)} collective-permute-done((f32[256,256]{1,0:T(8,128)S(1)}, f32[256,256]{1,0:T(8,128)S(1)}, u32[]{:S(2)}, u32[]{:S(2)}) %collective-permute-start.23) | collective-permute-done | bytes 262176 | tf_op jit(solution)/shard_map/ppermute | solution.py:337
  148.8 0.9 fusion
  150.0 4.2 %shard_map.129 = (f32[3,2048,256]{2,1,0:T(8,128)}, f32[2,128,128]{2,1,0:T(8,128)}, f32[2,128]{1,0:T(2,128)}, f32[2,128]{1,0:T(2,128)S(1)}) custom-call(s32[5]{0:T(128)S(1)} %stack.23.pos_ref, f32[256,256]{1,0:T(8,128)S(1)} %add_add_fusion.2.refs_0_, f32[256,256]{1,0:T(8,128)S(1)} %collective-permute-done.18.refs_1_, ...), custom_call_target="tpu_custom_call" | custom-call | tf_op jit(solution)/shard_map/pallas_call | solution.py:488
  154.2 0.6 slice_reduce_fusion
  (59 shorter events, 3.6 us)
Async XLA Ops:
  0.6 11.1 %copy-start.3 = (f32[2]{0:T(128)S(1)}, f32[2]{0:T(128)}, u32[]{:S(2)}) copy-start(f32[2]{0:T(128)} %base_ref.7) | copy-start | bytes 28
  0.6 11.1 %copy-start.2 = (f32[1,2,256]{2,1,0:T(2,128)S(1)}, f32[1,2,256]{2,1,0:T(2,128)}, u32[]{:S(2)}) copy-start(f32[1,2,256]{2,1,0:T(2,128)} %gate_ref.7) | copy-start | bytes 6148
  0.8 16.7 %copy-start = (f32[2,128,128]{2,1,0:T(8,128)S(1)}, f32[2,128,128]{2,1,0:T(8,128)}, u32[]{:S(2)}) copy-start(f32[2,128,128]{2,1,0:T(8,128)} %init_ref.3) | copy-start | bytes 393220
  0.8 16.7 %copy-start.1 = (bf16[1,256,256]{2,1,0:T(8,128)(2,1)S(1)}, bf16[1,256,256]{2,1,0:T(8,128)(2,1)}, u32[]{:S(2)}) copy-start(bf16[1,256,256]{2,1,0:T(8,128)(2,1)} %up_ref.3) | copy-start | bytes 393220
  0.8 16.7 %copy-start.4 = (f32[2,128]{1,0:T(2,128)S(1)}, f32[2,128]{1,0:T(2,128)}, u32[]{:S(2)}) copy-start(f32[2,128]{1,0:T(2,128)} %gain_ref.1) | copy-start | bytes 3076
  6.5 10.7 %collective-permute-start.4 = (f32[256,1024]{1,0:T(8,128)S(1)}, f32[256,1024]{1,0:T(8,128)S(1)}, u32[]{:S(2)}, u32[]{:S(2)}) collective-permute-start(f32[256,1024]{1,0:T(8,128)S(1)} %get-tuple-element.58), channel_id=1, source_target_pairs={{0,16},{16,0},{32,48},{48,32},{64,80},{80,64},{96,112},{112,96},{1... | collective-permute-start | bytes 3145736 | tf_op jit(solution)/shard_map/ppermute | solution.py:337
  7.2 8.4 %collective-permute-start = (f32[2,128,128]{2,1,0:T(8,128)S(1)}, f32[2,128,128]{2,1,0:T(8,128)S(1)}, u32[]{:S(2)}, u32[]{:S(2)}) collective-permute-start(f32[2,128,128]{2,1,0:T(8,128)S(1)} %get-tuple-element.50), channel_id=1, source_target_pairs={{0,4},{8,12},{1,5},{9,13},{2,6},{10,14},{3,7},{11,15},{16,20},{24,... | collective-permute-start | bytes 393224 | tf_op jit(solution)/shard_map/ppermute | solution.py:427
  10.5 7.0 %collective-permute-start.3 = (f32[2,128,128]{2,1,0:T(8,128)S(1)}, f32[2,128,128]{2,1,0:T(8,128)S(1)}, u32[]{:S(2)}, u32[]{:S(2)}) collective-permute-start(f32[2,128,128]{2,1,0:T(8,128)S(1)} %get-tuple-element.51.d_ref), channel_id=1, source_target_pairs={{8,12},{4,0},{9,13},{5,1},{10,14},{6,2},{11,15},{7,3},{24,28},{20,... | collective-permute-start | bytes 393224 | tf_op jit(solution)/shard_map/ppermute | solution.py:428
  15.9 1.6 %collective-permute-start.1 = (f32[2,128,128]{2,1,0:T(8,128)S(1)}, f32[2,128,128]{2,1,0:T(8,128)S(1)}, u32[]{:S(2)}, u32[]{:S(2)}) collective-permute-start(f32[2,128,128]{2,1,0:T(8,128)S(1)} %shard_map.120), channel_id=1, source_target_pairs={{4,8},{5,9},{6,10},{7,11},{20,24},{21,25},{22,26},{23,27},{36,40},... | collective-permute-start | bytes 393224 | tf_op jit(solution)/shard_map/ppermute | solution.py:443
  16.6 0.9 collective-permute-start.2
  19.7 10.4 %collective-permute-start.5 = (f32[2,128,128]{2,1,0:T(8,128)S(1)}, f32[2,128,128]{2,1,0:T(8,128)S(1)}, u32[]{:S(2)}, u32[]{:S(2)}) collective-permute-start(f32[2,128,128]{2,1,0:T(8,128)S(1)} %get-tuple-element.66.o_ref.p_ref), channel_id=1, source_target_pairs={{12,8},{4,0},{13,9},{5,1},{14,10},{6,2},{15,11},{7,3},{28,24},{20,... | collective-permute-start | bytes 393224 | tf_op jit(solution)/shard_map/ppermute | solution.py:451
  23.8 8.5 %collective-permute-start.8 = (f32[256,256]{1,0:T(8,128)S(1)}, f32[256,256]{1,0:T(8,128)S(1)}, u32[]{:S(2)}, u32[]{:S(2)}) collective-permute-start(f32[256,256]{1,0:T(8,128)S(1)} %get-tuple-element.65.own_ref.dq_ref), channel_id=1, source_target_pairs={{0,16},{16,0},{32,48},{48,32},{64,80},{80,64},{96,112},{112,96},{1... | collective-permute-start | bytes 786440 | tf_op jit(solution)/shard_map/ppermute | solution.py:337
  30.3 3.0 %collective-permute-start.6 = (f32[2,128,128]{2,1,0:T(8,128)S(1)}, f32[2,128,128]{2,1,0:T(8,128)S(1)}, u32[]{:S(2)}, u32[]{:S(2)}) collective-permute-start(f32[2,128,128]{2,1,0:T(8,128)S(1)} %shard_map.124), channel_id=1, source_target_pairs={{8,4},{9,5},{10,6},{11,7},{24,20},{25,21},{26,22},{27,23},{40,36},... | collective-permute-start | bytes 393224 | tf_op jit(solution)/shard_map/ppermute | solution.py:460
  31.0 8.6 %collective-permute-start.7 = (f32[2,128,128]{2,1,0:T(8,128)S(1)}, f32[2,128,128]{2,1,0:T(8,128)S(1)}, u32[]{:S(2)}, u32[]{:S(2)}) collective-permute-start(f32[2,128,128]{2,1,0:T(8,128)S(1)} %shard_map.124), channel_id=1, source_target_pairs={{8,0},{9,1},{10,2},{11,3},{24,16},{25,17},{26,18},{27,19},{40,32},... | collective-permute-start | bytes 393224 | tf_op jit(solution)/shard_map/ppermute | solution.py:461
  42.9 4.4 %collective-permute-start.25 = (f32[704,256]{1,0:T(8,128)S(1)}, f32[704,256]{1,0:T(8,128)S(1)}, u32[]{:S(2)}, u32[]{:S(2)}) collective-permute-start(f32[704,256]{1,0:T(8,128)S(1)} %get-tuple-element.77.both_ref.own_ref), channel_id=1, source_target_pairs={{0,16},{16,0},{32,48},{48,32},{64,80},{80,64},{96,112},{112,96},{1... | collective-permute-start | bytes 2162696 | tf_op jit(solution)/shard_map/ppermute | solution.py:337
  48.7 15.8 %collective-permute-start.27 = (f32[536,256]{1,0:T(8,128)S(1)}, f32[536,256]{1,0:T(8,128)S(1)}, u32[]{:S(2)}, u32[]{:S(2)}) collective-permute-start(f32[536,256]{1,0:T(8,128)S(1)} %get-tuple-element.87), channel_id=1, source_target_pairs={{0,32},{4,36},{8,40},{12,44},{16,20},{20,24},{24,28},{28,16},{32,6... | collective-permute-start | bytes 1646600 | tf_op jit(solution)/shard_map/ppermute | solution.py:332
  48.7 15.7 %collective-permute-start.28 = (f32[536,256]{1,0:T(8,128)S(1)}, f32[536,256]{1,0:T(8,128)S(1)}, u32[]{:S(2)}, u32[]{:S(2)}) collective-permute-start(f32[536,256]{1,0:T(8,128)S(1)} %get-tuple-element.88), channel_id=1, source_target_pairs={{0,96},{4,100},{8,104},{12,108},{16,28},{20,16},{24,20},{28,24},{3... | collective-permute-start | bytes 1646600 | tf_op jit(solution)/shard_map/ppermute | solution.py:332
  51.4 13.0 %collective-permute-start.26 = (f32[536,256]{1,0:T(8,128)S(1)}, f32[536,256]{1,0:T(8,128)S(1)}, u32[]{:S(2)}, u32[]{:S(2)}) collective-permute-start(f32[536,256]{1,0:T(8,128)S(1)} %get-tuple-element.86), channel_id=1, source_target_pairs={{0,64},{4,68},{8,72},{12,76},{16,24},{20,28},{24,16},{28,20},{32,9... | collective-permute-start | bytes 1646600 | tf_op jit(solution)/shard_map/ppermute | solution.py:332
  51.4 15.8 %collective-permute-start.13 = (f32[256,256]{1,0:T(8,128)S(1)}, f32[256,256]{1,0:T(8,128)S(1)}, u32[]{:S(2)}, u32[]{:S(2)}) collective-permute-start(f32[256,256]{1,0:T(8,128)S(1)} %get-tuple-element.83), channel_id=1, source_target_pairs={{0,32},{4,36},{8,40},{12,44},{16,20},{20,24},{24,28},{28,16},{32,6... | collective-permute-start | bytes 786440 | tf_op jit(solution)/shard_map/ppermute | solution.py:332
  52.0 17.3 %collective-permute-start.14 = (f32[256,256]{1,0:T(8,128)S(1)}, f32[256,256]{1,0:T(8,128)S(1)}, u32[]{:S(2)}, u32[]{:S(2)}) collective-permute-start(f32[256,256]{1,0:T(8,128)S(1)} %get-tuple-element.84), channel_id=1, source_target_pairs={{0,96},{4,100},{8,104},{12,108},{16,28},{20,16},{24,20},{28,24},{3... | collective-permute-start | bytes 786440 | tf_op jit(solution)/shard_map/ppermute | solution.py:332
  64.4 9.8 %collective-permute-start.12 = (f32[256,256]{1,0:T(8,128)S(1)}, f32[256,256]{1,0:T(8,128)S(1)}, u32[]{:S(2)}, u32[]{:S(2)}) collective-permute-start(f32[256,256]{1,0:T(8,128)S(1)} %get-tuple-element.82), channel_id=1, source_target_pairs={{0,64},{4,68},{8,72},{12,76},{16,24},{20,28},{24,16},{28,20},{32,9... | collective-permute-start | bytes 786440 | tf_op jit(solution)/shard_map/ppermute | solution.py:332
  64.6 31.8 %collective-permute-start.30 = (f32[536,256]{1,0:T(8,128)S(1)}, f32[536,256]{1,0:T(8,128)S(1)}, u32[]{:S(2)}, u32[]{:S(2)}) collective-permute-start(f32[536,256]{1,0:T(8,128)S(1)} %add_add_fusion.1), channel_id=1, source_target_pairs={{0,4},{4,8},{8,12},{12,0},{16,48},{20,52},{24,56},{28,60},{32,36},... | collective-permute-start | bytes 1646600 | tf_op jit(solution)/shard_map/ppermute | solution.py:332
  74.2 6.8 %collective-permute-start.16 = (f32[256,256]{1,0:T(8,128)S(1)}, f32[256,256]{1,0:T(8,128)S(1)}, u32[]{:S(2)}, u32[]{:S(2)}) collective-permute-start(f32[256,256]{1,0:T(8,128)S(1)} %add_add_fusion.3), channel_id=1, source_target_pairs={{0,4},{4,8},{8,12},{12,0},{16,48},{20,52},{24,56},{28,60},{32,36},... | collective-permute-start | bytes 786440 | tf_op jit(solution)/shard_map/ppermute | solution.py:332
  75.1 23.0 %collective-permute-start.31 = (f32[536,256]{1,0:T(8,128)S(1)}, f32[536,256]{1,0:T(8,128)S(1)}, u32[]{:S(2)}, u32[]{:S(2)}) collective-permute-start(f32[536,256]{1,0:T(8,128)S(1)} %add_add_fusion.1), channel_id=1, source_target_pairs={{0,12},{4,0},{8,4},{12,8},{16,112},{20,116},{24,120},{28,124},{32,... | collective-permute-start | bytes 1646600 | tf_op jit(solution)/shard_map/ppermute | solution.py:332
  77.0 21.2 %collective-permute-start.29 = (f32[536,256]{1,0:T(8,128)S(1)}, f32[536,256]{1,0:T(8,128)S(1)}, u32[]{:S(2)}, u32[]{:S(2)}) collective-permute-start(f32[536,256]{1,0:T(8,128)S(1)} %add_add_fusion.1), channel_id=1, source_target_pairs={{0,8},{4,12},{8,0},{12,4},{16,80},{20,84},{24,88},{28,92},{32,40},... | collective-permute-start | bytes 1646600 | tf_op jit(solution)/shard_map/ppermute | solution.py:332
  78.1 16.8 %collective-permute-start.17 = (f32[256,256]{1,0:T(8,128)S(1)}, f32[256,256]{1,0:T(8,128)S(1)}, u32[]{:S(2)}, u32[]{:S(2)}) collective-permute-start(f32[256,256]{1,0:T(8,128)S(1)} %add_add_fusion.3), channel_id=1, source_target_pairs={{0,12},{4,0},{8,4},{12,8},{16,112},{20,116},{24,120},{28,124},{32,... | collective-permute-start | bytes 786440 | tf_op jit(solution)/shard_map/ppermute | solution.py:332
  81.0 15.2 %collective-permute-start.15 = (f32[256,256]{1,0:T(8,128)S(1)}, f32[256,256]{1,0:T(8,128)S(1)}, u32[]{:S(2)}, u32[]{:S(2)}) collective-permute-start(f32[256,256]{1,0:T(8,128)S(1)} %add_add_fusion.3), channel_id=1, source_target_pairs={{0,8},{4,12},{8,0},{12,4},{16,80},{20,84},{24,88},{28,92},{32,40},... | collective-permute-start | bytes 786440 | tf_op jit(solution)/shard_map/ppermute | solution.py:332
  94.9 12.3 %collective-permute-start.10 = (f32[256,512]{1,0:T(8,128)S(1)}, f32[256,512]{1,0:T(8,128)S(1)}, u32[]{:S(2)}, u32[]{:S(2)}) collective-permute-start(f32[256,512]{1,0:T(8,128)S(1)} %get-tuple-element.80), channel_id=1, source_target_pairs={{0,1},{1,2},{2,3},{3,0},{4,5},{5,6},{6,7},{7,4},{8,9},{9,10},{10,1... | collective-permute-start | bytes 1572872 | tf_op jit(solution)/shard_map/ppermute | solution.py:483
  96.2 11.6 %collective-permute-start.11 = (f32[256,512]{1,0:T(8,128)S(1)}, f32[256,512]{1,0:T(8,128)S(1)}, u32[]{:S(2)}, u32[]{:S(2)}) collective-permute-start(f32[256,512]{1,0:T(8,128)S(1)} %get-tuple-element.81), channel_id=1, source_target_pairs={{0,3},{1,0},{2,1},{3,2},{4,7},{5,4},{6,5},{7,6},{8,11},{9,8},{10,9... | collective-permute-start | bytes 1572872 | tf_op jit(solution)/shard_map/ppermute | solution.py:483
  96.3 21.2 %collective-permute-start.9 = (f32[256,512]{1,0:T(8,128)S(1)}, f32[256,512]{1,0:T(8,128)S(1)}, u32[]{:S(2)}, u32[]{:S(2)}) collective-permute-start(f32[256,512]{1,0:T(8,128)S(1)} %get-tuple-element.79), channel_id=1, source_target_pairs={{0,2},{1,3},{2,0},{3,1},{4,6},{5,7},{6,4},{7,5},{8,10},{9,11},{10,... | collective-permute-start | bytes 1572872 | tf_op jit(solution)/shard_map/ppermute | solution.py:483
  98.1 19.5 %collective-permute-start.18 = (f32[256,256]{1,0:T(8,128)S(1)}, f32[256,256]{1,0:T(8,128)S(1)}, u32[]{:S(2)}, u32[]{:S(2)}) collective-permute-start(f32[256,256]{1,0:T(8,128)S(1)} %add_add_fusion.2.refs_0_), channel_id=1, source_target_pairs={{0,96},{4,100},{8,104},{12,108},{16,28},{20,16},{24,20},{28,24},{3... | collective-permute-start | bytes 786440 | tf_op jit(solution)/shard_map/ppermute | solution.py:332
  98.4 45.8 %collective-permute-start.32 = (f32[536,256]{1,0:T(8,128)S(1)}, f32[536,256]{1,0:T(8,128)S(1)}, u32[]{:S(2)}, u32[]{:S(2)}) collective-permute-start(f32[536,256]{1,0:T(8,128)S(1)} %add_add_fusion.refs_8_), channel_id=1, source_target_pairs={{0,96},{4,100},{8,104},{12,108},{16,28},{20,16},{24,20},{28,24},{3... | collective-permute-start | bytes 1646600 | tf_op jit(solution)/shard_map/ppermute | solution.py:332
  107.2 37.1 %collective-permute-start.33 = (f32[536,256]{1,0:T(8,128)S(1)}, f32[536,256]{1,0:T(8,128)S(1)}, u32[]{:S(2)}, u32[]{:S(2)}) collective-permute-start(f32[536,256]{1,0:T(8,128)S(1)} %add_add_fusion.refs_8_), channel_id=1, source_target_pairs={{0,32},{4,36},{8,40},{12,44},{16,20},{20,24},{24,28},{28,16},{32,6... | collective-permute-start | bytes 1646600 | tf_op jit(solution)/shard_map/ppermute | solution.py:332
  107.8 36.8 %collective-permute-start.34 = (f32[536,256]{1,0:T(8,128)S(1)}, f32[536,256]{1,0:T(8,128)S(1)}, u32[]{:S(2)}, u32[]{:S(2)}) collective-permute-start(f32[536,256]{1,0:T(8,128)S(1)} %add_add_fusion.refs_8_), channel_id=1, source_target_pairs={{0,64},{4,68},{8,72},{12,76},{16,24},{20,28},{24,16},{28,20},{32,9... | collective-permute-start | bytes 1646600 | tf_op jit(solution)/shard_map/ppermute | solution.py:332
  117.6 10.9 %collective-permute-start.19 = (f32[256,256]{1,0:T(8,128)S(1)}, f32[256,256]{1,0:T(8,128)S(1)}, u32[]{:S(2)}, u32[]{:S(2)}) collective-permute-start(f32[256,256]{1,0:T(8,128)S(1)} %add_add_fusion.2.refs_0_), channel_id=1, source_target_pairs={{0,32},{4,36},{8,40},{12,44},{16,20},{20,24},{24,28},{28,16},{32,6... | collective-permute-start | bytes 786440 | tf_op jit(solution)/shard_map/ppermute | solution.py:332
  117.6 25.0 %collective-permute-start.20 = (f32[256,256]{1,0:T(8,128)S(1)}, f32[256,256]{1,0:T(8,128)S(1)}, u32[]{:S(2)}, u32[]{:S(2)}) collective-permute-start(f32[256,256]{1,0:T(8,128)S(1)} %add_add_fusion.2.refs_0_), channel_id=1, source_target_pairs={{0,64},{4,68},{8,72},{12,76},{16,24},{20,28},{24,16},{28,20},{32,9... | collective-permute-start | bytes 786440 | tf_op jit(solution)/shard_map/ppermute | solution.py:332
  128.5 15.3 %collective-permute-start.21 = (f32[256,256]{1,0:T(8,128)S(1)}, f32[256,256]{1,0:T(8,128)S(1)}, u32[]{:S(2)}, u32[]{:S(2)}) collective-permute-start(f32[256,256]{1,0:T(8,128)S(1)} %add_add_fusion.2.refs_0_), channel_id=1, source_target_pairs={{0,16},{16,0},{32,48},{48,32},{64,80},{80,64},{96,112},{112,96},{1... | collective-permute-start | bytes 786440 | tf_op jit(solution)/shard_map/ppermute | solution.py:337
  142.6 2.2 %collective-permute-start.22 = (f32[256,256]{1,0:T(8,128)S(1)}, f32[256,256]{1,0:T(8,128)S(1)}, u32[]{:S(2)}, u32[]{:S(2)}) collective-permute-start(f32[256,256]{1,0:T(8,128)S(1)} %collective-permute-done.18.refs_1_), channel_id=1, source_target_pairs={{0,16},{16,0},{32,48},{48,32},{64,80},{80,64},{96,112},{112,96},{1... | collective-permute-start | bytes 786440 | tf_op jit(solution)/shard_map/ppermute | solution.py:337
  143.8 6.2 %collective-permute-start.35 = (f32[536,256]{1,0:T(8,128)S(1)}, f32[536,256]{1,0:T(8,128)S(1)}, u32[]{:S(2)}, u32[]{:S(2)}) collective-permute-start(f32[536,256]{1,0:T(8,128)S(1)} %add_add_fusion.refs_8_), channel_id=1, source_target_pairs={{0,16},{16,0},{32,48},{48,32},{64,80},{80,64},{96,112},{112,96},{1... | collective-permute-start | bytes 1646600 | tf_op jit(solution)/shard_map/ppermute | solution.py:337
  144.1 5.8 %collective-permute-start.36 = (f32[536,256]{1,0:T(8,128)S(1)}, f32[536,256]{1,0:T(8,128)S(1)}, u32[]{:S(2)}, u32[]{:S(2)}) collective-permute-start(f32[536,256]{1,0:T(8,128)S(1)} %collective-permute-done.32.refs_9_), channel_id=1, source_target_pairs={{0,16},{16,0},{32,48},{48,32},{64,80},{80,64},{96,112},{112,96},{1... | collective-permute-start | bytes 1646600 | tf_op jit(solution)/shard_map/ppermute | solution.py:337
  144.3 5.7 %collective-permute-start.37 = (f32[536,256]{1,0:T(8,128)S(1)}, f32[536,256]{1,0:T(8,128)S(1)}, u32[]{:S(2)}, u32[]{:S(2)}) collective-permute-start(f32[536,256]{1,0:T(8,128)S(1)} %collective-permute-done.33.refs_10_), channel_id=1, source_target_pairs={{0,16},{16,0},{32,48},{48,32},{64,80},{80,64},{96,112},{112,96},{1... | collective-permute-start | bytes 1646600 | tf_op jit(solution)/shard_map/ppermute | solution.py:337
  144.7 5.3 %collective-permute-start.38 = (f32[536,256]{1,0:T(8,128)S(1)}, f32[536,256]{1,0:T(8,128)S(1)}, u32[]{:S(2)}, u32[]{:S(2)}) collective-permute-start(f32[536,256]{1,0:T(8,128)S(1)} %collective-permute-done.34.refs_11_), channel_id=1, source_target_pairs={{0,16},{16,0},{32,48},{48,32},{64,80},{80,64},{96,112},{112,96},{1... | collective-permute-start | bytes 1646600 | tf_op jit(solution)/shard_map/ppermute | solution.py:337
  144.8 3.6 %collective-permute-start.23 = (f32[256,256]{1,0:T(8,128)S(1)}, f32[256,256]{1,0:T(8,128)S(1)}, u32[]{:S(2)}, u32[]{:S(2)}) collective-permute-start(f32[256,256]{1,0:T(8,128)S(1)} %collective-permute-done.19.refs_2_), channel_id=1, source_target_pairs={{0,16},{16,0},{32,48},{48,32},{64,80},{80,64},{96,112},{112,96},{1... | collective-permute-start | bytes 786440 | tf_op jit(solution)/shard_map/ppermute | solution.py:337
  148.4 1.5 collective-permute-start.24

commit v3 on v2

--- a/solution.py
+++ b/solution.py
@@ -209,27 +209,27 @@
 
 def keys_kernel(
     pos_ref, base_ref, gate_ref, rp_ref, mid_ref, far_ref, rd_ref, p_ref, d_ref, w_ref, k_ref, ninv_ref,
-    gram_ref, bt_ref, r_ref, x_ref, dk_ref, de_ref, dgain_ref, after_ref,
-    both_ref, gates_ref,
+    gram_ref, bt_ref, r_ref, x_ref, dk_ref, de_ref, dgain_ref, dq_ref,
+    all_ref, gates_ref,
 ):
-    del after_ref
     ctx = pos_ref[4]
     n = k_ref.shape[0]
     i, j = places(n)
     strict = (i // MB) > (j // MB)
-    both_ref[2 * n + HS : 2 * n + EXTRA, :] = jnp.zeros((EXTRA - HS, both_ref.shape[1]), F32)
+    all_ref[0:n, :] = dq_ref[...]
+    all_ref[3 * n + HS : 3 * n + EXTRA, :] = jnp.zeros((EXTRA - HS, all_ref.shape[1]), F32)
     for h in range(w_ref.shape[0]):
         first = rp_ref[h] + dot(rd_ref[h], far_ref[h], TN, 3)
         end = jnp.where(
             ctx == 0, first, jnp.where(ctx == 1, mid_ref[h], jnp.where(ctx == 2, rp_ref[h], 0.0))
         )
-        both_ref[2 * n : 2 * n + HS, span(h)] = jnp.where(ctx == 0, p_ref[h] + dot(d_ref[h], end, TN, 3), 0.0)
+        all_ref[3 * n : 3 * n + HS, span(h)] = jnp.where(ctx == 0, p_ref[h] + dot(d_ref[h], end, TN, 3), 0.0)
         w = w_ref[h]
         k = k_ref[:, span(h)]
         r = r_ref[:, span(h)]
         boost, e = rates_of(base_ref, gate_ref, h)
         x = x_ref[:, span(h)] + dot(bt_ref[h], end, TN, 3)
-        both_ref[n : 2 * n, span(h)] = x.astype(BF).astype(F32)
+        all_ref[2 * n : 3 * n, span(h)] = x.astype(BF).astype(F32)
         d_low = jnp.where(strict, -dot(x, r, NT, 3), 0.0)
         d_gram = d_low * e
         dk = (
@@ -241,11 +241,11 @@
         pull = to_row(jnp.sum(r * dot(k, end, NN, 3), axis=1, keepdims=True))
         de = de_ref[h : h + 1, :] + jnp.sum(d_low * gram_ref[h], axis=0, keepdims=True) + pull
         draw = ninv_ref[h] * (dk - k * jnp.sum(k * dk, -1, keepdims=True))
-        both_ref[0:n, span(h)] = draw.astype(BF).astype(F32)
+        all_ref[n : 2 * n, span(h)] = draw.astype(BF).astype(F32)
         d_boost = de / ((1.0 + boost) * (1.0 + boost))
         gates_ref[0, h : h + 1, :] = d_boost * base_ref[h]
-        both_ref[2 * n + HS : 2 * n + HS + 1, span(h)] = dgain_ref[h : h + 1, :]
-        both_ref[2 * n + HS + 1 : 2 * n + HS + 2, span(h)] = jnp.broadcast_to(
+        all_ref[3 * n + HS : 3 * n + HS + 1, span(h)] = dgain_ref[h : h + 1, :]
+        all_ref[3 * n + HS + 1 : 3 * n + HS + 2, span(h)] = jnp.broadcast_to(
             jnp.sum(d_boost * gate_ref[0, h : h + 1, :], axis=1, keepdims=True), (1, HS)
         )
 
@@ -256,59 +256,64 @@
 
 def product_kernel(pos_ref, tokt_ref, other_tokt_ref, own_ref, other_ref, *out_refs):
     n = tokt_ref.shape[1]
-    count = own_ref.shape[0] // n
-    if count > 1:
-        count = (own_ref.shape[0] - EXTRA) // n
     for turn, out_ref in zip(TURNS, out_refs):
         at = (pos_ref[1] + turn) & (RING - 1)
         rows = pl.ds(pl.multiple_of(at * CHUNK, CHUNK), CHUNK)
-        for m in range(count):
+        for m in range(3):
             out_ref[m * CHUNK : (m + 1) * CHUNK, :] = jnp.dot(
                 tokt_ref[rows, :], own_ref[m * n : (m + 1) * n, :].astype(BF), preferred_element_type=F32
             ) + jnp.dot(
                 other_tokt_ref[rows, :], other_ref[m * n : (m + 1) * n, :].astype(BF), preferred_element_type=F32
             )
-        if count > 1:
-            extra = pl.ds(pl.multiple_of(count * n + (pos_ref[0] * RING + at) * PIECE, 8), PIECE)
-            out_ref[count * CHUNK : count * CHUNK + PIECE, :] = own_ref[extra, :] + other_ref[extra, :]
-
-
-def token_kernel(pos_ref, w_ref, dq_ref, both_ref, *out_refs):
-    n = dq_ref.shape[0]
-    ds = [dq_ref[...].astype(BF), both_ref[0:n, :].astype(BF), both_ref[n : 2 * n, :].astype(BF)]
+        extra = pl.ds(pl.multiple_of(3 * n + (pos_ref[0] * RING + at) * PIECE, 8), PIECE)
+        out_ref[3 * CHUNK : 3 * CHUNK + PIECE, :] = own_ref[extra, :] + other_ref[extra, :]
+
+
+def token_kernel(w_ref, all_ref, out_ref, held_ref, sem):
+    n = out_ref.shape[1]
+    ds = [all_ref[m * n : (m + 1) * n, :].astype(BF) for m in range(3)]
     span_rows = w_ref.shape[1] // RING
-    for turn, out_ref in zip(TURNS, out_refs):
-        at = (pos_ref[3] + turn) & (RING - 1)
-        rows = pl.ds(pl.multiple_of(at * span_rows, span_rows), span_rows)
+    copies = []
+    for at in range(RING):
+        rows = slice(at * span_rows, (at + 1) * span_rows)
         total = lax.dot_general(ds[0], w_ref[0, rows, :], NT, preferred_element_type=F32)
         total = total + lax.dot_general(ds[1], w_ref[1, rows, :], NT, preferred_element_type=F32)
-        out_ref[...] = total + lax.dot_general(ds[2], w_ref[2, rows, :], NT, preferred_element_type=F32)
-
-
-def place_kernel(pos_ref, *refs):
-    out_ref, init_ref, gain_ref, rates_ref, extra_ref, sem, extra_sem = refs[16:]
+        held_ref[at] = total + lax.dot_general(ds[2], w_ref[2, rows, :], NT, preferred_element_type=F32)
+        copies.append(pltpu.make_async_copy(held_ref.at[at], out_ref.at[at], sem.at[at]))
+        copies[-1].start()
+    for copy in copies:
+        copy.wait()
+
+
+def sum_kernel(own_ref, back_ref, ahead_ref, far_ref, out_ref):
+    out_ref[...] = (own_ref[...] + far_ref[...]) + (back_ref[...] + ahead_ref[...])
+
+
+def place_kernel(pos_ref, *refs, half):
+    pieces = refs[:RING]
+    out_ref, extra_ref, sem = refs[-3:]
+    core = pos_ref[0] if half == 0 else 1 - pos_ref[0]
     copies = []
-    for m in range(8):
-        half, turn = m // RING, TURNS[m % RING]
-        core = pos_ref[0] if half == 0 else 1 - pos_ref[0]
-        at = core * RING + ((pos_ref[1 + half] + turn) & (RING - 1))
+    for m, piece in enumerate(pieces):
+        at = core * RING + ((pos_ref[1 + half] + TURNS[m]) & (RING - 1))
         rows = pl.ds(pl.multiple_of(at * CHUNK, CHUNK), CHUNK)
         for s in range(3):
-            piece = refs[m] if s == 0 else refs[8 + m]
-            start = 0 if s == 0 else (s - 1) * CHUNK
             copies.append(
-                pltpu.make_async_copy(piece.at[pl.ds(start, CHUNK), :], out_ref.at[s, rows, :], sem.at[s, m])
+                pltpu.make_async_copy(piece.at[pl.ds(s * CHUNK, CHUNK), :], out_ref.at[s, rows, :], sem.at[s, m])
             )
-        rows = pl.ds(pl.multiple_of(at * PIECE, 8), PIECE)
-        copies.append(
-            pltpu.make_async_copy(
-                refs[8 + m].at[pl.ds(2 * CHUNK, PIECE), :], extra_ref.at[rows, :], extra_sem.at[m]
-            )
-        )
     for copy in copies:
         copy.start()
+    for m, piece in enumerate(pieces):
+        at = (pos_ref[1 + half] + TURNS[m]) & (RING - 1)
+        extra_ref[pl.ds(pl.multiple_of(at * PIECE, 8), PIECE), :] = piece[3 * CHUNK : 3 * CHUNK + PIECE, :]
     for copy in copies:
         copy.wait()
+
+
+def small_kernel(pos_ref, own_ref, other_ref, init_ref, gain_ref, rates_ref, extra_ref):
+    rows = own_ref.shape[0]
+    extra_ref[pl.ds(pl.multiple_of(pos_ref[0] * rows, 8), rows), :] = own_ref[...]
+    extra_ref[pl.ds(pl.multiple_of((1 - pos_ref[0]) * rows, 8), rows), :] = other_ref[...]
     for h in range(init_ref.shape[0]):
         init_ref[h] = extra_ref[0:HS, span(h)]
         gain_ref[h : h + 1, :] = extra_ref[HS : HS + 1, span(h)]
@@ -335,25 +340,6 @@
 
 def swap(value):
     return lax.ppermute(value, "dp", [(i, i ^ 1) for i in range(2 * RING)])
-
-
-def reduce_products(pos, tokt, other_tokt, d):
-    other = swap(d)
-    rows = d.shape[0] if d.shape[0] == CHUNK else 2 * CHUNK + PIECE
-    return whole(product_kernel, (vmem(rows, d.shape[1]),) * RING, [SM] + [VM] * 4)(
-        pos, tokt, other_tokt, d, other
-    )
-
-
-def reduce_stream(products):
-    own, *away = products
-    from_back, from_ahead, from_far = round_turn(away, True)
-    part_sum = (own + from_far) + (from_back + from_ahead)
-    from_back, from_ahead, from_far = round_turn([part_sum] * 3, False)
-    total = (part_sum + from_far) + (from_back + from_ahead)
-    from_back, from_ahead, from_far = round_turn([total] * 3, True)
-    mine = [total, from_ahead, from_back, from_far]
-    return mine + [swap(piece) for piece in mine]
 
 
 VM = pl.BlockSpec(memory_space=pltpu.VMEM)
@@ -409,6 +395,7 @@
     small = vmem(heads, HS, HS)
     wspec = functools.partial(part, dims=(model, wide))
     tokens = hbm(tokens)
+    raw_weights = proj_weights
     proj_weights = hbm(proj_weights)
     anywhere = pl.BlockSpec(memory_space=pl.ANY)
 
@@ -459,42 +446,60 @@
     )
     back_mid = lax.ppermute(back_second, "ctx", [(2, 1)])
     back_far = lax.ppermute(back_second, "ctx", [(2, 0)])
-    query_products = reduce_products(pos, tokt, other_tokt, dq)
-
-    both, grad_gates = whole(
-        keys_kernel, (vmem(2 * n + EXTRA, wide), shape(1, heads, n)), [SM, SM] + [VM] * 17 + [anywhere]
+
+    grads, grad_gates = whole(
+        keys_kernel, (vmem(3 * n + EXTRA, wide), shape(1, heads, n)), [SM, SM] + [VM] * 18
     )(pos, base_rates, gate_values, back_near, back_mid, back_far, moved, pulled, decay, w, k, ninv, gram, bt, r, x,
-      dk, de, dgain, query_products[0])
-
-    both_products = reduce_products(pos, tokt, other_tokt, both)
-    query_pieces = reduce_stream(query_products)
-    both_pieces = reduce_stream(both_products)
-
-    quarter = vmem(n, model // RING)
-    own, *away = pl.pallas_call(
+      dk, de, dgain, dq)
+
+    chunk = vmem(3 * CHUNK + PIECE, wide)
+    own, *away = whole(product_kernel, (chunk,) * RING, [SM] + [VM] * 4)(
+        pos, tokt, other_tokt, grads, swap(grads)
+    )
+    away = round_turn(away, True)
+    summed = pl.pallas_call(
         token_kernel,
-        grid=(1,),
-        out_shape=(quarter,) * RING,
-        in_specs=[SM, full(3, model, wide), VM, VM],
-        out_specs=(VM,) * RING,
-        compiler_params=PARAMS,
-    )(pos, proj_weights, dq, both)
-    from_back, from_ahead, from_far = [
-        lax.ppermute(chunk, "head", [(i, (i + turn) % RING) for i in range(RING)])
-        for chunk, turn in zip(away, TURNS[1:])
-    ]
-    grad_tokens = ((own + from_far) + (from_back + from_ahead)).astype(BF).reshape(1, n, -1)
-
-    grad_proj, grad_init, grad_gain, rates = pl.pallas_call(
-        place_kernel,
-        out_shape=(shape(3, model, wide), shape(heads, HS, HS), shape(heads, HS), shape(heads, HS)),
-        in_specs=[SM] + [anywhere] * 16,
-        out_specs=(anywhere, VM, VM, VM),
-        scratch_shapes=[
-            pltpu.VMEM((EXTRA, wide), F32), pltpu.SemaphoreType.DMA((3, 8)), pltpu.SemaphoreType.DMA((8,))
-        ],
-        compiler_params=PARAMS,
-    )(pos, *query_pieces, *both_pieces)
+        out_shape=shape(RING, n, model // RING),
+        in_specs=[VM, VM],
+        out_specs=anywhere,
+        scratch_shapes=[pltpu.VMEM((RING, n, model // RING), F32), pltpu.SemaphoreType.DMA((RING,))],
+        compiler_params=PARAMS,
+    )(raw_weights, grads)
+    grad_tokens = lax.psum_scatter(summed, "head", scatter_dimension=0, tiled=True).astype(BF)
+
+    part_sum = whole(sum_kernel, chunk, [VM] * 4)(own, *away)
+    total = whole(sum_kernel, chunk, [VM] * 4)(part_sum, *round_turn([part_sum] * 3, False))
+    from_back, from_ahead, from_far = round_turn([total] * 3, True)
+    mine = [total, from_ahead, from_back, from_far]
+    others = [swap(piece) for piece in mine]
+
+    out, extra = shape(3, model, wide), vmem(EXTRA // 2, wide)
+    scratch = [pltpu.SemaphoreType.DMA((3, RING))]
+    placed, own_extra = pl.pallas_call(
+        functools.partial(place_kernel, half=0),
+        out_shape=(out, extra),
+        in_specs=[SM] + [VM] * RING,
+        out_specs=(anywhere, VM),
+        scratch_shapes=scratch,
+        compiler_params=PARAMS,
+    )(pos, *mine)
+    grad_proj, other_extra = pl.pallas_call(
+        functools.partial(place_kernel, half=1),
+        out_shape=(out, extra),
+        in_specs=[SM] + [VM] * RING + [anywhere],
+        out_specs=(anywhere, VM),
+        scratch_shapes=scratch,
+        input_output_aliases={RING + 1: 0},
+        compiler_params=PARAMS,
+    )(pos, *others, placed)
+    grad_init, grad_gain, rates = pl.pallas_call(
+        small_kernel,
+        out_shape=(shape(heads, HS, HS), shape(heads, HS), shape(heads, HS)),
+        in_specs=[SM, VM, VM],
+        out_specs=(VM, VM, VM),
+        scratch_shapes=[pltpu.VMEM((EXTRA, wide), F32)],
+        compiler_params=PARAMS,
+    )(pos, own_extra, other_extra)
     return (grad_tokens, grad_proj, grad_init, grad_gain, rates[:, 0], grad_gates)
 
 

time: 155 us -> 142 us (0.916)
  the two profiles are of different devices: /device:TPU:65 before, /device:TPU:1 now
where the time goes in v3:
time: 142 us; the launch traced here: 141 us
  waiting for transfers between devices  58.2 us (41%)
  starting transfers between devices  36.7 us (26%)
  Pallas kernels  29.5 us (21%)
  between operations  14.3 us (10%)
  other arithmetic  1.78 us (1%)
    ppermute x9, waiting for transfers between devices, round_turn(): lax.ppermute(chunk, ('dp', 'ctx'), moves(first, turn))  47 us
    ppermute x6, starting transfers between devices, swap(): return lax.ppermute(value, 'dp', [(i, i ^ 1) for i in range(2 * RING)])  16.2 us
    ppermute x9, starting transfers between devices, round_turn(): lax.ppermute(chunk, ('dp', 'ctx'), moves(first, turn))  11.2 us
    ppermute x1, waiting for transfers between devices, body(): back_far = lax.ppermute(back_second, 'ctx', [(2, 0)])  5.93 us
    pallas_call x1, Pallas kernels, body(): pl.pallas_call(maps_kernel, grid=(1,), out_shape=(wide_f32, wide_f32, vme...  5.7 us
    ppermute x1, waiting for transfers between devices, body(): back_near = lax.ppermute(pulled, 'ctx', [(3, 2), (1, 0)])  4.84 us
    pallas_call x1, Pallas kernels, body(): pl.pallas_call(reach_kernel, grid=(1,), out_shape=(wide_f32, square, wide...  3.88 us
    pallas_call x1, Pallas kernels, body(): pl.pallas_call(functools.partial(place_kernel, half=1), out_shape=(out, e...  3.65 us
  transfers between devices with their start and end apart: 23, of which 8 were waited for; matrix products, arithmetic and copies ran while one was open for 1% of the time, Pallas kernels for 9%

profile of v3, /device:TPU:1, one launch (start us, length us, event | category | flops | bytes accessed | tf_op | source)
XLA Modules:
  0.0 141.2 jit_solution(8648136872754917379)
XLA Ops:
  7.2 0.0 reduce-scatter.2.cloned.1.call-start
  7.3 0.1 stack.23.pos_ref
  7.4 5.7 %shard_map.118 = (f32[256,256]{1,0:T(8,128)S(1)}, f32[256,256]{1,0:T(8,128)S(1)}, f32[2,256,128]{2,1,0:T(8,128)S(1)}, f32[2,256,256]{2,1,0:T(8,128)S(1)}, f32[2,...) custom-call(s32[5]{0:T(128)S(1)} %stack.23.pos_ref, ...), custom_call_target="tpu_custom_call" | custom-call | tf_op jit(solution)/shard_map/pallas_call | solution.py:402
  13.1 1.5 %collective-permute-start.4 = (f32[256,1024]{1,0:T(8,128)S(1)}, f32[256,1024]{1,0:T(8,128)S(1)}, u32[]{:S(2)}, u32[]{:S(2)}) collective-permute-start(f32[256,1024]{1,0:T(8,128)S(1)} %get-tuple-element.53), channel_id=1, source_target_pairs={{0,16},{16,0},{32,48},{48,32},{64,80},{80,64},{96,112},{112,96},{1... | collective-permute-start | bytes 3145736 | tf_op jit(solution)/shard_map/ppermute | solution.py:342
  14.6 3.3 %collective-permute-start = (f32[2,128,128]{2,1,0:T(8,128)S(1)}, f32[2,128,128]{2,1,0:T(8,128)S(1)}, u32[]{:S(2)}, u32[]{:S(2)}) collective-permute-start(f32[2,128,128]{2,1,0:T(8,128)S(1)} %get-tuple-element.45), channel_id=1, source_target_pairs={{0,4},{8,12},{1,5},{9,13},{2,6},{10,14},{3,7},{11,15},{16,20},{24,... | collective-permute-start | bytes 393224 | tf_op jit(solution)/shard_map/ppermute | solution.py:414
  17.9 1.3 collective-permute-start.3
  19.2 3.9 %shard_map.119 = (f32[256,256]{1,0:T(8,128)S(1)}, f32[2,256,256]{2,1,0:T(8,128)S(1)}, f32[256,256]{1,0:T(8,128)S(1)}, f32[256,256]{1,0:T(8,128)S(1)}, f32[256,25...) custom-call(s32[5]{0:T(128)S(1)} %stack.23.pos_ref, f32[2]{0:T(128)S(1)} %copy-done.4, ...), custom_call_target="tpu_custom_call" | custom-call | tf_op jit(solution)/shard_map/pallas_call | solution.py:418
  23.1 0.2 shard_map.120
  23.3 0.8 collective-permute-start.2
  24.1 0.7 collective-permute-start.1
  24.8 0.2 shard_map.121.after_ref.other_tokt_ref
  25.1 2.1 %shard_map.122 = (f32[2,128,128]{2,1,0:T(8,128)S(1)}, f32[256,256]{1,0:T(8,128)S(1)}, f32[2,128,128]{2,1,0:T(8,128)S(1)}, f32[2,128]{1,0:T(2,128)S(1)}) custom-call(s32[5]{0:T(128)S(1)} %stack.23.pos_ref, f32[2,128,128]{2,1,0:T(8,128)S(1)} %copy-done.1, f32[2,128,128]{2,1,0:T(8,128)S(1)} %collective-permute-done.w_ref.near_ref, ...), custom_call_target="tpu_custom_call" | custom-call | tf_op jit(solution)/shard_map/pallas_call | solution.py:434
  27.2 1.3 collective-permute-start.5
  28.5 2.9 %shard_map.123 = (f32[256,256]{1,0:T(8,128)S(1)}, f32[256,256]{1,0:T(8,128)S(1)}, f32[256,256]{1,0:T(8,128)S(1)}, f32[256,256]{1,0:T(8,128)S(1)}, f32[2,256]{1,0:T(2,128)S(1)}) custom-call(f32[2]{0:T(128)S(1)} %copy-done.4, f32[1,2,256]{2,1,0:T(2,128)S(1)} %copy-done.3, f32[2,128,128]{2,1,0:T(8,128)S(1)} %get-tuple-element.55.w_ref, ...), custom_call_target="tpu_custom_call" | custom-call | tf_op jit(solution)/shard_map/pallas_call | solution.py:440
  31.4 4.8 %collective-permute-done.5.w_ref.rp_ref = f32[2,128,128]{2,1,0:T(8,128)S(1)} collective-permute-done((f32[2,128,128]{2,1,0:T(8,128)S(1)}, f32[2,128,128]{2,1,0:T(8,128)S(1)}, u32[]{:S(2)}, u32[]{:S(2)}) %collective-permute-start.5) | collective-permute-done | bytes 131104 | tf_op jit(solution)/shard_map/ppermute | solution.py:438
  36.2 0.2 shard_map.124
  36.5 1.3 collective-permute-start.7
  37.8 0.7 collective-permute-start.6
  38.4 5.9 %collective-permute-done.7.far_ref = f32[2,128,128]{2,1,0:T(8,128)S(1)} collective-permute-done((f32[2,128,128]{2,1,0:T(8,128)S(1)}, f32[2,128,128]{2,1,0:T(8,128)S(1)}, u32[]{:S(2)}, u32[]{:S(2)}) %collective-permute-start.7) | collective-permute-done | bytes 131104 | tf_op jit(solution)/shard_map/ppermute | solution.py:448
  44.4 3.3 %shard_map.125 = (f32[960,256]{1,0:T(8,128)S(1)}, f32[1,2,256]{2,1,0:T(2,128)}) custom-call(s32[5]{0:T(128)S(1)} %stack.23.pos_ref, f32[2]{0:T(128)S(1)} %copy-done.4, f32[1,2,256]{2,1,0:T(2,128)S(1)} %copy-done.3, f32[2,128,128]{2,1,0:T(8,128)S(1)} %collective-permute-done.5.w_ref.rp_ref, f32[2,128,128]{2,1,0:T(8,128)S(1)} %collective-permute-done.6.mid_ref, ...), custom_call_target="tpu_custom_call" | custom-call | tf_op jit(solution)/shard_map/pallas_call | solution.py:450
  47.7 4.3 %collective-permute-start.8 = (f32[960,256]{1,0:T(8,128)S(1)}, f32[960,256]{1,0:T(8,128)S(1)}, u32[]{:S(2)}, u32[]{:S(2)}) collective-permute-start(f32[960,256]{1,0:T(8,128)S(1)} %get-tuple-element.70.all_ref.own_ref), channel_id=1, source_target_pairs={{0,16},{16,0},{32,48},{48,32},{64,80},{80,64},{96,112},{112,96},{1... | collective-permute-start | bytes 2949128 | tf_op jit(solution)/shard_map/ppermute | solution.py:342
  52.0 1.8 %shard_map.126 = f32[4,256,512]{2,1,0:T(8,128)} custom-call(bf16[3,2048,256]{2,1,0:T(8,128)(2,1)S(1)} %copy-done, f32[960,256]{1,0:T(8,128)S(1)} %get-tuple-element.70.all_ref.own_ref), custom_call_target="tpu_custom_call" | custom-call | tf_op jit(solution)/shard_map/pallas_call | solution.py:460
  53.8 0.3 collective-permute-done.8.other_ref
  54.2 1.5 %shard_map.127 = (f32[792,256]{1,0:T(8,128)S(1)}, f32[792,256]{1,0:T(8,128)S(1)}, f32[792,256]{1,0:T(8,128)S(1)}, f32[792,256]{1,0:T(8,128)S(1)}) custom-call(s32[5]{0:T(128)S(1)} %stack.23.pos_ref, bf16[1024,256]{1,0:T(8,128)(2,1)S(1)} %get-tuple-element.71.tokt_ref, bf16[1024,256]{1,0:T(8,128)(2,1)S(1)} %shard_map.121.after_ref.other_tokt_ref, ...), custom_call_target="tpu_custom_call" | custom-call | tf_op jit(solution)/shard_map/pallas_call | solution.py:456
  55.7 1.1 collective-permute-start.9
  56.7 1.7 %collective-permute-start.10 = (f32[792,256]{1,0:T(8,128)S(1)}, f32[792,256]{1,0:T(8,128)S(1)}, u32[]{:S(2)}, u32[]{:S(2)}) collective-permute-start(f32[792,256]{1,0:T(8,128)S(1)} %get-tuple-element.74), channel_id=1, source_target_pairs={{0,96},{4,100},{8,104},{12,108},{16,28},{20,16},{24,20},{28,24},{3... | collective-permute-start | bytes 2433032 | tf_op jit(solution)/shard_map/ppermute | solution.py:337
  58.4 0.2 collective-permute-start.11
  58.6 18.5 %collective-permute-done.9.back_ref = f32[792,256]{1,0:T(8,128)S(1)} collective-permute-done((f32[792,256]{1,0:T(8,128)S(1)}, f32[792,256]{1,0:T(8,128)S(1)}, u32[]{:S(2)}, u32[]{:S(2)}) %collective-permute-start.9) | collective-permute-done | bytes 811040 | tf_op jit(solution)/shard_map/ppermute | solution.py:337
  77.2 0.2 shard_map.128.own_ref
  77.4 2.8 %collective-permute-start.14 = (f32[792,256]{1,0:T(8,128)S(1)}, f32[792,256]{1,0:T(8,128)S(1)}, u32[]{:S(2)}, u32[]{:S(2)}) collective-permute-start(f32[792,256]{1,0:T(8,128)S(1)} %shard_map.128.own_ref), channel_id=1, source_target_pairs={{0,8},{4,12},{8,0},{12,4},{16,80},{20,84},{24,88},{28,92},{32,40},... | collective-permute-start | bytes 2433032 | tf_op jit(solution)/shard_map/ppermute | solution.py:337
  80.2 0.9 collective-permute-start.13
  81.0 0.6 collective-permute-start.12
  81.7 8.7 %collective-permute-done.14.far_ref = f32[792,256]{1,0:T(8,128)S(1)} collective-permute-done((f32[792,256]{1,0:T(8,128)S(1)}, f32[792,256]{1,0:T(8,128)S(1)}, u32[]{:S(2)}, u32[]{:S(2)}) %collective-permute-start.14) | collective-permute-done | bytes 811040 | tf_op jit(solution)/shard_map/ppermute | solution.py:337
  90.4 8.8 %collective-permute-done.13.ahead_ref = f32[792,256]{1,0:T(8,128)S(1)} collective-permute-done((f32[792,256]{1,0:T(8,128)S(1)}, f32[792,256]{1,0:T(8,128)S(1)}, u32[]{:S(2)}, u32[]{:S(2)}) %collective-permute-start.13) | collective-permute-done | bytes 811040 | tf_op jit(solution)/shard_map/ppermute | solution.py:337
  99.2 0.2 shard_map.129.refs_0_
  99.4 1.4 collective-permute-start.20
  100.7 2.0 %collective-permute-start.18 = (f32[792,256]{1,0:T(8,128)S(1)}, f32[792,256]{1,0:T(8,128)S(1)}, u32[]{:S(2)}, u32[]{:S(2)}) collective-permute-start(f32[792,256]{1,0:T(8,128)S(1)} %shard_map.129.refs_0_), channel_id=1, source_target_pairs={{0,32},{4,36},{8,40},{12,44},{16,20},{20,24},{24,28},{28,16},{32,6... | collective-permute-start | bytes 2433032 | tf_op jit(solution)/shard_map/ppermute | solution.py:337
  102.7 0.7 collective-permute-start.16
  103.4 3.0 %collective-permute-start.15 = (f32[792,256]{1,0:T(8,128)S(1)}, f32[792,256]{1,0:T(8,128)}, u32[]{:S(2)}, u32[]{:S(2)}) collective-permute-start(f32[792,256]{1,0:T(8,128)S(1)} %shard_map.129.refs_0_), channel_id=1, source_target_pairs={{0,16},{16,0},{32,48},{48,32},{64,80},{80,64},{96,112},{112,96},{1... | collective-permute-start | bytes 2433032 | tf_op jit(solution)/shard_map/ppermute | solution.py:342
  106.4 6.0 %collective-permute-done.20.refs_3_ = f32[792,256]{1,0:T(8,128)S(1)} collective-permute-done((f32[792,256]{1,0:T(8,128)S(1)}, f32[792,256]{1,0:T(8,128)S(1)}, u32[]{:S(2)}, u32[]{:S(2)}) %collective-permute-start.20) | collective-permute-done | bytes 811040 | tf_op jit(solution)/shard_map/ppermute | solution.py:337
  112.4 3.7 %collective-permute-start.21 = (f32[792,256]{1,0:T(8,128)S(1)}, f32[792,256]{1,0:T(8,128)}, u32[]{:S(2)}, u32[]{:S(2)}) collective-permute-start(f32[792,256]{1,0:T(8,128)S(1)} %collective-permute-done.20.refs_3_), channel_id=1, source_target_pairs={{0,16},{16,0},{32,48},{48,32},{64,80},{80,64},{96,112},{112,96},{1... | collective-permute-start | bytes 2433032 | tf_op jit(solution)/shard_map/ppermute | solution.py:342
  116.1 4.9 %collective-permute-done.18.refs_2_ = f32[792,256]{1,0:T(8,128)S(1)} collective-permute-done((f32[792,256]{1,0:T(8,128)S(1)}, f32[792,256]{1,0:T(8,128)S(1)}, u32[]{:S(2)}, u32[]{:S(2)}) %collective-permute-start.18) | collective-permute-done | bytes 811040 | tf_op jit(solution)/shard_map/ppermute | solution.py:337
  121.0 3.7 %collective-permute-start.19 = (f32[792,256]{1,0:T(8,128)S(1)}, f32[792,256]{1,0:T(8,128)}, u32[]{:S(2)}, u32[]{:S(2)}) collective-permute-start(f32[792,256]{1,0:T(8,128)S(1)} %collective-permute-done.18.refs_2_), channel_id=1, source_target_pairs={{0,16},{16,0},{32,48},{48,32},{64,80},{80,64},{96,112},{112,96},{1... | collective-permute-start | bytes 2433032 | tf_op jit(solution)/shard_map/ppermute | solution.py:342
  124.7 2.3 %shard_map.130 = (f32[3,2048,256]{2,1,0:T(8,128)}, f32[96,256]{1,0:T(8,128)S(1)}) custom-call(s32[5]{0:T(128)S(1)} %stack.23.pos_ref, f32[792,256]{1,0:T(8,128)S(1)} %shard_map.129.refs_0_, f32[792,256]{1,0:T(8,128)S(1)} %collective-permute-done.16.refs_1_, f32[792,256]{1,0:T(8,128)S(1)} %collective-permute-done.18.refs_2_, ...), custom_call_target="tpu_custom_call" | custom-call | tf_op jit(solution)/shard_map/pallas_call | solution.py:478
  127.1 1.8 %convert_element_type.3 = bf16[1,256,512]{2,1,0:T(8,128)(2,1)} convert(f32[1,256,512]{2,1,0:T(8,128)} %reduce-scatter.2.cloned.1.call-done) | non-fusion elementwise | flops 131072 | bytes 786432 | tf_op jit(solution)/shard_map/convert_element_type | solution.py:468
  128.9 3.6 %shard_map.131 = (f32[3,2048,256]{2,1,0:T(8,128)}, f32[96,256]{1,0:T(8,128)S(1)}) custom-call(s32[5]{0:T(128)S(1)} %stack.23.pos_ref, f32[792,256]{1,0:T(8,128)} %collective-permute-done.15.refs_0_, f32[792,256]{1,0:T(8,128)} %collective-permute-done.17.refs_1_, f32[792,256]{1,0:T(8,128)} %collective-permute-done.19.refs_2_, ...), custom_call_target="tpu_custom_call", output_to_operand_aliasing={{0}: (5, {})} | custom-call | tf_op jit(solution)/shard_map/pallas_call | solution.py:486
  132.5 1.2 shard_map.132
  133.7 0.6 slice_reduce_fusion
  (29 shorter events, 0.1 us)
Async XLA Ops:
  7.2 12.0 %copy-start.3 = (f32[1,2,256]{2,1,0:T(2,128)S(1)}, f32[1,2,256]{2,1,0:T(2,128)}, u32[]{:S(2)}) copy-start(f32[1,2,256]{2,1,0:T(2,128)} %gate_ref.7) | copy-start | bytes 6148
  7.2 12.0 %copy-start.4 = (f32[2]{0:T(128)S(1)}, f32[2]{0:T(128)}, u32[]{:S(2)}) copy-start(f32[2]{0:T(128)} %base_ref.7) | copy-start | bytes 28
  7.2 119.9 %reduce-scatter.2.cloned.1.call-start = ((), (), s32[]{:S(2)}) async-start(), calls=%async_computation.1 | async-start | bytes 2621440 | tf_op jit(solution)/shard_map/reduce_scatter | solution.py:468
  7.3 17.7 %copy-start.1 = (f32[2,128,128]{2,1,0:T(8,128)S(1)}, f32[2,128,128]{2,1,0:T(8,128)}, u32[]{:S(2)}) copy-start(f32[2,128,128]{2,1,0:T(8,128)} %init_ref.3) | copy-start | bytes 393220
  7.3 17.7 %copy-start.2 = (bf16[1,256,256]{2,1,0:T(8,128)(2,1)S(1)}, bf16[1,256,256]{2,1,0:T(8,128)(2,1)}, u32[]{:S(2)}) copy-start(bf16[1,256,256]{2,1,0:T(8,128)(2,1)} %up_ref.3) | copy-start | bytes 393220
  7.4 17.7 %copy-start.5 = (f32[2,128]{1,0:T(2,128)S(1)}, f32[2,128]{1,0:T(2,128)}, u32[]{:S(2)}) copy-start(f32[2,128]{1,0:T(2,128)} %gain_ref.1) | copy-start | bytes 3076
  13.1 11.7 %collective-permute-start.4 = (f32[256,1024]{1,0:T(8,128)S(1)}, f32[256,1024]{1,0:T(8,128)S(1)}, u32[]{:S(2)}, u32[]{:S(2)}) collective-permute-start(f32[256,1024]{1,0:T(8,128)S(1)} %get-tuple-element.53), channel_id=1, source_target_pairs={{0,16},{16,0},{32,48},{48,32},{64,80},{80,64},{96,112},{112,96},{1... | collective-permute-start | bytes 3145736 | tf_op jit(solution)/shard_map/ppermute | solution.py:342
  14.6 8.5 %collective-permute-start = (f32[2,128,128]{2,1,0:T(8,128)S(1)}, f32[2,128,128]{2,1,0:T(8,128)S(1)}, u32[]{:S(2)}, u32[]{:S(2)}) collective-permute-start(f32[2,128,128]{2,1,0:T(8,128)S(1)} %get-tuple-element.45), channel_id=1, source_target_pairs={{0,4},{8,12},{1,5},{9,13},{2,6},{10,14},{3,7},{11,15},{16,20},{24,... | collective-permute-start | bytes 393224 | tf_op jit(solution)/shard_map/ppermute | solution.py:414
  17.9 7.1 %collective-permute-start.3 = (f32[2,128,128]{2,1,0:T(8,128)S(1)}, f32[2,128,128]{2,1,0:T(8,128)S(1)}, u32[]{:S(2)}, u32[]{:S(2)}) collective-permute-start(f32[2,128,128]{2,1,0:T(8,128)S(1)} %get-tuple-element.46.d_ref), channel_id=1, source_target_pairs={{8,12},{4,0},{9,13},{5,1},{10,14},{6,2},{11,15},{7,3},{24,28},{20,... | collective-permute-start | bytes 393224 | tf_op jit(solution)/shard_map/ppermute | solution.py:415
  23.1 28.9 %copy-start = (bf16[3,2048,256]{2,1,0:T(8,128)(2,1)S(1)}, bf16[3,2048,256]{2,1,0:T(8,128)(2,1)}, u32[]{:S(2)}) copy-start(bf16[3,2048,256]{2,1,0:T(8,128)(2,1)} %w_ref.1) | copy-start | bytes 9437188
  23.3 1.7 %collective-permute-start.2 = (f32[2,128,128]{2,1,0:T(8,128)S(1)}, f32[2,128,128]{2,1,0:T(8,128)S(1)}, u32[]{:S(2)}, u32[]{:S(2)}) collective-permute-start(f32[2,128,128]{2,1,0:T(8,128)S(1)} %shard_map.120), channel_id=1, source_target_pairs={{4,12},{5,13},{6,14},{7,15},{20,28},{21,29},{22,30},{23,31},{36,44... | collective-permute-start | bytes 393224 | tf_op jit(solution)/shard_map/ppermute | solution.py:431
  24.1 0.9 collective-permute-start.1
  27.2 9.0 %collective-permute-start.5 = (f32[2,128,128]{2,1,0:T(8,128)S(1)}, f32[2,128,128]{2,1,0:T(8,128)S(1)}, u32[]{:S(2)}, u32[]{:S(2)}) collective-permute-start(f32[2,128,128]{2,1,0:T(8,128)S(1)} %get-tuple-element.54.o_ref.p_ref), channel_id=1, source_target_pairs={{12,8},{4,0},{13,9},{5,1},{14,10},{6,2},{15,11},{7,3},{28,24},{20,... | collective-permute-start | bytes 393224 | tf_op jit(solution)/shard_map/ppermute | solution.py:438
  36.5 7.9 %collective-permute-start.7 = (f32[2,128,128]{2,1,0:T(8,128)S(1)}, f32[2,128,128]{2,1,0:T(8,128)S(1)}, u32[]{:S(2)}, u32[]{:S(2)}) collective-permute-start(f32[2,128,128]{2,1,0:T(8,128)S(1)} %shard_map.124), channel_id=1, source_target_pairs={{8,0},{9,1},{10,2},{11,3},{24,16},{25,17},{26,18},{27,19},{40,32},... | collective-permute-start | bytes 393224 | tf_op jit(solution)/shard_map/ppermute | solution.py:448
  37.8 6.6 %collective-permute-start.6 = (f32[2,128,128]{2,1,0:T(8,128)S(1)}, f32[2,128,128]{2,1,0:T(8,128)S(1)}, u32[]{:S(2)}, u32[]{:S(2)}) collective-permute-start(f32[2,128,128]{2,1,0:T(8,128)S(1)} %shard_map.124), channel_id=1, source_target_pairs={{8,4},{9,5},{10,6},{11,7},{24,20},{25,21},{26,22},{27,23},{40,36},... | collective-permute-start | bytes 393224 | tf_op jit(solution)/shard_map/ppermute | solution.py:447
  47.7 6.4 %collective-permute-start.8 = (f32[960,256]{1,0:T(8,128)S(1)}, f32[960,256]{1,0:T(8,128)S(1)}, u32[]{:S(2)}, u32[]{:S(2)}) collective-permute-start(f32[960,256]{1,0:T(8,128)S(1)} %get-tuple-element.70.all_ref.own_ref), channel_id=1, source_target_pairs={{0,16},{16,0},{32,48},{48,32},{64,80},{80,64},{96,112},{112,96},{1... | collective-permute-start | bytes 2949128 | tf_op jit(solution)/shard_map/ppermute | solution.py:342
  55.7 21.5 %collective-permute-start.9 = (f32[792,256]{1,0:T(8,128)S(1)}, f32[792,256]{1,0:T(8,128)S(1)}, u32[]{:S(2)}, u32[]{:S(2)}) collective-permute-start(f32[792,256]{1,0:T(8,128)S(1)} %get-tuple-element.73), channel_id=1, source_target_pairs={{0,32},{4,36},{8,40},{12,44},{16,20},{20,24},{24,28},{28,16},{32,6... | collective-permute-start | bytes 2433032 | tf_op jit(solution)/shard_map/ppermute | solution.py:337
  56.7 20.4 %collective-permute-start.10 = (f32[792,256]{1,0:T(8,128)S(1)}, f32[792,256]{1,0:T(8,128)S(1)}, u32[]{:S(2)}, u32[]{:S(2)}) collective-permute-start(f32[792,256]{1,0:T(8,128)S(1)} %get-tuple-element.74), channel_id=1, source_target_pairs={{0,96},{4,100},{8,104},{12,108},{16,28},{20,16},{24,20},{28,24},{3... | collective-permute-start | bytes 2433032 | tf_op jit(solution)/shard_map/ppermute | solution.py:337
  58.4 18.7 %collective-permute-start.11 = (f32[792,256]{1,0:T(8,128)S(1)}, f32[792,256]{1,0:T(8,128)S(1)}, u32[]{:S(2)}, u32[]{:S(2)}) collective-permute-start(f32[792,256]{1,0:T(8,128)S(1)} %get-tuple-element.75), channel_id=1, source_target_pairs={{0,64},{4,68},{8,72},{12,76},{16,24},{20,28},{24,16},{28,20},{32,9... | collective-permute-start | bytes 2433032 | tf_op jit(solution)/shard_map/ppermute | solution.py:337
  77.4 13.0 %collective-permute-start.14 = (f32[792,256]{1,0:T(8,128)S(1)}, f32[792,256]{1,0:T(8,128)S(1)}, u32[]{:S(2)}, u32[]{:S(2)}) collective-permute-start(f32[792,256]{1,0:T(8,128)S(1)} %shard_map.128.own_ref), channel_id=1, source_target_pairs={{0,8},{4,12},{8,0},{12,4},{16,80},{20,84},{24,88},{28,92},{32,40},... | collective-permute-start | bytes 2433032 | tf_op jit(solution)/shard_map/ppermute | solution.py:337
  80.2 19.0 %collective-permute-start.13 = (f32[792,256]{1,0:T(8,128)S(1)}, f32[792,256]{1,0:T(8,128)S(1)}, u32[]{:S(2)}, u32[]{:S(2)}) collective-permute-start(f32[792,256]{1,0:T(8,128)S(1)} %shard_map.128.own_ref), channel_id=1, source_target_pairs={{0,12},{4,0},{8,4},{12,8},{16,112},{20,116},{24,120},{28,124},{32,... | collective-permute-start | bytes 2433032 | tf_op jit(solution)/shard_map/ppermute | solution.py:337
  81.0 18.1 %collective-permute-start.12 = (f32[792,256]{1,0:T(8,128)S(1)}, f32[792,256]{1,0:T(8,128)S(1)}, u32[]{:S(2)}, u32[]{:S(2)}) collective-permute-start(f32[792,256]{1,0:T(8,128)S(1)} %shard_map.128.own_ref), channel_id=1, source_target_pairs={{0,4},{4,8},{8,12},{12,0},{16,48},{20,52},{24,56},{28,60},{32,36},... | collective-permute-start | bytes 2433032 | tf_op jit(solution)/shard_map/ppermute | solution.py:337
  99.4 13.0 %collective-permute-start.20 = (f32[792,256]{1,0:T(8,128)S(1)}, f32[792,256]{1,0:T(8,128)S(1)}, u32[]{:S(2)}, u32[]{:S(2)}) collective-permute-start(f32[792,256]{1,0:T(8,128)S(1)} %shard_map.129.refs_0_), channel_id=1, source_target_pairs={{0,64},{4,68},{8,72},{12,76},{16,24},{20,28},{24,16},{28,20},{32,9... | collective-permute-start | bytes 2433032 | tf_op jit(solution)/shard_map/ppermute | solution.py:337
  100.7 20.3 %collective-permute-start.18 = (f32[792,256]{1,0:T(8,128)S(1)}, f32[792,256]{1,0:T(8,128)S(1)}, u32[]{:S(2)}, u32[]{:S(2)}) collective-permute-start(f32[792,256]{1,0:T(8,128)S(1)} %shard_map.129.refs_0_), channel_id=1, source_target_pairs={{0,32},{4,36},{8,40},{12,44},{16,20},{20,24},{24,28},{28,16},{32,6... | collective-permute-start | bytes 2433032 | tf_op jit(solution)/shard_map/ppermute | solution.py:337
  102.7 22.0 %collective-permute-start.16 = (f32[792,256]{1,0:T(8,128)S(1)}, f32[792,256]{1,0:T(8,128)S(1)}, u32[]{:S(2)}, u32[]{:S(2)}) collective-permute-start(f32[792,256]{1,0:T(8,128)S(1)} %shard_map.129.refs_0_), channel_id=1, source_target_pairs={{0,96},{4,100},{8,104},{12,108},{16,28},{20,16},{24,20},{28,24},{3... | collective-permute-start | bytes 2433032 | tf_op jit(solution)/shard_map/ppermute | solution.py:337
  103.4 25.4 %collective-permute-start.15 = (f32[792,256]{1,0:T(8,128)S(1)}, f32[792,256]{1,0:T(8,128)}, u32[]{:S(2)}, u32[]{:S(2)}) collective-permute-start(f32[792,256]{1,0:T(8,128)S(1)} %shard_map.129.refs_0_), channel_id=1, source_target_pairs={{0,16},{16,0},{32,48},{48,32},{64,80},{80,64},{96,112},{112,96},{1... | collective-permute-start | bytes 2433032 | tf_op jit(solution)/shard_map/ppermute | solution.py:342
  112.4 16.5 %collective-permute-start.21 = (f32[792,256]{1,0:T(8,128)S(1)}, f32[792,256]{1,0:T(8,128)}, u32[]{:S(2)}, u32[]{:S(2)}) collective-permute-start(f32[792,256]{1,0:T(8,128)S(1)} %collective-permute-done.20.refs_3_), channel_id=1, source_target_pairs={{0,16},{16,0},{32,48},{48,32},{64,80},{80,64},{96,112},{112,96},{1... | collective-permute-start | bytes 2433032 | tf_op jit(solution)/shard_map/ppermute | solution.py:342
  121.0 7.8 %collective-permute-start.19 = (f32[792,256]{1,0:T(8,128)S(1)}, f32[792,256]{1,0:T(8,128)}, u32[]{:S(2)}, u32[]{:S(2)}) collective-permute-start(f32[792,256]{1,0:T(8,128)S(1)} %collective-permute-done.18.refs_2_), channel_id=1, source_target_pairs={{0,16},{16,0},{32,48},{48,32},{64,80},{80,64},{96,112},{112,96},{1... | collective-permute-start | bytes 2433032 | tf_op jit(solution)/shard_map/ppermute | solution.py:342
  124.7 4.1 %collective-permute-start.17 = (f32[792,256]{1,0:T(8,128)S(1)}, f32[792,256]{1,0:T(8,128)}, u32[]{:S(2)}, u32[]{:S(2)}) collective-permute-start(f32[792,256]{1,0:T(8,128)S(1)} %collective-permute-done.16.refs_1_), channel_id=1, source_target_pairs={{0,16},{16,0},{32,48},{48,32},{64,80},{80,64},{96,112},{112,96},{1... | collective-permute-start | bytes 2433032 | tf_op jit(solution)/shard_map/ppermute | solution.py:342
Sparse Core Ops, SparseCore 0:
  54.0 29.8 reduce-scatter.1

commit v4 on v3

--- a/solution.py
+++ b/solution.py
@@ -269,55 +269,66 @@
         out_ref[3 * CHUNK : 3 * CHUNK + PIECE, :] = own_ref[extra, :] + other_ref[extra, :]
 
 
-def token_kernel(w_ref, all_ref, out_ref, held_ref, sem):
-    n = out_ref.shape[1]
+def token_kernel(pos_ref, w_ref, all_ref, *out_refs):
+    n = out_refs[0].shape[0]
     ds = [all_ref[m * n : (m + 1) * n, :].astype(BF) for m in range(3)]
-    span_rows = w_ref.shape[1] // RING
-    copies = []
-    for at in range(RING):
-        rows = slice(at * span_rows, (at + 1) * span_rows)
+    quarter = w_ref.shape[1] // RING
+    for turn, out_ref in zip(TURNS, out_refs):
+        at = (pos_ref[3] + turn) & (RING - 1)
+        rows = pl.ds(pl.multiple_of(at * quarter, quarter), quarter)
         total = lax.dot_general(ds[0], w_ref[0, rows, :], NT, preferred_element_type=F32)
         total = total + lax.dot_general(ds[1], w_ref[1, rows, :], NT, preferred_element_type=F32)
-        held_ref[at] = total + lax.dot_general(ds[2], w_ref[2, rows, :], NT, preferred_element_type=F32)
-        copies.append(pltpu.make_async_copy(held_ref.at[at], out_ref.at[at], sem.at[at]))
-        copies[-1].start()
-    for copy in copies:
-        copy.wait()
-
-
-def sum_kernel(own_ref, back_ref, ahead_ref, far_ref, out_ref):
-    out_ref[...] = (own_ref[...] + far_ref[...]) + (back_ref[...] + ahead_ref[...])
-
-
-def place_kernel(pos_ref, *refs, half):
-    pieces = refs[:RING]
-    out_ref, extra_ref, sem = refs[-3:]
-    core = pos_ref[0] if half == 0 else 1 - pos_ref[0]
+        out_ref[...] = total + lax.dot_general(ds[2], w_ref[2, rows, :], NT, preferred_element_type=F32)
+
+
+def sum_kernel(own_ref, back_ref, ahead_ref, far_ref, *refs):
+    refs[-1][...] = (own_ref[...] + far_ref[...]) + (back_ref[...] + ahead_ref[...])
+
+
+def place_kernel(pos_ref, *refs, which):
+    pieces = refs[: len(which)]
+    out_ref, sem = refs[-2:]
     copies = []
-    for m, piece in enumerate(pieces):
+    for g, ((half, m), piece) in enumerate(zip(which, pieces)):
+        core = pos_ref[0] if half == 0 else 1 - pos_ref[0]
         at = core * RING + ((pos_ref[1 + half] + TURNS[m]) & (RING - 1))
         rows = pl.ds(pl.multiple_of(at * CHUNK, CHUNK), CHUNK)
         for s in range(3):
             copies.append(
-                pltpu.make_async_copy(piece.at[pl.ds(s * CHUNK, CHUNK), :], out_ref.at[s, rows, :], sem.at[s, m])
+                pltpu.make_async_copy(piece.at[pl.ds(s * CHUNK, CHUNK), :], out_ref.at[s, rows, :], sem.at[s, g])
             )
     for copy in copies:
         copy.start()
-    for m, piece in enumerate(pieces):
-        at = (pos_ref[1 + half] + TURNS[m]) & (RING - 1)
-        extra_ref[pl.ds(pl.multiple_of(at * PIECE, 8), PIECE), :] = piece[3 * CHUNK : 3 * CHUNK + PIECE, :]
     for copy in copies:
         copy.wait()
 
 
-def small_kernel(pos_ref, own_ref, other_ref, init_ref, gain_ref, rates_ref, extra_ref):
-    rows = own_ref.shape[0]
-    extra_ref[pl.ds(pl.multiple_of(pos_ref[0] * rows, 8), rows), :] = own_ref[...]
-    extra_ref[pl.ds(pl.multiple_of((1 - pos_ref[0]) * rows, 8), rows), :] = other_ref[...]
+def last_kernel(pos_ref, *refs, which):
+    pieces = refs[: 2 * RING]
+    out_ref, init_ref, gain_ref, rates_ref, extra_ref, sem = refs[-6:]
+    copies = []
+    for g, (half, m) in enumerate(which):
+        core = pos_ref[0] if half == 0 else 1 - pos_ref[0]
+        at = core * RING + ((pos_ref[1 + half] + TURNS[m]) & (RING - 1))
+        rows = pl.ds(pl.multiple_of(at * CHUNK, CHUNK), CHUNK)
+        for s in range(3):
+            copies.append(
+                pltpu.make_async_copy(
+                    pieces[half * RING + m].at[pl.ds(s * CHUNK, CHUNK), :], out_ref.at[s, rows, :], sem.at[s, g]
+                )
+            )
+    for copy in copies:
+        copy.start()
+    for p, piece in enumerate(pieces):
+        core = pos_ref[0] if p < RING else 1 - pos_ref[0]
+        at = core * RING + ((pos_ref[1 + p // RING] + TURNS[p % RING]) & (RING - 1))
+        extra_ref[pl.ds(pl.multiple_of(at * PIECE, 8), PIECE), :] = piece[3 * CHUNK : 3 * CHUNK + PIECE, :]
     for h in range(init_ref.shape[0]):
         init_ref[h] = extra_ref[0:HS, span(h)]
         gain_ref[h : h + 1, :] = extra_ref[HS : HS + 1, span(h)]
-        rates_ref[h : h + 1, :] = extra_ref[HS + 1 : HS + 2, span(h)]
+        rates_ref[h] = extra_ref[HS + 1, h * HS]
+    for copy in copies:
+        copy.wait()
 
 
 def moves(first, by):
@@ -457,50 +468,43 @@
         pos, tokt, other_tokt, grads, swap(grads)
     )
     away = round_turn(away, True)
-    summed = pl.pallas_call(
-        token_kernel,
-        out_shape=shape(RING, n, model // RING),
-        in_specs=[VM, VM],
-        out_specs=anywhere,
-        scratch_shapes=[pltpu.VMEM((RING, n, model // RING), F32), pltpu.SemaphoreType.DMA((RING,))],
-        compiler_params=PARAMS,
-    )(raw_weights, grads)
-    grad_tokens = lax.psum_scatter(summed, "head", scatter_dimension=0, tiled=True).astype(BF)
-
-    part_sum = whole(sum_kernel, chunk, [VM] * 4)(own, *away)
-    total = whole(sum_kernel, chunk, [VM] * 4)(part_sum, *round_turn([part_sum] * 3, False))
+    quarters = whole(token_kernel, (vmem(n, model // RING),) * RING, [SM, VM, VM])(pos, raw_weights, grads)
+    from_back, from_ahead, from_far = [
+        lax.ppermute(terms, "head", [(i, (i + turn) % RING) for i in range(RING)])
+        for terms, turn in zip(quarters[1:], TURNS[1:])
+    ]
+    grad_tokens = ((quarters[0] + from_far) + (from_back + from_ahead)).astype(BF).reshape(1, n, -1)
+
+    part_sum = whole(sum_kernel, chunk, [VM] * 4 + [anywhere] * 2)(own, *away, from_back, from_ahead)
+    total = whole(sum_kernel, chunk, [VM] * 4 + [anywhere])(part_sum, *round_turn([part_sum] * 3, False), grad_tokens)
     from_back, from_ahead, from_far = round_turn([total] * 3, True)
     mine = [total, from_ahead, from_back, from_far]
     others = [swap(piece) for piece in mine]
 
-    out, extra = shape(3, model, wide), vmem(EXTRA // 2, wide)
-    scratch = [pltpu.SemaphoreType.DMA((3, RING))]
-    placed, own_extra = pl.pallas_call(
-        functools.partial(place_kernel, half=0),
-        out_shape=(out, extra),
-        in_specs=[SM] + [VM] * RING,
-        out_specs=(anywhere, VM),
-        scratch_shapes=scratch,
+    out = shape(3, model, wide)
+    placed = None
+    for which in (((0, 0), (0, 1), (0, 2), (0, 3), (1, 0), (1, 3)),):
+        given = [(mine, others)[half][m] for half, m in which] + ([] if placed is None else [placed])
+        placed = pl.pallas_call(
+            functools.partial(place_kernel, which=which),
+            out_shape=out,
+            in_specs=[SM] + [VM] * len(which) + [anywhere] * (len(given) - len(which)),
+            out_specs=anywhere,
+            scratch_shapes=[pltpu.SemaphoreType.DMA((3, len(which)))],
+            input_output_aliases={} if placed is None else {len(which) + 1: 0},
+            compiler_params=PARAMS,
+        )(pos, *given)
+    which = ((1, 1), (1, 2))
+    grad_proj, grad_init, grad_gain, grad_rates = pl.pallas_call(
+        functools.partial(last_kernel, which=which),
+        out_shape=(out, shape(heads, HS, HS), shape(heads, HS), shape(heads)),
+        in_specs=[SM] + [VM] * 8 + [anywhere],
+        out_specs=(anywhere, VM, VM, SM),
+        scratch_shapes=[pltpu.VMEM((EXTRA, wide), F32), pltpu.SemaphoreType.DMA((3, len(which)))],
+        input_output_aliases={9: 0},
         compiler_params=PARAMS,
-    )(pos, *mine)
-    grad_proj, other_extra = pl.pallas_call(
-        functools.partial(place_kernel, half=1),
-        out_shape=(out, extra),
-        in_specs=[SM] + [VM] * RING + [anywhere],
-        out_specs=(anywhere, VM),
-        scratch_shapes=scratch,
-        input_output_aliases={RING + 1: 0},
-        compiler_params=PARAMS,
-    )(pos, *others, placed)
-    grad_init, grad_gain, rates = pl.pallas_call(
-        small_kernel,
-        out_shape=(shape(heads, HS, HS), shape(heads, HS), shape(heads, HS)),
-        in_specs=[SM, VM, VM],
-        out_specs=(VM, VM, VM),
-        scratch_shapes=[pltpu.VMEM((EXTRA, wide), F32)],
-        compiler_params=PARAMS,
-    )(pos, own_extra, other_extra)
-    return (grad_tokens, grad_proj, grad_init, grad_gain, rates[:, 0], grad_gates)
+    )(pos, *mine, *others, placed)
+    return (grad_tokens, grad_proj, grad_init, grad_gain, grad_rates, grad_gates)
 
 
 def solution(mesh):

time: 142 us -> 125 us (0.88)
  between operations: 14.3 us -> 1.12 us
  starting transfers between devices: 36.7 us -> 44.7 us
  waiting for transfers between devices: 58.2 us -> 50.8 us
  Pallas kernels: 29.5 us -> 27.3 us
  other arithmetic: 1.78 us -> 0.24 us
    ppermute x9, waiting for transfers between devices: 47 us -> 18 us  [round_turn(): lax.ppermute(chunk, ('dp', 'ctx'), moves(first, turn))]
    ppermute x0 -> x3, waiting for transfers between devices: none -> 19.6 us  [body(): lax.ppermute(terms, 'head', [(i, (i + turn) % RING) for i in range(RING)])]
    ppermute x0 -> x3, starting transfers between devices: none -> 7.53 us  [body(): lax.ppermute(terms, 'head', [(i, (i + turn) % RING) for i in range(RING)])]
    pallas_call x6 -> x5, Pallas kernels: 9.39 us -> 7.2 us  [the longest x1 2.86 us: body(): pl.pallas_call(functools.partial(place_kernel, which=which), out_shape=ou...]
    ppermute x6, waiting for transfers between devices: 0.33 us -> 2.4 us  [swap(): return lax.ppermute(value, 'dp', [(i, i ^ 1) for i in range(2 * RING)])]
    convert_element_type x1 -> x0, other arithmetic: 1.78 us -> none  [body(): lax.psum_scatter(summed, 'head', scatter_dimension=0, tiled=True).astype(BF)]
  transfers between devices with their start and end apart: 23 -> 25, of which waited for: 8 -> 10; matrix products, arithmetic and copies ran while one was open for 1% -> 0% of each run, Pallas kernels for 9% -> 9%
where the time goes in v4:
time: 125 us; the launch traced here: 124 us
  waiting for transfers between devices  50.8 us (41%)
  starting transfers between devices  44.7 us (36%)
  Pallas kernels  27.3 us (22%)
    ppermute x3, waiting for transfers between devices, body(): lax.ppermute(terms, 'head', [(i, (i + turn) % RING) for i in range(RING)])  19.6 us
    ppermute x9, waiting for transfers between devices, round_turn(): lax.ppermute(chunk, ('dp', 'ctx'), moves(first, turn))  18 us
    ppermute x6, starting transfers between devices, swap(): return lax.ppermute(value, 'dp', [(i, i ^ 1) for i in range(2 * RING)])  16.5 us
    ppermute x9, starting transfers between devices, round_turn(): lax.ppermute(chunk, ('dp', 'ctx'), moves(first, turn))  11.2 us
    ppermute x3, starting transfers between devices, body(): lax.ppermute(terms, 'head', [(i, (i + turn) % RING) for i in range(RING)])  7.53 us
    ppermute x1, waiting for transfers between devices, body(): back_far = lax.ppermute(back_second, 'ctx', [(2, 0)])  5.93 us
    pallas_call x1, Pallas kernels, body(): pl.pallas_call(maps_kernel, grid=(1,), out_shape=(wide_f32, wide_f32, vme...  5.71 us
    ppermute x1, waiting for transfers between devices, body(): back_near = lax.ppermute(pulled, 'ctx', [(3, 2), (1, 0)])  4.86 us
  transfers between devices with their start and end apart: 25, of which 10 were waited for; matrix products, arithmetic and copies ran while one was open for 0% of the time, Pallas kernels for 9%

profile of v4, /device:TPU:1, one launch (start us, length us, event | category | flops | bytes accessed | tf_op | source)
XLA Modules:
  0.0 124.3 jit_solution(2606242111335586889)
XLA Ops:
  0.8 5.7 %shard_map.118 = (f32[256,256]{1,0:T(8,128)S(1)}, f32[256,256]{1,0:T(8,128)S(1)}, f32[2,256,128]{2,1,0:T(8,128)S(1)}, f32[2,256,256]{2,1,0:T(8,128)S(1)}, f32[2,...) custom-call(s32[5]{0:T(128)S(1)} %stack.23.pos_ref, ...), custom_call_target="tpu_custom_call" | custom-call | tf_op jit(solution)/shard_map/pallas_call | solution.py:413
  6.5 1.5 %collective-permute-start.4 = (f32[256,1024]{1,0:T(8,128)S(1)}, f32[256,1024]{1,0:T(8,128)S(1)}, u32[]{:S(2)}, u32[]{:S(2)}) collective-permute-start(f32[256,1024]{1,0:T(8,128)S(1)} %get-tuple-element.54), channel_id=1, source_target_pairs={{0,16},{16,0},{32,48},{48,32},{64,80},{80,64},{96,112},{112,96},{1... | collective-permute-start | bytes 3145736 | tf_op jit(solution)/shard_map/ppermute | solution.py:353
  8.0 3.3 %collective-permute-start = (f32[2,128,128]{2,1,0:T(8,128)S(1)}, f32[2,128,128]{2,1,0:T(8,128)S(1)}, u32[]{:S(2)}, u32[]{:S(2)}) collective-permute-start(f32[2,128,128]{2,1,0:T(8,128)S(1)} %get-tuple-element.46), channel_id=1, source_target_pairs={{0,4},{8,12},{1,5},{9,13},{2,6},{10,14},{3,7},{11,15},{16,20},{24,... | collective-permute-start | bytes 393224 | tf_op jit(solution)/shard_map/ppermute | solution.py:425
  11.3 1.3 %collective-permute-start.3 = (f32[2,128,128]{2,1,0:T(8,128)S(1)}, f32[2,128,128]{2,1,0:T(8,128)S(1)}, u32[]{:S(2)}, u32[]{:S(2)}) collective-permute-start(f32[2,128,128]{2,1,0:T(8,128)S(1)} %get-tuple-element.47.d_ref), channel_id=1, source_target_pairs={{8,12},{4,0},{9,13},{5,1},{10,14},{6,2},{11,15},{7,3},{24,28},{20,... | collective-permute-start | bytes 393224 | tf_op jit(solution)/shard_map/ppermute | solution.py:426
  12.6 3.9 %shard_map.119 = (f32[256,256]{1,0:T(8,128)S(1)}, f32[2,256,256]{2,1,0:T(8,128)S(1)}, f32[256,256]{1,0:T(8,128)S(1)}, f32[256,256]{1,0:T(8,128)S(1)}, f32[256,25...) custom-call(s32[5]{0:T(128)S(1)} %stack.23.pos_ref, f32[2]{0:T(128)S(1)} %copy-done.5, ...), custom_call_target="tpu_custom_call" | custom-call | tf_op jit(solution)/shard_map/pallas_call | solution.py:429
  16.5 0.2 shard_map.120
  16.7 0.8 collective-permute-start.2
  17.5 0.8 collective-permute-start.1
  18.3 0.2 shard_map.121.after_ref.other_tokt_ref
  18.6 2.1 %shard_map.122 = (f32[2,128,128]{2,1,0:T(8,128)S(1)}, f32[256,256]{1,0:T(8,128)S(1)}, f32[2,128,128]{2,1,0:T(8,128)S(1)}, f32[2,128]{1,0:T(2,128)S(1)}) custom-call(s32[5]{0:T(128)S(1)} %stack.23.pos_ref, f32[2,128,128]{2,1,0:T(8,128)S(1)} %copy-done.2, f32[2,128,128]{2,1,0:T(8,128)S(1)} %collective-permute-done.w_ref.near_ref, ...), custom_call_target="tpu_custom_call" | custom-call | tf_op jit(solution)/shard_map/pallas_call | solution.py:445
  20.8 1.3 %collective-permute-start.5 = (f32[2,128,128]{2,1,0:T(8,128)S(1)}, f32[2,128,128]{2,1,0:T(8,128)S(1)}, u32[]{:S(2)}, u32[]{:S(2)}) collective-permute-start(f32[2,128,128]{2,1,0:T(8,128)S(1)} %get-tuple-element.55.o_ref.p_ref), channel_id=1, source_target_pairs={{12,8},{4,0},{13,9},{5,1},{14,10},{6,2},{15,11},{7,3},{28,24},{20,... | collective-permute-start | bytes 393224 | tf_op jit(solution)/shard_map/ppermute | solution.py:449
  22.1 2.9 %shard_map.123 = (f32[256,256]{1,0:T(8,128)S(1)}, f32[256,256]{1,0:T(8,128)S(1)}, f32[256,256]{1,0:T(8,128)S(1)}, f32[256,256]{1,0:T(8,128)S(1)}, f32[2,256]{1,0:T(2,128)S(1)}) custom-call(f32[2]{0:T(128)S(1)} %copy-done.5, f32[1,2,256]{2,1,0:T(2,128)S(1)} %copy-done.4, f32[2,128,128]{2,1,0:T(8,128)S(1)} %get-tuple-element.56.w_ref, ...), custom_call_target="tpu_custom_call" | custom-call | tf_op jit(solution)/shard_map/pallas_call | solution.py:451
  24.9 4.9 %collective-permute-done.5.w_ref.rp_ref = f32[2,128,128]{2,1,0:T(8,128)S(1)} collective-permute-done((f32[2,128,128]{2,1,0:T(8,128)S(1)}, f32[2,128,128]{2,1,0:T(8,128)S(1)}, u32[]{:S(2)}, u32[]{:S(2)}) %collective-permute-start.5) | collective-permute-done | bytes 131104 | tf_op jit(solution)/shard_map/ppermute | solution.py:449
  29.8 0.2 shard_map.124
  30.0 1.3 %collective-permute-start.7 = (f32[2,128,128]{2,1,0:T(8,128)S(1)}, f32[2,128,128]{2,1,0:T(8,128)S(1)}, u32[]{:S(2)}, u32[]{:S(2)}) collective-permute-start(f32[2,128,128]{2,1,0:T(8,128)S(1)} %shard_map.124), channel_id=1, source_target_pairs={{8,0},{9,1},{10,2},{11,3},{24,16},{25,17},{26,18},{27,19},{40,32},... | collective-permute-start | bytes 393224 | tf_op jit(solution)/shard_map/ppermute | solution.py:459
  31.3 0.7 collective-permute-start.6
  32.0 5.9 %collective-permute-done.7.far_ref = f32[2,128,128]{2,1,0:T(8,128)S(1)} collective-permute-done((f32[2,128,128]{2,1,0:T(8,128)S(1)}, f32[2,128,128]{2,1,0:T(8,128)S(1)}, u32[]{:S(2)}, u32[]{:S(2)}) %collective-permute-start.7) | collective-permute-done | bytes 131104 | tf_op jit(solution)/shard_map/ppermute | solution.py:459
  37.9 3.3 %shard_map.125 = (f32[960,256]{1,0:T(8,128)S(1)}, f32[1,2,256]{2,1,0:T(2,128)}) custom-call(s32[5]{0:T(128)S(1)} %stack.23.pos_ref, f32[2]{0:T(128)S(1)} %copy-done.5, f32[1,2,256]{2,1,0:T(2,128)S(1)} %copy-done.4, f32[2,128,128]{2,1,0:T(8,128)S(1)} %collective-permute-done.5.w_ref.rp_ref, f32[2,128,128]{2,1,0:T(8,128)S(1)} %collective-permute-done.6.mid_ref, ...), custom_call_target="tpu_custom_call" | custom-call | tf_op jit(solution)/shard_map/pallas_call | solution.py:461
  41.3 4.4 %collective-permute-start.11 = (f32[960,256]{1,0:T(8,128)S(1)}, f32[960,256]{1,0:T(8,128)S(1)}, u32[]{:S(2)}, u32[]{:S(2)}) collective-permute-start(f32[960,256]{1,0:T(8,128)S(1)} %get-tuple-element.71.all_ref.own_ref), channel_id=1, source_target_pairs={{0,16},{16,0},{32,48},{48,32},{64,80},{80,64},{96,112},{112,96},{1... | collective-permute-start | bytes 2949128 | tf_op jit(solution)/shard_map/ppermute | solution.py:353
  45.7 2.2 %collective-permute-done.11.other_ref = f32[960,256]{1,0:T(8,128)S(1)} collective-permute-done((f32[960,256]{1,0:T(8,128)S(1)}, f32[960,256]{1,0:T(8,128)S(1)}, u32[]{:S(2)}, u32[]{:S(2)}) %collective-permute-start.11) | collective-permute-done | bytes 983072 | tf_op jit(solution)/shard_map/ppermute | solution.py:353
  47.9 1.6 %shard_map.127 = (f32[792,256]{1,0:T(8,128)S(1)}, f32[792,256]{1,0:T(8,128)S(1)}, f32[792,256]{1,0:T(8,128)S(1)}, f32[792,256]{1,0:T(8,128)S(1)}) custom-call(s32[5]{0:T(128)S(1)} %stack.23.pos_ref, bf16[1024,256]{1,0:T(8,128)(2,1)S(1)} %get-tuple-element.76.tokt_ref, bf16[1024,256]{1,0:T(8,128)(2,1)S(1)} %shard_map.121.after_ref.other_tokt_ref, ...), custom_call_target="tpu_custom_call" | custom-call | tf_op jit(solution)/shard_map/pallas_call | solution.py:467
  49.4 1.2 collective-permute-start.12
  50.7 1.7 %collective-permute-start.13 = (f32[792,256]{1,0:T(8,128)S(1)}, f32[792,256]{1,0:T(8,128)S(1)}, u32[]{:S(2)}, u32[]{:S(2)}) collective-permute-start(f32[792,256]{1,0:T(8,128)S(1)} %get-tuple-element.79), channel_id=1, source_target_pairs={{0,96},{4,100},{8,104},{12,108},{16,28},{20,16},{24,20},{28,24},{3... | collective-permute-start | bytes 2433032 | tf_op jit(solution)/shard_map/ppermute | solution.py:348
  52.5 1.5 %shard_map.126 = (f32[256,512]{1,0:T(8,128)S(1)}, f32[256,512]{1,0:T(8,128)S(1)}, f32[256,512]{1,0:T(8,128)S(1)}, f32[256,512]{1,0:T(8,128)S(1)}) custom-call(s32[5]{0:T(128)S(1)} %stack.23.pos_ref, bf16[3,2048,256]{2,1,0:T(8,128)(2,1)S(1)} %copy-done, f32[960,256]{1,0:T(8,128)S(1)} %get-tuple-element.71.all_ref.own_ref), custom_call_target="tpu_custom_call" | custom-call | tf_op jit(solution)/shard_map/pallas_call | solution.py:471
  54.1 1.7 %collective-permute-start.9 = (f32[256,512]{1,0:T(8,128)S(1)}, f32[256,512]{1,0:T(8,128)S(1)}, u32[]{:S(2)}, u32[]{:S(2)}) collective-permute-start(f32[256,512]{1,0:T(8,128)S(1)} %get-tuple-element.74), channel_id=1, source_target_pairs={{0,1},{1,2},{2,3},{3,0},{4,5},{5,6},{6,7},{7,4},{8,9},{9,10},{10,1... | collective-permute-start | bytes 1572872 | tf_op jit(solution)/shard_map/ppermute | solution.py:473
  55.8 2.2 %collective-permute-start.10 = (f32[256,512]{1,0:T(8,128)S(1)}, f32[256,512]{1,0:T(8,128)S(1)}, u32[]{:S(2)}, u32[]{:S(2)}) collective-permute-start(f32[256,512]{1,0:T(8,128)S(1)} %get-tuple-element.75), channel_id=1, source_target_pairs={{0,3},{1,0},{2,1},{3,2},{4,7},{5,4},{6,5},{7,6},{8,11},{9,8},{10,9... | collective-permute-start | bytes 1572872 | tf_op jit(solution)/shard_map/ppermute | solution.py:473
  58.0 9.6 %collective-permute-done.9.refs_0_ = f32[256,512]{1,0:T(8,128)S(1)} collective-permute-done((f32[256,512]{1,0:T(8,128)S(1)}, f32[256,512]{1,0:T(8,128)S(1)}, u32[]{:S(2)}, u32[]{:S(2)}) %collective-permute-start.9) | collective-permute-done | bytes 524320 | tf_op jit(solution)/shard_map/ppermute | solution.py:473
  67.6 3.4 %collective-permute-done.12.back_ref = f32[792,256]{1,0:T(8,128)S(1)} collective-permute-done((f32[792,256]{1,0:T(8,128)S(1)}, f32[792,256]{1,0:T(8,128)S(1)}, u32[]{:S(2)}, u32[]{:S(2)}) %collective-permute-start.12) | collective-permute-done | bytes 811040 | tf_op jit(solution)/shard_map/ppermute | solution.py:348
  71.0 0.2 shard_map.128.own_ref
  71.2 2.5 %collective-permute-start.17 = (f32[792,256]{1,0:T(8,128)S(1)}, f32[792,256]{1,0:T(8,128)S(1)}, u32[]{:S(2)}, u32[]{:S(2)}) collective-permute-start(f32[792,256]{1,0:T(8,128)S(1)} %shard_map.128.own_ref), channel_id=1, source_target_pairs={{0,8},{4,12},{8,0},{12,4},{16,80},{20,84},{24,88},{28,92},{32,40},... | collective-permute-start | bytes 2433032 | tf_op jit(solution)/shard_map/ppermute | solution.py:348
  73.7 1.0 collective-permute-start.16
  74.7 0.5 collective-permute-start.15
  75.2 3.6 %collective-permute-start.8 = (f32[256,512]{1,0:T(8,128)S(1)}, f32[256,512]{1,0:T(8,128)S(1)}, u32[]{:S(2)}, u32[]{:S(2)}) collective-permute-start(f32[256,512]{1,0:T(8,128)S(1)} %get-tuple-element.73), channel_id=1, source_target_pairs={{0,2},{1,3},{2,0},{3,1},{4,6},{5,7},{6,4},{7,5},{8,10},{9,11},{10,... | collective-permute-start | bytes 1572872 | tf_op jit(solution)/shard_map/ppermute | solution.py:473
  78.8 10.0 %collective-permute-done.8 = f32[256,512]{1,0:T(8,128)S(1)} collective-permute-done((f32[256,512]{1,0:T(8,128)S(1)}, f32[256,512]{1,0:T(8,128)S(1)}, u32[]{:S(2)}, u32[]{:S(2)}) %collective-permute-start.8) | collective-permute-done | bytes 524320 | tf_op jit(solution)/shard_map/ppermute | solution.py:473
  88.8 0.2 fusion.refs_0_
  89.1 3.9 %collective-permute-done.16.ahead_ref = f32[792,256]{1,0:T(8,128)S(1)} collective-permute-done((f32[792,256]{1,0:T(8,128)S(1)}, f32[792,256]{1,0:T(8,128)S(1)}, u32[]{:S(2)}, u32[]{:S(2)}) %collective-permute-start.16) | collective-permute-done | bytes 811040 | tf_op jit(solution)/shard_map/ppermute | solution.py:348
  93.0 0.2 shard_map.129.refs_0_
  93.2 1.4 %collective-permute-start.20 = (f32[792,256]{1,0:T(8,128)S(1)}, f32[792,256]{1,0:T(8,128)S(1)}, u32[]{:S(2)}, u32[]{:S(2)}) collective-permute-start(f32[792,256]{1,0:T(8,128)S(1)} %shard_map.129.refs_0_), channel_id=1, source_target_pairs={{0,64},{4,68},{8,72},{12,76},{16,24},{20,28},{24,16},{28,20},{32,9... | collective-permute-start | bytes 2433032 | tf_op jit(solution)/shard_map/ppermute | solution.py:348
  94.6 1.6 %collective-permute-start.19 = (f32[792,256]{1,0:T(8,128)S(1)}, f32[792,256]{1,0:T(8,128)S(1)}, u32[]{:S(2)}, u32[]{:S(2)}) collective-permute-start(f32[792,256]{1,0:T(8,128)S(1)} %shard_map.129.refs_0_), channel_id=1, source_target_pairs={{0,32},{4,36},{8,40},{12,44},{16,20},{20,24},{24,28},{28,16},{32,6... | collective-permute-start | bytes 2433032 | tf_op jit(solution)/shard_map/ppermute | solution.py:348
  96.2 1.1 collective-permute-start.18
  97.3 3.0 %collective-permute-start.21 = (f32[792,256]{1,0:T(8,128)S(1)}, f32[792,256]{1,0:T(8,128)S(1)}, u32[]{:S(2)}, u32[]{:S(2)}) collective-permute-start(f32[792,256]{1,0:T(8,128)S(1)} %shard_map.129.refs_0_), channel_id=1, source_target_pairs={{0,16},{16,0},{32,48},{48,32},{64,80},{80,64},{96,112},{112,96},{1... | collective-permute-start | bytes 2433032 | tf_op jit(solution)/shard_map/ppermute | solution.py:353
  100.3 5.9 %collective-permute-done.20.refs_3_ = f32[792,256]{1,0:T(8,128)S(1)} collective-permute-done((f32[792,256]{1,0:T(8,128)S(1)}, f32[792,256]{1,0:T(8,128)S(1)}, u32[]{:S(2)}, u32[]{:S(2)}) %collective-permute-start.20) | collective-permute-done | bytes 811040 | tf_op jit(solution)/shard_map/ppermute | solution.py:348
  106.2 3.8 %collective-permute-start.24 = (f32[792,256]{1,0:T(8,128)S(1)}, f32[792,256]{1,0:T(8,128)S(1)}, u32[]{:S(2)}, u32[]{:S(2)}) collective-permute-start(f32[792,256]{1,0:T(8,128)S(1)} %collective-permute-done.20.refs_3_), channel_id=1, source_target_pairs={{0,16},{16,0},{32,48},{48,32},{64,80},{80,64},{96,112},{112,96},{1... | collective-permute-start | bytes 2433032 | tf_op jit(solution)/shard_map/ppermute | solution.py:353
  110.0 4.8 %collective-permute-done.19.refs_2_ = f32[792,256]{1,0:T(8,128)S(1)} collective-permute-done((f32[792,256]{1,0:T(8,128)S(1)}, f32[792,256]{1,0:T(8,128)S(1)}, u32[]{:S(2)}, u32[]{:S(2)}) %collective-permute-start.19) | collective-permute-done | bytes 811040 | tf_op jit(solution)/shard_map/ppermute | solution.py:348
  114.9 3.8 %collective-permute-start.23 = (f32[792,256]{1,0:T(8,128)S(1)}, f32[792,256]{1,0:T(8,128)S(1)}, u32[]{:S(2)}, u32[]{:S(2)}) collective-permute-start(f32[792,256]{1,0:T(8,128)S(1)} %collective-permute-done.19.refs_2_), channel_id=1, source_target_pairs={{0,16},{16,0},{32,48},{48,32},{64,80},{80,64},{96,112},{112,96},{1... | collective-permute-start | bytes 2433032 | tf_op jit(solution)/shard_map/ppermute | solution.py:353
  118.7 2.9 %shard_map.130.refs_8_ = f32[3,2048,256]{2,1,0:T(8,128)} custom-call(s32[5]{0:T(128)S(1)} %stack.23.pos_ref, f32[792,256]{1,0:T(8,128)S(1)} %shard_map.129.refs_0_, f32[792,256]{1,0:T(8,128)S(1)} %collective-permute-done.18.refs_1_, f32[792,256]{1,0:T(8,128)S(1)} %collective-permute-done.19.refs_2_, f32[792,256]{1,0:T(8,128)S(1)} %collective-permute-done.20.refs_3_, ...), custom_call_target="tpu_custom_call" | custom-call | tf_op jit(solution)/shard_map/pallas_call | solution.py:488
  121.5 0.2 collective-permute-done.22.refs_5_
  121.7 2.4 %shard_map.131 = (f32[3,2048,256]{2,1,0:T(8,128)}, f32[2,128,128]{2,1,0:T(8,128)}, f32[2,128]{1,0:T(2,128)}, f32[2]{0:T(128)}) custom-call(s32[5]{0:T(128)S(1)} %stack.23.pos_ref, f32[792,256]{1,0:T(8,128)S(1)} %shard_map.129.refs_0_, f32[792,256]{1,0:T(8,128)S(1)} %collective-permute-done.18.refs_1_, ...), custom_call_target="tpu_custom_call", output_to_operand_aliasing={{0}: (9, {})} | custom-call | tf_op jit(solution)/shard_map/pallas_call | solution.py:498
  (32 shorter events, 0.3 us)
Async XLA Ops:
  0.6 11.9 %copy-start.4 = (f32[1,2,256]{2,1,0:T(2,128)S(1)}, f32[1,2,256]{2,1,0:T(2,128)}, u32[]{:S(2)}) copy-start(f32[1,2,256]{2,1,0:T(2,128)} %gate_ref.7) | copy-start | bytes 6148
  0.6 11.9 %copy-start.5 = (f32[2]{0:T(128)S(1)}, f32[2]{0:T(128)}, u32[]{:S(2)}) copy-start(f32[2]{0:T(128)} %base_ref.7) | copy-start | bytes 28
  0.8 17.8 %copy-start.2 = (f32[2,128,128]{2,1,0:T(8,128)S(1)}, f32[2,128,128]{2,1,0:T(8,128)}, u32[]{:S(2)}) copy-start(f32[2,128,128]{2,1,0:T(8,128)} %init_ref.3) | copy-start | bytes 393220
  0.8 17.8 %copy-start.3 = (bf16[1,256,256]{2,1,0:T(8,128)(2,1)S(1)}, bf16[1,256,256]{2,1,0:T(8,128)(2,1)}, u32[]{:S(2)}) copy-start(bf16[1,256,256]{2,1,0:T(8,128)(2,1)} %up_ref.3) | copy-start | bytes 393220
  0.8 17.8 %copy-start.6 = (f32[2,128]{1,0:T(2,128)S(1)}, f32[2,128]{1,0:T(2,128)}, u32[]{:S(2)}) copy-start(f32[2,128]{1,0:T(2,128)} %gain_ref.1) | copy-start | bytes 3076
  6.5 11.8 %collective-permute-start.4 = (f32[256,1024]{1,0:T(8,128)S(1)}, f32[256,1024]{1,0:T(8,128)S(1)}, u32[]{:S(2)}, u32[]{:S(2)}) collective-permute-start(f32[256,1024]{1,0:T(8,128)S(1)} %get-tuple-element.54), channel_id=1, source_target_pairs={{0,16},{16,0},{32,48},{48,32},{64,80},{80,64},{96,112},{112,96},{1... | collective-permute-start | bytes 3145736 | tf_op jit(solution)/shard_map/ppermute | solution.py:353
  8.0 8.5 %collective-permute-start = (f32[2,128,128]{2,1,0:T(8,128)S(1)}, f32[2,128,128]{2,1,0:T(8,128)S(1)}, u32[]{:S(2)}, u32[]{:S(2)}) collective-permute-start(f32[2,128,128]{2,1,0:T(8,128)S(1)} %get-tuple-element.46), channel_id=1, source_target_pairs={{0,4},{8,12},{1,5},{9,13},{2,6},{10,14},{3,7},{11,15},{16,20},{24,... | collective-permute-start | bytes 393224 | tf_op jit(solution)/shard_map/ppermute | solution.py:425
  11.3 7.3 %collective-permute-start.3 = (f32[2,128,128]{2,1,0:T(8,128)S(1)}, f32[2,128,128]{2,1,0:T(8,128)S(1)}, u32[]{:S(2)}, u32[]{:S(2)}) collective-permute-start(f32[2,128,128]{2,1,0:T(8,128)S(1)} %get-tuple-element.47.d_ref), channel_id=1, source_target_pairs={{8,12},{4,0},{9,13},{5,1},{10,14},{6,2},{11,15},{7,3},{24,28},{20,... | collective-permute-start | bytes 393224 | tf_op jit(solution)/shard_map/ppermute | solution.py:426
  16.7 35.8 %copy-start = (bf16[3,2048,256]{2,1,0:T(8,128)(2,1)S(1)}, bf16[3,2048,256]{2,1,0:T(8,128)(2,1)}, u32[]{:S(2)}) copy-start(bf16[3,2048,256]{2,1,0:T(8,128)(2,1)} %w_ref.1) | copy-start | bytes 9437188
  16.7 1.9 %collective-permute-start.2 = (f32[2,128,128]{2,1,0:T(8,128)S(1)}, f32[2,128,128]{2,1,0:T(8,128)S(1)}, u32[]{:S(2)}, u32[]{:S(2)}) collective-permute-start(f32[2,128,128]{2,1,0:T(8,128)S(1)} %shard_map.120), channel_id=1, source_target_pairs={{4,12},{5,13},{6,14},{7,15},{20,28},{21,29},{22,30},{23,31},{36,44... | collective-permute-start | bytes 393224 | tf_op jit(solution)/shard_map/ppermute | solution.py:442
  17.5 1.1 collective-permute-start.1
  20.8 9.0 %collective-permute-start.5 = (f32[2,128,128]{2,1,0:T(8,128)S(1)}, f32[2,128,128]{2,1,0:T(8,128)S(1)}, u32[]{:S(2)}, u32[]{:S(2)}) collective-permute-start(f32[2,128,128]{2,1,0:T(8,128)S(1)} %get-tuple-element.55.o_ref.p_ref), channel_id=1, source_target_pairs={{12,8},{4,0},{13,9},{5,1},{14,10},{6,2},{15,11},{7,3},{28,24},{20,... | collective-permute-start | bytes 393224 | tf_op jit(solution)/shard_map/ppermute | solution.py:449
  30.0 7.9 %collective-permute-start.7 = (f32[2,128,128]{2,1,0:T(8,128)S(1)}, f32[2,128,128]{2,1,0:T(8,128)S(1)}, u32[]{:S(2)}, u32[]{:S(2)}) collective-permute-start(f32[2,128,128]{2,1,0:T(8,128)S(1)} %shard_map.124), channel_id=1, source_target_pairs={{8,0},{9,1},{10,2},{11,3},{24,16},{25,17},{26,18},{27,19},{40,32},... | collective-permute-start | bytes 393224 | tf_op jit(solution)/shard_map/ppermute | solution.py:459
  31.3 6.6 %collective-permute-start.6 = (f32[2,128,128]{2,1,0:T(8,128)S(1)}, f32[2,128,128]{2,1,0:T(8,128)S(1)}, u32[]{:S(2)}, u32[]{:S(2)}) collective-permute-start(f32[2,128,128]{2,1,0:T(8,128)S(1)} %shard_map.124), channel_id=1, source_target_pairs={{8,4},{9,5},{10,6},{11,7},{24,20},{25,21},{26,22},{27,23},{40,36},... | collective-permute-start | bytes 393224 | tf_op jit(solution)/shard_map/ppermute | solution.py:458
  41.3 6.6 %collective-permute-start.11 = (f32[960,256]{1,0:T(8,128)S(1)}, f32[960,256]{1,0:T(8,128)S(1)}, u32[]{:S(2)}, u32[]{:S(2)}) collective-permute-start(f32[960,256]{1,0:T(8,128)S(1)} %get-tuple-element.71.all_ref.own_ref), channel_id=1, source_target_pairs={{0,16},{16,0},{32,48},{48,32},{64,80},{80,64},{96,112},{112,96},{1... | collective-permute-start | bytes 2949128 | tf_op jit(solution)/shard_map/ppermute | solution.py:353
  49.4 21.5 %collective-permute-start.12 = (f32[792,256]{1,0:T(8,128)S(1)}, f32[792,256]{1,0:T(8,128)S(1)}, u32[]{:S(2)}, u32[]{:S(2)}) collective-permute-start(f32[792,256]{1,0:T(8,128)S(1)} %get-tuple-element.78), channel_id=1, source_target_pairs={{0,32},{4,36},{8,40},{12,44},{16,20},{20,24},{24,28},{28,16},{32,6... | collective-permute-start | bytes 2433032 | tf_op jit(solution)/shard_map/ppermute | solution.py:348
  50.7 20.3 %collective-permute-start.13 = (f32[792,256]{1,0:T(8,128)S(1)}, f32[792,256]{1,0:T(8,128)S(1)}, u32[]{:S(2)}, u32[]{:S(2)}) collective-permute-start(f32[792,256]{1,0:T(8,128)S(1)} %get-tuple-element.79), channel_id=1, source_target_pairs={{0,96},{4,100},{8,104},{12,108},{16,28},{20,16},{24,20},{28,24},{3... | collective-permute-start | bytes 2433032 | tf_op jit(solution)/shard_map/ppermute | solution.py:348
  52.4 18.6 %collective-permute-start.14 = (f32[792,256]{1,0:T(8,128)S(1)}, f32[792,256]{1,0:T(8,128)S(1)}, u32[]{:S(2)}, u32[]{:S(2)}) collective-permute-start(f32[792,256]{1,0:T(8,128)S(1)} %get-tuple-element.80), channel_id=1, source_target_pairs={{0,64},{4,68},{8,72},{12,76},{16,24},{20,28},{24,16},{28,20},{32,9... | collective-permute-start | bytes 2433032 | tf_op jit(solution)/shard_map/ppermute | solution.py:348
  54.1 13.5 %collective-permute-start.9 = (f32[256,512]{1,0:T(8,128)S(1)}, f32[256,512]{1,0:T(8,128)S(1)}, u32[]{:S(2)}, u32[]{:S(2)}) collective-permute-start(f32[256,512]{1,0:T(8,128)S(1)} %get-tuple-element.74), channel_id=1, source_target_pairs={{0,1},{1,2},{2,3},{3,0},{4,5},{5,6},{6,7},{7,4},{8,9},{9,10},{10,1... | collective-permute-start | bytes 1572872 | tf_op jit(solution)/shard_map/ppermute | solution.py:473
  55.8 11.8 %collective-permute-start.10 = (f32[256,512]{1,0:T(8,128)S(1)}, f32[256,512]{1,0:T(8,128)S(1)}, u32[]{:S(2)}, u32[]{:S(2)}) collective-permute-start(f32[256,512]{1,0:T(8,128)S(1)} %get-tuple-element.75), channel_id=1, source_target_pairs={{0,3},{1,0},{2,1},{3,2},{4,7},{5,4},{6,5},{7,6},{8,11},{9,8},{10,9... | collective-permute-start | bytes 1572872 | tf_op jit(solution)/shard_map/ppermute | solution.py:473
  71.2 17.9 %collective-permute-start.17 = (f32[792,256]{1,0:T(8,128)S(1)}, f32[792,256]{1,0:T(8,128)S(1)}, u32[]{:S(2)}, u32[]{:S(2)}) collective-permute-start(f32[792,256]{1,0:T(8,128)S(1)} %shard_map.128.own_ref), channel_id=1, source_target_pairs={{0,8},{4,12},{8,0},{12,4},{16,80},{20,84},{24,88},{28,92},{32,40},... | collective-permute-start | bytes 2433032 | tf_op jit(solution)/shard_map/ppermute | solution.py:348
  73.7 19.3 %collective-permute-start.16 = (f32[792,256]{1,0:T(8,128)S(1)}, f32[792,256]{1,0:T(8,128)S(1)}, u32[]{:S(2)}, u32[]{:S(2)}) collective-permute-start(f32[792,256]{1,0:T(8,128)S(1)} %shard_map.128.own_ref), channel_id=1, source_target_pairs={{0,12},{4,0},{8,4},{12,8},{16,112},{20,116},{24,120},{28,124},{32,... | collective-permute-start | bytes 2433032 | tf_op jit(solution)/shard_map/ppermute | solution.py:348
  74.7 18.3 %collective-permute-start.15 = (f32[792,256]{1,0:T(8,128)S(1)}, f32[792,256]{1,0:T(8,128)S(1)}, u32[]{:S(2)}, u32[]{:S(2)}) collective-permute-start(f32[792,256]{1,0:T(8,128)S(1)} %shard_map.128.own_ref), channel_id=1, source_target_pairs={{0,4},{4,8},{8,12},{12,0},{16,48},{20,52},{24,56},{28,60},{32,36},... | collective-permute-start | bytes 2433032 | tf_op jit(solution)/shard_map/ppermute | solution.py:348
  75.2 13.6 %collective-permute-start.8 = (f32[256,512]{1,0:T(8,128)S(1)}, f32[256,512]{1,0:T(8,128)S(1)}, u32[]{:S(2)}, u32[]{:S(2)}) collective-permute-start(f32[256,512]{1,0:T(8,128)S(1)} %get-tuple-element.73), channel_id=1, source_target_pairs={{0,2},{1,3},{2,0},{3,1},{4,6},{5,7},{6,4},{7,5},{8,10},{9,11},{10,... | collective-permute-start | bytes 1572872 | tf_op jit(solution)/shard_map/ppermute | solution.py:473
  89.1 32.5 %copy-start.1 = (bf16[1,256,512]{2,1,0:T(8,128)(2,1)}, bf16[1,256,512]{2,1,0:T(8,128)(2,1)S(1)}, u32[]{:S(2)}) copy-start(bf16[1,256,512]{2,1,0:T(8,128)(2,1)S(1)} %fusion.refs_0_) | copy-start | bytes 786436
  93.2 13.0 %collective-permute-start.20 = (f32[792,256]{1,0:T(8,128)S(1)}, f32[792,256]{1,0:T(8,128)S(1)}, u32[]{:S(2)}, u32[]{:S(2)}) collective-permute-start(f32[792,256]{1,0:T(8,128)S(1)} %shard_map.129.refs_0_), channel_id=1, source_target_pairs={{0,64},{4,68},{8,72},{12,76},{16,24},{20,28},{24,16},{28,20},{32,9... | collective-permute-start | bytes 2433032 | tf_op jit(solution)/shard_map/ppermute | solution.py:348
  94.6 20.2 %collective-permute-start.19 = (f32[792,256]{1,0:T(8,128)S(1)}, f32[792,256]{1,0:T(8,128)S(1)}, u32[]{:S(2)}, u32[]{:S(2)}) collective-permute-start(f32[792,256]{1,0:T(8,128)S(1)} %shard_map.129.refs_0_), channel_id=1, source_target_pairs={{0,32},{4,36},{8,40},{12,44},{16,20},{20,24},{24,28},{28,16},{32,6... | collective-permute-start | bytes 2433032 | tf_op jit(solution)/shard_map/ppermute | solution.py:348
  96.2 22.4 %collective-permute-start.18 = (f32[792,256]{1,0:T(8,128)S(1)}, f32[792,256]{1,0:T(8,128)S(1)}, u32[]{:S(2)}, u32[]{:S(2)}) collective-permute-start(f32[792,256]{1,0:T(8,128)S(1)} %shard_map.129.refs_0_), channel_id=1, source_target_pairs={{0,96},{4,100},{8,104},{12,108},{16,28},{20,16},{24,20},{28,24},{3... | collective-permute-start | bytes 2433032 | tf_op jit(solution)/shard_map/ppermute | solution.py:348
  97.3 21.4 %collective-permute-start.21 = (f32[792,256]{1,0:T(8,128)S(1)}, f32[792,256]{1,0:T(8,128)S(1)}, u32[]{:S(2)}, u32[]{:S(2)}) collective-permute-start(f32[792,256]{1,0:T(8,128)S(1)} %shard_map.129.refs_0_), channel_id=1, source_target_pairs={{0,16},{16,0},{32,48},{48,32},{64,80},{80,64},{96,112},{112,96},{1... | collective-permute-start | bytes 2433032 | tf_op jit(solution)/shard_map/ppermute | solution.py:353
  106.2 12.4 %collective-permute-start.24 = (f32[792,256]{1,0:T(8,128)S(1)}, f32[792,256]{1,0:T(8,128)S(1)}, u32[]{:S(2)}, u32[]{:S(2)}) collective-permute-start(f32[792,256]{1,0:T(8,128)S(1)} %collective-permute-done.20.refs_3_), channel_id=1, source_target_pairs={{0,16},{16,0},{32,48},{48,32},{64,80},{80,64},{96,112},{112,96},{1... | collective-permute-start | bytes 2433032 | tf_op jit(solution)/shard_map/ppermute | solution.py:353
  114.9 6.7 %collective-permute-start.23 = (f32[792,256]{1,0:T(8,128)S(1)}, f32[792,256]{1,0:T(8,128)S(1)}, u32[]{:S(2)}, u32[]{:S(2)}) collective-permute-start(f32[792,256]{1,0:T(8,128)S(1)} %collective-permute-done.19.refs_2_), channel_id=1, source_target_pairs={{0,16},{16,0},{32,48},{48,32},{64,80},{80,64},{96,112},{112,96},{1... | collective-permute-start | bytes 2433032 | tf_op jit(solution)/shard_map/ppermute | solution.py:353
  118.6 3.1 %collective-permute-start.22 = (f32[792,256]{1,0:T(8,128)S(1)}, f32[792,256]{1,0:T(8,128)S(1)}, u32[]{:S(2)}, u32[]{:S(2)}) collective-permute-start(f32[792,256]{1,0:T(8,128)S(1)} %collective-permute-done.18.refs_1_), channel_id=1, source_target_pairs={{0,16},{16,0},{32,48},{48,32},{64,80},{80,64},{96,112},{112,96},{1... | collective-permute-start | bytes 2433032 | tf_op jit(solution)/shard_map/ppermute | solution.py:353

commit v5 on v4

--- a/solution.py
+++ b/solution.py
@@ -12,7 +12,8 @@
 RING = 4
 TURNS = (0, 1, 3, 2)
 CHUNK = 256
-PIECE = 24
+SLICE = CHUNK // RING
+PIECE = 32
 EXTRA = 2 * RING * PIECE
 F32 = jnp.float32
 BF = jnp.bfloat16
@@ -281,13 +282,36 @@
         out_ref[...] = total + lax.dot_general(ds[2], w_ref[2, rows, :], NT, preferred_element_type=F32)
 
 
-def sum_kernel(own_ref, back_ref, ahead_ref, far_ref, *refs):
-    refs[-1][...] = (own_ref[...] + far_ref[...]) + (back_ref[...] + ahead_ref[...])
+def slice_rows(pos_ref, turn):
+    at = (pos_ref[2] + turn) & (RING - 1)
+    taken = [
+        (pl.ds(pl.multiple_of(m * CHUNK + at * SLICE, SLICE), SLICE), slice(m * SLICE, (m + 1) * SLICE))
+        for m in range(3)
+    ]
+    few = PIECE // RING
+    extra = pl.ds(pl.multiple_of(3 * CHUNK + at * few, few), few)
+    return taken + [(extra, slice(3 * SLICE, 3 * SLICE + few))]
+
+
+def split_kernel(pos_ref, own_ref, back_ref, ahead_ref, far_ref, *refs):
+    for turn, out_ref in zip(TURNS, refs[-RING:]):
+        for rows, to in slice_rows(pos_ref, turn):
+            out_ref[to, :] = (own_ref[rows, :] + far_ref[rows, :]) + (back_ref[rows, :] + ahead_ref[rows, :])
+
+
+def sum_kernel(own_ref, back_ref, ahead_ref, far_ref, out_ref):
+    out_ref[...] = (own_ref[...] + far_ref[...]) + (back_ref[...] + ahead_ref[...])
+
+
+def join_kernel(pos_ref, own_ref, ahead_ref, back_ref, far_ref, *refs):
+    for turn, part_ref in zip(TURNS, (own_ref, ahead_ref, back_ref, far_ref)):
+        for rows, to in slice_rows(pos_ref, turn):
+            refs[-1][rows, :] = part_ref[to, :]
 
 
 def place_kernel(pos_ref, *refs, which):
     pieces = refs[: len(which)]
-    out_ref, sem = refs[-2:]
+    out_ref, sem = refs[len(refs) - 3 if len(refs) == len(which) + 4 else -2], refs[-1]
     copies = []
     for g, ((half, m), piece) in enumerate(zip(which, pieces)):
         core = pos_ref[0] if half == 0 else 1 - pos_ref[0]
@@ -475,25 +499,35 @@
     ]
     grad_tokens = ((quarters[0] + from_far) + (from_back + from_ahead)).astype(BF).reshape(1, n, -1)
 
-    part_sum = whole(sum_kernel, chunk, [VM] * 4 + [anywhere] * 2)(own, *away, from_back, from_ahead)
-    total = whole(sum_kernel, chunk, [VM] * 4 + [anywhere])(part_sum, *round_turn([part_sum] * 3, False), grad_tokens)
+    piece = vmem(3 * SLICE + PIECE // RING, wide)
+    own, *away = whole(split_kernel, (piece,) * RING, [SM] + [VM] * 4 + [anywhere] * 2)(
+        pos, own, *away, from_back, from_ahead
+    )
+    part_sum = whole(sum_kernel, piece, [VM] * 4)(own, *round_turn(away, False))
+    from_back, from_ahead, from_far = round_turn([part_sum] * 3, False)
+    total = whole(join_kernel, chunk, [SM] + [VM] * 4 + [anywhere])(
+        pos, part_sum, from_ahead, from_back, from_far, grad_tokens
+    )
     from_back, from_ahead, from_far = round_turn([total] * 3, True)
+    out = shape(3, model, wide)
+
+    def place(which, extra, extra_out, extra_spec, aliases):
+        given = [(mine, others)[half][m] for half, m in which]
+        return pl.pallas_call(
+            functools.partial(place_kernel, which=which),
+            out_shape=(out,) + extra_out,
+            in_specs=[SM] + [VM] * len(given) + [extra_spec],
+            out_specs=(anywhere,) + (VM,) * len(extra_out),
+            scratch_shapes=[pltpu.SemaphoreType.DMA((3, len(which)))],
+            input_output_aliases={len(given) + 1: aliases},
+            compiler_params=PARAMS,
+        )(pos, *given, extra)
+
     mine = [total, from_ahead, from_back, from_far]
-    others = [swap(piece) for piece in mine]
-
-    out = shape(3, model, wide)
-    placed = None
-    for which in (((0, 0), (0, 1), (0, 2), (0, 3), (1, 0), (1, 3)),):
-        given = [(mine, others)[half][m] for half, m in which] + ([] if placed is None else [placed])
-        placed = pl.pallas_call(
-            functools.partial(place_kernel, which=which),
-            out_shape=out,
-            in_specs=[SM] + [VM] * len(which) + [anywhere] * (len(given) - len(which)),
-            out_specs=anywhere,
-            scratch_shapes=[pltpu.SemaphoreType.DMA((3, len(which)))],
-            input_output_aliases={} if placed is None else {len(which) + 1: 0},
-            compiler_params=PARAMS,
-        )(pos, *given)
+    others = [swap(total)]
+    placed, mine[3] = place(((0, 0), (1, 0)), from_far, (chunk,), VM, 1)
+    others += [swap(given) for given in mine[1:]]
+    (placed,) = place(((0, 1), (0, 2), (0, 3), (1, 3)), placed, (), anywhere, 0)
     which = ((1, 1), (1, 2))
     grad_proj, grad_init, grad_gain, grad_rates = pl.pallas_call(
         functools.partial(last_kernel, which=which),

time: 125 us -> 137 us (1.096)
  starting transfers between devices: 44.7 us -> 70.4 us
  waiting for transfers between devices: 50.8 us -> 35.4 us
  Pallas kernels: 27.3 us -> 29.4 us
    ppermute x6, starting transfers between devices: 16.5 us -> 31.8 us  [swap(): return lax.ppermute(value, 'dp', [(i, i ^ 1) for i in range(2 * RING)])]
    ppermute x9 -> x12, starting transfers between devices: 11.2 us -> 23.8 us  [round_turn(): lax.ppermute(chunk, ('dp', 'ctx'), moves(first, turn))]
    ppermute x3, waiting for transfers between devices: 19.6 us -> 7.59 us  [body(): lax.ppermute(terms, 'head', [(i, (i + turn) % RING) for i in range(RING)])]
    pallas_call x3 -> x5, Pallas kernels: 3.24 us -> 5.39 us  [the longest x2 4.03 us: place(): pl.pallas_call(functools.partial(place_kernel, which=which), out_shape=(o...]
    ppermute x3, starting transfers between devices: 7.53 us -> 5.58 us  [body(): lax.ppermute(terms, 'head', [(i, (i + turn) % RING) for i in range(RING)])]
    ppermute x9 -> x12, waiting for transfers between devices: 18 us -> 16.3 us  [round_turn(): lax.ppermute(chunk, ('dp', 'ctx'), moves(first, turn))]
    ppermute x6, waiting for transfers between devices: 2.4 us -> 0.8 us  [swap(): return lax.ppermute(value, 'dp', [(i, i ^ 1) for i in range(2 * RING)])]
  transfers between devices with their start and end apart: 25 -> 28, of which waited for: 10 -> 10; matrix products, arithmetic and copies ran while one was open for 0% -> 0% of each run, Pallas kernels for 9% -> 11%
where the time goes in v5:
time: 137 us
  starting transfers between devices  70.4 us (51%)
  waiting for transfers between devices  35.4 us (26%)
  Pallas kernels  29.4 us (21%)
    ppermute x6, starting transfers between devices, swap(): return lax.ppermute(value, 'dp', [(i, i ^ 1) for i in range(2 * RING)])  31.8 us
    ppermute x12, starting transfers between devices, round_turn(): lax.ppermute(chunk, ('dp', 'ctx'), moves(first, turn))  23.8 us
    ppermute x12, waiting for transfers between devices, round_turn(): lax.ppermute(chunk, ('dp', 'ctx'), moves(first, turn))  16.3 us
    ppermute x3, waiting for transfers between devices, body(): lax.ppermute(terms, 'head', [(i, (i + turn) % RING) for i in range(RING)])  7.59 us
    ppermute x1, waiting for transfers between devices, body(): back_far = lax.ppermute(back_second, 'ctx', [(2, 0)])  5.93 us
    pallas_call x1, Pallas kernels, body(): pl.pallas_call(maps_kernel, grid=(1,), out_shape=(wide_f32, wide_f32, vme...  5.71 us
    ppermute x3, starting transfers between devices, body(): lax.ppermute(terms, 'head', [(i, (i + turn) % RING) for i in range(RING)])  5.58 us
    ppermute x1, waiting for transfers between devices, body(): back_near = lax.ppermute(pulled, 'ctx', [(3, 2), (1, 0)])  4.85 us
  transfers between devices with their start and end apart: 28, of which 10 were waited for; matrix products, arithmetic and copies ran while one was open for 0% of the time, Pallas kernels for 11%

profile of v5, /device:TPU:1, one launch (start us, length us, event | category | flops | bytes accessed | tf_op | source)
XLA Modules:
  0.0 136.8 jit_solution(6694066150503304975)
XLA Ops:
  0.8 5.7 %shard_map.118 = (f32[256,256]{1,0:T(8,128)S(1)}, f32[256,256]{1,0:T(8,128)S(1)}, f32[2,256,128]{2,1,0:T(8,128)S(1)}, f32[2,256,256]{2,1,0:T(8,128)S(1)}, f32[2,...) custom-call(s32[5]{0:T(128)S(1)} %stack.23.pos_ref, ...), custom_call_target="tpu_custom_call" | custom-call | tf_op jit(solution)/shard_map/pallas_call | solution.py:437
  6.5 1.5 %collective-permute-start.4 = (f32[256,1024]{1,0:T(8,128)S(1)}, f32[256,1024]{1,0:T(8,128)S(1)}, u32[]{:S(2)}, u32[]{:S(2)}) collective-permute-start(f32[256,1024]{1,0:T(8,128)S(1)} %get-tuple-element.60), channel_id=1, source_target_pairs={{0,16},{16,0},{32,48},{48,32},{64,80},{80,64},{96,112},{112,96},{1... | collective-permute-start | bytes 3145736 | tf_op jit(solution)/shard_map/ppermute | solution.py:377
  8.0 3.3 %collective-permute-start = (f32[2,128,128]{2,1,0:T(8,128)S(1)}, f32[2,128,128]{2,1,0:T(8,128)S(1)}, u32[]{:S(2)}, u32[]{:S(2)}) collective-permute-start(f32[2,128,128]{2,1,0:T(8,128)S(1)} %get-tuple-element.52), channel_id=1, source_target_pairs={{0,4},{8,12},{1,5},{9,13},{2,6},{10,14},{3,7},{11,15},{16,20},{24,... | collective-permute-start | bytes 393224 | tf_op jit(solution)/shard_map/ppermute | solution.py:449
  11.3 1.3 collective-permute-start.3
  12.6 3.9 %shard_map.119 = (f32[256,256]{1,0:T(8,128)S(1)}, f32[2,256,256]{2,1,0:T(8,128)S(1)}, f32[256,256]{1,0:T(8,128)S(1)}, f32[256,256]{1,0:T(8,128)S(1)}, f32[256,25...) custom-call(s32[5]{0:T(128)S(1)} %stack.23.pos_ref, f32[2]{0:T(128)S(1)} %copy-done.5, ...), custom_call_target="tpu_custom_call" | custom-call | tf_op jit(solution)/shard_map/pallas_call | solution.py:453
  16.7 0.8 collective-permute-start.2
  17.5 0.7 collective-permute-start.1
  18.5 2.1 %shard_map.122 = (f32[2,128,128]{2,1,0:T(8,128)S(1)}, f32[256,256]{1,0:T(8,128)S(1)}, f32[2,128,128]{2,1,0:T(8,128)S(1)}, f32[2,128]{1,0:T(2,128)S(1)}) custom-call(s32[5]{0:T(128)S(1)} %stack.23.pos_ref, f32[2,128,128]{2,1,0:T(8,128)S(1)} %copy-done.2, f32[2,128,128]{2,1,0:T(8,128)S(1)} %collective-permute-done.w_ref.near_ref, ...), custom_call_target="tpu_custom_call" | custom-call | tf_op jit(solution)/shard_map/pallas_call | solution.py:469
  20.6 1.3 collective-permute-start.5
  21.9 2.9 %shard_map.123 = (f32[256,256]{1,0:T(8,128)S(1)}, f32[256,256]{1,0:T(8,128)S(1)}, f32[256,256]{1,0:T(8,128)S(1)}, f32[256,256]{1,0:T(8,128)S(1)}, f32[2,256]{1,0:T(2,128)S(1)}) custom-call(f32[2]{0:T(128)S(1)} %copy-done.5, f32[1,2,256]{2,1,0:T(2,128)S(1)} %copy-done.4, f32[2,128,128]{2,1,0:T(8,128)S(1)} %get-tuple-element.62.w_ref, ...), custom_call_target="tpu_custom_call" | custom-call | tf_op jit(solution)/shard_map/pallas_call | solution.py:475
  24.8 4.8 %collective-permute-done.5.w_ref.rp_ref = f32[2,128,128]{2,1,0:T(8,128)S(1)} collective-permute-done((f32[2,128,128]{2,1,0:T(8,128)S(1)}, f32[2,128,128]{2,1,0:T(8,128)S(1)}, u32[]{:S(2)}, u32[]{:S(2)}) %collective-permute-start.5) | collective-permute-done | bytes 131104 | tf_op jit(solution)/shard_map/ppermute | solution.py:473
  29.6 0.2 shard_map.124
  29.9 1.3 collective-permute-start.7
  31.2 0.7 collective-permute-start.6
  31.9 5.9 %collective-permute-done.7.far_ref = f32[2,128,128]{2,1,0:T(8,128)S(1)} collective-permute-done((f32[2,128,128]{2,1,0:T(8,128)S(1)}, f32[2,128,128]{2,1,0:T(8,128)S(1)}, u32[]{:S(2)}, u32[]{:S(2)}) %collective-permute-start.7) | collective-permute-done | bytes 131104 | tf_op jit(solution)/shard_map/ppermute | solution.py:483
  37.8 3.3 %shard_map.125 = (f32[1024,256]{1,0:T(8,128)S(1)}, f32[1,2,256]{2,1,0:T(2,128)}) custom-call(s32[5]{0:T(128)S(1)} %stack.23.pos_ref, f32[2]{0:T(128)S(1)} %copy-done.5, f32[1,2,256]{2,1,0:T(2,128)S(1)} %copy-done.4, f32[2,128,128]{2,1,0:T(8,128)S(1)} %collective-permute-done.5.w_ref.rp_ref, f32[2,128,128]{2,1,0:T(8,128)S(1)} %collective-permute-done.6.mid_ref, ...), custom_call_target="tpu_custom_call" | custom-call | tf_op jit(solution)/shard_map/pallas_call | solution.py:485
  41.1 4.2 %collective-permute-start.11 = (f32[1024,256]{1,0:T(8,128)S(1)}, f32[1024,256]{1,0:T(8,128)S(1)}, u32[]{:S(2)}, u32[]{:S(2)}) collective-permute-start(f32[1024,256]{1,0:T(8,128)S(1)} %get-tuple-element.77.all_ref.own_ref), channel_id=1, source_target_pairs={{0,16},{16,0},{32,48},{48,32},{64,80},{80,64},{96,112},{112,96},{1... | collective-permute-start | bytes 3145736 | tf_op jit(solution)/shard_map/ppermute | solution.py:377
  45.4 1.6 %shard_map.126 = (f32[256,512]{1,0:T(8,128)S(1)}, f32[256,512]{1,0:T(8,128)S(1)}, f32[256,512]{1,0:T(8,128)S(1)}, f32[256,512]{1,0:T(8,128)S(1)}) custom-call(s32[5]{0:T(128)S(1)} %stack.23.pos_ref, bf16[3,2048,256]{2,1,0:T(8,128)(2,1)S(1)} %copy-done, f32[1024,256]{1,0:T(8,128)S(1)} %get-tuple-element.77.all_ref.own_ref), custom_call_target="tpu_custom_call" | custom-call | tf_op jit(solution)/shard_map/pallas_call | solution.py:495
  46.9 1.9 %collective-permute-start.9 = (f32[256,512]{1,0:T(8,128)S(1)}, f32[256,512]{1,0:T(8,128)S(1)}, u32[]{:S(2)}, u32[]{:S(2)}) collective-permute-start(f32[256,512]{1,0:T(8,128)S(1)} %get-tuple-element.80), channel_id=1, source_target_pairs={{0,1},{1,2},{2,3},{3,0},{4,5},{5,6},{6,7},{7,4},{8,9},{9,10},{10,1... | collective-permute-start | bytes 1572872 | tf_op jit(solution)/shard_map/ppermute | solution.py:497
  48.8 1.5 %shard_map.127 = (f32[800,256]{1,0:T(8,128)S(1)}, f32[800,256]{1,0:T(8,128)S(1)}, f32[800,256]{1,0:T(8,128)S(1)}, f32[800,256]{1,0:T(8,128)S(1)}) custom-call(s32[5]{0:T(128)S(1)} %stack.23.pos_ref, bf16[1024,256]{1,0:T(8,128)(2,1)S(1)} %get-tuple-element.82.tokt_ref, bf16[1024,256]{1,0:T(8,128)(2,1)S(1)} %shard_map.121.after_ref.other_tokt_ref, ...), custom_call_target="tpu_custom_call" | custom-call | tf_op jit(solution)/shard_map/pallas_call | solution.py:491
  50.4 1.1 collective-permute-start.12
  51.4 1.7 %collective-permute-start.13 = (f32[800,256]{1,0:T(8,128)S(1)}, f32[800,256]{1,0:T(8,128)S(1)}, u32[]{:S(2)}, u32[]{:S(2)}) collective-permute-start(f32[800,256]{1,0:T(8,128)S(1)} %get-tuple-element.85), channel_id=1, source_target_pairs={{0,96},{4,100},{8,104},{12,108},{16,28},{20,16},{24,20},{28,24},{3... | collective-permute-start | bytes 2457608 | tf_op jit(solution)/shard_map/ppermute | solution.py:372
  53.3 2.6 %collective-permute-start.10 = (f32[256,512]{1,0:T(8,128)S(1)}, f32[256,512]{1,0:T(8,128)S(1)}, u32[]{:S(2)}, u32[]{:S(2)}) collective-permute-start(f32[256,512]{1,0:T(8,128)S(1)} %get-tuple-element.81), channel_id=1, source_target_pairs={{0,3},{1,0},{2,1},{3,2},{4,7},{5,4},{6,5},{7,6},{8,11},{9,8},{10,9... | collective-permute-start | bytes 1572872 | tf_op jit(solution)/shard_map/ppermute | solution.py:497
  55.9 7.4 %collective-permute-done.9.refs_0_ = f32[256,512]{1,0:T(8,128)S(1)} collective-permute-done((f32[256,512]{1,0:T(8,128)S(1)}, f32[256,512]{1,0:T(8,128)S(1)}, u32[]{:S(2)}, u32[]{:S(2)}) %collective-permute-start.9) | collective-permute-done | bytes 524320 | tf_op jit(solution)/shard_map/ppermute | solution.py:497
  63.3 1.1 collective-permute-start.8
  64.6 7.3 %collective-permute-done.12.back_ref = f32[800,256]{1,0:T(8,128)S(1)} collective-permute-done((f32[800,256]{1,0:T(8,128)S(1)}, f32[800,256]{1,0:T(8,128)S(1)}, u32[]{:S(2)}, u32[]{:S(2)}) %collective-permute-start.12) | collective-permute-done | bytes 819232 | tf_op jit(solution)/shard_map/ppermute | solution.py:372
  71.9 0.7 shard_map.128
  72.6 1.3 collective-permute-start.15
  73.9 1.5 %collective-permute-start.16 = (f32[200,256]{1,0:T(8,128)S(1)}, f32[200,256]{1,0:T(8,128)S(1)}, u32[]{:S(2)}, u32[]{:S(2)}) collective-permute-start(f32[200,256]{1,0:T(8,128)S(1)} %get-tuple-element.89), channel_id=1, source_target_pairs={{0,12},{4,0},{8,4},{12,8},{16,112},{20,116},{24,120},{28,124},{32,... | collective-permute-start | bytes 614408 | tf_op jit(solution)/shard_map/ppermute | solution.py:372
  75.4 1.5 %collective-permute-start.17 = (f32[200,256]{1,0:T(8,128)S(1)}, f32[200,256]{1,0:T(8,128)S(1)}, u32[]{:S(2)}, u32[]{:S(2)}) collective-permute-start(f32[200,256]{1,0:T(8,128)S(1)} %get-tuple-element.90), channel_id=1, source_target_pairs={{0,8},{4,12},{8,0},{12,4},{16,80},{20,84},{24,88},{28,92},{32,40},... | collective-permute-start | bytes 614408 | tf_op jit(solution)/shard_map/ppermute | solution.py:372
  76.9 1.8 %collective-permute-done.15.back_ref = f32[200,256]{1,0:T(8,128)S(1)} collective-permute-done((f32[200,256]{1,0:T(8,128)S(1)}, f32[200,256]{1,0:T(8,128)S(1)}, u32[]{:S(2)}, u32[]{:S(2)}) %collective-permute-start.15) | collective-permute-done | bytes 204832 | tf_op jit(solution)/shard_map/ppermute | solution.py:372
  78.7 3.0 %collective-permute-done.17.far_ref = f32[200,256]{1,0:T(8,128)S(1)} collective-permute-done((f32[200,256]{1,0:T(8,128)S(1)}, f32[200,256]{1,0:T(8,128)S(1)}, u32[]{:S(2)}, u32[]{:S(2)}) %collective-permute-start.17) | collective-permute-done | bytes 204832 | tf_op jit(solution)/shard_map/ppermute | solution.py:372
  81.7 1.4 %collective-permute-start.20 = (f32[200,256]{1,0:T(8,128)S(1)}, f32[200,256]{1,0:T(8,128)S(1)}, u32[]{:S(2)}, u32[]{:S(2)}) collective-permute-start(f32[200,256]{1,0:T(8,128)S(1)} %shard_map.129.own_ref), channel_id=1, source_target_pairs={{0,8},{4,12},{8,0},{12,4},{16,80},{20,84},{24,88},{28,92},{32,40},... | collective-permute-start | bytes 614408 | tf_op jit(solution)/shard_map/ppermute | solution.py:372
  83.1 0.9 collective-permute-start.19
  84.1 1.7 %collective-permute-start.18 = (f32[200,256]{1,0:T(8,128)S(1)}, f32[200,256]{1,0:T(8,128)S(1)}, u32[]{:S(2)}, u32[]{:S(2)}) collective-permute-start(f32[200,256]{1,0:T(8,128)S(1)} %shard_map.129.own_ref), channel_id=1, source_target_pairs={{0,12},{4,0},{8,4},{12,8},{16,112},{20,116},{24,120},{28,124},{32,... | collective-permute-start | bytes 614408 | tf_op jit(solution)/shard_map/ppermute | solution.py:372
  85.8 0.2 fusion.refs_0_
  86.1 2.2 %collective-permute-done.20.far_ref = f32[200,256]{1,0:T(8,128)S(1)} collective-permute-done((f32[200,256]{1,0:T(8,128)S(1)}, f32[200,256]{1,0:T(8,128)S(1)}, u32[]{:S(2)}, u32[]{:S(2)}) %collective-permute-start.20) | collective-permute-done | bytes 204832 | tf_op jit(solution)/shard_map/ppermute | solution.py:372
  88.2 2.0 %collective-permute-done.19.back_ref = f32[200,256]{1,0:T(8,128)S(1)} collective-permute-done((f32[200,256]{1,0:T(8,128)S(1)}, f32[200,256]{1,0:T(8,128)S(1)}, u32[]{:S(2)}, u32[]{:S(2)}) %collective-permute-start.19) | collective-permute-done | bytes 204832 | tf_op jit(solution)/shard_map/ppermute | solution.py:372
  90.2 0.6 shard_map.130.refs_0_
  90.8 9.1 %collective-permute-start.24 = (f32[800,256]{1,0:T(8,128)S(1)}, f32[800,256]{1,0:T(8,128)S(1)}, u32[]{:S(2)}, u32[]{:S(2)}) collective-permute-start(f32[800,256]{1,0:T(8,128)S(1)} %shard_map.130.refs_0_), channel_id=1, source_target_pairs={{0,64},{4,68},{8,72},{12,76},{16,24},{20,28},{24,16},{28,20},{32,9... | collective-permute-start | bytes 2457608 | tf_op jit(solution)/shard_map/ppermute | solution.py:372
  99.9 8.8 %collective-permute-start.23 = (f32[800,256]{1,0:T(8,128)S(1)}, f32[800,256]{1,0:T(8,128)S(1)}, u32[]{:S(2)}, u32[]{:S(2)}) collective-permute-start(f32[800,256]{1,0:T(8,128)S(1)} %shard_map.130.refs_0_), channel_id=1, source_target_pairs={{0,16},{16,0},{32,48},{48,32},{64,80},{80,64},{96,112},{112,96},{1... | collective-permute-start | bytes 2457608 | tf_op jit(solution)/shard_map/ppermute | solution.py:377
  108.7 3.4 %collective-permute-start.21 = (f32[800,256]{1,0:T(8,128)S(1)}, f32[800,256]{1,0:T(8,128)S(1)}, u32[]{:S(2)}, u32[]{:S(2)}) collective-permute-start(f32[800,256]{1,0:T(8,128)S(1)} %shard_map.130.refs_0_), channel_id=1, source_target_pairs={{0,96},{4,100},{8,104},{12,108},{16,28},{20,16},{24,20},{28,24},{3... | collective-permute-start | bytes 2457608 | tf_op jit(solution)/shard_map/ppermute | solution.py:372
  112.1 1.7 %shard_map.131 = (f32[3,2048,256]{2,1,0:T(8,128)}, f32[800,256]{1,0:T(8,128)S(1)}) custom-call(s32[5]{0:T(128)S(1)} %stack.23.pos_ref, f32[800,256]{1,0:T(8,128)S(1)} %shard_map.130.refs_0_, f32[800,256]{1,0:T(8,128)S(1)} %collective-permute-done.23.refs_1_.refs_4_, f32[800,256]{1,0:T(8,128)S(1)} %collective-permute-done.24.refs_2_), custom_call_target="tpu_custom_call", output_to_operand_aliasing={{1}: (3, {})} | custom-call | tf_op jit(solution)/shard_map/pallas_call | solution.py:516
  113.8 10.6 %collective-permute-start.27 = (f32[800,256]{1,0:T(8,128)S(1)}, f32[800,256]{1,0:T(8,128)S(1)}, u32[]{:S(2)}, u32[]{:S(2)}) collective-permute-start(f32[800,256]{1,0:T(8,128)S(1)} %get-tuple-element.91.refs_2_.refs_3_), channel_id=1, source_target_pairs={{0,16},{16,0},{32,48},{48,32},{64,80},{80,64},{96,112},{112,96},{1... | collective-permute-start | bytes 2457608 | tf_op jit(solution)/shard_map/ppermute | solution.py:377
  124.4 6.7 %collective-permute-start.26 = (f32[800,256]{1,0:T(8,128)S(1)}, f32[800,256]{1,0:T(8,128)S(1)}, u32[]{:S(2)}, u32[]{:S(2)}) collective-permute-start(f32[800,256]{1,0:T(8,128)S(1)} %collective-permute-done.22.refs_1_.refs_2_), channel_id=1, source_target_pairs={{0,16},{16,0},{32,48},{48,32},{64,80},{80,64},{96,112},{112,96},{1... | collective-permute-start | bytes 2457608 | tf_op jit(solution)/shard_map/ppermute | solution.py:377
  131.1 2.3 %shard_map.132.refs_8_ = f32[3,2048,256]{2,1,0:T(8,128)} custom-call(s32[5]{0:T(128)S(1)} %stack.23.pos_ref, f32[800,256]{1,0:T(8,128)S(1)} %collective-permute-done.21.refs_0_.refs_1_, f32[800,256]{1,0:T(8,128)S(1)} %collective-permute-done.22.refs_1_.refs_2_, f32[800,256]{1,0:T(8,128)S(1)} %get-tuple-element.91.refs_2_.refs_3_, ...), custom_call_target="tpu_custom_call", output_to_operand_aliasing={{}: (5, {})} | custom-call | tf_op jit(solution)/shard_map/pallas_call | solution.py:516
  133.4 0.8 collective-permute-done.25.refs_5_
  134.2 2.4 %shard_map.133 = (f32[3,2048,256]{2,1,0:T(8,128)}, f32[2,128,128]{2,1,0:T(8,128)}, f32[2,128]{1,0:T(2,128)}, f32[2]{0:T(128)}) custom-call(s32[5]{0:T(128)S(1)} %stack.23.pos_ref, f32[800,256]{1,0:T(8,128)S(1)} %shard_map.130.refs_0_, f32[800,256]{1,0:T(8,128)S(1)} %collective-permute-done.21.refs_0_.refs_1_, ...), custom_call_target="tpu_custom_call", output_to_operand_aliasing={{0}: (9, {})} | custom-call | tf_op jit(solution)/shard_map/pallas_call | solution.py:532
  (40 shorter events, 1.0 us)
Async XLA Ops:
  0.6 11.9 %copy-start.4 = (f32[1,2,256]{2,1,0:T(2,128)S(1)}, f32[1,2,256]{2,1,0:T(2,128)}, u32[]{:S(2)}) copy-start(f32[1,2,256]{2,1,0:T(2,128)} %gate_ref.7) | copy-start | bytes 6148
  0.6 11.9 %copy-start.5 = (f32[2]{0:T(128)S(1)}, f32[2]{0:T(128)}, u32[]{:S(2)}) copy-start(f32[2]{0:T(128)} %base_ref.7) | copy-start | bytes 28
  0.8 17.7 %copy-start.2 = (f32[2,128,128]{2,1,0:T(8,128)S(1)}, f32[2,128,128]{2,1,0:T(8,128)}, u32[]{:S(2)}) copy-start(f32[2,128,128]{2,1,0:T(8,128)} %init_ref.3) | copy-start | bytes 393220
  0.8 17.7 %copy-start.3 = (bf16[1,256,256]{2,1,0:T(8,128)(2,1)S(1)}, bf16[1,256,256]{2,1,0:T(8,128)(2,1)}, u32[]{:S(2)}) copy-start(bf16[1,256,256]{2,1,0:T(8,128)(2,1)} %up_ref.3) | copy-start | bytes 393220
  0.8 17.7 %copy-start.6 = (f32[2,128]{1,0:T(2,128)S(1)}, f32[2,128]{1,0:T(2,128)}, u32[]{:S(2)}) copy-start(f32[2,128]{1,0:T(2,128)} %gain_ref.1) | copy-start | bytes 3076
  6.5 11.7 %collective-permute-start.4 = (f32[256,1024]{1,0:T(8,128)S(1)}, f32[256,1024]{1,0:T(8,128)S(1)}, u32[]{:S(2)}, u32[]{:S(2)}) collective-permute-start(f32[256,1024]{1,0:T(8,128)S(1)} %get-tuple-element.60), channel_id=1, source_target_pairs={{0,16},{16,0},{32,48},{48,32},{64,80},{80,64},{96,112},{112,96},{1... | collective-permute-start | bytes 3145736 | tf_op jit(solution)/shard_map/ppermute | solution.py:377
  8.0 8.5 %collective-permute-start = (f32[2,128,128]{2,1,0:T(8,128)S(1)}, f32[2,128,128]{2,1,0:T(8,128)S(1)}, u32[]{:S(2)}, u32[]{:S(2)}) collective-permute-start(f32[2,128,128]{2,1,0:T(8,128)S(1)} %get-tuple-element.52), channel_id=1, source_target_pairs={{0,4},{8,12},{1,5},{9,13},{2,6},{10,14},{3,7},{11,15},{16,20},{24,... | collective-permute-start | bytes 393224 | tf_op jit(solution)/shard_map/ppermute | solution.py:449
  11.3 7.1 %collective-permute-start.3 = (f32[2,128,128]{2,1,0:T(8,128)S(1)}, f32[2,128,128]{2,1,0:T(8,128)S(1)}, u32[]{:S(2)}, u32[]{:S(2)}) collective-permute-start(f32[2,128,128]{2,1,0:T(8,128)S(1)} %get-tuple-element.53.d_ref), channel_id=1, source_target_pairs={{8,12},{4,0},{9,13},{5,1},{10,14},{6,2},{11,15},{7,3},{24,28},{20,... | collective-permute-start | bytes 393224 | tf_op jit(solution)/shard_map/ppermute | solution.py:450
  16.5 28.9 %copy-start = (bf16[3,2048,256]{2,1,0:T(8,128)(2,1)S(1)}, bf16[3,2048,256]{2,1,0:T(8,128)(2,1)}, u32[]{:S(2)}) copy-start(bf16[3,2048,256]{2,1,0:T(8,128)(2,1)} %w_ref.1) | copy-start | bytes 9437188
  16.7 1.7 %collective-permute-start.2 = (f32[2,128,128]{2,1,0:T(8,128)S(1)}, f32[2,128,128]{2,1,0:T(8,128)S(1)}, u32[]{:S(2)}, u32[]{:S(2)}) collective-permute-start(f32[2,128,128]{2,1,0:T(8,128)S(1)} %shard_map.120), channel_id=1, source_target_pairs={{4,12},{5,13},{6,14},{7,15},{20,28},{21,29},{22,30},{23,31},{36,44... | collective-permute-start | bytes 393224 | tf_op jit(solution)/shard_map/ppermute | solution.py:466
  17.5 0.9 collective-permute-start.1
  20.6 9.0 %collective-permute-start.5 = (f32[2,128,128]{2,1,0:T(8,128)S(1)}, f32[2,128,128]{2,1,0:T(8,128)S(1)}, u32[]{:S(2)}, u32[]{:S(2)}) collective-permute-start(f32[2,128,128]{2,1,0:T(8,128)S(1)} %get-tuple-element.61.o_ref.p_ref), channel_id=1, source_target_pairs={{12,8},{4,0},{13,9},{5,1},{14,10},{6,2},{15,11},{7,3},{28,24},{20,... | collective-permute-start | bytes 393224 | tf_op jit(solution)/shard_map/ppermute | solution.py:473
  29.9 7.9 %collective-permute-start.7 = (f32[2,128,128]{2,1,0:T(8,128)S(1)}, f32[2,128,128]{2,1,0:T(8,128)S(1)}, u32[]{:S(2)}, u32[]{:S(2)}) collective-permute-start(f32[2,128,128]{2,1,0:T(8,128)S(1)} %shard_map.124), channel_id=1, source_target_pairs={{8,0},{9,1},{10,2},{11,3},{24,16},{25,17},{26,18},{27,19},{40,32},... | collective-permute-start | bytes 393224 | tf_op jit(solution)/shard_map/ppermute | solution.py:483
  31.2 6.6 %collective-permute-start.6 = (f32[2,128,128]{2,1,0:T(8,128)S(1)}, f32[2,128,128]{2,1,0:T(8,128)S(1)}, u32[]{:S(2)}, u32[]{:S(2)}) collective-permute-start(f32[2,128,128]{2,1,0:T(8,128)S(1)} %shard_map.124), channel_id=1, source_target_pairs={{8,4},{9,5},{10,6},{11,7},{24,20},{25,21},{26,22},{27,23},{40,36},... | collective-permute-start | bytes 393224 | tf_op jit(solution)/shard_map/ppermute | solution.py:482
  41.1 7.7 %collective-permute-start.11 = (f32[1024,256]{1,0:T(8,128)S(1)}, f32[1024,256]{1,0:T(8,128)S(1)}, u32[]{:S(2)}, u32[]{:S(2)}) collective-permute-start(f32[1024,256]{1,0:T(8,128)S(1)} %get-tuple-element.77.all_ref.own_ref), channel_id=1, source_target_pairs={{0,16},{16,0},{32,48},{48,32},{64,80},{80,64},{96,112},{112,96},{1... | collective-permute-start | bytes 3145736 | tf_op jit(solution)/shard_map/ppermute | solution.py:377
  46.9 16.3 %collective-permute-start.9 = (f32[256,512]{1,0:T(8,128)S(1)}, f32[256,512]{1,0:T(8,128)S(1)}, u32[]{:S(2)}, u32[]{:S(2)}) collective-permute-start(f32[256,512]{1,0:T(8,128)S(1)} %get-tuple-element.80), channel_id=1, source_target_pairs={{0,1},{1,2},{2,3},{3,0},{4,5},{5,6},{6,7},{7,4},{8,9},{9,10},{10,1... | collective-permute-start | bytes 1572872 | tf_op jit(solution)/shard_map/ppermute | solution.py:497
  50.4 21.5 %collective-permute-start.12 = (f32[800,256]{1,0:T(8,128)S(1)}, f32[800,256]{1,0:T(8,128)S(1)}, u32[]{:S(2)}, u32[]{:S(2)}) collective-permute-start(f32[800,256]{1,0:T(8,128)S(1)} %get-tuple-element.84), channel_id=1, source_target_pairs={{0,32},{4,36},{8,40},{12,44},{16,20},{20,24},{24,28},{28,16},{32,6... | collective-permute-start | bytes 2457608 | tf_op jit(solution)/shard_map/ppermute | solution.py:372
  51.4 20.5 %collective-permute-start.13 = (f32[800,256]{1,0:T(8,128)S(1)}, f32[800,256]{1,0:T(8,128)S(1)}, u32[]{:S(2)}, u32[]{:S(2)}) collective-permute-start(f32[800,256]{1,0:T(8,128)S(1)} %get-tuple-element.85), channel_id=1, source_target_pairs={{0,96},{4,100},{8,104},{12,108},{16,28},{20,16},{24,20},{28,24},{3... | collective-permute-start | bytes 2457608 | tf_op jit(solution)/shard_map/ppermute | solution.py:372
  53.1 18.8 %collective-permute-start.14 = (f32[800,256]{1,0:T(8,128)S(1)}, f32[800,256]{1,0:T(8,128)S(1)}, u32[]{:S(2)}, u32[]{:S(2)}) collective-permute-start(f32[800,256]{1,0:T(8,128)S(1)} %get-tuple-element.86), channel_id=1, source_target_pairs={{0,64},{4,68},{8,72},{12,76},{16,24},{20,28},{24,16},{28,20},{32,9... | collective-permute-start | bytes 2457608 | tf_op jit(solution)/shard_map/ppermute | solution.py:372
  53.3 11.3 %collective-permute-start.10 = (f32[256,512]{1,0:T(8,128)S(1)}, f32[256,512]{1,0:T(8,128)S(1)}, u32[]{:S(2)}, u32[]{:S(2)}) collective-permute-start(f32[256,512]{1,0:T(8,128)S(1)} %get-tuple-element.81), channel_id=1, source_target_pairs={{0,3},{1,0},{2,1},{3,2},{4,7},{5,4},{6,5},{7,6},{8,11},{9,8},{10,9... | collective-permute-start | bytes 1572872 | tf_op jit(solution)/shard_map/ppermute | solution.py:497
  63.3 22.6 %collective-permute-start.8 = (f32[256,512]{1,0:T(8,128)S(1)}, f32[256,512]{1,0:T(8,128)S(1)}, u32[]{:S(2)}, u32[]{:S(2)}) collective-permute-start(f32[256,512]{1,0:T(8,128)S(1)} %get-tuple-element.79), channel_id=1, source_target_pairs={{0,2},{1,3},{2,0},{3,1},{4,6},{5,7},{6,4},{7,5},{8,10},{9,11},{10,... | collective-permute-start | bytes 1572872 | tf_op jit(solution)/shard_map/ppermute | solution.py:497
  72.6 6.1 %collective-permute-start.15 = (f32[200,256]{1,0:T(8,128)S(1)}, f32[200,256]{1,0:T(8,128)S(1)}, u32[]{:S(2)}, u32[]{:S(2)}) collective-permute-start(f32[200,256]{1,0:T(8,128)S(1)} %get-tuple-element.88), channel_id=1, source_target_pairs={{0,4},{4,8},{8,12},{12,0},{16,48},{20,52},{24,56},{28,60},{32,36},... | collective-permute-start | bytes 614408 | tf_op jit(solution)/shard_map/ppermute | solution.py:372
  73.9 4.8 %collective-permute-start.16 = (f32[200,256]{1,0:T(8,128)S(1)}, f32[200,256]{1,0:T(8,128)S(1)}, u32[]{:S(2)}, u32[]{:S(2)}) collective-permute-start(f32[200,256]{1,0:T(8,128)S(1)} %get-tuple-element.89), channel_id=1, source_target_pairs={{0,12},{4,0},{8,4},{12,8},{16,112},{20,116},{24,120},{28,124},{32,... | collective-permute-start | bytes 614408 | tf_op jit(solution)/shard_map/ppermute | solution.py:372
  75.4 6.3 %collective-permute-start.17 = (f32[200,256]{1,0:T(8,128)S(1)}, f32[200,256]{1,0:T(8,128)S(1)}, u32[]{:S(2)}, u32[]{:S(2)}) collective-permute-start(f32[200,256]{1,0:T(8,128)S(1)} %get-tuple-element.90), channel_id=1, source_target_pairs={{0,8},{4,12},{8,0},{12,4},{16,80},{20,84},{24,88},{28,92},{32,40},... | collective-permute-start | bytes 614408 | tf_op jit(solution)/shard_map/ppermute | solution.py:372
  81.7 6.5 %collective-permute-start.20 = (f32[200,256]{1,0:T(8,128)S(1)}, f32[200,256]{1,0:T(8,128)S(1)}, u32[]{:S(2)}, u32[]{:S(2)}) collective-permute-start(f32[200,256]{1,0:T(8,128)S(1)} %shard_map.129.own_ref), channel_id=1, source_target_pairs={{0,8},{4,12},{8,0},{12,4},{16,80},{20,84},{24,88},{28,92},{32,40},... | collective-permute-start | bytes 614408 | tf_op jit(solution)/shard_map/ppermute | solution.py:372
  83.1 7.0 %collective-permute-start.19 = (f32[200,256]{1,0:T(8,128)S(1)}, f32[200,256]{1,0:T(8,128)S(1)}, u32[]{:S(2)}, u32[]{:S(2)}) collective-permute-start(f32[200,256]{1,0:T(8,128)S(1)} %shard_map.129.own_ref), channel_id=1, source_target_pairs={{0,4},{4,8},{8,12},{12,0},{16,48},{20,52},{24,56},{28,60},{32,36},... | collective-permute-start | bytes 614408 | tf_op jit(solution)/shard_map/ppermute | solution.py:372
  84.1 6.1 %collective-permute-start.18 = (f32[200,256]{1,0:T(8,128)S(1)}, f32[200,256]{1,0:T(8,128)S(1)}, u32[]{:S(2)}, u32[]{:S(2)}) collective-permute-start(f32[200,256]{1,0:T(8,128)S(1)} %shard_map.129.own_ref), channel_id=1, source_target_pairs={{0,12},{4,0},{8,4},{12,8},{16,112},{20,116},{24,120},{28,124},{32,... | collective-permute-start | bytes 614408 | tf_op jit(solution)/shard_map/ppermute | solution.py:372
  86.1 47.4 %copy-start.1 = (bf16[1,256,512]{2,1,0:T(8,128)(2,1)}, bf16[1,256,512]{2,1,0:T(8,128)(2,1)S(1)}, u32[]{:S(2)}) copy-start(bf16[1,256,512]{2,1,0:T(8,128)(2,1)S(1)} %fusion.refs_0_) | copy-start | bytes 786436
  90.8 21.3 %collective-permute-start.24 = (f32[800,256]{1,0:T(8,128)S(1)}, f32[800,256]{1,0:T(8,128)S(1)}, u32[]{:S(2)}, u32[]{:S(2)}) collective-permute-start(f32[800,256]{1,0:T(8,128)S(1)} %shard_map.130.refs_0_), channel_id=1, source_target_pairs={{0,64},{4,68},{8,72},{12,76},{16,24},{20,28},{24,16},{28,20},{32,9... | collective-permute-start | bytes 2457608 | tf_op jit(solution)/shard_map/ppermute | solution.py:372
  99.9 12.2 %collective-permute-start.23 = (f32[800,256]{1,0:T(8,128)S(1)}, f32[800,256]{1,0:T(8,128)S(1)}, u32[]{:S(2)}, u32[]{:S(2)}) collective-permute-start(f32[800,256]{1,0:T(8,128)S(1)} %shard_map.130.refs_0_), channel_id=1, source_target_pairs={{0,16},{16,0},{32,48},{48,32},{64,80},{80,64},{96,112},{112,96},{1... | collective-permute-start | bytes 2457608 | tf_op jit(solution)/shard_map/ppermute | solution.py:377
  108.7 15.7 %collective-permute-start.22 = (f32[800,256]{1,0:T(8,128)S(1)}, f32[800,256]{1,0:T(8,128)S(1)}, u32[]{:S(2)}, u32[]{:S(2)}) collective-permute-start(f32[800,256]{1,0:T(8,128)S(1)} %shard_map.130.refs_0_), channel_id=1, source_target_pairs={{0,32},{4,36},{8,40},{12,44},{16,20},{20,24},{24,28},{28,16},{32,6... | collective-permute-start | bytes 2457608 | tf_op jit(solution)/shard_map/ppermute | solution.py:372
  108.7 22.4 %collective-permute-start.21 = (f32[800,256]{1,0:T(8,128)S(1)}, f32[800,256]{1,0:T(8,128)S(1)}, u32[]{:S(2)}, u32[]{:S(2)}) collective-permute-start(f32[800,256]{1,0:T(8,128)S(1)} %shard_map.130.refs_0_), channel_id=1, source_target_pairs={{0,96},{4,100},{8,104},{12,108},{16,28},{20,16},{24,20},{28,24},{3... | collective-permute-start | bytes 2457608 | tf_op jit(solution)/shard_map/ppermute | solution.py:372
  113.8 17.3 %collective-permute-start.27 = (f32[800,256]{1,0:T(8,128)S(1)}, f32[800,256]{1,0:T(8,128)S(1)}, u32[]{:S(2)}, u32[]{:S(2)}) collective-permute-start(f32[800,256]{1,0:T(8,128)S(1)} %get-tuple-element.91.refs_2_.refs_3_), channel_id=1, source_target_pairs={{0,16},{16,0},{32,48},{48,32},{64,80},{80,64},{96,112},{112,96},{1... | collective-permute-start | bytes 2457608 | tf_op jit(solution)/shard_map/ppermute | solution.py:377
  124.4 9.1 %collective-permute-start.26 = (f32[800,256]{1,0:T(8,128)S(1)}, f32[800,256]{1,0:T(8,128)S(1)}, u32[]{:S(2)}, u32[]{:S(2)}) collective-permute-start(f32[800,256]{1,0:T(8,128)S(1)} %collective-permute-done.22.refs_1_.refs_2_), channel_id=1, source_target_pairs={{0,16},{16,0},{32,48},{48,32},{64,80},{80,64},{96,112},{112,96},{1... | collective-permute-start | bytes 2457608 | tf_op jit(solution)/shard_map/ppermute | solution.py:377
  131.1 3.1 %collective-permute-start.25 = (f32[800,256]{1,0:T(8,128)S(1)}, f32[800,256]{1,0:T(8,128)S(1)}, u32[]{:S(2)}, u32[]{:S(2)}) collective-permute-start(f32[800,256]{1,0:T(8,128)S(1)} %collective-permute-done.21.refs_0_.refs_1_), channel_id=1, source_target_pairs={{0,16},{16,0},{32,48},{48,32},{64,80},{80,64},{96,112},{112,96},{1... | collective-permute-start | bytes 2457608 | tf_op jit(solution)/shard_map/ppermute | solution.py:377

commit v6 on v5

--- a/solution.py
+++ b/solution.py
@@ -148,10 +148,10 @@
         zv_ref[:, span(h)] = dot(mix, rv, NN, 3)
 
 
-def step_kernel(d_ref, w_ref, o_ref, after_ref, out_ref, *, transposed):
+def step_kernel(d_ref, w_ref, o_ref, after_ref, out_ref):
     del after_ref
     for h in range(d_ref.shape[0]):
-        out_ref[h] = o_ref[h] + dot(d_ref[h], w_ref[h], TN if transposed else NN, 3)
+        out_ref[h] = o_ref[h] + dot(d_ref[h], w_ref[h], NN, 3)
 
 
 def norm_kernel(
@@ -209,7 +209,7 @@
 
 
 def keys_kernel(
-    pos_ref, base_ref, gate_ref, rp_ref, mid_ref, far_ref, rd_ref, p_ref, d_ref, w_ref, k_ref, ninv_ref,
+    pos_ref, base_ref, gate_ref, one_ref, two_ref, three_ref, rd_ref, rd_one_ref, rd_two_ref, p_ref, d_ref, w_ref, k_ref, ninv_ref,
     gram_ref, bt_ref, r_ref, x_ref, dk_ref, de_ref, dgain_ref, dq_ref,
     all_ref, gates_ref,
 ):
@@ -220,10 +220,8 @@
     all_ref[0:n, :] = dq_ref[...]
     all_ref[3 * n + HS : 3 * n + EXTRA, :] = jnp.zeros((EXTRA - HS, all_ref.shape[1]), F32)
     for h in range(w_ref.shape[0]):
-        first = rp_ref[h] + dot(rd_ref[h], far_ref[h], TN, 3)
-        end = jnp.where(
-            ctx == 0, first, jnp.where(ctx == 1, mid_ref[h], jnp.where(ctx == 2, rp_ref[h], 0.0))
-        )
+        step = jnp.where(ctx == 0, rd_ref[h], rd_one_ref[h])
+        end = one_ref[h] + dot(step, two_ref[h] + dot(rd_two_ref[h], three_ref[h], TN, 3), TN, 3)
         all_ref[3 * n : 3 * n + HS, span(h)] = jnp.where(ctx == 0, p_ref[h] + dot(d_ref[h], end, TN, 3), 0.0)
         w = w_ref[h]
         k = k_ref[:, span(h)]
@@ -255,7 +253,8 @@
     out_ref[...] = other_ref[...].T.astype(BF)
 
 
-def product_kernel(pos_ref, tokt_ref, other_tokt_ref, own_ref, other_ref, *out_refs):
+def product_kernel(pos_ref, tokt_ref, other_tokt_ref, own_ref, other_ref, *refs):
+    out_refs = refs[2 : 2 + RING]
     n = tokt_ref.shape[1]
     for turn, out_ref in zip(TURNS, out_refs):
         at = (pos_ref[1] + turn) & (RING - 1)
@@ -294,7 +293,7 @@
 
 
 def split_kernel(pos_ref, own_ref, back_ref, ahead_ref, far_ref, *refs):
-    for turn, out_ref in zip(TURNS, refs[-RING:]):
+    for turn, out_ref in zip(TURNS, refs[3 : 3 + RING]):
         for rows, to in slice_rows(pos_ref, turn):
             out_ref[to, :] = (own_ref[rows, :] + far_ref[rows, :]) + (back_ref[rows, :] + ahead_ref[rows, :])
 
@@ -394,12 +393,13 @@
     return pltpu.with_memory_space_constraint(value, pltpu.HBM)
 
 
-def whole(kernel, outs, specs):
+def whole(kernel, outs, specs, aliases=None):
     return pl.pallas_call(
         kernel,
         out_shape=outs,
         in_specs=specs,
         out_specs=tuple(VM for _ in outs) if isinstance(outs, tuple) else VM,
+        input_output_aliases=aliases or {},
         compiler_params=PARAMS,
     )
 
@@ -448,6 +448,8 @@
 
     near = lax.ppermute(send, "ctx", [(0, 1), (2, 3)])
     moved = lax.ppermute(decay, "ctx", [(2, 3), (1, 0)])
+    moved_one = lax.ppermute(decay, "ctx", [(2, 1)])
+    moved_two = lax.ppermute(decay, "ctx", [(2, 0)])
     got_half = swap(other_half)
 
     q, score, rv, y, qt, zv, tokt = pl.pallas_call(
@@ -459,7 +461,7 @@
         compiler_params=PARAMS,
     )(pos, base_rates, tokens, proj_weights, gate_values, k, v, inv)
 
-    second = whole(functools.partial(step_kernel, transposed=False), small, [VM] * 3 + [anywhere])(
+    second = whole(step_kernel, small, [VM] * 3 + [anywhere])(
         decay, near, offset, qt
     )
     mid = lax.ppermute(second, "ctx", [(1, 2)])
@@ -470,39 +472,39 @@
         norm_kernel, (small, wide_f32, small, vmem(heads, HS)), [SM] + [VM] * 9 + [anywhere]
     )(pos, init_weight, near, mid, far, moved, qt, zv, cotangent, out_gain, other_tokt)
 
-    back_near = lax.ppermute(pulled, "ctx", [(3, 2), (1, 0)])
+    back_one = lax.ppermute(pulled, "ctx", [(3, 2), (2, 1), (1, 0)])
+    back_two = lax.ppermute(pulled, "ctx", [(3, 1), (2, 0)])
+    back_three = lax.ppermute(pulled, "ctx", [(3, 0)])
 
     dq, r, x, dk, de = whole(
         query_kernel, (wide_f32, wide_f32, wide_f32, wide_f32, vmem(heads, n)), [SM] + [VM] * 10
     )(base_rates, gate_values, w, back, cotangent, q, score, rv, y, k, inv)
 
-    back_second = whole(functools.partial(step_kernel, transposed=True), small, [VM] * 3 + [anywhere])(
-        decay, back_near, pulled, de
-    )
-    back_mid = lax.ppermute(back_second, "ctx", [(2, 1)])
-    back_far = lax.ppermute(back_second, "ctx", [(2, 0)])
-
     grads, grad_gates = whole(
-        keys_kernel, (vmem(3 * n + EXTRA, wide), shape(1, heads, n)), [SM, SM] + [VM] * 18
-    )(pos, base_rates, gate_values, back_near, back_mid, back_far, moved, pulled, decay, w, k, ninv, gram, bt, r, x,
+        keys_kernel, (vmem(3 * n + EXTRA, wide), shape(1, heads, n)), [SM, SM] + [VM] * 20
+    )(pos, base_rates, gate_values, back_one, back_two, back_three, moved, moved_one, moved_two, pulled, decay, w, k, ninv, gram, bt, r, x,
       dk, de, dgain, dq)
 
     chunk = vmem(3 * CHUNK + PIECE, wide)
-    own, *away = whole(product_kernel, (chunk,) * RING, [SM] + [VM] * 4)(
-        pos, tokt, other_tokt, grads, swap(grads)
-    )
-    away = round_turn(away, True)
-    quarters = whole(token_kernel, (vmem(n, model // RING),) * RING, [SM, VM, VM])(pos, raw_weights, grads)
-    from_back, from_ahead, from_far = [
-        lax.ppermute(terms, "head", [(i, (i + turn) % RING) for i in range(RING)])
-        for terms, turn in zip(quarters[1:], TURNS[1:])
-    ]
+    quarter = vmem(n, model // RING)
+    quarters = whole(token_kernel, (quarter,) * RING, [SM, VM, VM])(pos, raw_weights, grads)
+
+    def along_head(terms, turn):
+        return lax.ppermute(terms, "head", [(i, (i + turn) % RING) for i in range(RING)])
+
+    *chunks, near_one, near_two = whole(
+        product_kernel, (chunk,) * RING + (quarter,) * 2, [SM] + [VM] * 6, {5: RING, 6: RING + 1}
+    )(pos, tokt, other_tokt, grads, swap(grads), quarters[1], quarters[2])
+    own, away = chunks[0], round_turn(chunks[1:], True)
+    from_back, from_ahead = along_head(near_one, 1), along_head(near_two, 3)
+
+    piece = vmem(3 * SLICE + PIECE // RING, wide)
+    *pieces, far_quarter = whole(
+        split_kernel, (piece,) * RING + (quarter,), [SM] + [VM] * 5 + [anywhere] * 2, {5: RING}
+    )(pos, own, *away, quarters[3], from_back, from_ahead)
+    from_far = along_head(far_quarter, 2)
     grad_tokens = ((quarters[0] + from_far) + (from_back + from_ahead)).astype(BF).reshape(1, n, -1)
-
-    piece = vmem(3 * SLICE + PIECE // RING, wide)
-    own, *away = whole(split_kernel, (piece,) * RING, [SM] + [VM] * 4 + [anywhere] * 2)(
-        pos, own, *away, from_back, from_ahead
-    )
+    own, away = pieces[0], pieces[1:]
     part_sum = whole(sum_kernel, piece, [VM] * 4)(own, *round_turn(away, False))
     from_back, from_ahead, from_far = round_turn([part_sum] * 3, False)
     total = whole(join_kernel, chunk, [SM] + [VM] * 4 + [anywhere])(

time: 137 us -> 122 us (0.89)
  starting transfers between devices: 70.4 us -> 54.7 us
    ppermute x6, starting transfers between devices: 31.8 us -> 18 us  [swap(): return lax.ppermute(value, 'dp', [(i, i ^ 1) for i in range(2 * RING)])]
    ppermute x12, starting transfers between devices: 23.8 us -> 17.4 us  [round_turn(): lax.ppermute(chunk, ('dp', 'ctx'), moves(first, turn))]
    ppermute x6 -> x8, starting transfers between devices: 8.83 us -> 13.3 us  [the longest x3 7.44 us: along_head(): lax.ppermute(terms, 'head', [(i, (i + turn) % RING) for i in range(RING)])]
    ppermute x6 -> x8, waiting for transfers between devices: 18.4 us -> 15.5 us  [the longest x3 11.7 us: along_head(): lax.ppermute(terms, 'head', [(i, (i + turn) % RING) for i in range(RING)])]
    ppermute x12, waiting for transfers between devices: 16.3 us -> 19.1 us  [round_turn(): lax.ppermute(chunk, ('dp', 'ctx'), moves(first, turn))]
    pallas_call x5 -> x4, Pallas kernels: 4.21 us -> 3.97 us  [the longest x1 1.55 us: body(): whole(token_kernel, (quarter,) * RING, [SM, VM, VM])]
  transfers between devices with their start and end apart: 28 -> 30, of which waited for: 10 -> 13; matrix products, arithmetic and copies ran while one was open for 0% -> 0% of each run, Pallas kernels for 11% -> 12%
where the time goes in v6:
time: 122 us
  starting transfers between devices  54.7 us (45%)
  waiting for transfers between devices  36.1 us (30%)
  Pallas kernels  29.5 us (24%)
    ppermute x12, waiting for transfers between devices, round_turn(): lax.ppermute(chunk, ('dp', 'ctx'), moves(first, turn))  19.1 us
    ppermute x6, starting transfers between devices, swap(): return lax.ppermute(value, 'dp', [(i, i ^ 1) for i in range(2 * RING)])  18 us
    ppermute x12, starting transfers between devices, round_turn(): lax.ppermute(chunk, ('dp', 'ctx'), moves(first, turn))  17.4 us
    ppermute x3, waiting for transfers between devices, along_head(): lax.ppermute(terms, 'head', [(i, (i + turn) % RING) for i in range(RING)])  11.7 us
    ppermute x3, starting transfers between devices, along_head(): lax.ppermute(terms, 'head', [(i, (i + turn) % RING) for i in range(RING)])  7.44 us
    pallas_call x1, Pallas kernels, body(): pl.pallas_call(maps_kernel, grid=(1,), out_shape=(wide_f32, wide_f32, vme...  5.71 us
    pallas_call x2, Pallas kernels, place(): pl.pallas_call(functools.partial(place_kernel, which=which), out_shape=(o...  4.03 us
    pallas_call x1, Pallas kernels, body(): pl.pallas_call(reach_kernel, grid=(1,), out_shape=(wide_f32, square, wide...  3.89 us
  transfers between devices with their start and end apart: 30, of which 13 were waited for; matrix products, arithmetic and copies ran while one was open for 0% of the time, Pallas kernels for 12%

profile of v6, /device:TPU:1, one launch (start us, length us, event | category | flops | bytes accessed | tf_op | source)
XLA Modules:
  0.0 121.8 jit_solution(9149591097290626324)
XLA Ops:
  0.8 5.7 %shard_map.118 = (f32[256,256]{1,0:T(8,128)S(1)}, f32[256,256]{1,0:T(8,128)S(1)}, f32[2,256,128]{2,1,0:T(8,128)S(1)}, f32[2,256,256]{2,1,0:T(8,128)S(1)}, f32[2,...) custom-call(s32[5]{0:T(128)S(1)} %stack.23.pos_ref, ...), custom_call_target="tpu_custom_call" | custom-call | tf_op jit(solution)/shard_map/pallas_call | solution.py:437
  6.5 1.5 %collective-permute-start.4 = (f32[256,1024]{1,0:T(8,128)S(1)}, f32[256,1024]{1,0:T(8,128)S(1)}, u32[]{:S(2)}, u32[]{:S(2)}) collective-permute-start(f32[256,1024]{1,0:T(8,128)S(1)} %get-tuple-element.63), channel_id=1, source_target_pairs={{0,16},{16,0},{32,48},{48,32},{64,80},{80,64},{96,112},{112,96},{1... | collective-permute-start | bytes 3145736 | tf_op jit(solution)/shard_map/ppermute | solution.py:376
  8.0 3.3 %collective-permute-start = (f32[2,128,128]{2,1,0:T(8,128)S(1)}, f32[2,128,128]{2,1,0:T(8,128)S(1)}, u32[]{:S(2)}, u32[]{:S(2)}) collective-permute-start(f32[2,128,128]{2,1,0:T(8,128)S(1)} %get-tuple-element.55), channel_id=1, source_target_pairs={{0,4},{8,12},{1,5},{9,13},{2,6},{10,14},{3,7},{11,15},{16,20},{24,... | collective-permute-start | bytes 393224 | tf_op jit(solution)/shard_map/ppermute | solution.py:449
  11.3 1.3 %collective-permute-start.3 = (f32[2,128,128]{2,1,0:T(8,128)S(1)}, f32[2,128,128]{2,1,0:T(8,128)S(1)}, u32[]{:S(2)}, u32[]{:S(2)}) collective-permute-start(f32[2,128,128]{2,1,0:T(8,128)S(1)} %get-tuple-element.56.d_ref), channel_id=1, source_target_pairs={{8,12},{4,0},{9,13},{5,1},{10,14},{6,2},{11,15},{7,3},{24,28},{20,... | collective-permute-start | bytes 393224 | tf_op jit(solution)/shard_map/ppermute | solution.py:450
  12.6 3.9 %shard_map.119 = (f32[256,256]{1,0:T(8,128)S(1)}, f32[2,256,256]{2,1,0:T(8,128)S(1)}, f32[256,256]{1,0:T(8,128)S(1)}, f32[256,256]{1,0:T(8,128)S(1)}, f32[256,25...) custom-call(s32[5]{0:T(128)S(1)} %stack.23.pos_ref, f32[2]{0:T(128)S(1)} %copy-done.5, ...), custom_call_target="tpu_custom_call" | custom-call | tf_op jit(solution)/shard_map/pallas_call | solution.py:455
  16.7 0.8 collective-permute-start.2
  18.2 1.3 %collective-permute-start.9 = (f32[2,128,128]{2,1,0:T(8,128)S(1)}, f32[2,128,128]{2,1,0:T(8,128)S(1)}, u32[]{:S(2)}, u32[]{:S(2)}) collective-permute-start(f32[2,128,128]{2,1,0:T(8,128)S(1)} %get-tuple-element.56.d_ref), channel_id=1, source_target_pairs={{8,0},{9,1},{10,2},{11,3},{24,16},{25,17},{26,18},{27,19},{40,32},... | collective-permute-start | bytes 393224 | tf_op jit(solution)/shard_map/ppermute | solution.py:452
  20.5 2.1 %shard_map.122 = (f32[2,128,128]{2,1,0:T(8,128)S(1)}, f32[256,256]{1,0:T(8,128)S(1)}, f32[2,128,128]{2,1,0:T(8,128)S(1)}, f32[2,128]{1,0:T(2,128)S(1)}) custom-call(s32[5]{0:T(128)S(1)} %stack.23.pos_ref, f32[2,128,128]{2,1,0:T(8,128)S(1)} %copy-done.2, f32[2,128,128]{2,1,0:T(8,128)S(1)} %collective-permute-done.w_ref.near_ref, ...), custom_call_target="tpu_custom_call" | custom-call | tf_op jit(solution)/shard_map/pallas_call | solution.py:471
  22.6 1.3 %collective-permute-start.7 = (f32[2,128,128]{2,1,0:T(8,128)S(1)}, f32[2,128,128]{2,1,0:T(8,128)S(1)}, u32[]{:S(2)}, u32[]{:S(2)}) collective-permute-start(f32[2,128,128]{2,1,0:T(8,128)S(1)} %get-tuple-element.64.p_ref), channel_id=1, source_target_pairs={{12,0},{13,1},{14,2},{15,3},{28,16},{29,17},{30,18},{31,19},{44,32... | collective-permute-start | bytes 393224 | tf_op jit(solution)/shard_map/ppermute | solution.py:477
  23.9 1.3 %collective-permute-start.6 = (f32[2,128,128]{2,1,0:T(8,128)S(1)}, f32[2,128,128]{2,1,0:T(8,128)S(1)}, u32[]{:S(2)}, u32[]{:S(2)}) collective-permute-start(f32[2,128,128]{2,1,0:T(8,128)S(1)} %get-tuple-element.64.p_ref), channel_id=1, source_target_pairs={{12,4},{8,0},{13,5},{9,1},{14,6},{10,2},{15,7},{11,3},{28,20},{24,... | collective-permute-start | bytes 393224 | tf_op jit(solution)/shard_map/ppermute | solution.py:476
  25.2 1.3 %collective-permute-start.5 = (f32[2,128,128]{2,1,0:T(8,128)S(1)}, f32[2,128,128]{2,1,0:T(8,128)S(1)}, u32[]{:S(2)}, u32[]{:S(2)}) collective-permute-start(f32[2,128,128]{2,1,0:T(8,128)S(1)} %get-tuple-element.64.p_ref), channel_id=1, source_target_pairs={{12,8},{8,4},{4,0},{13,9},{9,5},{5,1},{14,10},{10,6},{6,2},{15,11}... | collective-permute-start | bytes 393224 | tf_op jit(solution)/shard_map/ppermute | solution.py:475
  26.5 2.9 %shard_map.123 = (f32[256,256]{1,0:T(8,128)S(1)}, f32[256,256]{1,0:T(8,128)S(1)}, f32[256,256]{1,0:T(8,128)S(1)}, f32[256,256]{1,0:T(8,128)S(1)}, f32[2,256]{1,0:T(2,128)S(1)}) custom-call(f32[2]{0:T(128)S(1)} %copy-done.5, f32[1,2,256]{2,1,0:T(2,128)S(1)} %copy-done.4, f32[2,128,128]{2,1,0:T(8,128)S(1)} %get-tuple-element.65.w_ref, ...), custom_call_target="tpu_custom_call" | custom-call | tf_op jit(solution)/shard_map/pallas_call | solution.py:479
  29.4 1.8 %collective-permute-done.7.three_ref = f32[2,128,128]{2,1,0:T(8,128)S(1)} collective-permute-done((f32[2,128,128]{2,1,0:T(8,128)S(1)}, f32[2,128,128]{2,1,0:T(8,128)S(1)}, u32[]{:S(2)}, u32[]{:S(2)}) %collective-permute-start.7) | collective-permute-done | bytes 131104 | tf_op jit(solution)/shard_map/ppermute | solution.py:477
  31.1 2.0 %collective-permute-done.6.two_ref = f32[2,128,128]{2,1,0:T(8,128)S(1)} collective-permute-done((f32[2,128,128]{2,1,0:T(8,128)S(1)}, f32[2,128,128]{2,1,0:T(8,128)S(1)}, u32[]{:S(2)}, u32[]{:S(2)}) %collective-permute-start.6) | collective-permute-done | bytes 131104 | tf_op jit(solution)/shard_map/ppermute | solution.py:476
  33.2 3.6 %shard_map.124 = (f32[1024,256]{1,0:T(8,128)S(1)}, f32[1,2,256]{2,1,0:T(2,128)}) custom-call(s32[5]{0:T(128)S(1)} %stack.23.pos_ref, f32[2]{0:T(128)S(1)} %copy-done.5, f32[1,2,256]{2,1,0:T(2,128)S(1)} %copy-done.4, f32[2,128,128]{2,1,0:T(8,128)S(1)} %collective-permute-done.5.one_ref, f32[2,128,128]{2,1,0:T(8,128)S(1)} %collective-permute-done.6.two_ref, ...), custom_call_target="tpu_custom_call" | custom-call | tf_op jit(solution)/shard_map/pallas_call | solution.py:483
  36.8 3.4 %collective-permute-start.10 = (f32[1024,256]{1,0:T(8,128)S(1)}, f32[1024,256]{1,0:T(8,128)S(1)}, u32[]{:S(2)}, u32[]{:S(2)}) collective-permute-start(f32[1024,256]{1,0:T(8,128)S(1)} %get-tuple-element.80.all_ref.own_ref), channel_id=1, source_target_pairs={{0,16},{16,0},{32,48},{48,32},{64,80},{80,64},{96,112},{112,96},{1... | collective-permute-start | bytes 3145736 | tf_op jit(solution)/shard_map/ppermute | solution.py:376
  40.2 1.5 %shard_map.125 = (f32[256,512]{1,0:T(8,128)S(1)}, f32[256,512]{1,0:T(8,128)S(1)}, f32[256,512]{1,0:T(8,128)S(1)}, f32[256,512]{1,0:T(8,128)S(1)}) custom-call(s32[5]{0:T(128)S(1)} %stack.23.pos_ref, bf16[3,2048,256]{2,1,0:T(8,128)(2,1)S(1)} %copy-done, f32[1024,256]{1,0:T(8,128)S(1)} %get-tuple-element.80.all_ref.own_ref), custom_call_target="tpu_custom_call" | custom-call | tf_op jit(solution)/shard_map/pallas_call | solution.py:490
  42.5 1.5 %shard_map.126 = (f32[800,256]{1,0:T(8,128)S(1)}, f32[800,256]{1,0:T(8,128)S(1)}, f32[800,256]{1,0:T(8,128)S(1)}, f32[800,256]{1,0:T(8,128)S(1)}, f32[256,512]{1,0:T(8,128)S(1)}, /*index=5*/f32[256,512]{1,0:T(8,128)S(1)}) custom-call(s32[5]{0:T(128)S(1)} %stack.23.pos_ref, ...), custom_call_target="tpu_custom_call", output_to_operand_aliasing={{4}: (5, {}), {5}: (6, {})} | custom-call | tf_op jit(solution)/shard_map/pallas_call | solution.py:495
  44.0 2.6 %collective-permute-start.11 = (f32[800,256]{1,0:T(8,128)S(1)}, f32[800,256]{1,0:T(8,128)S(1)}, u32[]{:S(2)}, u32[]{:S(2)}) collective-permute-start(f32[800,256]{1,0:T(8,128)S(1)} %get-tuple-element.86), channel_id=1, source_target_pairs={{0,32},{4,36},{8,40},{12,44},{16,20},{20,24},{24,28},{28,16},{32,6... | collective-permute-start | bytes 2457608 | tf_op jit(solution)/shard_map/ppermute | solution.py:371
  46.7 2.2 %collective-permute-start.13 = (f32[800,256]{1,0:T(8,128)S(1)}, f32[800,256]{1,0:T(8,128)S(1)}, u32[]{:S(2)}, u32[]{:S(2)}) collective-permute-start(f32[800,256]{1,0:T(8,128)S(1)} %get-tuple-element.88), channel_id=1, source_target_pairs={{0,64},{4,68},{8,72},{12,76},{16,24},{20,28},{24,16},{28,20},{32,9... | collective-permute-start | bytes 2457608 | tf_op jit(solution)/shard_map/ppermute | solution.py:371
  48.9 1.6 %collective-permute-start.14 = (f32[256,512]{1,0:T(8,128)S(1)}, f32[256,512]{1,0:T(8,128)S(1)}, u32[]{:S(2)}, u32[]{:S(2)}) collective-permute-start(f32[256,512]{1,0:T(8,128)S(1)} %get-tuple-element.90), channel_id=1, source_target_pairs={{0,1},{1,2},{2,3},{3,0},{4,5},{5,6},{6,7},{7,4},{8,9},{9,10},{10,1... | collective-permute-start | bytes 1572872 | tf_op jit(solution)/shard_map/ppermute | solution.py:493
  50.5 2.1 %collective-permute-start.15 = (f32[256,512]{1,0:T(8,128)S(1)}, f32[256,512]{1,0:T(8,128)S(1)}, u32[]{:S(2)}, u32[]{:S(2)}) collective-permute-start(f32[256,512]{1,0:T(8,128)S(1)} %get-tuple-element.91), channel_id=1, source_target_pairs={{0,3},{1,0},{2,1},{3,2},{4,7},{5,4},{6,5},{7,6},{8,11},{9,8},{10,9... | collective-permute-start | bytes 1572872 | tf_op jit(solution)/shard_map/ppermute | solution.py:493
  52.7 11.7 %collective-permute-done.14.refs_1_ = f32[256,512]{1,0:T(8,128)S(1)} collective-permute-done((f32[256,512]{1,0:T(8,128)S(1)}, f32[256,512]{1,0:T(8,128)S(1)}, u32[]{:S(2)}, u32[]{:S(2)}) %collective-permute-start.14) | collective-permute-done | bytes 524320 | tf_op jit(solution)/shard_map/ppermute | solution.py:493
  64.4 1.8 %collective-permute-done.13.far_ref = f32[800,256]{1,0:T(8,128)S(1)} collective-permute-done((f32[800,256]{1,0:T(8,128)S(1)}, f32[800,256]{1,0:T(8,128)S(1)}, u32[]{:S(2)}, u32[]{:S(2)}) %collective-permute-start.13) | collective-permute-done | bytes 819232 | tf_op jit(solution)/shard_map/ppermute | solution.py:371
  66.9 3.7 %collective-permute-start.16 = (f32[256,512]{1,0:T(8,128)S(1)}, f32[256,512]{1,0:T(8,128)S(1)}, u32[]{:S(2)}, u32[]{:S(2)}) collective-permute-start(f32[256,512]{1,0:T(8,128)S(1)} %get-tuple-element.92), channel_id=1, source_target_pairs={{0,2},{1,3},{2,0},{3,1},{4,6},{5,7},{6,4},{7,5},{8,10},{9,11},{10,... | collective-permute-start | bytes 1572872 | tf_op jit(solution)/shard_map/ppermute | solution.py:493
  70.6 0.9 collective-permute-start.17
  71.5 1.8 %collective-permute-start.18 = (f32[200,256]{1,0:T(8,128)S(1)}, f32[200,256]{1,0:T(8,128)S(1)}, u32[]{:S(2)}, u32[]{:S(2)}) collective-permute-start(f32[200,256]{1,0:T(8,128)S(1)} %get-tuple-element.95), channel_id=1, source_target_pairs={{0,12},{4,0},{8,4},{12,8},{16,112},{20,116},{24,120},{28,124},{32,... | collective-permute-start | bytes 614408 | tf_op jit(solution)/shard_map/ppermute | solution.py:371
  73.3 1.2 %collective-permute-start.19 = (f32[200,256]{1,0:T(8,128)S(1)}, f32[200,256]{1,0:T(8,128)S(1)}, u32[]{:S(2)}, u32[]{:S(2)}) collective-permute-start(f32[200,256]{1,0:T(8,128)S(1)} %get-tuple-element.96), channel_id=1, source_target_pairs={{0,8},{4,12},{8,0},{12,4},{16,80},{20,84},{24,88},{28,92},{32,40},... | collective-permute-start | bytes 614408 | tf_op jit(solution)/shard_map/ppermute | solution.py:371
  74.5 2.2 %collective-permute-done.17.back_ref = f32[200,256]{1,0:T(8,128)S(1)} collective-permute-done((f32[200,256]{1,0:T(8,128)S(1)}, f32[200,256]{1,0:T(8,128)S(1)}, u32[]{:S(2)}, u32[]{:S(2)}) %collective-permute-start.17) | collective-permute-done | bytes 204832 | tf_op jit(solution)/shard_map/ppermute | solution.py:371
  76.7 1.5 %collective-permute-done.18.ahead_ref = f32[200,256]{1,0:T(8,128)S(1)} collective-permute-done((f32[200,256]{1,0:T(8,128)S(1)}, f32[200,256]{1,0:T(8,128)S(1)}, u32[]{:S(2)}, u32[]{:S(2)}) %collective-permute-start.18) | collective-permute-done | bytes 204832 | tf_op jit(solution)/shard_map/ppermute | solution.py:371
  78.2 1.7 %collective-permute-done.19.far_ref = f32[200,256]{1,0:T(8,128)S(1)} collective-permute-done((f32[200,256]{1,0:T(8,128)S(1)}, f32[200,256]{1,0:T(8,128)S(1)}, u32[]{:S(2)}, u32[]{:S(2)}) %collective-permute-start.19) | collective-permute-done | bytes 204832 | tf_op jit(solution)/shard_map/ppermute | solution.py:371
  80.0 1.1 collective-permute-start.22
  81.1 1.2 %collective-permute-start.21 = (f32[200,256]{1,0:T(8,128)S(1)}, f32[200,256]{1,0:T(8,128)S(1)}, u32[]{:S(2)}, u32[]{:S(2)}) collective-permute-start(f32[200,256]{1,0:T(8,128)S(1)} %shard_map.128.own_ref), channel_id=1, source_target_pairs={{0,4},{4,8},{8,12},{12,0},{16,48},{20,52},{24,56},{28,60},{32,36},... | collective-permute-start | bytes 614408 | tf_op jit(solution)/shard_map/ppermute | solution.py:371
  82.3 1.4 %collective-permute-start.20 = (f32[200,256]{1,0:T(8,128)S(1)}, f32[200,256]{1,0:T(8,128)S(1)}, u32[]{:S(2)}, u32[]{:S(2)}) collective-permute-start(f32[200,256]{1,0:T(8,128)S(1)} %shard_map.128.own_ref), channel_id=1, source_target_pairs={{0,12},{4,0},{8,4},{12,8},{16,112},{20,116},{24,120},{28,124},{32,... | collective-permute-start | bytes 614408 | tf_op jit(solution)/shard_map/ppermute | solution.py:371
  84.0 2.3 %collective-permute-done.22.far_ref = f32[200,256]{1,0:T(8,128)S(1)} collective-permute-done((f32[200,256]{1,0:T(8,128)S(1)}, f32[200,256]{1,0:T(8,128)S(1)}, u32[]{:S(2)}, u32[]{:S(2)}) %collective-permute-start.22) | collective-permute-done | bytes 204832 | tf_op jit(solution)/shard_map/ppermute | solution.py:371
  86.3 2.4 %collective-permute-done.21.back_ref = f32[200,256]{1,0:T(8,128)S(1)} collective-permute-done((f32[200,256]{1,0:T(8,128)S(1)}, f32[200,256]{1,0:T(8,128)S(1)}, u32[]{:S(2)}, u32[]{:S(2)}) %collective-permute-start.21) | collective-permute-done | bytes 204832 | tf_op jit(solution)/shard_map/ppermute | solution.py:371
  89.3 2.1 %collective-permute-start.26 = (f32[800,256]{1,0:T(8,128)S(1)}, f32[800,256]{1,0:T(8,128)S(1)}, u32[]{:S(2)}, u32[]{:S(2)}) collective-permute-start(f32[800,256]{1,0:T(8,128)S(1)} %shard_map.129.refs_0_), channel_id=1, source_target_pairs={{0,64},{4,68},{8,72},{12,76},{16,24},{20,28},{24,16},{28,20},{32,9... | collective-permute-start | bytes 2457608 | tf_op jit(solution)/shard_map/ppermute | solution.py:371
  91.3 3.0 %collective-permute-start.25 = (f32[800,256]{1,0:T(8,128)S(1)}, f32[800,256]{1,0:T(8,128)S(1)}, u32[]{:S(2)}, u32[]{:S(2)}) collective-permute-start(f32[800,256]{1,0:T(8,128)S(1)} %shard_map.129.refs_0_), channel_id=1, source_target_pairs={{0,16},{16,0},{32,48},{48,32},{64,80},{80,64},{96,112},{112,96},{1... | collective-permute-start | bytes 2457608 | tf_op jit(solution)/shard_map/ppermute | solution.py:376
  94.3 1.1 collective-permute-start.24
  95.4 1.6 %collective-permute-start.23 = (f32[800,256]{1,0:T(8,128)S(1)}, f32[800,256]{1,0:T(8,128)S(1)}, u32[]{:S(2)}, u32[]{:S(2)}) collective-permute-start(f32[800,256]{1,0:T(8,128)S(1)} %shard_map.129.refs_0_), channel_id=1, source_target_pairs={{0,96},{4,100},{8,104},{12,108},{16,28},{20,16},{24,20},{28,24},{3... | collective-permute-start | bytes 2457608 | tf_op jit(solution)/shard_map/ppermute | solution.py:371
  97.0 5.4 %collective-permute-done.26.refs_2_ = f32[800,256]{1,0:T(8,128)S(1)} collective-permute-done((f32[800,256]{1,0:T(8,128)S(1)}, f32[800,256]{1,0:T(8,128)S(1)}, u32[]{:S(2)}, u32[]{:S(2)}) %collective-permute-start.26) | collective-permute-done | bytes 819232 | tf_op jit(solution)/shard_map/ppermute | solution.py:371
  102.4 1.7 %shard_map.130 = (f32[3,2048,256]{2,1,0:T(8,128)}, f32[800,256]{1,0:T(8,128)S(1)}) custom-call(s32[5]{0:T(128)S(1)} %stack.23.pos_ref, f32[800,256]{1,0:T(8,128)S(1)} %shard_map.129.refs_0_, f32[800,256]{1,0:T(8,128)S(1)} %collective-permute-done.25.refs_1_.refs_4_, f32[800,256]{1,0:T(8,128)S(1)} %collective-permute-done.26.refs_2_), custom_call_target="tpu_custom_call", output_to_operand_aliasing={{1}: (3, {})} | custom-call | tf_op jit(solution)/shard_map/pallas_call | solution.py:518
  104.1 5.1 %collective-permute-start.29 = (f32[800,256]{1,0:T(8,128)S(1)}, f32[800,256]{1,0:T(8,128)S(1)}, u32[]{:S(2)}, u32[]{:S(2)}) collective-permute-start(f32[800,256]{1,0:T(8,128)S(1)} %get-tuple-element.97.refs_2_.refs_3_), channel_id=1, source_target_pairs={{0,16},{16,0},{32,48},{48,32},{64,80},{80,64},{96,112},{112,96},{1... | collective-permute-start | bytes 2457608 | tf_op jit(solution)/shard_map/ppermute | solution.py:376
  109.3 1.8 %collective-permute-done.24.refs_1_.refs_2_ = f32[800,256]{1,0:T(8,128)S(1)} collective-permute-done((f32[800,256]{1,0:T(8,128)S(1)}, f32[800,256]{1,0:T(8,128)S(1)}, u32[]{:S(2)}, u32[]{:S(2)}) %collective-permute-start.24) | collective-permute-done | bytes 819232 | tf_op jit(solution)/shard_map/ppermute | solution.py:371
  111.1 5.0 %collective-permute-start.28 = (f32[800,256]{1,0:T(8,128)S(1)}, f32[800,256]{1,0:T(8,128)S(1)}, u32[]{:S(2)}, u32[]{:S(2)}) collective-permute-start(f32[800,256]{1,0:T(8,128)S(1)} %collective-permute-done.24.refs_1_.refs_2_), channel_id=1, source_target_pairs={{0,16},{16,0},{32,48},{48,32},{64,80},{80,64},{96,112},{112,96},{1... | collective-permute-start | bytes 2457608 | tf_op jit(solution)/shard_map/ppermute | solution.py:376
  116.1 2.3 %shard_map.131.refs_8_ = f32[3,2048,256]{2,1,0:T(8,128)} custom-call(s32[5]{0:T(128)S(1)} %stack.23.pos_ref, f32[800,256]{1,0:T(8,128)S(1)} %collective-permute-done.23.refs_0_.refs_1_, f32[800,256]{1,0:T(8,128)S(1)} %collective-permute-done.24.refs_1_.refs_2_, f32[800,256]{1,0:T(8,128)S(1)} %get-tuple-element.97.refs_2_.refs_3_, ...), custom_call_target="tpu_custom_call", output_to_operand_aliasing={{}: (5, {})} | custom-call | tf_op jit(solution)/shard_map/pallas_call | solution.py:518
  118.5 0.8 collective-permute-done.27.refs_5_
  119.2 2.4 %shard_map.132 = (f32[3,2048,256]{2,1,0:T(8,128)}, f32[2,128,128]{2,1,0:T(8,128)}, f32[2,128]{1,0:T(2,128)}, f32[2]{0:T(128)}) custom-call(s32[5]{0:T(128)S(1)} %stack.23.pos_ref, f32[800,256]{1,0:T(8,128)S(1)} %shard_map.129.refs_0_, f32[800,256]{1,0:T(8,128)S(1)} %collective-permute-done.23.refs_0_.refs_1_, ...), custom_call_target="tpu_custom_call", output_to_operand_aliasing={{0}: (9, {})} | custom-call | tf_op jit(solution)/shard_map/pallas_call | solution.py:534
  (43 shorter events, 4.3 us)
Async XLA Ops:
  0.6 11.9 %copy-start.4 = (f32[1,2,256]{2,1,0:T(2,128)S(1)}, f32[1,2,256]{2,1,0:T(2,128)}, u32[]{:S(2)}) copy-start(f32[1,2,256]{2,1,0:T(2,128)} %gate_ref.7) | copy-start | bytes 6148
  0.6 11.9 %copy-start.5 = (f32[2]{0:T(128)S(1)}, f32[2]{0:T(128)}, u32[]{:S(2)}) copy-start(f32[2]{0:T(128)} %base_ref.7) | copy-start | bytes 28
  0.8 19.7 %copy-start.2 = (f32[2,128,128]{2,1,0:T(8,128)S(1)}, f32[2,128,128]{2,1,0:T(8,128)}, u32[]{:S(2)}) copy-start(f32[2,128,128]{2,1,0:T(8,128)} %init_ref.3) | copy-start | bytes 393220
  0.8 19.7 %copy-start.3 = (bf16[1,256,256]{2,1,0:T(8,128)(2,1)S(1)}, bf16[1,256,256]{2,1,0:T(8,128)(2,1)}, u32[]{:S(2)}) copy-start(bf16[1,256,256]{2,1,0:T(8,128)(2,1)} %up_ref.3) | copy-start | bytes 393220
  0.8 19.7 %copy-start.6 = (f32[2,128]{1,0:T(2,128)S(1)}, f32[2,128]{1,0:T(2,128)}, u32[]{:S(2)}) copy-start(f32[2,128]{1,0:T(2,128)} %gain_ref.1) | copy-start | bytes 3076
  6.5 13.0 %collective-permute-start.4 = (f32[256,1024]{1,0:T(8,128)S(1)}, f32[256,1024]{1,0:T(8,128)S(1)}, u32[]{:S(2)}, u32[]{:S(2)}) collective-permute-start(f32[256,1024]{1,0:T(8,128)S(1)} %get-tuple-element.63), channel_id=1, source_target_pairs={{0,16},{16,0},{32,48},{48,32},{64,80},{80,64},{96,112},{112,96},{1... | collective-permute-start | bytes 3145736 | tf_op jit(solution)/shard_map/ppermute | solution.py:376
  8.0 8.5 %collective-permute-start = (f32[2,128,128]{2,1,0:T(8,128)S(1)}, f32[2,128,128]{2,1,0:T(8,128)S(1)}, u32[]{:S(2)}, u32[]{:S(2)}) collective-permute-start(f32[2,128,128]{2,1,0:T(8,128)S(1)} %get-tuple-element.55), channel_id=1, source_target_pairs={{0,4},{8,12},{1,5},{9,13},{2,6},{10,14},{3,7},{11,15},{16,20},{24,... | collective-permute-start | bytes 393224 | tf_op jit(solution)/shard_map/ppermute | solution.py:449
  11.3 9.1 %collective-permute-start.3 = (f32[2,128,128]{2,1,0:T(8,128)S(1)}, f32[2,128,128]{2,1,0:T(8,128)S(1)}, u32[]{:S(2)}, u32[]{:S(2)}) collective-permute-start(f32[2,128,128]{2,1,0:T(8,128)S(1)} %get-tuple-element.56.d_ref), channel_id=1, source_target_pairs={{8,12},{4,0},{9,13},{5,1},{10,14},{6,2},{11,15},{7,3},{24,28},{20,... | collective-permute-start | bytes 393224 | tf_op jit(solution)/shard_map/ppermute | solution.py:450
  16.5 23.7 %copy-start = (bf16[3,2048,256]{2,1,0:T(8,128)(2,1)S(1)}, bf16[3,2048,256]{2,1,0:T(8,128)(2,1)}, u32[]{:S(2)}) copy-start(bf16[3,2048,256]{2,1,0:T(8,128)(2,1)} %w_ref.1) | copy-start | bytes 9437188
  16.7 3.7 %collective-permute-start.2 = (f32[2,128,128]{2,1,0:T(8,128)S(1)}, f32[2,128,128]{2,1,0:T(8,128)S(1)}, u32[]{:S(2)}, u32[]{:S(2)}) collective-permute-start(f32[2,128,128]{2,1,0:T(8,128)S(1)} %shard_map.120), channel_id=1, source_target_pairs={{4,12},{5,13},{6,14},{7,15},{20,28},{21,29},{22,30},{23,31},{36,44... | collective-permute-start | bytes 393224 | tf_op jit(solution)/shard_map/ppermute | solution.py:468
  17.5 2.9 %collective-permute-start.1 = (f32[2,128,128]{2,1,0:T(8,128)S(1)}, f32[2,128,128]{2,1,0:T(8,128)S(1)}, u32[]{:S(2)}, u32[]{:S(2)}) collective-permute-start(f32[2,128,128]{2,1,0:T(8,128)S(1)} %shard_map.120), channel_id=1, source_target_pairs={{4,8},{5,9},{6,10},{7,11},{20,24},{21,25},{22,26},{23,27},{36,40},... | collective-permute-start | bytes 393224 | tf_op jit(solution)/shard_map/ppermute | solution.py:467
  18.2 11.2 %collective-permute-start.9 = (f32[2,128,128]{2,1,0:T(8,128)S(1)}, f32[2,128,128]{2,1,0:T(8,128)S(1)}, u32[]{:S(2)}, u32[]{:S(2)}) collective-permute-start(f32[2,128,128]{2,1,0:T(8,128)S(1)} %get-tuple-element.56.d_ref), channel_id=1, source_target_pairs={{8,0},{9,1},{10,2},{11,3},{24,16},{25,17},{26,18},{27,19},{40,32},... | collective-permute-start | bytes 393224 | tf_op jit(solution)/shard_map/ppermute | solution.py:452
  19.5 9.9 %collective-permute-start.8 = (f32[2,128,128]{2,1,0:T(8,128)S(1)}, f32[2,128,128]{2,1,0:T(8,128)S(1)}, u32[]{:S(2)}, u32[]{:S(2)}) collective-permute-start(f32[2,128,128]{2,1,0:T(8,128)S(1)} %get-tuple-element.56.d_ref), channel_id=1, source_target_pairs={{8,4},{9,5},{10,6},{11,7},{24,20},{25,21},{26,22},{27,23},{40,36},... | collective-permute-start | bytes 393224 | tf_op jit(solution)/shard_map/ppermute | solution.py:451
  22.6 8.5 %collective-permute-start.7 = (f32[2,128,128]{2,1,0:T(8,128)S(1)}, f32[2,128,128]{2,1,0:T(8,128)S(1)}, u32[]{:S(2)}, u32[]{:S(2)}) collective-permute-start(f32[2,128,128]{2,1,0:T(8,128)S(1)} %get-tuple-element.64.p_ref), channel_id=1, source_target_pairs={{12,0},{13,1},{14,2},{15,3},{28,16},{29,17},{30,18},{31,19},{44,32... | collective-permute-start | bytes 393224 | tf_op jit(solution)/shard_map/ppermute | solution.py:477
  23.9 9.2 %collective-permute-start.6 = (f32[2,128,128]{2,1,0:T(8,128)S(1)}, f32[2,128,128]{2,1,0:T(8,128)S(1)}, u32[]{:S(2)}, u32[]{:S(2)}) collective-permute-start(f32[2,128,128]{2,1,0:T(8,128)S(1)} %get-tuple-element.64.p_ref), channel_id=1, source_target_pairs={{12,4},{8,0},{13,5},{9,1},{14,6},{10,2},{15,7},{11,3},{28,20},{24,... | collective-permute-start | bytes 393224 | tf_op jit(solution)/shard_map/ppermute | solution.py:476
  25.2 7.9 %collective-permute-start.5 = (f32[2,128,128]{2,1,0:T(8,128)S(1)}, f32[2,128,128]{2,1,0:T(8,128)S(1)}, u32[]{:S(2)}, u32[]{:S(2)}) collective-permute-start(f32[2,128,128]{2,1,0:T(8,128)S(1)} %get-tuple-element.64.p_ref), channel_id=1, source_target_pairs={{12,8},{8,4},{4,0},{13,9},{9,5},{5,1},{14,10},{10,6},{6,2},{15,11}... | collective-permute-start | bytes 393224 | tf_op jit(solution)/shard_map/ppermute | solution.py:475
  36.8 5.7 %collective-permute-start.10 = (f32[1024,256]{1,0:T(8,128)S(1)}, f32[1024,256]{1,0:T(8,128)S(1)}, u32[]{:S(2)}, u32[]{:S(2)}) collective-permute-start(f32[1024,256]{1,0:T(8,128)S(1)} %get-tuple-element.80.all_ref.own_ref), channel_id=1, source_target_pairs={{0,16},{16,0},{32,48},{48,32},{64,80},{80,64},{96,112},{112,96},{1... | collective-permute-start | bytes 3145736 | tf_op jit(solution)/shard_map/ppermute | solution.py:376
  44.0 20.4 %collective-permute-start.11 = (f32[800,256]{1,0:T(8,128)S(1)}, f32[800,256]{1,0:T(8,128)S(1)}, u32[]{:S(2)}, u32[]{:S(2)}) collective-permute-start(f32[800,256]{1,0:T(8,128)S(1)} %get-tuple-element.86), channel_id=1, source_target_pairs={{0,32},{4,36},{8,40},{12,44},{16,20},{20,24},{24,28},{28,16},{32,6... | collective-permute-start | bytes 2457608 | tf_op jit(solution)/shard_map/ppermute | solution.py:371
  46.6 17.8 %collective-permute-start.12 = (f32[800,256]{1,0:T(8,128)S(1)}, f32[800,256]{1,0:T(8,128)S(1)}, u32[]{:S(2)}, u32[]{:S(2)}) collective-permute-start(f32[800,256]{1,0:T(8,128)S(1)} %get-tuple-element.87), channel_id=1, source_target_pairs={{0,96},{4,100},{8,104},{12,108},{16,28},{20,16},{24,20},{28,24},{3... | collective-permute-start | bytes 2457608 | tf_op jit(solution)/shard_map/ppermute | solution.py:371
  46.7 19.5 %collective-permute-start.13 = (f32[800,256]{1,0:T(8,128)S(1)}, f32[800,256]{1,0:T(8,128)S(1)}, u32[]{:S(2)}, u32[]{:S(2)}) collective-permute-start(f32[800,256]{1,0:T(8,128)S(1)} %get-tuple-element.88), channel_id=1, source_target_pairs={{0,64},{4,68},{8,72},{12,76},{16,24},{20,28},{24,16},{28,20},{32,9... | collective-permute-start | bytes 2457608 | tf_op jit(solution)/shard_map/ppermute | solution.py:371
  48.9 15.5 %collective-permute-start.14 = (f32[256,512]{1,0:T(8,128)S(1)}, f32[256,512]{1,0:T(8,128)S(1)}, u32[]{:S(2)}, u32[]{:S(2)}) collective-permute-start(f32[256,512]{1,0:T(8,128)S(1)} %get-tuple-element.90), channel_id=1, source_target_pairs={{0,1},{1,2},{2,3},{3,0},{4,5},{5,6},{6,7},{7,4},{8,9},{9,10},{10,1... | collective-permute-start | bytes 1572872 | tf_op jit(solution)/shard_map/ppermute | solution.py:493
  50.5 13.9 %collective-permute-start.15 = (f32[256,512]{1,0:T(8,128)S(1)}, f32[256,512]{1,0:T(8,128)S(1)}, u32[]{:S(2)}, u32[]{:S(2)}) collective-permute-start(f32[256,512]{1,0:T(8,128)S(1)} %get-tuple-element.91), channel_id=1, source_target_pairs={{0,3},{1,0},{2,1},{3,2},{4,7},{5,4},{6,5},{7,6},{8,11},{9,8},{10,9... | collective-permute-start | bytes 1572872 | tf_op jit(solution)/shard_map/ppermute | solution.py:493
  66.9 16.8 %collective-permute-start.16 = (f32[256,512]{1,0:T(8,128)S(1)}, f32[256,512]{1,0:T(8,128)S(1)}, u32[]{:S(2)}, u32[]{:S(2)}) collective-permute-start(f32[256,512]{1,0:T(8,128)S(1)} %get-tuple-element.92), channel_id=1, source_target_pairs={{0,2},{1,3},{2,0},{3,1},{4,6},{5,7},{6,4},{7,5},{8,10},{9,11},{10,... | collective-permute-start | bytes 1572872 | tf_op jit(solution)/shard_map/ppermute | solution.py:493
  70.6 6.1 %collective-permute-start.17 = (f32[200,256]{1,0:T(8,128)S(1)}, f32[200,256]{1,0:T(8,128)S(1)}, u32[]{:S(2)}, u32[]{:S(2)}) collective-permute-start(f32[200,256]{1,0:T(8,128)S(1)} %get-tuple-element.94), channel_id=1, source_target_pairs={{0,4},{4,8},{8,12},{12,0},{16,48},{20,52},{24,56},{28,60},{32,36},... | collective-permute-start | bytes 614408 | tf_op jit(solution)/shard_map/ppermute | solution.py:371
  71.5 6.7 %collective-permute-start.18 = (f32[200,256]{1,0:T(8,128)S(1)}, f32[200,256]{1,0:T(8,128)S(1)}, u32[]{:S(2)}, u32[]{:S(2)}) collective-permute-start(f32[200,256]{1,0:T(8,128)S(1)} %get-tuple-element.95), channel_id=1, source_target_pairs={{0,12},{4,0},{8,4},{12,8},{16,112},{20,116},{24,120},{28,124},{32,... | collective-permute-start | bytes 614408 | tf_op jit(solution)/shard_map/ppermute | solution.py:371
  73.3 6.6 %collective-permute-start.19 = (f32[200,256]{1,0:T(8,128)S(1)}, f32[200,256]{1,0:T(8,128)S(1)}, u32[]{:S(2)}, u32[]{:S(2)}) collective-permute-start(f32[200,256]{1,0:T(8,128)S(1)} %get-tuple-element.96), channel_id=1, source_target_pairs={{0,8},{4,12},{8,0},{12,4},{16,80},{20,84},{24,88},{28,92},{32,40},... | collective-permute-start | bytes 614408 | tf_op jit(solution)/shard_map/ppermute | solution.py:371
  80.0 6.3 %collective-permute-start.22 = (f32[200,256]{1,0:T(8,128)S(1)}, f32[200,256]{1,0:T(8,128)S(1)}, u32[]{:S(2)}, u32[]{:S(2)}) collective-permute-start(f32[200,256]{1,0:T(8,128)S(1)} %shard_map.128.own_ref), channel_id=1, source_target_pairs={{0,8},{4,12},{8,0},{12,4},{16,80},{20,84},{24,88},{28,92},{32,40},... | collective-permute-start | bytes 614408 | tf_op jit(solution)/shard_map/ppermute | solution.py:371
  81.1 7.6 %collective-permute-start.21 = (f32[200,256]{1,0:T(8,128)S(1)}, f32[200,256]{1,0:T(8,128)S(1)}, u32[]{:S(2)}, u32[]{:S(2)}) collective-permute-start(f32[200,256]{1,0:T(8,128)S(1)} %shard_map.128.own_ref), channel_id=1, source_target_pairs={{0,4},{4,8},{8,12},{12,0},{16,48},{20,52},{24,56},{28,60},{32,36},... | collective-permute-start | bytes 614408 | tf_op jit(solution)/shard_map/ppermute | solution.py:371
  82.3 6.3 %collective-permute-start.20 = (f32[200,256]{1,0:T(8,128)S(1)}, f32[200,256]{1,0:T(8,128)S(1)}, u32[]{:S(2)}, u32[]{:S(2)}) collective-permute-start(f32[200,256]{1,0:T(8,128)S(1)} %shard_map.128.own_ref), channel_id=1, source_target_pairs={{0,12},{4,0},{8,4},{12,8},{16,112},{20,116},{24,120},{28,124},{32,... | collective-permute-start | bytes 614408 | tf_op jit(solution)/shard_map/ppermute | solution.py:371
  84.0 34.4 %copy-start.1 = (bf16[1,256,512]{2,1,0:T(8,128)(2,1)}, bf16[1,256,512]{2,1,0:T(8,128)(2,1)S(1)}, u32[]{:S(2)}) copy-start(bf16[1,256,512]{2,1,0:T(8,128)(2,1)S(1)} %fusion.refs_0_) | copy-start | bytes 786436
  89.3 13.1 %collective-permute-start.26 = (f32[800,256]{1,0:T(8,128)S(1)}, f32[800,256]{1,0:T(8,128)S(1)}, u32[]{:S(2)}, u32[]{:S(2)}) collective-permute-start(f32[800,256]{1,0:T(8,128)S(1)} %shard_map.129.refs_0_), channel_id=1, source_target_pairs={{0,64},{4,68},{8,72},{12,76},{16,24},{20,28},{24,16},{28,20},{32,9... | collective-permute-start | bytes 2457608 | tf_op jit(solution)/shard_map/ppermute | solution.py:371
  91.3 11.0 %collective-permute-start.25 = (f32[800,256]{1,0:T(8,128)S(1)}, f32[800,256]{1,0:T(8,128)S(1)}, u32[]{:S(2)}, u32[]{:S(2)}) collective-permute-start(f32[800,256]{1,0:T(8,128)S(1)} %shard_map.129.refs_0_), channel_id=1, source_target_pairs={{0,16},{16,0},{32,48},{48,32},{64,80},{80,64},{96,112},{112,96},{1... | collective-permute-start | bytes 2457608 | tf_op jit(solution)/shard_map/ppermute | solution.py:376
  94.3 16.8 %collective-permute-start.24 = (f32[800,256]{1,0:T(8,128)S(1)}, f32[800,256]{1,0:T(8,128)S(1)}, u32[]{:S(2)}, u32[]{:S(2)}) collective-permute-start(f32[800,256]{1,0:T(8,128)S(1)} %shard_map.129.refs_0_), channel_id=1, source_target_pairs={{0,32},{4,36},{8,40},{12,44},{16,20},{20,24},{24,28},{28,16},{32,6... | collective-permute-start | bytes 2457608 | tf_op jit(solution)/shard_map/ppermute | solution.py:371
  95.4 20.7 %collective-permute-start.23 = (f32[800,256]{1,0:T(8,128)S(1)}, f32[800,256]{1,0:T(8,128)S(1)}, u32[]{:S(2)}, u32[]{:S(2)}) collective-permute-start(f32[800,256]{1,0:T(8,128)S(1)} %shard_map.129.refs_0_), channel_id=1, source_target_pairs={{0,96},{4,100},{8,104},{12,108},{16,28},{20,16},{24,20},{28,24},{3... | collective-permute-start | bytes 2457608 | tf_op jit(solution)/shard_map/ppermute | solution.py:371
  104.1 12.0 %collective-permute-start.29 = (f32[800,256]{1,0:T(8,128)S(1)}, f32[800,256]{1,0:T(8,128)S(1)}, u32[]{:S(2)}, u32[]{:S(2)}) collective-permute-start(f32[800,256]{1,0:T(8,128)S(1)} %get-tuple-element.97.refs_2_.refs_3_), channel_id=1, source_target_pairs={{0,16},{16,0},{32,48},{48,32},{64,80},{80,64},{96,112},{112,96},{1... | collective-permute-start | bytes 2457608 | tf_op jit(solution)/shard_map/ppermute | solution.py:376
  111.1 7.3 %collective-permute-start.28 = (f32[800,256]{1,0:T(8,128)S(1)}, f32[800,256]{1,0:T(8,128)S(1)}, u32[]{:S(2)}, u32[]{:S(2)}) collective-permute-start(f32[800,256]{1,0:T(8,128)S(1)} %collective-permute-done.24.refs_1_.refs_2_), channel_id=1, source_target_pairs={{0,16},{16,0},{32,48},{48,32},{64,80},{80,64},{96,112},{112,96},{1... | collective-permute-start | bytes 2457608 | tf_op jit(solution)/shard_map/ppermute | solution.py:376
  116.1 3.1 %collective-permute-start.27 = (f32[800,256]{1,0:T(8,128)S(1)}, f32[800,256]{1,0:T(8,128)S(1)}, u32[]{:S(2)}, u32[]{:S(2)}) collective-permute-start(f32[800,256]{1,0:T(8,128)S(1)} %collective-permute-done.23.refs_0_.refs_1_), channel_id=1, source_target_pairs={{0,16},{16,0},{32,48},{48,32},{64,80},{80,64},{96,112},{112,96},{1... | collective-permute-start | bytes 2457608 | tf_op jit(solution)/shard_map/ppermute | solution.py:376

commit v7 on v6

--- a/solution.py
+++ b/solution.py
@@ -160,27 +160,36 @@
 ):
     del after_ref
     ctx = pos_ref[4]
-    for h in range(init_ref.shape[0]):
-        last = dot(rd_ref[h], far_ref[h], NN, 3) + near_ref[h]
-        start = jnp.where(
-            ctx == 0, init_ref[h], jnp.where(ctx == 1, near_ref[h], jnp.where(ctx == 2, mid_ref[h], last))
+    heads = range(init_ref.shape[0])
+    lasts = [dot(rd_ref[h], far_ref[h], NN, 3) + near_ref[h] for h in heads]
+    starts = [
+        jnp.where(
+            ctx == 0, init_ref[h], jnp.where(ctx == 1, near_ref[h], jnp.where(ctx == 2, mid_ref[h], lasts[h]))
         )
-        w_ref[h] = start
-        qt = qt_ref[:, span(h)]
-        z = dot(qt, start, NN, 3) + zv_ref[:, span(h)]
-        up = up_ref[0, :, span(h)].astype(F32)
-        centred = z - jnp.mean(z, -1, keepdims=True)
-        inv_std = lax.rsqrt(jnp.mean(centred * centred, -1, keepdims=True) + 1e-05)
-        normed = centred * inv_std
-        weighted = up * gain_ref[h : h + 1, :]
-        back = inv_std * (
-            weighted
-            - jnp.mean(weighted, -1, keepdims=True)
-            - normed * jnp.mean(weighted * normed, -1, keepdims=True)
+        for h in heads
+    ]
+    qts = [qt_ref[:, span(h)] for h in heads]
+    zs = [dot(qts[h], starts[h], NN, 3) + zv_ref[:, span(h)] for h in heads]
+    ups = [up_ref[0, :, span(h)].astype(F32) for h in heads]
+    centred = [z - jnp.mean(z, -1, keepdims=True) for z in zs]
+    inv_stds = [lax.rsqrt(jnp.mean(c * c, -1, keepdims=True) + 1e-05) for c in centred]
+    normed = [c * inv_std for c, inv_std in zip(centred, inv_stds)]
+    weighted = [ups[h] * gain_ref[h : h + 1, :] for h in heads]
+    backs = [
+        inv_stds[h]
+        * (
+            weighted[h]
+            - jnp.mean(weighted[h], -1, keepdims=True)
+            - normed[h] * jnp.mean(weighted[h] * normed[h], -1, keepdims=True)
         )
-        h_ref[:, span(h)] = back
-        p_ref[h] = dot(qt, back, TN, 3)
-        dgain_ref[h : h + 1, :] = jnp.sum(up * normed, axis=0, keepdims=True)
+        for h in heads
+    ]
+    pulled = [dot(qts[h], backs[h], TN, 3) for h in heads]
+    for h in heads:
+        w_ref[h] = starts[h]
+        h_ref[:, span(h)] = backs[h]
+        p_ref[h] = pulled[h]
+        dgain_ref[h : h + 1, :] = jnp.sum(ups[h] * normed[h], axis=0, keepdims=True)
 
 
 def query_kernel(
@@ -217,31 +226,35 @@
     n = k_ref.shape[0]
     i, j = places(n)
     strict = (i // MB) > (j // MB)
+    heads = range(w_ref.shape[0])
+    steps = [jnp.where(ctx == 0, rd_ref[h], rd_one_ref[h]) for h in heads]
+    inner = [two_ref[h] + dot(rd_two_ref[h], three_ref[h], TN, 3) for h in heads]
+    ends = [one_ref[h] + dot(steps[h], inner[h], TN, 3) for h in heads]
+    ks = [k_ref[:, span(h)] for h in heads]
+    rs = [r_ref[:, span(h)] for h in heads]
+    rates = [rates_of(base_ref, gate_ref, h) for h in heads]
+    xs = [x_ref[:, span(h)] + dot(bt_ref[h], ends[h], TN, 3) for h in heads]
+    d_lows = [jnp.where(strict, -dot(xs[h], rs[h], NT, 3), 0.0) for h in heads]
+    begins = [jnp.where(ctx == 0, p_ref[h] + dot(d_ref[h], ends[h], TN, 3), 0.0) for h in heads]
+    pulls = [to_row(jnp.sum(rs[h] * dot(ks[h], ends[h], NN, 3), axis=1, keepdims=True)) for h in heads]
+    dks = [
+        dk_ref[:, span(h)] - dot(xs[h], w_ref[h], NT, 3) + to_col(rates[h][1]) * dot(rs[h], ends[h], NT, 3)
+        for h in heads
+    ]
+    d_grams = [d_lows[h] * rates[h][1] for h in heads]
+    dks = [dks[h] + dot(d_grams[h] + d_grams[h].T, ks[h], NN, 3) for h in heads]
+    draws = [ninv_ref[h] * (dks[h] - ks[h] * jnp.sum(ks[h] * dks[h], -1, keepdims=True)) for h in heads]
+    des = [
+        de_ref[h : h + 1, :] + jnp.sum(d_lows[h] * gram_ref[h], axis=0, keepdims=True) + pulls[h] for h in heads
+    ]
     all_ref[0:n, :] = dq_ref[...]
     all_ref[3 * n + HS : 3 * n + EXTRA, :] = jnp.zeros((EXTRA - HS, all_ref.shape[1]), F32)
-    for h in range(w_ref.shape[0]):
-        step = jnp.where(ctx == 0, rd_ref[h], rd_one_ref[h])
-        end = one_ref[h] + dot(step, two_ref[h] + dot(rd_two_ref[h], three_ref[h], TN, 3), TN, 3)
-        all_ref[3 * n : 3 * n + HS, span(h)] = jnp.where(ctx == 0, p_ref[h] + dot(d_ref[h], end, TN, 3), 0.0)
-        w = w_ref[h]
-        k = k_ref[:, span(h)]
-        r = r_ref[:, span(h)]
-        boost, e = rates_of(base_ref, gate_ref, h)
-        x = x_ref[:, span(h)] + dot(bt_ref[h], end, TN, 3)
-        all_ref[2 * n : 3 * n, span(h)] = x.astype(BF).astype(F32)
-        d_low = jnp.where(strict, -dot(x, r, NT, 3), 0.0)
-        d_gram = d_low * e
-        dk = (
-            dk_ref[:, span(h)]
-            - dot(x, w, NT, 3)
-            + to_col(e) * dot(r, end, NT, 3)
-            + dot(d_gram + d_gram.T, k, NN, 3)
-        )
-        pull = to_row(jnp.sum(r * dot(k, end, NN, 3), axis=1, keepdims=True))
-        de = de_ref[h : h + 1, :] + jnp.sum(d_low * gram_ref[h], axis=0, keepdims=True) + pull
-        draw = ninv_ref[h] * (dk - k * jnp.sum(k * dk, -1, keepdims=True))
-        all_ref[n : 2 * n, span(h)] = draw.astype(BF).astype(F32)
-        d_boost = de / ((1.0 + boost) * (1.0 + boost))
+    for h in heads:
+        boost = rates[h][0]
+        all_ref[n : 2 * n, span(h)] = draws[h].astype(BF).astype(F32)
+        all_ref[2 * n : 3 * n, span(h)] = xs[h].astype(BF).astype(F32)
+        all_ref[3 * n : 3 * n + HS, span(h)] = begins[h]
+        d_boost = des[h] / ((1.0 + boost) * (1.0 + boost))
         gates_ref[0, h : h + 1, :] = d_boost * base_ref[h]
         all_ref[3 * n + HS : 3 * n + HS + 1, span(h)] = dgain_ref[h : h + 1, :]
         all_ref[3 * n + HS + 1 : 3 * n + HS + 2, span(h)] = jnp.broadcast_to(
@@ -293,7 +306,7 @@
 
 
 def split_kernel(pos_ref, own_ref, back_ref, ahead_ref, far_ref, *refs):
-    for turn, out_ref in zip(TURNS, refs[3 : 3 + RING]):
+    for turn, out_ref in zip(TURNS, refs[-RING:]):
         for rows, to in slice_rows(pos_ref, turn):
             out_ref[to, :] = (own_ref[rows, :] + far_ref[rows, :]) + (back_ref[rows, :] + ahead_ref[rows, :])
 
@@ -492,17 +505,14 @@
     def along_head(terms, turn):
         return lax.ppermute(terms, "head", [(i, (i + turn) % RING) for i in range(RING)])
 
-    *chunks, near_one, near_two = whole(
+    *chunks, near_two, far_quarter = whole(
         product_kernel, (chunk,) * RING + (quarter,) * 2, [SM] + [VM] * 6, {5: RING, 6: RING + 1}
-    )(pos, tokt, other_tokt, grads, swap(grads), quarters[1], quarters[2])
+    )(pos, tokt, other_tokt, grads, swap(grads), *quarters[2:])
     own, away = chunks[0], round_turn(chunks[1:], True)
-    from_back, from_ahead = along_head(near_one, 1), along_head(near_two, 3)
+    from_back, from_ahead, from_far = along_head(quarters[1], 1), along_head(near_two, 3), along_head(far_quarter, 2)
 
     piece = vmem(3 * SLICE + PIECE // RING, wide)
-    *pieces, far_quarter = whole(
-        split_kernel, (piece,) * RING + (quarter,), [SM] + [VM] * 5 + [anywhere] * 2, {5: RING}
-    )(pos, own, *away, quarters[3], from_back, from_ahead)
-    from_far = along_head(far_quarter, 2)
+    pieces = whole(split_kernel, (piece,) * RING, [SM] + [VM] * 4 + [anywhere] * 2)(pos, own, *away, from_back, from_ahead)
     grad_tokens = ((quarters[0] + from_far) + (from_back + from_ahead)).astype(BF).reshape(1, n, -1)
     own, away = pieces[0], pieces[1:]
     part_sum = whole(sum_kernel, piece, [VM] * 4)(own, *round_turn(away, False))

time: 122 us -> 124 us (1.016)
  starting transfers between devices: 54.7 us -> 59.4 us
  Pallas kernels: 29.5 us -> 27.8 us
    ppermute x12, starting transfers between devices: 17.4 us -> 24 us  [round_turn(): lax.ppermute(chunk, ('dp', 'ctx'), moves(first, turn))]
    ppermute x3, starting transfers between devices: 7.44 us -> 5.58 us  [along_head(): lax.ppermute(terms, 'head', [(i, (i + turn) % RING) for i in range(RING)])]
    ppermute x12, waiting for transfers between devices: 19.1 us -> 20.8 us  [round_turn(): lax.ppermute(chunk, ('dp', 'ctx'), moves(first, turn))]
    ppermute x3, waiting for transfers between devices: 11.7 us -> 10.1 us  [along_head(): lax.ppermute(terms, 'head', [(i, (i + turn) % RING) for i in range(RING)])]
  transfers between devices with their start and end apart: 30 -> 30, of which waited for: 13 -> 13; matrix products, arithmetic and copies ran while one was open for 0% -> 0% of each run, Pallas kernels for 12% -> 13%
where the time goes in v7:
time: 124 us
  starting transfers between devices  59.4 us (48%)
  waiting for transfers between devices  35.4 us (29%)
  Pallas kernels  27.8 us (22%)
    ppermute x12, starting transfers between devices, round_turn(): lax.ppermute(chunk, ('dp', 'ctx'), moves(first, turn))  24 us
    ppermute x12, waiting for transfers between devices, round_turn(): lax.ppermute(chunk, ('dp', 'ctx'), moves(first, turn))  20.8 us
    ppermute x6, starting transfers between devices, swap(): return lax.ppermute(value, 'dp', [(i, i ^ 1) for i in range(2 * RING)])  17.9 us
    ppermute x3, waiting for transfers between devices, along_head(): lax.ppermute(terms, 'head', [(i, (i + turn) % RING) for i in range(RING)])  10.1 us
    pallas_call x1, Pallas kernels, body(): pl.pallas_call(maps_kernel, grid=(1,), out_shape=(wide_f32, wide_f32, vme...  5.71 us
    ppermute x3, starting transfers between devices, along_head(): lax.ppermute(terms, 'head', [(i, (i + turn) % RING) for i in range(RING)])  5.58 us
    pallas_call x2, Pallas kernels, place(): pl.pallas_call(functools.partial(place_kernel, which=which), out_shape=(o...  4.03 us
    pallas_call x1, Pallas kernels, body(): pl.pallas_call(reach_kernel, grid=(1,), out_shape=(wide_f32, square, wide...  3.89 us
  transfers between devices with their start and end apart: 30, of which 13 were waited for; matrix products, arithmetic and copies ran while one was open for 0% of the time, Pallas kernels for 13%

profile of v7, /device:TPU:1, one launch (start us, length us, event | category | flops | bytes accessed | tf_op | source)
XLA Modules:
  0.0 124.1 jit_solution(606647791366315555)
XLA Ops:
  0.8 5.7 %shard_map.118 = (f32[256,256]{1,0:T(8,128)S(1)}, f32[256,256]{1,0:T(8,128)S(1)}, f32[2,256,128]{2,1,0:T(8,128)S(1)}, f32[2,256,256]{2,1,0:T(8,128)S(1)}, f32[2,...) custom-call(s32[5]{0:T(128)S(1)} %stack.23.pos_ref, ...), custom_call_target="tpu_custom_call" | custom-call | tf_op jit(solution)/shard_map/pallas_call | solution.py:450
  6.5 1.5 %collective-permute-start.4 = (f32[256,1024]{1,0:T(8,128)S(1)}, f32[256,1024]{1,0:T(8,128)S(1)}, u32[]{:S(2)}, u32[]{:S(2)}) collective-permute-start(f32[256,1024]{1,0:T(8,128)S(1)} %get-tuple-element.62), channel_id=1, source_target_pairs={{0,16},{16,0},{32,48},{48,32},{64,80},{80,64},{96,112},{112,96},{1... | collective-permute-start | bytes 3145736 | tf_op jit(solution)/shard_map/ppermute | solution.py:389
  8.0 3.3 %collective-permute-start = (f32[2,128,128]{2,1,0:T(8,128)S(1)}, f32[2,128,128]{2,1,0:T(8,128)S(1)}, u32[]{:S(2)}, u32[]{:S(2)}) collective-permute-start(f32[2,128,128]{2,1,0:T(8,128)S(1)} %get-tuple-element.54), channel_id=1, source_target_pairs={{0,4},{8,12},{1,5},{9,13},{2,6},{10,14},{3,7},{11,15},{16,20},{24,... | collective-permute-start | bytes 393224 | tf_op jit(solution)/shard_map/ppermute | solution.py:462
  11.3 1.3 %collective-permute-start.3 = (f32[2,128,128]{2,1,0:T(8,128)S(1)}, f32[2,128,128]{2,1,0:T(8,128)S(1)}, u32[]{:S(2)}, u32[]{:S(2)}) collective-permute-start(f32[2,128,128]{2,1,0:T(8,128)S(1)} %get-tuple-element.55.d_ref), channel_id=1, source_target_pairs={{8,12},{4,0},{9,13},{5,1},{10,14},{6,2},{11,15},{7,3},{24,28},{20,... | collective-permute-start | bytes 393224 | tf_op jit(solution)/shard_map/ppermute | solution.py:463
  12.6 3.9 %shard_map.119 = (f32[256,256]{1,0:T(8,128)S(1)}, f32[2,256,256]{2,1,0:T(8,128)S(1)}, f32[256,256]{1,0:T(8,128)S(1)}, f32[256,256]{1,0:T(8,128)S(1)}, f32[256,25...) custom-call(s32[5]{0:T(128)S(1)} %stack.23.pos_ref, f32[2]{0:T(128)S(1)} %copy-done.5, ...), custom_call_target="tpu_custom_call" | custom-call | tf_op jit(solution)/shard_map/pallas_call | solution.py:468
  16.7 0.8 collective-permute-start.2
  17.5 0.7 collective-permute-start.1
  18.2 1.3 %collective-permute-start.9 = (f32[2,128,128]{2,1,0:T(8,128)S(1)}, f32[2,128,128]{2,1,0:T(8,128)S(1)}, u32[]{:S(2)}, u32[]{:S(2)}) collective-permute-start(f32[2,128,128]{2,1,0:T(8,128)S(1)} %get-tuple-element.55.d_ref), channel_id=1, source_target_pairs={{8,0},{9,1},{10,2},{11,3},{24,16},{25,17},{26,18},{27,19},{40,32},... | collective-permute-start | bytes 393224 | tf_op jit(solution)/shard_map/ppermute | solution.py:465
  20.5 1.5 %shard_map.122 = (f32[2,128,128]{2,1,0:T(8,128)S(1)}, f32[256,256]{1,0:T(8,128)S(1)}, f32[2,128,128]{2,1,0:T(8,128)S(1)}, f32[2,128]{1,0:T(2,128)S(1)}) custom-call(s32[5]{0:T(128)S(1)} %stack.23.pos_ref, f32[2,128,128]{2,1,0:T(8,128)S(1)} %copy-done.2, f32[2,128,128]{2,1,0:T(8,128)S(1)} %collective-permute-done.w_ref.near_ref, ...), custom_call_target="tpu_custom_call" | custom-call | tf_op jit(solution)/shard_map/pallas_call | solution.py:484
  22.0 1.3 %collective-permute-start.7 = (f32[2,128,128]{2,1,0:T(8,128)S(1)}, f32[2,128,128]{2,1,0:T(8,128)S(1)}, u32[]{:S(2)}, u32[]{:S(2)}) collective-permute-start(f32[2,128,128]{2,1,0:T(8,128)S(1)} %get-tuple-element.63.p_ref), channel_id=1, source_target_pairs={{12,0},{13,1},{14,2},{15,3},{28,16},{29,17},{30,18},{31,19},{44,32... | collective-permute-start | bytes 393224 | tf_op jit(solution)/shard_map/ppermute | solution.py:490
  23.3 1.3 %collective-permute-start.6 = (f32[2,128,128]{2,1,0:T(8,128)S(1)}, f32[2,128,128]{2,1,0:T(8,128)S(1)}, u32[]{:S(2)}, u32[]{:S(2)}) collective-permute-start(f32[2,128,128]{2,1,0:T(8,128)S(1)} %get-tuple-element.63.p_ref), channel_id=1, source_target_pairs={{12,4},{8,0},{13,5},{9,1},{14,6},{10,2},{15,7},{11,3},{28,20},{24,... | collective-permute-start | bytes 393224 | tf_op jit(solution)/shard_map/ppermute | solution.py:489
  24.6 1.3 %collective-permute-start.5 = (f32[2,128,128]{2,1,0:T(8,128)S(1)}, f32[2,128,128]{2,1,0:T(8,128)S(1)}, u32[]{:S(2)}, u32[]{:S(2)}) collective-permute-start(f32[2,128,128]{2,1,0:T(8,128)S(1)} %get-tuple-element.63.p_ref), channel_id=1, source_target_pairs={{12,8},{8,4},{4,0},{13,9},{9,5},{5,1},{14,10},{10,6},{6,2},{15,11}... | collective-permute-start | bytes 393224 | tf_op jit(solution)/shard_map/ppermute | solution.py:488
  25.9 2.9 %shard_map.123 = (f32[256,256]{1,0:T(8,128)S(1)}, f32[256,256]{1,0:T(8,128)S(1)}, f32[256,256]{1,0:T(8,128)S(1)}, f32[256,256]{1,0:T(8,128)S(1)}, f32[2,256]{1,0:T(2,128)S(1)}) custom-call(f32[2]{0:T(128)S(1)} %copy-done.5, f32[1,2,256]{2,1,0:T(2,128)S(1)} %copy-done.4, f32[2,128,128]{2,1,0:T(8,128)S(1)} %get-tuple-element.64.w_ref, ...), custom_call_target="tpu_custom_call" | custom-call | tf_op jit(solution)/shard_map/pallas_call | solution.py:492
  28.8 1.8 %collective-permute-done.7.three_ref = f32[2,128,128]{2,1,0:T(8,128)S(1)} collective-permute-done((f32[2,128,128]{2,1,0:T(8,128)S(1)}, f32[2,128,128]{2,1,0:T(8,128)S(1)}, u32[]{:S(2)}, u32[]{:S(2)}) %collective-permute-start.7) | collective-permute-done | bytes 131104 | tf_op jit(solution)/shard_map/ppermute | solution.py:490
  30.5 2.0 %collective-permute-done.6.two_ref = f32[2,128,128]{2,1,0:T(8,128)S(1)} collective-permute-done((f32[2,128,128]{2,1,0:T(8,128)S(1)}, f32[2,128,128]{2,1,0:T(8,128)S(1)}, u32[]{:S(2)}, u32[]{:S(2)}) %collective-permute-start.6) | collective-permute-done | bytes 131104 | tf_op jit(solution)/shard_map/ppermute | solution.py:489
  32.6 2.5 %shard_map.124 = (f32[1024,256]{1,0:T(8,128)S(1)}, f32[1,2,256]{2,1,0:T(2,128)}) custom-call(s32[5]{0:T(128)S(1)} %stack.23.pos_ref, f32[2]{0:T(128)S(1)} %copy-done.5, f32[1,2,256]{2,1,0:T(2,128)S(1)} %copy-done.4, f32[2,128,128]{2,1,0:T(8,128)S(1)} %collective-permute-done.5.one_ref, f32[2,128,128]{2,1,0:T(8,128)S(1)} %collective-permute-done.6.two_ref, ...), custom_call_target="tpu_custom_call" | custom-call | tf_op jit(solution)/shard_map/pallas_call | solution.py:496
  35.1 3.4 %collective-permute-start.10 = (f32[1024,256]{1,0:T(8,128)S(1)}, f32[1024,256]{1,0:T(8,128)S(1)}, u32[]{:S(2)}, u32[]{:S(2)}) collective-permute-start(f32[1024,256]{1,0:T(8,128)S(1)} %get-tuple-element.79.all_ref.own_ref), channel_id=1, source_target_pairs={{0,16},{16,0},{32,48},{48,32},{64,80},{80,64},{96,112},{112,96},{1... | collective-permute-start | bytes 3145736 | tf_op jit(solution)/shard_map/ppermute | solution.py:389
  38.5 1.5 %shard_map.125 = (f32[256,512]{1,0:T(8,128)S(1)}, f32[256,512]{1,0:T(8,128)S(1)}, f32[256,512]{1,0:T(8,128)S(1)}, f32[256,512]{1,0:T(8,128)S(1)}) custom-call(s32[5]{0:T(128)S(1)} %stack.23.pos_ref, bf16[3,2048,256]{2,1,0:T(8,128)(2,1)S(1)} %copy-done, f32[1024,256]{1,0:T(8,128)S(1)} %get-tuple-element.79.all_ref.own_ref), custom_call_target="tpu_custom_call" | custom-call | tf_op jit(solution)/shard_map/pallas_call | solution.py:503
  40.0 1.9 %collective-permute-start.12 = (f32[256,512]{1,0:T(8,128)S(1)}, f32[256,512]{1,0:T(8,128)S(1)}, u32[]{:S(2)}, u32[]{:S(2)}) collective-permute-start(f32[256,512]{1,0:T(8,128)S(1)} %get-tuple-element.85), channel_id=1, source_target_pairs={{0,1},{1,2},{2,3},{3,0},{4,5},{5,6},{6,7},{7,4},{8,9},{9,10},{10,1... | collective-permute-start | bytes 1572872 | tf_op jit(solution)/shard_map/ppermute | solution.py:506
  41.9 1.5 %shard_map.126 = (f32[800,256]{1,0:T(8,128)S(1)}, f32[800,256]{1,0:T(8,128)S(1)}, f32[800,256]{1,0:T(8,128)S(1)}, f32[800,256]{1,0:T(8,128)S(1)}, f32[256,512]{1,0:T(8,128)S(1)}, /*index=5*/f32[256,512]{1,0:T(8,128)S(1)}) custom-call(s32[5]{0:T(128)S(1)} %stack.23.pos_ref, ...), custom_call_target="tpu_custom_call", output_to_operand_aliasing={{4}: (5, {}), {5}: (6, {})} | custom-call | tf_op jit(solution)/shard_map/pallas_call | solution.py:508
  43.5 2.6 %collective-permute-start.14 = (f32[800,256]{1,0:T(8,128)S(1)}, f32[800,256]{1,0:T(8,128)S(1)}, u32[]{:S(2)}, u32[]{:S(2)}) collective-permute-start(f32[800,256]{1,0:T(8,128)S(1)} %get-tuple-element.88), channel_id=1, source_target_pairs={{0,32},{4,36},{8,40},{12,44},{16,20},{20,24},{24,28},{28,16},{32,6... | collective-permute-start | bytes 2457608 | tf_op jit(solution)/shard_map/ppermute | solution.py:384
  46.2 2.2 %collective-permute-start.16 = (f32[800,256]{1,0:T(8,128)S(1)}, f32[800,256]{1,0:T(8,128)S(1)}, u32[]{:S(2)}, u32[]{:S(2)}) collective-permute-start(f32[800,256]{1,0:T(8,128)S(1)} %get-tuple-element.90), channel_id=1, source_target_pairs={{0,64},{4,68},{8,72},{12,76},{16,24},{20,28},{24,16},{28,20},{32,9... | collective-permute-start | bytes 2457608 | tf_op jit(solution)/shard_map/ppermute | solution.py:384
  48.4 2.6 %collective-permute-start.13 = (f32[256,512]{1,0:T(8,128)S(1)}, f32[256,512]{1,0:T(8,128)S(1)}, u32[]{:S(2)}, u32[]{:S(2)}) collective-permute-start(f32[256,512]{1,0:T(8,128)S(1)} %get-tuple-element.86), channel_id=1, source_target_pairs={{0,3},{1,0},{2,1},{3,2},{4,7},{5,4},{6,5},{7,6},{8,11},{9,8},{10,9... | collective-permute-start | bytes 1572872 | tf_op jit(solution)/shard_map/ppermute | solution.py:506
  51.0 5.4 %collective-permute-done.12.refs_0_ = f32[256,512]{1,0:T(8,128)S(1)} collective-permute-done((f32[256,512]{1,0:T(8,128)S(1)}, f32[256,512]{1,0:T(8,128)S(1)}, u32[]{:S(2)}, u32[]{:S(2)}) %collective-permute-start.12) | collective-permute-done | bytes 524320 | tf_op jit(solution)/shard_map/ppermute | solution.py:506
  56.3 1.1 collective-permute-start.11
  57.4 4.7 %collective-permute-done.13.refs_1_ = f32[256,512]{1,0:T(8,128)S(1)} collective-permute-done((f32[256,512]{1,0:T(8,128)S(1)}, f32[256,512]{1,0:T(8,128)S(1)}, u32[]{:S(2)}, u32[]{:S(2)}) %collective-permute-start.13) | collective-permute-done | bytes 524320 | tf_op jit(solution)/shard_map/ppermute | solution.py:506
  62.1 3.6 %collective-permute-done.16.far_ref = f32[800,256]{1,0:T(8,128)S(1)} collective-permute-done((f32[800,256]{1,0:T(8,128)S(1)}, f32[800,256]{1,0:T(8,128)S(1)}, u32[]{:S(2)}, u32[]{:S(2)}) %collective-permute-start.16) | collective-permute-done | bytes 819232 | tf_op jit(solution)/shard_map/ppermute | solution.py:384
  65.7 0.7 shard_map.127
  66.4 9.3 %collective-permute-start.17 = (f32[200,256]{1,0:T(8,128)S(1)}, f32[200,256]{1,0:T(8,128)S(1)}, u32[]{:S(2)}, u32[]{:S(2)}) collective-permute-start(f32[200,256]{1,0:T(8,128)S(1)} %get-tuple-element.92), channel_id=1, source_target_pairs={{0,4},{4,8},{8,12},{12,0},{16,48},{20,52},{24,56},{28,60},{32,36},... | collective-permute-start | bytes 614408 | tf_op jit(solution)/shard_map/ppermute | solution.py:384
  75.7 1.1 collective-permute-start.18
  76.7 2.0 %collective-permute-start.19 = (f32[200,256]{1,0:T(8,128)S(1)}, f32[200,256]{1,0:T(8,128)S(1)}, u32[]{:S(2)}, u32[]{:S(2)}) collective-permute-start(f32[200,256]{1,0:T(8,128)S(1)} %get-tuple-element.94), channel_id=1, source_target_pairs={{0,8},{4,12},{8,0},{12,4},{16,80},{20,84},{24,88},{28,92},{32,40},... | collective-permute-start | bytes 614408 | tf_op jit(solution)/shard_map/ppermute | solution.py:384
  78.7 1.4 %collective-permute-done.17.back_ref = f32[200,256]{1,0:T(8,128)S(1)} collective-permute-done((f32[200,256]{1,0:T(8,128)S(1)}, f32[200,256]{1,0:T(8,128)S(1)}, u32[]{:S(2)}, u32[]{:S(2)}) %collective-permute-start.17) | collective-permute-done | bytes 204832 | tf_op jit(solution)/shard_map/ppermute | solution.py:384
  80.6 2.9 %collective-permute-done.19.far_ref = f32[200,256]{1,0:T(8,128)S(1)} collective-permute-done((f32[200,256]{1,0:T(8,128)S(1)}, f32[200,256]{1,0:T(8,128)S(1)}, u32[]{:S(2)}, u32[]{:S(2)}) %collective-permute-start.19) | collective-permute-done | bytes 204832 | tf_op jit(solution)/shard_map/ppermute | solution.py:384
  83.5 1.4 %collective-permute-start.22 = (f32[200,256]{1,0:T(8,128)S(1)}, f32[200,256]{1,0:T(8,128)S(1)}, u32[]{:S(2)}, u32[]{:S(2)}) collective-permute-start(f32[200,256]{1,0:T(8,128)S(1)} %shard_map.128.own_ref), channel_id=1, source_target_pairs={{0,8},{4,12},{8,0},{12,4},{16,80},{20,84},{24,88},{28,92},{32,40},... | collective-permute-start | bytes 614408 | tf_op jit(solution)/shard_map/ppermute | solution.py:384
  84.9 0.9 collective-permute-start.21
  85.9 1.7 %collective-permute-start.20 = (f32[200,256]{1,0:T(8,128)S(1)}, f32[200,256]{1,0:T(8,128)S(1)}, u32[]{:S(2)}, u32[]{:S(2)}) collective-permute-start(f32[200,256]{1,0:T(8,128)S(1)} %shard_map.128.own_ref), channel_id=1, source_target_pairs={{0,12},{4,0},{8,4},{12,8},{16,112},{20,116},{24,120},{28,124},{32,... | collective-permute-start | bytes 614408 | tf_op jit(solution)/shard_map/ppermute | solution.py:384
  87.9 1.9 %collective-permute-done.22.far_ref = f32[200,256]{1,0:T(8,128)S(1)} collective-permute-done((f32[200,256]{1,0:T(8,128)S(1)}, f32[200,256]{1,0:T(8,128)S(1)}, u32[]{:S(2)}, u32[]{:S(2)}) %collective-permute-start.22) | collective-permute-done | bytes 204832 | tf_op jit(solution)/shard_map/ppermute | solution.py:384
  89.8 2.4 %collective-permute-done.21.back_ref = f32[200,256]{1,0:T(8,128)S(1)} collective-permute-done((f32[200,256]{1,0:T(8,128)S(1)}, f32[200,256]{1,0:T(8,128)S(1)}, u32[]{:S(2)}, u32[]{:S(2)}) %collective-permute-start.21) | collective-permute-done | bytes 204832 | tf_op jit(solution)/shard_map/ppermute | solution.py:384
  92.9 5.4 %collective-permute-start.25 = (f32[800,256]{1,0:T(8,128)S(1)}, f32[800,256]{1,0:T(8,128)S(1)}, u32[]{:S(2)}, u32[]{:S(2)}) collective-permute-start(f32[800,256]{1,0:T(8,128)S(1)} %shard_map.129.refs_0_), channel_id=1, source_target_pairs={{0,16},{16,0},{32,48},{48,32},{64,80},{80,64},{96,112},{112,96},{1... | collective-permute-start | bytes 2457608 | tf_op jit(solution)/shard_map/ppermute | solution.py:389
  98.3 2.7 %collective-permute-start.23 = (f32[800,256]{1,0:T(8,128)S(1)}, f32[800,256]{1,0:T(8,128)S(1)}, u32[]{:S(2)}, u32[]{:S(2)}) collective-permute-start(f32[800,256]{1,0:T(8,128)S(1)} %shard_map.129.refs_0_), channel_id=1, source_target_pairs={{0,96},{4,100},{8,104},{12,108},{16,28},{20,16},{24,20},{28,24},{3... | collective-permute-start | bytes 2457608 | tf_op jit(solution)/shard_map/ppermute | solution.py:384
  100.9 5.0 %collective-permute-done.26.refs_2_ = f32[800,256]{1,0:T(8,128)S(1)} collective-permute-done((f32[800,256]{1,0:T(8,128)S(1)}, f32[800,256]{1,0:T(8,128)S(1)}, u32[]{:S(2)}, u32[]{:S(2)}) %collective-permute-start.26) | collective-permute-done | bytes 819232 | tf_op jit(solution)/shard_map/ppermute | solution.py:384
  105.9 1.7 %shard_map.130 = (f32[3,2048,256]{2,1,0:T(8,128)}, f32[800,256]{1,0:T(8,128)S(1)}) custom-call(s32[5]{0:T(128)S(1)} %stack.23.pos_ref, f32[800,256]{1,0:T(8,128)S(1)} %shard_map.129.refs_0_, f32[800,256]{1,0:T(8,128)S(1)} %collective-permute-done.25.refs_1_.refs_4_, f32[800,256]{1,0:T(8,128)S(1)} %collective-permute-done.26.refs_2_), custom_call_target="tpu_custom_call", output_to_operand_aliasing={{1}: (3, {})} | custom-call | tf_op jit(solution)/shard_map/pallas_call | solution.py:528
  107.7 3.9 %collective-permute-start.29 = (f32[800,256]{1,0:T(8,128)S(1)}, f32[800,256]{1,0:T(8,128)S(1)}, u32[]{:S(2)}, u32[]{:S(2)}) collective-permute-start(f32[800,256]{1,0:T(8,128)S(1)} %get-tuple-element.95.refs_2_.refs_3_), channel_id=1, source_target_pairs={{0,16},{16,0},{32,48},{48,32},{64,80},{80,64},{96,112},{112,96},{1... | collective-permute-start | bytes 2457608 | tf_op jit(solution)/shard_map/ppermute | solution.py:389
  111.5 3.1 %collective-permute-done.24.refs_1_.refs_2_ = f32[800,256]{1,0:T(8,128)S(1)} collective-permute-done((f32[800,256]{1,0:T(8,128)S(1)}, f32[800,256]{1,0:T(8,128)S(1)}, u32[]{:S(2)}, u32[]{:S(2)}) %collective-permute-start.24) | collective-permute-done | bytes 819232 | tf_op jit(solution)/shard_map/ppermute | solution.py:384
  114.6 3.7 %collective-permute-start.28 = (f32[800,256]{1,0:T(8,128)S(1)}, f32[800,256]{1,0:T(8,128)S(1)}, u32[]{:S(2)}, u32[]{:S(2)}) collective-permute-start(f32[800,256]{1,0:T(8,128)S(1)} %collective-permute-done.24.refs_1_.refs_2_), channel_id=1, source_target_pairs={{0,16},{16,0},{32,48},{48,32},{64,80},{80,64},{96,112},{112,96},{1... | collective-permute-start | bytes 2457608 | tf_op jit(solution)/shard_map/ppermute | solution.py:389
  118.4 2.3 %shard_map.131.refs_8_ = f32[3,2048,256]{2,1,0:T(8,128)} custom-call(s32[5]{0:T(128)S(1)} %stack.23.pos_ref, f32[800,256]{1,0:T(8,128)S(1)} %collective-permute-done.23.refs_0_.refs_1_, f32[800,256]{1,0:T(8,128)S(1)} %collective-permute-done.24.refs_1_.refs_2_, f32[800,256]{1,0:T(8,128)S(1)} %get-tuple-element.95.refs_2_.refs_3_, ...), custom_call_target="tpu_custom_call", output_to_operand_aliasing={{}: (5, {})} | custom-call | tf_op jit(solution)/shard_map/pallas_call | solution.py:528
  120.7 0.8 collective-permute-done.27.refs_5_
  121.5 2.4 %shard_map.132 = (f32[3,2048,256]{2,1,0:T(8,128)}, f32[2,128,128]{2,1,0:T(8,128)}, f32[2,128]{1,0:T(2,128)}, f32[2]{0:T(128)}) custom-call(s32[5]{0:T(128)S(1)} %stack.23.pos_ref, f32[800,256]{1,0:T(8,128)S(1)} %shard_map.129.refs_0_, f32[800,256]{1,0:T(8,128)S(1)} %collective-permute-done.23.refs_0_.refs_1_, ...), custom_call_target="tpu_custom_call", output_to_operand_aliasing={{0}: (9, {})} | custom-call | tf_op jit(solution)/shard_map/pallas_call | solution.py:544
  (43 shorter events, 2.8 us)
Async XLA Ops:
  0.6 11.9 %copy-start.4 = (f32[1,2,256]{2,1,0:T(2,128)S(1)}, f32[1,2,256]{2,1,0:T(2,128)}, u32[]{:S(2)}) copy-start(f32[1,2,256]{2,1,0:T(2,128)} %gate_ref.7) | copy-start | bytes 6148
  0.6 11.9 %copy-start.5 = (f32[2]{0:T(128)S(1)}, f32[2]{0:T(128)}, u32[]{:S(2)}) copy-start(f32[2]{0:T(128)} %base_ref.7) | copy-start | bytes 28
  0.8 19.7 %copy-start.2 = (f32[2,128,128]{2,1,0:T(8,128)S(1)}, f32[2,128,128]{2,1,0:T(8,128)}, u32[]{:S(2)}) copy-start(f32[2,128,128]{2,1,0:T(8,128)} %init_ref.3) | copy-start | bytes 393220
  0.8 19.7 %copy-start.3 = (bf16[1,256,256]{2,1,0:T(8,128)(2,1)S(1)}, bf16[1,256,256]{2,1,0:T(8,128)(2,1)}, u32[]{:S(2)}) copy-start(bf16[1,256,256]{2,1,0:T(8,128)(2,1)} %up_ref.3) | copy-start | bytes 393220
  0.8 19.7 %copy-start.6 = (f32[2,128]{1,0:T(2,128)S(1)}, f32[2,128]{1,0:T(2,128)}, u32[]{:S(2)}) copy-start(f32[2,128]{1,0:T(2,128)} %gain_ref.1) | copy-start | bytes 3076
  6.5 13.0 %collective-permute-start.4 = (f32[256,1024]{1,0:T(8,128)S(1)}, f32[256,1024]{1,0:T(8,128)S(1)}, u32[]{:S(2)}, u32[]{:S(2)}) collective-permute-start(f32[256,1024]{1,0:T(8,128)S(1)} %get-tuple-element.62), channel_id=1, source_target_pairs={{0,16},{16,0},{32,48},{48,32},{64,80},{80,64},{96,112},{112,96},{1... | collective-permute-start | bytes 3145736 | tf_op jit(solution)/shard_map/ppermute | solution.py:389
  8.0 8.5 %collective-permute-start = (f32[2,128,128]{2,1,0:T(8,128)S(1)}, f32[2,128,128]{2,1,0:T(8,128)S(1)}, u32[]{:S(2)}, u32[]{:S(2)}) collective-permute-start(f32[2,128,128]{2,1,0:T(8,128)S(1)} %get-tuple-element.54), channel_id=1, source_target_pairs={{0,4},{8,12},{1,5},{9,13},{2,6},{10,14},{3,7},{11,15},{16,20},{24,... | collective-permute-start | bytes 393224 | tf_op jit(solution)/shard_map/ppermute | solution.py:462
  11.3 9.1 %collective-permute-start.3 = (f32[2,128,128]{2,1,0:T(8,128)S(1)}, f32[2,128,128]{2,1,0:T(8,128)S(1)}, u32[]{:S(2)}, u32[]{:S(2)}) collective-permute-start(f32[2,128,128]{2,1,0:T(8,128)S(1)} %get-tuple-element.55.d_ref), channel_id=1, source_target_pairs={{8,12},{4,0},{9,13},{5,1},{10,14},{6,2},{11,15},{7,3},{24,28},{20,... | collective-permute-start | bytes 393224 | tf_op jit(solution)/shard_map/ppermute | solution.py:463
  16.5 22.0 %copy-start = (bf16[3,2048,256]{2,1,0:T(8,128)(2,1)S(1)}, bf16[3,2048,256]{2,1,0:T(8,128)(2,1)}, u32[]{:S(2)}) copy-start(bf16[3,2048,256]{2,1,0:T(8,128)(2,1)} %w_ref.1) | copy-start | bytes 9437188
  16.7 3.7 %collective-permute-start.2 = (f32[2,128,128]{2,1,0:T(8,128)S(1)}, f32[2,128,128]{2,1,0:T(8,128)S(1)}, u32[]{:S(2)}, u32[]{:S(2)}) collective-permute-start(f32[2,128,128]{2,1,0:T(8,128)S(1)} %shard_map.120), channel_id=1, source_target_pairs={{4,12},{5,13},{6,14},{7,15},{20,28},{21,29},{22,30},{23,31},{36,44... | collective-permute-start | bytes 393224 | tf_op jit(solution)/shard_map/ppermute | solution.py:481
  17.5 2.9 %collective-permute-start.1 = (f32[2,128,128]{2,1,0:T(8,128)S(1)}, f32[2,128,128]{2,1,0:T(8,128)S(1)}, u32[]{:S(2)}, u32[]{:S(2)}) collective-permute-start(f32[2,128,128]{2,1,0:T(8,128)S(1)} %shard_map.120), channel_id=1, source_target_pairs={{4,8},{5,9},{6,10},{7,11},{20,24},{21,25},{22,26},{23,27},{36,40},... | collective-permute-start | bytes 393224 | tf_op jit(solution)/shard_map/ppermute | solution.py:480
  18.2 10.6 %collective-permute-start.9 = (f32[2,128,128]{2,1,0:T(8,128)S(1)}, f32[2,128,128]{2,1,0:T(8,128)S(1)}, u32[]{:S(2)}, u32[]{:S(2)}) collective-permute-start(f32[2,128,128]{2,1,0:T(8,128)S(1)} %get-tuple-element.55.d_ref), channel_id=1, source_target_pairs={{8,0},{9,1},{10,2},{11,3},{24,16},{25,17},{26,18},{27,19},{40,32},... | collective-permute-start | bytes 393224 | tf_op jit(solution)/shard_map/ppermute | solution.py:465
  19.5 9.3 %collective-permute-start.8 = (f32[2,128,128]{2,1,0:T(8,128)S(1)}, f32[2,128,128]{2,1,0:T(8,128)S(1)}, u32[]{:S(2)}, u32[]{:S(2)}) collective-permute-start(f32[2,128,128]{2,1,0:T(8,128)S(1)} %get-tuple-element.55.d_ref), channel_id=1, source_target_pairs={{8,4},{9,5},{10,6},{11,7},{24,20},{25,21},{26,22},{27,23},{40,36},... | collective-permute-start | bytes 393224 | tf_op jit(solution)/shard_map/ppermute | solution.py:464
  22.0 8.5 %collective-permute-start.7 = (f32[2,128,128]{2,1,0:T(8,128)S(1)}, f32[2,128,128]{2,1,0:T(8,128)S(1)}, u32[]{:S(2)}, u32[]{:S(2)}) collective-permute-start(f32[2,128,128]{2,1,0:T(8,128)S(1)} %get-tuple-element.63.p_ref), channel_id=1, source_target_pairs={{12,0},{13,1},{14,2},{15,3},{28,16},{29,17},{30,18},{31,19},{44,32... | collective-permute-start | bytes 393224 | tf_op jit(solution)/shard_map/ppermute | solution.py:490
  23.3 9.2 %collective-permute-start.6 = (f32[2,128,128]{2,1,0:T(8,128)S(1)}, f32[2,128,128]{2,1,0:T(8,128)S(1)}, u32[]{:S(2)}, u32[]{:S(2)}) collective-permute-start(f32[2,128,128]{2,1,0:T(8,128)S(1)} %get-tuple-element.63.p_ref), channel_id=1, source_target_pairs={{12,4},{8,0},{13,5},{9,1},{14,6},{10,2},{15,7},{11,3},{28,20},{24,... | collective-permute-start | bytes 393224 | tf_op jit(solution)/shard_map/ppermute | solution.py:489
  24.6 7.9 %collective-permute-start.5 = (f32[2,128,128]{2,1,0:T(8,128)S(1)}, f32[2,128,128]{2,1,0:T(8,128)S(1)}, u32[]{:S(2)}, u32[]{:S(2)}) collective-permute-start(f32[2,128,128]{2,1,0:T(8,128)S(1)} %get-tuple-element.63.p_ref), channel_id=1, source_target_pairs={{12,8},{8,4},{4,0},{13,9},{9,5},{5,1},{14,10},{10,6},{6,2},{15,11}... | collective-permute-start | bytes 393224 | tf_op jit(solution)/shard_map/ppermute | solution.py:488
  35.1 6.8 %collective-permute-start.10 = (f32[1024,256]{1,0:T(8,128)S(1)}, f32[1024,256]{1,0:T(8,128)S(1)}, u32[]{:S(2)}, u32[]{:S(2)}) collective-permute-start(f32[1024,256]{1,0:T(8,128)S(1)} %get-tuple-element.79.all_ref.own_ref), channel_id=1, source_target_pairs={{0,16},{16,0},{32,48},{48,32},{64,80},{80,64},{96,112},{112,96},{1... | collective-permute-start | bytes 3145736 | tf_op jit(solution)/shard_map/ppermute | solution.py:389
  40.0 16.3 %collective-permute-start.12 = (f32[256,512]{1,0:T(8,128)S(1)}, f32[256,512]{1,0:T(8,128)S(1)}, u32[]{:S(2)}, u32[]{:S(2)}) collective-permute-start(f32[256,512]{1,0:T(8,128)S(1)} %get-tuple-element.85), channel_id=1, source_target_pairs={{0,1},{1,2},{2,3},{3,0},{4,5},{5,6},{6,7},{7,4},{8,9},{9,10},{10,1... | collective-permute-start | bytes 1572872 | tf_op jit(solution)/shard_map/ppermute | solution.py:506
  43.5 18.7 %collective-permute-start.14 = (f32[800,256]{1,0:T(8,128)S(1)}, f32[800,256]{1,0:T(8,128)S(1)}, u32[]{:S(2)}, u32[]{:S(2)}) collective-permute-start(f32[800,256]{1,0:T(8,128)S(1)} %get-tuple-element.88), channel_id=1, source_target_pairs={{0,32},{4,36},{8,40},{12,44},{16,20},{20,24},{24,28},{28,16},{32,6... | collective-permute-start | bytes 2457608 | tf_op jit(solution)/shard_map/ppermute | solution.py:384
  46.1 16.0 %collective-permute-start.15 = (f32[800,256]{1,0:T(8,128)S(1)}, f32[800,256]{1,0:T(8,128)S(1)}, u32[]{:S(2)}, u32[]{:S(2)}) collective-permute-start(f32[800,256]{1,0:T(8,128)S(1)} %get-tuple-element.89), channel_id=1, source_target_pairs={{0,96},{4,100},{8,104},{12,108},{16,28},{20,16},{24,20},{28,24},{3... | collective-permute-start | bytes 2457608 | tf_op jit(solution)/shard_map/ppermute | solution.py:384
  46.2 19.5 %collective-permute-start.16 = (f32[800,256]{1,0:T(8,128)S(1)}, f32[800,256]{1,0:T(8,128)S(1)}, u32[]{:S(2)}, u32[]{:S(2)}) collective-permute-start(f32[800,256]{1,0:T(8,128)S(1)} %get-tuple-element.90), channel_id=1, source_target_pairs={{0,64},{4,68},{8,72},{12,76},{16,24},{20,28},{24,16},{28,20},{32,9... | collective-permute-start | bytes 2457608 | tf_op jit(solution)/shard_map/ppermute | solution.py:384
  48.4 13.8 %collective-permute-start.13 = (f32[256,512]{1,0:T(8,128)S(1)}, f32[256,512]{1,0:T(8,128)S(1)}, u32[]{:S(2)}, u32[]{:S(2)}) collective-permute-start(f32[256,512]{1,0:T(8,128)S(1)} %get-tuple-element.86), channel_id=1, source_target_pairs={{0,3},{1,0},{2,1},{3,2},{4,7},{5,4},{6,5},{7,6},{8,11},{9,8},{10,9... | collective-permute-start | bytes 1572872 | tf_op jit(solution)/shard_map/ppermute | solution.py:506
  56.3 31.3 %collective-permute-start.11 = (f32[256,512]{1,0:T(8,128)S(1)}, f32[256,512]{1,0:T(8,128)S(1)}, u32[]{:S(2)}, u32[]{:S(2)}) collective-permute-start(f32[256,512]{1,0:T(8,128)S(1)} %get-tuple-element.84), channel_id=1, source_target_pairs={{0,2},{1,3},{2,0},{3,1},{4,6},{5,7},{6,4},{7,5},{8,10},{9,11},{10,... | collective-permute-start | bytes 1572872 | tf_op jit(solution)/shard_map/ppermute | solution.py:506
  66.4 13.7 %collective-permute-start.17 = (f32[200,256]{1,0:T(8,128)S(1)}, f32[200,256]{1,0:T(8,128)S(1)}, u32[]{:S(2)}, u32[]{:S(2)}) collective-permute-start(f32[200,256]{1,0:T(8,128)S(1)} %get-tuple-element.92), channel_id=1, source_target_pairs={{0,4},{4,8},{8,12},{12,0},{16,48},{20,52},{24,56},{28,60},{32,36},... | collective-permute-start | bytes 614408 | tf_op jit(solution)/shard_map/ppermute | solution.py:384
  75.7 4.9 %collective-permute-start.18 = (f32[200,256]{1,0:T(8,128)S(1)}, f32[200,256]{1,0:T(8,128)S(1)}, u32[]{:S(2)}, u32[]{:S(2)}) collective-permute-start(f32[200,256]{1,0:T(8,128)S(1)} %get-tuple-element.93), channel_id=1, source_target_pairs={{0,12},{4,0},{8,4},{12,8},{16,112},{20,116},{24,120},{28,124},{32,... | collective-permute-start | bytes 614408 | tf_op jit(solution)/shard_map/ppermute | solution.py:384
  76.7 6.7 %collective-permute-start.19 = (f32[200,256]{1,0:T(8,128)S(1)}, f32[200,256]{1,0:T(8,128)S(1)}, u32[]{:S(2)}, u32[]{:S(2)}) collective-permute-start(f32[200,256]{1,0:T(8,128)S(1)} %get-tuple-element.94), channel_id=1, source_target_pairs={{0,8},{4,12},{8,0},{12,4},{16,80},{20,84},{24,88},{28,92},{32,40},... | collective-permute-start | bytes 614408 | tf_op jit(solution)/shard_map/ppermute | solution.py:384
  83.5 6.3 %collective-permute-start.22 = (f32[200,256]{1,0:T(8,128)S(1)}, f32[200,256]{1,0:T(8,128)S(1)}, u32[]{:S(2)}, u32[]{:S(2)}) collective-permute-start(f32[200,256]{1,0:T(8,128)S(1)} %shard_map.128.own_ref), channel_id=1, source_target_pairs={{0,8},{4,12},{8,0},{12,4},{16,80},{20,84},{24,88},{28,92},{32,40},... | collective-permute-start | bytes 614408 | tf_op jit(solution)/shard_map/ppermute | solution.py:384
  84.9 7.3 %collective-permute-start.21 = (f32[200,256]{1,0:T(8,128)S(1)}, f32[200,256]{1,0:T(8,128)S(1)}, u32[]{:S(2)}, u32[]{:S(2)}) collective-permute-start(f32[200,256]{1,0:T(8,128)S(1)} %shard_map.128.own_ref), channel_id=1, source_target_pairs={{0,4},{4,8},{8,12},{12,0},{16,48},{20,52},{24,56},{28,60},{32,36},... | collective-permute-start | bytes 614408 | tf_op jit(solution)/shard_map/ppermute | solution.py:384
  85.9 6.3 %collective-permute-start.20 = (f32[200,256]{1,0:T(8,128)S(1)}, f32[200,256]{1,0:T(8,128)S(1)}, u32[]{:S(2)}, u32[]{:S(2)}) collective-permute-start(f32[200,256]{1,0:T(8,128)S(1)} %shard_map.128.own_ref), channel_id=1, source_target_pairs={{0,12},{4,0},{8,4},{12,8},{16,112},{20,116},{24,120},{28,124},{32,... | collective-permute-start | bytes 614408 | tf_op jit(solution)/shard_map/ppermute | solution.py:384
  87.8 32.8 %copy-start.1 = (bf16[1,256,512]{2,1,0:T(8,128)(2,1)}, bf16[1,256,512]{2,1,0:T(8,128)(2,1)S(1)}, u32[]{:S(2)}) copy-start(bf16[1,256,512]{2,1,0:T(8,128)(2,1)S(1)} %fusion.refs_0_) | copy-start | bytes 786436
  92.8 13.1 %collective-permute-start.26 = (f32[800,256]{1,0:T(8,128)S(1)}, f32[800,256]{1,0:T(8,128)S(1)}, u32[]{:S(2)}, u32[]{:S(2)}) collective-permute-start(f32[800,256]{1,0:T(8,128)S(1)} %shard_map.129.refs_0_), channel_id=1, source_target_pairs={{0,64},{4,68},{8,72},{12,76},{16,24},{20,28},{24,16},{28,20},{32,9... | collective-permute-start | bytes 2457608 | tf_op jit(solution)/shard_map/ppermute | solution.py:384
  92.9 13.0 %collective-permute-start.25 = (f32[800,256]{1,0:T(8,128)S(1)}, f32[800,256]{1,0:T(8,128)S(1)}, u32[]{:S(2)}, u32[]{:S(2)}) collective-permute-start(f32[800,256]{1,0:T(8,128)S(1)} %shard_map.129.refs_0_), channel_id=1, source_target_pairs={{0,16},{16,0},{32,48},{48,32},{64,80},{80,64},{96,112},{112,96},{1... | collective-permute-start | bytes 2457608 | tf_op jit(solution)/shard_map/ppermute | solution.py:389
  98.3 16.4 %collective-permute-start.24 = (f32[800,256]{1,0:T(8,128)S(1)}, f32[800,256]{1,0:T(8,128)S(1)}, u32[]{:S(2)}, u32[]{:S(2)}) collective-permute-start(f32[800,256]{1,0:T(8,128)S(1)} %shard_map.129.refs_0_), channel_id=1, source_target_pairs={{0,32},{4,36},{8,40},{12,44},{16,20},{20,24},{24,28},{28,16},{32,6... | collective-permute-start | bytes 2457608 | tf_op jit(solution)/shard_map/ppermute | solution.py:384
  98.3 20.1 %collective-permute-start.23 = (f32[800,256]{1,0:T(8,128)S(1)}, f32[800,256]{1,0:T(8,128)S(1)}, u32[]{:S(2)}, u32[]{:S(2)}) collective-permute-start(f32[800,256]{1,0:T(8,128)S(1)} %shard_map.129.refs_0_), channel_id=1, source_target_pairs={{0,96},{4,100},{8,104},{12,108},{16,28},{20,16},{24,20},{28,24},{3... | collective-permute-start | bytes 2457608 | tf_op jit(solution)/shard_map/ppermute | solution.py:384
  107.7 10.7 %collective-permute-start.29 = (f32[800,256]{1,0:T(8,128)S(1)}, f32[800,256]{1,0:T(8,128)S(1)}, u32[]{:S(2)}, u32[]{:S(2)}) collective-permute-start(f32[800,256]{1,0:T(8,128)S(1)} %get-tuple-element.95.refs_2_.refs_3_), channel_id=1, source_target_pairs={{0,16},{16,0},{32,48},{48,32},{64,80},{80,64},{96,112},{112,96},{1... | collective-permute-start | bytes 2457608 | tf_op jit(solution)/shard_map/ppermute | solution.py:389
  114.6 6.1 %collective-permute-start.28 = (f32[800,256]{1,0:T(8,128)S(1)}, f32[800,256]{1,0:T(8,128)S(1)}, u32[]{:S(2)}, u32[]{:S(2)}) collective-permute-start(f32[800,256]{1,0:T(8,128)S(1)} %collective-permute-done.24.refs_1_.refs_2_), channel_id=1, source_target_pairs={{0,16},{16,0},{32,48},{48,32},{64,80},{80,64},{96,112},{112,96},{1... | collective-permute-start | bytes 2457608 | tf_op jit(solution)/shard_map/ppermute | solution.py:389
  118.4 3.1 %collective-permute-start.27 = (f32[800,256]{1,0:T(8,128)S(1)}, f32[800,256]{1,0:T(8,128)S(1)}, u32[]{:S(2)}, u32[]{:S(2)}) collective-permute-start(f32[800,256]{1,0:T(8,128)S(1)} %collective-permute-done.23.refs_0_.refs_1_), channel_id=1, source_target_pairs={{0,16},{16,0},{32,48},{48,32},{64,80},{80,64},{96,112},{112,96},{1... | collective-permute-start | bytes 2457608 | tf_op jit(solution)/shard_map/ppermute | solution.py:389

commit v8 on v7

--- a/solution.py
+++ b/solution.py
@@ -91,34 +91,28 @@
     i, j = places(n)
     strict = (i // MB) > (j // MB)
     heads = range(init_ref.shape[0])
-    ks, kts, es, lows = [], [], [], []
+    kraws = [kraw_all[:, span(h)] for h in heads]
+    ninvs = [lax.rsqrt(jnp.sum(kraw * kraw, -1, keepdims=True) + 1e-06) for kraw in kraws]
+    ks = [kraw * ninv for kraw, ninv in zip(kraws, ninvs)]
+    kts = [k.T for k in ks]
+    es = [rates_of(base_ref, gate_ref, h)[1] for h in heads]
+    grams = [dot(k, kt, NN, 3) for k, kt in zip(ks, kts)]
+    inverses = unit_lower_inverses([jnp.where(strict, gram * e, 0.0) for gram, e in zip(grams, es)])
+    a, b = places(HS)
+    bts = [dot(kts[h] * es[h], inverses[h], NN, 3) for h in heads]
+    decays = [jnp.where(a == b, 1.0, 0.0) - dot(bts[h], ks[h], NN, 3) for h in heads]
+    offsets = [dot(bts[h], v_all[:, span(h)], NN, 3) for h in heads]
+    firsts = [dot(decays[h], init_ref[h], NN, 3) + offsets[h] for h in heads]
+    v_ref[...] = v_all
     for h in heads:
-        kraw = kraw_all[:, span(h)]
-        ninv = lax.rsqrt(jnp.sum(kraw * kraw, -1, keepdims=True) + 1e-06)
-        k = kraw * ninv
-        kt = k.T
-        _, e = rates_of(base_ref, gate_ref, h)
-        gram = dot(k, kt, NN, 3)
-        ninv_ref[h] = jnp.broadcast_to(ninv, (n, HS))
-        k_ref[:, span(h)] = k
-        gram_ref[h] = gram
-        ks.append(k)
-        kts.append(kt)
-        es.append(e)
-        lows.append(jnp.where(strict, gram * e, 0.0))
-    v_ref[...] = v_all
-    inverses = unit_lower_inverses(lows)
-    a, b = places(HS)
-    for h in heads:
-        bt = dot(kts[h] * es[h], inverses[h], NN, 3)
+        send_ref[h] = jnp.where(pos_ref[4] == 0, firsts[h], offsets[h])
+        d_ref[h] = decays[h]
+        o_ref[h] = offsets[h]
+        k_ref[:, span(h)] = ks[h]
+        ninv_ref[h] = jnp.broadcast_to(ninvs[h], (n, HS))
+        gram_ref[h] = grams[h]
         inv_ref[h] = inverses[h]
-        bt_ref[h] = bt
-        decay = jnp.where(a == b, 1.0, 0.0) - dot(bt, ks[h], NN, 3)
-        offset = dot(bt, v_all[:, span(h)], NN, 3)
-        d_ref[h] = decay
-        o_ref[h] = offset
-        first = dot(decay, init_ref[h], NN, 3) + offset
-        send_ref[h] = jnp.where(pos_ref[4] == 0, first, offset)
+        bt_ref[h] = bts[h]
 
 
 def reach_kernel(
@@ -512,7 +506,7 @@
     from_back, from_ahead, from_far = along_head(quarters[1], 1), along_head(near_two, 3), along_head(far_quarter, 2)
 
     piece = vmem(3 * SLICE + PIECE // RING, wide)
-    pieces = whole(split_kernel, (piece,) * RING, [SM] + [VM] * 4 + [anywhere] * 2)(pos, own, *away, from_back, from_ahead)
+    pieces = whole(split_kernel, (piece,) * RING, [SM] + [VM] * 4 + [anywhere])(pos, own, *away, from_back)
     grad_tokens = ((quarters[0] + from_far) + (from_back + from_ahead)).astype(BF).reshape(1, n, -1)
     own, away = pieces[0], pieces[1:]
     part_sum = whole(sum_kernel, piece, [VM] * 4)(own, *round_turn(away, False))

time: 124 us -> 124 us (level)
  the two profiles are of different devices: /device:TPU:1 before, /device:TPU:123 now
where the time goes in v8:
time: 124 us
  starting transfers between devices  58 us (47%)
  waiting for transfers between devices  37.1 us (30%)
  Pallas kernels  27.6 us (22%)
    ppermute x6, starting transfers between devices, swap(): return lax.ppermute(value, 'dp', [(i, i ^ 1) for i in range(2 * RING)])  30.4 us
    ppermute x12, waiting for transfers between devices, round_turn(): lax.ppermute(chunk, ('dp', 'ctx'), moves(first, turn))  26.6 us
    ppermute x12, starting transfers between devices, round_turn(): lax.ppermute(chunk, ('dp', 'ctx'), moves(first, turn))  14 us
    pallas_call x1, Pallas kernels, body(): pl.pallas_call(maps_kernel, grid=(1,), out_shape=(wide_f32, wide_f32, vme...  5.56 us
    ppermute x3, waiting for transfers between devices, along_head(): lax.ppermute(terms, 'head', [(i, (i + turn) % RING) for i in range(RING)])  5.06 us
    pallas_call x2, Pallas kernels, place(): pl.pallas_call(functools.partial(place_kernel, which=which), out_shape=(o...  4.03 us
    pallas_call x1, Pallas kernels, body(): pl.pallas_call(reach_kernel, grid=(1,), out_shape=(wide_f32, square, wide...  3.89 us
    ppermute x1, waiting for transfers between devices, body(): far = lax.ppermute(second, 'ctx', [(1, 3)])  3.65 us
  transfers between devices with their start and end apart: 30, of which 15 were waited for; matrix products, arithmetic and copies ran while one was open for 0% of the time, Pallas kernels for 13%

profile of v8, /device:TPU:123, one launch (start us, length us, event | category | flops | bytes accessed | tf_op | source)
XLA Modules:
  0.0 124.2 jit_solution(9095841358075029594)
XLA Ops:
  0.8 5.6 %shard_map.118 = (f32[256,256]{1,0:T(8,128)S(1)}, f32[256,256]{1,0:T(8,128)S(1)}, f32[2,256,128]{2,1,0:T(8,128)S(1)}, f32[2,256,256]{2,1,0:T(8,128)S(1)}, f32[2,...) custom-call(s32[5]{0:T(128)S(1)} %stack.23.pos_ref, ...), custom_call_target="tpu_custom_call" | custom-call | tf_op jit(solution)/shard_map/pallas_call | solution.py:444
  6.3 0.8 collective-permute-start.4
  7.1 1.3 %collective-permute-start = (f32[2,128,128]{2,1,0:T(8,128)S(1)}, f32[2,128,128]{2,1,0:T(8,128)S(1)}, u32[]{:S(2)}, u32[]{:S(2)}) collective-permute-start(f32[2,128,128]{2,1,0:T(8,128)S(1)} %get-tuple-element.54), channel_id=1, source_target_pairs={{0,4},{8,12},{1,5},{9,13},{2,6},{10,14},{3,7},{11,15},{16,20},{24,... | collective-permute-start | bytes 393224 | tf_op jit(solution)/shard_map/ppermute | solution.py:456
  8.4 1.3 %collective-permute-start.3 = (f32[2,128,128]{2,1,0:T(8,128)S(1)}, f32[2,128,128]{2,1,0:T(8,128)S(1)}, u32[]{:S(2)}, u32[]{:S(2)}) collective-permute-start(f32[2,128,128]{2,1,0:T(8,128)S(1)} %get-tuple-element.55.d_ref), channel_id=1, source_target_pairs={{8,12},{4,0},{9,13},{5,1},{10,14},{6,2},{11,15},{7,3},{24,28},{20,... | collective-permute-start | bytes 393224 | tf_op jit(solution)/shard_map/ppermute | solution.py:457
  9.7 3.9 %shard_map.119 = (f32[256,256]{1,0:T(8,128)S(1)}, f32[2,256,256]{2,1,0:T(8,128)S(1)}, f32[256,256]{1,0:T(8,128)S(1)}, f32[256,256]{1,0:T(8,128)S(1)}, f32[256,25...) custom-call(s32[5]{0:T(128)S(1)} %stack.23.pos_ref, f32[2]{0:T(128)S(1)} %copy-done.5, ...), custom_call_target="tpu_custom_call" | custom-call | tf_op jit(solution)/shard_map/pallas_call | solution.py:462
  14.3 1.4 %collective-permute-start.2 = (f32[2,128,128]{2,1,0:T(8,128)S(1)}, f32[2,128,128]{2,1,0:T(8,128)S(1)}, u32[]{:S(2)}, u32[]{:S(2)}) collective-permute-start(f32[2,128,128]{2,1,0:T(8,128)S(1)} %shard_map.120), channel_id=1, source_target_pairs={{4,12},{5,13},{6,14},{7,15},{20,28},{21,29},{22,30},{23,31},{36,44... | collective-permute-start | bytes 393224 | tf_op jit(solution)/shard_map/ppermute | solution.py:475
  15.7 0.7 collective-permute-start.1
  16.4 0.7 collective-permute-start.9
  17.1 0.7 collective-permute-start.8
  18.0 3.7 %collective-permute-done.2.far_ref = f32[2,128,128]{2,1,0:T(8,128)S(1)} collective-permute-done((f32[2,128,128]{2,1,0:T(8,128)S(1)}, f32[2,128,128]{2,1,0:T(8,128)S(1)}, u32[]{:S(2)}, u32[]{:S(2)}) %collective-permute-start.2) | collective-permute-done | bytes 131104 | tf_op jit(solution)/shard_map/ppermute | solution.py:475
  21.7 1.5 %shard_map.122 = (f32[2,128,128]{2,1,0:T(8,128)S(1)}, f32[256,256]{1,0:T(8,128)S(1)}, f32[2,128,128]{2,1,0:T(8,128)S(1)}, f32[2,128]{1,0:T(2,128)S(1)}) custom-call(s32[5]{0:T(128)S(1)} %stack.23.pos_ref, f32[2,128,128]{2,1,0:T(8,128)S(1)} %copy-done.2, f32[2,128,128]{2,1,0:T(8,128)S(1)} %collective-permute-done.w_ref.near_ref, ...), custom_call_target="tpu_custom_call" | custom-call | tf_op jit(solution)/shard_map/pallas_call | solution.py:478
  23.2 1.3 %collective-permute-start.7 = (f32[2,128,128]{2,1,0:T(8,128)S(1)}, f32[2,128,128]{2,1,0:T(8,128)S(1)}, u32[]{:S(2)}, u32[]{:S(2)}) collective-permute-start(f32[2,128,128]{2,1,0:T(8,128)S(1)} %get-tuple-element.63.p_ref), channel_id=1, source_target_pairs={{12,0},{13,1},{14,2},{15,3},{28,16},{29,17},{30,18},{31,19},{44,32... | collective-permute-start | bytes 393224 | tf_op jit(solution)/shard_map/ppermute | solution.py:484
  24.5 2.5 %collective-permute-start.6 = (f32[2,128,128]{2,1,0:T(8,128)S(1)}, f32[2,128,128]{2,1,0:T(8,128)S(1)}, u32[]{:S(2)}, u32[]{:S(2)}) collective-permute-start(f32[2,128,128]{2,1,0:T(8,128)S(1)} %get-tuple-element.63.p_ref), channel_id=1, source_target_pairs={{12,4},{8,0},{13,5},{9,1},{14,6},{10,2},{15,7},{11,3},{28,20},{24,... | collective-permute-start | bytes 393224 | tf_op jit(solution)/shard_map/ppermute | solution.py:483
  27.0 1.6 %collective-permute-start.5 = (f32[2,128,128]{2,1,0:T(8,128)S(1)}, f32[2,128,128]{2,1,0:T(8,128)S(1)}, u32[]{:S(2)}, u32[]{:S(2)}) collective-permute-start(f32[2,128,128]{2,1,0:T(8,128)S(1)} %get-tuple-element.63.p_ref), channel_id=1, source_target_pairs={{12,8},{8,4},{4,0},{13,9},{9,5},{5,1},{14,10},{10,6},{6,2},{15,11}... | collective-permute-start | bytes 393224 | tf_op jit(solution)/shard_map/ppermute | solution.py:482
  28.6 2.9 %shard_map.123 = (f32[256,256]{1,0:T(8,128)S(1)}, f32[256,256]{1,0:T(8,128)S(1)}, f32[256,256]{1,0:T(8,128)S(1)}, f32[256,256]{1,0:T(8,128)S(1)}, f32[2,256]{1,0:T(2,128)S(1)}) custom-call(f32[2]{0:T(128)S(1)} %copy-done.5, f32[1,2,256]{2,1,0:T(2,128)S(1)} %copy-done.4, f32[2,128,128]{2,1,0:T(8,128)S(1)} %get-tuple-element.64.w_ref, ...), custom_call_target="tpu_custom_call" | custom-call | tf_op jit(solution)/shard_map/pallas_call | solution.py:486
  31.5 2.5 %shard_map.124 = (f32[1024,256]{1,0:T(8,128)S(1)}, f32[1,2,256]{2,1,0:T(2,128)}) custom-call(s32[5]{0:T(128)S(1)} %stack.23.pos_ref, f32[2]{0:T(128)S(1)} %copy-done.5, f32[1,2,256]{2,1,0:T(2,128)S(1)} %copy-done.4, f32[2,128,128]{2,1,0:T(8,128)S(1)} %collective-permute-done.5.one_ref, f32[2,128,128]{2,1,0:T(8,128)S(1)} %collective-permute-done.6.two_ref, ...), custom_call_target="tpu_custom_call" | custom-call | tf_op jit(solution)/shard_map/pallas_call | solution.py:490
  34.1 2.2 %collective-permute-start.10 = (f32[1024,256]{1,0:T(8,128)S(1)}, f32[1024,256]{1,0:T(8,128)S(1)}, u32[]{:S(2)}, u32[]{:S(2)}) collective-permute-start(f32[1024,256]{1,0:T(8,128)S(1)} %get-tuple-element.79.all_ref.own_ref), channel_id=1, source_target_pairs={{0,16},{16,0},{32,48},{48,32},{64,80},{80,64},{96,112},{112,96},{1... | collective-permute-start | bytes 3145736 | tf_op jit(solution)/shard_map/ppermute | solution.py:383
  36.2 1.5 %shard_map.125 = (f32[256,512]{1,0:T(8,128)S(1)}, f32[256,512]{1,0:T(8,128)S(1)}, f32[256,512]{1,0:T(8,128)S(1)}, f32[256,512]{1,0:T(8,128)S(1)}) custom-call(s32[5]{0:T(128)S(1)} %stack.23.pos_ref, bf16[3,2048,256]{2,1,0:T(8,128)(2,1)S(1)} %copy-done, f32[1024,256]{1,0:T(8,128)S(1)} %get-tuple-element.79.all_ref.own_ref), custom_call_target="tpu_custom_call" | custom-call | tf_op jit(solution)/shard_map/pallas_call | solution.py:497
  38.5 1.5 %shard_map.126 = (f32[800,256]{1,0:T(8,128)S(1)}, f32[800,256]{1,0:T(8,128)S(1)}, f32[800,256]{1,0:T(8,128)S(1)}, f32[800,256]{1,0:T(8,128)S(1)}, f32[256,512]{1,0:T(8,128)S(1)}, /*index=5*/f32[256,512]{1,0:T(8,128)S(1)}) custom-call(s32[5]{0:T(128)S(1)} %stack.23.pos_ref, ...), custom_call_target="tpu_custom_call", output_to_operand_aliasing={{4}: (5, {}), {5}: (6, {})} | custom-call | tf_op jit(solution)/shard_map/pallas_call | solution.py:502
  40.0 1.3 %collective-permute-start.14 = (f32[800,256]{1,0:T(8,128)S(1)}, f32[800,256]{1,0:T(8,128)S(1)}, u32[]{:S(2)}, u32[]{:S(2)}) collective-permute-start(f32[800,256]{1,0:T(8,128)S(1)} %get-tuple-element.88), channel_id=1, source_target_pairs={{0,32},{4,36},{8,40},{12,44},{16,20},{20,24},{24,28},{28,16},{32,6... | collective-permute-start | bytes 2457608 | tf_op jit(solution)/shard_map/ppermute | solution.py:378
  41.3 1.1 collective-permute-start.15
  42.4 2.7 %collective-permute-start.16 = (f32[800,256]{1,0:T(8,128)S(1)}, f32[800,256]{1,0:T(8,128)S(1)}, u32[]{:S(2)}, u32[]{:S(2)}) collective-permute-start(f32[800,256]{1,0:T(8,128)S(1)} %get-tuple-element.90), channel_id=1, source_target_pairs={{0,64},{4,68},{8,72},{12,76},{16,24},{20,28},{24,16},{28,20},{32,9... | collective-permute-start | bytes 2457608 | tf_op jit(solution)/shard_map/ppermute | solution.py:378
  45.1 1.4 %collective-permute-start.11 = (f32[256,512]{1,0:T(8,128)S(1)}, f32[256,512]{1,0:T(8,128)S(1)}, u32[]{:S(2)}, u32[]{:S(2)}) collective-permute-start(f32[256,512]{1,0:T(8,128)S(1)} %get-tuple-element.84), channel_id=1, source_target_pairs={{0,2},{1,3},{2,0},{3,1},{4,6},{5,7},{6,4},{7,5},{8,10},{9,11},{10,... | collective-permute-start | bytes 1572872 | tf_op jit(solution)/shard_map/ppermute | solution.py:500
  46.5 5.1 %collective-permute-done.12.refs_0_ = f32[256,512]{1,0:T(8,128)S(1)} collective-permute-done((f32[256,512]{1,0:T(8,128)S(1)}, f32[256,512]{1,0:T(8,128)S(1)}, u32[]{:S(2)}, u32[]{:S(2)}) %collective-permute-start.12) | collective-permute-done | bytes 524320 | tf_op jit(solution)/shard_map/ppermute | solution.py:500
  52.3 1.7 %collective-permute-done.15.ahead_ref = f32[800,256]{1,0:T(8,128)S(1)} collective-permute-done((f32[800,256]{1,0:T(8,128)S(1)}, f32[800,256]{1,0:T(8,128)S(1)}, u32[]{:S(2)}, u32[]{:S(2)}) %collective-permute-start.15) | collective-permute-done | bytes 819232 | tf_op jit(solution)/shard_map/ppermute | solution.py:378
  54.0 9.6 %collective-permute-done.16.far_ref = f32[800,256]{1,0:T(8,128)S(1)} collective-permute-done((f32[800,256]{1,0:T(8,128)S(1)}, f32[800,256]{1,0:T(8,128)S(1)}, u32[]{:S(2)}, u32[]{:S(2)}) %collective-permute-start.16) | collective-permute-done | bytes 819232 | tf_op jit(solution)/shard_map/ppermute | solution.py:378
  63.6 0.7 shard_map.127
  64.3 1.3 %collective-permute-start.17 = (f32[200,256]{1,0:T(8,128)S(1)}, f32[200,256]{1,0:T(8,128)S(1)}, u32[]{:S(2)}, u32[]{:S(2)}) collective-permute-start(f32[200,256]{1,0:T(8,128)S(1)} %get-tuple-element.92), channel_id=1, source_target_pairs={{0,4},{4,8},{8,12},{12,0},{16,48},{20,52},{24,56},{28,60},{32,36},... | collective-permute-start | bytes 614408 | tf_op jit(solution)/shard_map/ppermute | solution.py:378
  65.8 1.8 %collective-permute-start.19 = (f32[200,256]{1,0:T(8,128)S(1)}, f32[200,256]{1,0:T(8,128)S(1)}, u32[]{:S(2)}, u32[]{:S(2)}) collective-permute-start(f32[200,256]{1,0:T(8,128)S(1)} %get-tuple-element.94), channel_id=1, source_target_pairs={{0,8},{4,12},{8,0},{12,4},{16,80},{20,84},{24,88},{28,92},{32,40},... | collective-permute-start | bytes 614408 | tf_op jit(solution)/shard_map/ppermute | solution.py:378
  67.7 1.6 %collective-permute-done.17.back_ref = f32[200,256]{1,0:T(8,128)S(1)} collective-permute-done((f32[200,256]{1,0:T(8,128)S(1)}, f32[200,256]{1,0:T(8,128)S(1)}, u32[]{:S(2)}, u32[]{:S(2)}) %collective-permute-start.17) | collective-permute-done | bytes 204832 | tf_op jit(solution)/shard_map/ppermute | solution.py:378
  69.3 1.2 collective-permute-done.18.ahead_ref
  70.5 2.5 %collective-permute-done.19.far_ref = f32[200,256]{1,0:T(8,128)S(1)} collective-permute-done((f32[200,256]{1,0:T(8,128)S(1)}, f32[200,256]{1,0:T(8,128)S(1)}, u32[]{:S(2)}, u32[]{:S(2)}) %collective-permute-start.19) | collective-permute-done | bytes 204832 | tf_op jit(solution)/shard_map/ppermute | solution.py:378
  73.1 1.8 %collective-permute-start.22 = (f32[200,256]{1,0:T(8,128)S(1)}, f32[200,256]{1,0:T(8,128)S(1)}, u32[]{:S(2)}, u32[]{:S(2)}) collective-permute-start(f32[200,256]{1,0:T(8,128)S(1)} %shard_map.128.own_ref), channel_id=1, source_target_pairs={{0,8},{4,12},{8,0},{12,4},{16,80},{20,84},{24,88},{28,92},{32,40},... | collective-permute-start | bytes 614408 | tf_op jit(solution)/shard_map/ppermute | solution.py:378
  74.9 1.4 %collective-permute-start.20 = (f32[200,256]{1,0:T(8,128)S(1)}, f32[200,256]{1,0:T(8,128)S(1)}, u32[]{:S(2)}, u32[]{:S(2)}) collective-permute-start(f32[200,256]{1,0:T(8,128)S(1)} %shard_map.128.own_ref), channel_id=1, source_target_pairs={{0,12},{4,0},{8,4},{12,8},{16,112},{20,116},{24,120},{28,124},{32,... | collective-permute-start | bytes 614408 | tf_op jit(solution)/shard_map/ppermute | solution.py:378
  76.6 2.8 %collective-permute-done.22.far_ref = f32[200,256]{1,0:T(8,128)S(1)} collective-permute-done((f32[200,256]{1,0:T(8,128)S(1)}, f32[200,256]{1,0:T(8,128)S(1)}, u32[]{:S(2)}, u32[]{:S(2)}) %collective-permute-start.22) | collective-permute-done | bytes 204832 | tf_op jit(solution)/shard_map/ppermute | solution.py:378
  79.4 1.4 %collective-permute-done.21.back_ref = f32[200,256]{1,0:T(8,128)S(1)} collective-permute-done((f32[200,256]{1,0:T(8,128)S(1)}, f32[200,256]{1,0:T(8,128)S(1)}, u32[]{:S(2)}, u32[]{:S(2)}) %collective-permute-start.21) | collective-permute-done | bytes 204832 | tf_op jit(solution)/shard_map/ppermute | solution.py:378
  80.7 1.0 collective-permute-done.20.ahead_ref
  81.7 0.6 shard_map.129.refs_0_
  82.3 0.9 collective-permute-start.26
  83.2 5.9 %collective-permute-start.25 = (f32[800,256]{1,0:T(8,128)S(1)}, f32[800,256]{1,0:T(8,128)S(1)}, u32[]{:S(2)}, u32[]{:S(2)}) collective-permute-start(f32[800,256]{1,0:T(8,128)S(1)} %shard_map.129.refs_0_), channel_id=1, source_target_pairs={{0,16},{16,0},{32,48},{48,32},{64,80},{80,64},{96,112},{112,96},{1... | collective-permute-start | bytes 2457608 | tf_op jit(solution)/shard_map/ppermute | solution.py:383
  89.2 1.4 %collective-permute-start.23 = (f32[800,256]{1,0:T(8,128)S(1)}, f32[800,256]{1,0:T(8,128)S(1)}, u32[]{:S(2)}, u32[]{:S(2)}) collective-permute-start(f32[800,256]{1,0:T(8,128)S(1)} %shard_map.129.refs_0_), channel_id=1, source_target_pairs={{0,96},{4,100},{8,104},{12,108},{16,28},{20,16},{24,20},{28,24},{3... | collective-permute-start | bytes 2457608 | tf_op jit(solution)/shard_map/ppermute | solution.py:378
  90.6 4.6 %collective-permute-done.26.refs_2_ = f32[800,256]{1,0:T(8,128)S(1)} collective-permute-done((f32[800,256]{1,0:T(8,128)S(1)}, f32[800,256]{1,0:T(8,128)S(1)}, u32[]{:S(2)}, u32[]{:S(2)}) %collective-permute-start.26) | collective-permute-done | bytes 819232 | tf_op jit(solution)/shard_map/ppermute | solution.py:378
  95.2 1.7 %shard_map.130 = (f32[3,2048,256]{2,1,0:T(8,128)}, f32[800,256]{1,0:T(8,128)S(1)}) custom-call(s32[5]{0:T(128)S(1)} %stack.23.pos_ref, f32[800,256]{1,0:T(8,128)S(1)} %shard_map.129.refs_0_, f32[800,256]{1,0:T(8,128)S(1)} %collective-permute-done.25.refs_1_.refs_4_, f32[800,256]{1,0:T(8,128)S(1)} %collective-permute-done.26.refs_2_), custom_call_target="tpu_custom_call", output_to_operand_aliasing={{1}: (3, {})} | custom-call | tf_op jit(solution)/shard_map/pallas_call | solution.py:522
  97.0 5.7 %collective-permute-start.29 = (f32[800,256]{1,0:T(8,128)S(1)}, f32[800,256]{1,0:T(8,128)S(1)}, u32[]{:S(2)}, u32[]{:S(2)}) collective-permute-start(f32[800,256]{1,0:T(8,128)S(1)} %get-tuple-element.95.refs_2_.refs_3_), channel_id=1, source_target_pairs={{0,16},{16,0},{32,48},{48,32},{64,80},{80,64},{96,112},{112,96},{1... | collective-permute-start | bytes 2457608 | tf_op jit(solution)/shard_map/ppermute | solution.py:383
  102.7 15.8 %collective-permute-start.28 = (f32[800,256]{1,0:T(8,128)S(1)}, f32[800,256]{1,0:T(8,128)S(1)}, u32[]{:S(2)}, u32[]{:S(2)}) collective-permute-start(f32[800,256]{1,0:T(8,128)S(1)} %collective-permute-done.24.refs_1_.refs_2_), channel_id=1, source_target_pairs={{0,16},{16,0},{32,48},{48,32},{64,80},{80,64},{96,112},{112,96},{1... | collective-permute-start | bytes 2457608 | tf_op jit(solution)/shard_map/ppermute | solution.py:383
  118.5 2.3 %shard_map.131.refs_8_ = f32[3,2048,256]{2,1,0:T(8,128)} custom-call(s32[5]{0:T(128)S(1)} %stack.23.pos_ref, f32[800,256]{1,0:T(8,128)S(1)} %collective-permute-done.23.refs_0_.refs_1_, f32[800,256]{1,0:T(8,128)S(1)} %collective-permute-done.24.refs_1_.refs_2_, f32[800,256]{1,0:T(8,128)S(1)} %get-tuple-element.95.refs_2_.refs_3_, ...), custom_call_target="tpu_custom_call", output_to_operand_aliasing={{}: (5, {})} | custom-call | tf_op jit(solution)/shard_map/pallas_call | solution.py:522
  120.9 0.8 collective-permute-done.27.refs_5_
  121.6 2.4 %shard_map.132 = (f32[3,2048,256]{2,1,0:T(8,128)}, f32[2,128,128]{2,1,0:T(8,128)}, f32[2,128]{1,0:T(2,128)}, f32[2]{0:T(128)}) custom-call(s32[5]{0:T(128)S(1)} %stack.23.pos_ref, f32[800,256]{1,0:T(8,128)S(1)} %shard_map.129.refs_0_, f32[800,256]{1,0:T(8,128)S(1)} %collective-permute-done.23.refs_0_.refs_1_, ...), custom_call_target="tpu_custom_call", output_to_operand_aliasing={{0}: (9, {})} | custom-call | tf_op jit(solution)/shard_map/pallas_call | solution.py:538
  (43 shorter events, 3.2 us)
Async XLA Ops:
  0.6 9.1 %copy-start.4 = (f32[1,2,256]{2,1,0:T(2,128)S(1)}, f32[1,2,256]{2,1,0:T(2,128)}, u32[]{:S(2)}) copy-start(f32[1,2,256]{2,1,0:T(2,128)} %gate_ref.7) | copy-start | bytes 6148
  0.6 9.0 %copy-start.5 = (f32[2]{0:T(128)S(1)}, f32[2]{0:T(128)}, u32[]{:S(2)}) copy-start(f32[2]{0:T(128)} %base_ref.7) | copy-start | bytes 28
  0.8 20.9 %copy-start.2 = (f32[2,128,128]{2,1,0:T(8,128)S(1)}, f32[2,128,128]{2,1,0:T(8,128)}, u32[]{:S(2)}) copy-start(f32[2,128,128]{2,1,0:T(8,128)} %init_ref.3) | copy-start | bytes 393220
  0.8 20.9 %copy-start.3 = (bf16[1,256,256]{2,1,0:T(8,128)(2,1)S(1)}, bf16[1,256,256]{2,1,0:T(8,128)(2,1)}, u32[]{:S(2)}) copy-start(bf16[1,256,256]{2,1,0:T(8,128)(2,1)} %up_ref.3) | copy-start | bytes 393220
  0.8 20.9 %copy-start.6 = (f32[2,128]{1,0:T(2,128)S(1)}, f32[2,128]{1,0:T(2,128)}, u32[]{:S(2)}) copy-start(f32[2,128]{1,0:T(2,128)} %gain_ref.1) | copy-start | bytes 3076
  6.3 10.7 %collective-permute-start.4 = (f32[256,1024]{1,0:T(8,128)S(1)}, f32[256,1024]{1,0:T(8,128)S(1)}, u32[]{:S(2)}, u32[]{:S(2)}) collective-permute-start(f32[256,1024]{1,0:T(8,128)S(1)} %get-tuple-element.62), channel_id=1, source_target_pairs={{0,16},{16,0},{32,48},{48,32},{64,80},{80,64},{96,112},{112,96},{1... | collective-permute-start | bytes 3145736 | tf_op jit(solution)/shard_map/ppermute | solution.py:383
  7.1 7.0 %collective-permute-start = (f32[2,128,128]{2,1,0:T(8,128)S(1)}, f32[2,128,128]{2,1,0:T(8,128)S(1)}, u32[]{:S(2)}, u32[]{:S(2)}) collective-permute-start(f32[2,128,128]{2,1,0:T(8,128)S(1)} %get-tuple-element.54), channel_id=1, source_target_pairs={{0,4},{8,12},{1,5},{9,13},{2,6},{10,14},{3,7},{11,15},{16,20},{24,... | collective-permute-start | bytes 393224 | tf_op jit(solution)/shard_map/ppermute | solution.py:456
  8.4 9.6 %collective-permute-start.3 = (f32[2,128,128]{2,1,0:T(8,128)S(1)}, f32[2,128,128]{2,1,0:T(8,128)S(1)}, u32[]{:S(2)}, u32[]{:S(2)}) collective-permute-start(f32[2,128,128]{2,1,0:T(8,128)S(1)} %get-tuple-element.55.d_ref), channel_id=1, source_target_pairs={{8,12},{4,0},{9,13},{5,1},{10,14},{6,2},{11,15},{7,3},{24,28},{20,... | collective-permute-start | bytes 393224 | tf_op jit(solution)/shard_map/ppermute | solution.py:457
  13.6 22.6 %copy-start = (bf16[3,2048,256]{2,1,0:T(8,128)(2,1)S(1)}, bf16[3,2048,256]{2,1,0:T(8,128)(2,1)}, u32[]{:S(2)}) copy-start(bf16[3,2048,256]{2,1,0:T(8,128)(2,1)} %w_ref.1) | copy-start | bytes 9437188
  14.3 7.3 %collective-permute-start.2 = (f32[2,128,128]{2,1,0:T(8,128)S(1)}, f32[2,128,128]{2,1,0:T(8,128)S(1)}, u32[]{:S(2)}, u32[]{:S(2)}) collective-permute-start(f32[2,128,128]{2,1,0:T(8,128)S(1)} %shard_map.120), channel_id=1, source_target_pairs={{4,12},{5,13},{6,14},{7,15},{20,28},{21,29},{22,30},{23,31},{36,44... | collective-permute-start | bytes 393224 | tf_op jit(solution)/shard_map/ppermute | solution.py:475
  15.7 5.9 %collective-permute-start.1 = (f32[2,128,128]{2,1,0:T(8,128)S(1)}, f32[2,128,128]{2,1,0:T(8,128)S(1)}, u32[]{:S(2)}, u32[]{:S(2)}) collective-permute-start(f32[2,128,128]{2,1,0:T(8,128)S(1)} %shard_map.120), channel_id=1, source_target_pairs={{4,8},{5,9},{6,10},{7,11},{20,24},{21,25},{22,26},{23,27},{36,40},... | collective-permute-start | bytes 393224 | tf_op jit(solution)/shard_map/ppermute | solution.py:474
  16.4 15.1 %collective-permute-start.9 = (f32[2,128,128]{2,1,0:T(8,128)S(1)}, f32[2,128,128]{2,1,0:T(8,128)S(1)}, u32[]{:S(2)}, u32[]{:S(2)}) collective-permute-start(f32[2,128,128]{2,1,0:T(8,128)S(1)} %get-tuple-element.55.d_ref), channel_id=1, source_target_pairs={{8,0},{9,1},{10,2},{11,3},{24,16},{25,17},{26,18},{27,19},{40,32},... | collective-permute-start | bytes 393224 | tf_op jit(solution)/shard_map/ppermute | solution.py:459
  17.1 14.4 %collective-permute-start.8 = (f32[2,128,128]{2,1,0:T(8,128)S(1)}, f32[2,128,128]{2,1,0:T(8,128)S(1)}, u32[]{:S(2)}, u32[]{:S(2)}) collective-permute-start(f32[2,128,128]{2,1,0:T(8,128)S(1)} %get-tuple-element.55.d_ref), channel_id=1, source_target_pairs={{8,4},{9,5},{10,6},{11,7},{24,20},{25,21},{26,22},{27,23},{40,36},... | collective-permute-start | bytes 393224 | tf_op jit(solution)/shard_map/ppermute | solution.py:458
  23.2 8.3 %collective-permute-start.7 = (f32[2,128,128]{2,1,0:T(8,128)S(1)}, f32[2,128,128]{2,1,0:T(8,128)S(1)}, u32[]{:S(2)}, u32[]{:S(2)}) collective-permute-start(f32[2,128,128]{2,1,0:T(8,128)S(1)} %get-tuple-element.63.p_ref), channel_id=1, source_target_pairs={{12,0},{13,1},{14,2},{15,3},{28,16},{29,17},{30,18},{31,19},{44,32... | collective-permute-start | bytes 393224 | tf_op jit(solution)/shard_map/ppermute | solution.py:484
  24.5 7.0 %collective-permute-start.6 = (f32[2,128,128]{2,1,0:T(8,128)S(1)}, f32[2,128,128]{2,1,0:T(8,128)S(1)}, u32[]{:S(2)}, u32[]{:S(2)}) collective-permute-start(f32[2,128,128]{2,1,0:T(8,128)S(1)} %get-tuple-element.63.p_ref), channel_id=1, source_target_pairs={{12,4},{8,0},{13,5},{9,1},{14,6},{10,2},{15,7},{11,3},{28,20},{24,... | collective-permute-start | bytes 393224 | tf_op jit(solution)/shard_map/ppermute | solution.py:483
  27.0 4.5 %collective-permute-start.5 = (f32[2,128,128]{2,1,0:T(8,128)S(1)}, f32[2,128,128]{2,1,0:T(8,128)S(1)}, u32[]{:S(2)}, u32[]{:S(2)}) collective-permute-start(f32[2,128,128]{2,1,0:T(8,128)S(1)} %get-tuple-element.63.p_ref), channel_id=1, source_target_pairs={{12,8},{8,4},{4,0},{13,9},{9,5},{5,1},{14,10},{10,6},{6,2},{15,11}... | collective-permute-start | bytes 393224 | tf_op jit(solution)/shard_map/ppermute | solution.py:482
  34.1 4.4 %collective-permute-start.10 = (f32[1024,256]{1,0:T(8,128)S(1)}, f32[1024,256]{1,0:T(8,128)S(1)}, u32[]{:S(2)}, u32[]{:S(2)}) collective-permute-start(f32[1024,256]{1,0:T(8,128)S(1)} %get-tuple-element.79.all_ref.own_ref), channel_id=1, source_target_pairs={{0,16},{16,0},{32,48},{48,32},{64,80},{80,64},{96,112},{112,96},{1... | collective-permute-start | bytes 3145736 | tf_op jit(solution)/shard_map/ppermute | solution.py:383
  37.8 13.8 %collective-permute-start.12 = (f32[256,512]{1,0:T(8,128)S(1)}, f32[256,512]{1,0:T(8,128)S(1)}, u32[]{:S(2)}, u32[]{:S(2)}) collective-permute-start(f32[256,512]{1,0:T(8,128)S(1)} %get-tuple-element.85), channel_id=1, source_target_pairs={{0,1},{1,2},{2,3},{3,0},{4,5},{5,6},{6,7},{7,4},{8,9},{9,10},{10,1... | collective-permute-start | bytes 1572872 | tf_op jit(solution)/shard_map/ppermute | solution.py:500
  40.0 12.3 %collective-permute-start.14 = (f32[800,256]{1,0:T(8,128)S(1)}, f32[800,256]{1,0:T(8,128)S(1)}, u32[]{:S(2)}, u32[]{:S(2)}) collective-permute-start(f32[800,256]{1,0:T(8,128)S(1)} %get-tuple-element.88), channel_id=1, source_target_pairs={{0,32},{4,36},{8,40},{12,44},{16,20},{20,24},{24,28},{28,16},{32,6... | collective-permute-start | bytes 2457608 | tf_op jit(solution)/shard_map/ppermute | solution.py:378
  41.3 12.7 %collective-permute-start.15 = (f32[800,256]{1,0:T(8,128)S(1)}, f32[800,256]{1,0:T(8,128)S(1)}, u32[]{:S(2)}, u32[]{:S(2)}) collective-permute-start(f32[800,256]{1,0:T(8,128)S(1)} %get-tuple-element.89), channel_id=1, source_target_pairs={{0,96},{4,100},{8,104},{12,108},{16,28},{20,16},{24,20},{28,24},{3... | collective-permute-start | bytes 2457608 | tf_op jit(solution)/shard_map/ppermute | solution.py:378
  42.4 21.2 %collective-permute-start.16 = (f32[800,256]{1,0:T(8,128)S(1)}, f32[800,256]{1,0:T(8,128)S(1)}, u32[]{:S(2)}, u32[]{:S(2)}) collective-permute-start(f32[800,256]{1,0:T(8,128)S(1)} %get-tuple-element.90), channel_id=1, source_target_pairs={{0,64},{4,68},{8,72},{12,76},{16,24},{20,28},{24,16},{28,20},{32,9... | collective-permute-start | bytes 2457608 | tf_op jit(solution)/shard_map/ppermute | solution.py:378
  45.1 31.2 %collective-permute-start.11 = (f32[256,512]{1,0:T(8,128)S(1)}, f32[256,512]{1,0:T(8,128)S(1)}, u32[]{:S(2)}, u32[]{:S(2)}) collective-permute-start(f32[256,512]{1,0:T(8,128)S(1)} %get-tuple-element.84), channel_id=1, source_target_pairs={{0,2},{1,3},{2,0},{3,1},{4,6},{5,7},{6,4},{7,5},{8,10},{9,11},{10,... | collective-permute-start | bytes 1572872 | tf_op jit(solution)/shard_map/ppermute | solution.py:500
  51.6 24.7 %collective-permute-start.13 = (f32[256,512]{1,0:T(8,128)S(1)}, f32[256,512]{1,0:T(8,128)S(1)}, u32[]{:S(2)}, u32[]{:S(2)}) collective-permute-start(f32[256,512]{1,0:T(8,128)S(1)} %get-tuple-element.86), channel_id=1, source_target_pairs={{0,3},{1,0},{2,1},{3,2},{4,7},{5,4},{6,5},{7,6},{8,11},{9,8},{10,9... | collective-permute-start | bytes 1572872 | tf_op jit(solution)/shard_map/ppermute | solution.py:500
  64.3 5.0 %collective-permute-start.17 = (f32[200,256]{1,0:T(8,128)S(1)}, f32[200,256]{1,0:T(8,128)S(1)}, u32[]{:S(2)}, u32[]{:S(2)}) collective-permute-start(f32[200,256]{1,0:T(8,128)S(1)} %get-tuple-element.92), channel_id=1, source_target_pairs={{0,4},{4,8},{8,12},{12,0},{16,48},{20,52},{24,56},{28,60},{32,36},... | collective-permute-start | bytes 614408 | tf_op jit(solution)/shard_map/ppermute | solution.py:378
  65.6 4.9 %collective-permute-start.18 = (f32[200,256]{1,0:T(8,128)S(1)}, f32[200,256]{1,0:T(8,128)S(1)}, u32[]{:S(2)}, u32[]{:S(2)}) collective-permute-start(f32[200,256]{1,0:T(8,128)S(1)} %get-tuple-element.93), channel_id=1, source_target_pairs={{0,12},{4,0},{8,4},{12,8},{16,112},{20,116},{24,120},{28,124},{32,... | collective-permute-start | bytes 614408 | tf_op jit(solution)/shard_map/ppermute | solution.py:378
  65.8 7.2 %collective-permute-start.19 = (f32[200,256]{1,0:T(8,128)S(1)}, f32[200,256]{1,0:T(8,128)S(1)}, u32[]{:S(2)}, u32[]{:S(2)}) collective-permute-start(f32[200,256]{1,0:T(8,128)S(1)} %get-tuple-element.94), channel_id=1, source_target_pairs={{0,8},{4,12},{8,0},{12,4},{16,80},{20,84},{24,88},{28,92},{32,40},... | collective-permute-start | bytes 614408 | tf_op jit(solution)/shard_map/ppermute | solution.py:378
  73.1 6.3 %collective-permute-start.22 = (f32[200,256]{1,0:T(8,128)S(1)}, f32[200,256]{1,0:T(8,128)S(1)}, u32[]{:S(2)}, u32[]{:S(2)}) collective-permute-start(f32[200,256]{1,0:T(8,128)S(1)} %shard_map.128.own_ref), channel_id=1, source_target_pairs={{0,8},{4,12},{8,0},{12,4},{16,80},{20,84},{24,88},{28,92},{32,40},... | collective-permute-start | bytes 614408 | tf_op jit(solution)/shard_map/ppermute | solution.py:378
  74.8 5.9 %collective-permute-start.21 = (f32[200,256]{1,0:T(8,128)S(1)}, f32[200,256]{1,0:T(8,128)S(1)}, u32[]{:S(2)}, u32[]{:S(2)}) collective-permute-start(f32[200,256]{1,0:T(8,128)S(1)} %shard_map.128.own_ref), channel_id=1, source_target_pairs={{0,4},{4,8},{8,12},{12,0},{16,48},{20,52},{24,56},{28,60},{32,36},... | collective-permute-start | bytes 614408 | tf_op jit(solution)/shard_map/ppermute | solution.py:378
  74.9 6.8 %collective-permute-start.20 = (f32[200,256]{1,0:T(8,128)S(1)}, f32[200,256]{1,0:T(8,128)S(1)}, u32[]{:S(2)}, u32[]{:S(2)}) collective-permute-start(f32[200,256]{1,0:T(8,128)S(1)} %shard_map.128.own_ref), channel_id=1, source_target_pairs={{0,12},{4,0},{8,4},{12,8},{16,112},{20,116},{24,120},{28,124},{32,... | collective-permute-start | bytes 614408 | tf_op jit(solution)/shard_map/ppermute | solution.py:378
  76.6 44.3 %copy-start.1 = (bf16[1,256,512]{2,1,0:T(8,128)(2,1)}, bf16[1,256,512]{2,1,0:T(8,128)(2,1)S(1)}, u32[]{:S(2)}) copy-start(bf16[1,256,512]{2,1,0:T(8,128)(2,1)S(1)} %fusion.refs_0_) | copy-start | bytes 786436
  82.3 12.9 %collective-permute-start.26 = (f32[800,256]{1,0:T(8,128)S(1)}, f32[800,256]{1,0:T(8,128)S(1)}, u32[]{:S(2)}, u32[]{:S(2)}) collective-permute-start(f32[800,256]{1,0:T(8,128)S(1)} %shard_map.129.refs_0_), channel_id=1, source_target_pairs={{0,64},{4,68},{8,72},{12,76},{16,24},{20,28},{24,16},{28,20},{32,9... | collective-permute-start | bytes 2457608 | tf_op jit(solution)/shard_map/ppermute | solution.py:378
  83.2 12.0 %collective-permute-start.25 = (f32[800,256]{1,0:T(8,128)S(1)}, f32[800,256]{1,0:T(8,128)S(1)}, u32[]{:S(2)}, u32[]{:S(2)}) collective-permute-start(f32[800,256]{1,0:T(8,128)S(1)} %shard_map.129.refs_0_), channel_id=1, source_target_pairs={{0,16},{16,0},{32,48},{48,32},{64,80},{80,64},{96,112},{112,96},{1... | collective-permute-start | bytes 2457608 | tf_op jit(solution)/shard_map/ppermute | solution.py:383
  89.2 13.5 %collective-permute-start.24 = (f32[800,256]{1,0:T(8,128)S(1)}, f32[800,256]{1,0:T(8,128)S(1)}, u32[]{:S(2)}, u32[]{:S(2)}) collective-permute-start(f32[800,256]{1,0:T(8,128)S(1)} %shard_map.129.refs_0_), channel_id=1, source_target_pairs={{0,32},{4,36},{8,40},{12,44},{16,20},{20,24},{24,28},{28,16},{32,6... | collective-permute-start | bytes 2457608 | tf_op jit(solution)/shard_map/ppermute | solution.py:378
  89.2 29.3 %collective-permute-start.23 = (f32[800,256]{1,0:T(8,128)S(1)}, f32[800,256]{1,0:T(8,128)S(1)}, u32[]{:S(2)}, u32[]{:S(2)}) collective-permute-start(f32[800,256]{1,0:T(8,128)S(1)} %shard_map.129.refs_0_), channel_id=1, source_target_pairs={{0,96},{4,100},{8,104},{12,108},{16,28},{20,16},{24,20},{28,24},{3... | collective-permute-start | bytes 2457608 | tf_op jit(solution)/shard_map/ppermute | solution.py:378
  97.0 21.6 %collective-permute-start.29 = (f32[800,256]{1,0:T(8,128)S(1)}, f32[800,256]{1,0:T(8,128)S(1)}, u32[]{:S(2)}, u32[]{:S(2)}) collective-permute-start(f32[800,256]{1,0:T(8,128)S(1)} %get-tuple-element.95.refs_2_.refs_3_), channel_id=1, source_target_pairs={{0,16},{16,0},{32,48},{48,32},{64,80},{80,64},{96,112},{112,96},{1... | collective-permute-start | bytes 2457608 | tf_op jit(solution)/shard_map/ppermute | solution.py:383
  102.7 18.1 %collective-permute-start.28 = (f32[800,256]{1,0:T(8,128)S(1)}, f32[800,256]{1,0:T(8,128)S(1)}, u32[]{:S(2)}, u32[]{:S(2)}) collective-permute-start(f32[800,256]{1,0:T(8,128)S(1)} %collective-permute-done.24.refs_1_.refs_2_), channel_id=1, source_target_pairs={{0,16},{16,0},{32,48},{48,32},{64,80},{80,64},{96,112},{112,96},{1... | collective-permute-start | bytes 2457608 | tf_op jit(solution)/shard_map/ppermute | solution.py:383
  118.5 3.1 %collective-permute-start.27 = (f32[800,256]{1,0:T(8,128)S(1)}, f32[800,256]{1,0:T(8,128)S(1)}, u32[]{:S(2)}, u32[]{:S(2)}) collective-permute-start(f32[800,256]{1,0:T(8,128)S(1)} %collective-permute-done.23.refs_0_.refs_1_), channel_id=1, source_target_pairs={{0,16},{16,0},{32,48},{48,32},{64,80},{80,64},{96,112},{112,96},{1... | collective-permute-start | bytes 2457608 | tf_op jit(solution)/shard_map/ppermute | solution.py:383

commit v9 on v8

--- a/solution.py
+++ b/solution.py
@@ -315,9 +315,9 @@
             refs[-1][rows, :] = part_ref[to, :]
 
 
-def place_kernel(pos_ref, *refs, which):
+def place_kernel(pos_ref, *refs, which, passed):
     pieces = refs[: len(which)]
-    out_ref, sem = refs[len(refs) - 3 if len(refs) == len(which) + 4 else -2], refs[-1]
+    out_ref, sem = refs[-3 if passed else -2], refs[-1]
     copies = []
     for g, ((half, m), piece) in enumerate(zip(which, pieces)):
         core = pos_ref[0] if half == 0 else 1 - pos_ref[0]
@@ -329,6 +329,8 @@
             )
     for copy in copies:
         copy.start()
+    if passed:
+        refs[-2][...] = pieces[0][...]
     for copy in copies:
         copy.wait()
 
@@ -517,23 +519,23 @@
     from_back, from_ahead, from_far = round_turn([total] * 3, True)
     out = shape(3, model, wide)
 
-    def place(which, extra, extra_out, extra_spec, aliases):
-        given = [(mine, others)[half][m] for half, m in which]
+    def place(which, passed, *placed):
+        given = [sides[half][m] for half, m in which]
         return pl.pallas_call(
-            functools.partial(place_kernel, which=which),
-            out_shape=(out,) + extra_out,
-            in_specs=[SM] + [VM] * len(given) + [extra_spec],
-            out_specs=(anywhere,) + (VM,) * len(extra_out),
+            functools.partial(place_kernel, which=which, passed=passed),
+            out_shape=(out, chunk) if passed else (out,),
+            in_specs=[SM] + [VM] * len(given) + [anywhere] * len(placed),
+            out_specs=(anywhere, VM) if passed else (anywhere,),
             scratch_shapes=[pltpu.SemaphoreType.DMA((3, len(which)))],
-            input_output_aliases={len(given) + 1: aliases},
+            input_output_aliases={len(given) + 1: 0} if placed else {},
             compiler_params=PARAMS,
-        )(pos, *given, extra)
-
-    mine = [total, from_ahead, from_back, from_far]
-    others = [swap(total)]
-    placed, mine[3] = place(((0, 0), (1, 0)), from_far, (chunk,), VM, 1)
-    others += [swap(given) for given in mine[1:]]
-    (placed,) = place(((0, 1), (0, 2), (0, 3), (1, 3)), placed, (), anywhere, 0)
+        )(pos, *given, *placed)
+
+    mine, others = [total, from_ahead, from_back, from_far], []
+    sides = (mine, others)
+    placed, own_piece = place(((0, 0), (0, 3)), True)
+    others += [swap(given) for given in [own_piece] + mine[1:]]
+    (placed,) = place(((0, 1), (0, 2), (1, 0), (1, 3)), False, placed)
     which = ((1, 1), (1, 2))
     grad_proj, grad_init, grad_gain, grad_rates = pl.pallas_call(
         functools.partial(last_kernel, which=which),

time: 124 us -> 125 us (level)
  starting transfers between devices: 58 us -> 52.1 us
  waiting for transfers between devices: 37.1 us -> 43 us
    ppermute x12, waiting for transfers between devices: 26.6 us -> 32.5 us  [round_turn(): lax.ppermute(chunk, ('dp', 'ctx'), moves(first, turn))]
    ppermute x6, starting transfers between devices: 30.4 us -> 24.5 us  [swap(): return lax.ppermute(value, 'dp', [(i, i ^ 1) for i in range(2 * RING)])]
where the time goes in v9:
time: 125 us; the launch traced here: 124 us
  starting transfers between devices  52.1 us (42%)
  waiting for transfers between devices  43 us (34%)
  Pallas kernels  27.6 us (22%)
    ppermute x12, waiting for transfers between devices, round_turn(): lax.ppermute(chunk, ('dp', 'ctx'), moves(first, turn))  32.5 us
    ppermute x6, starting transfers between devices, swap(): return lax.ppermute(value, 'dp', [(i, i ^ 1) for i in range(2 * RING)])  24.5 us
    ppermute x12, starting transfers between devices, round_turn(): lax.ppermute(chunk, ('dp', 'ctx'), moves(first, turn))  14 us
    pallas_call x1, Pallas kernels, body(): pl.pallas_call(maps_kernel, grid=(1,), out_shape=(wide_f32, wide_f32, vme...  5.56 us
    ppermute x3, waiting for transfers between devices, along_head(): lax.ppermute(terms, 'head', [(i, (i + turn) % RING) for i in range(RING)])  5.06 us
    pallas_call x2, Pallas kernels, place(): pl.pallas_call(functools.partial(place_kernel, which=which, passed=passed...  4.03 us
    pallas_call x1, Pallas kernels, body(): pl.pallas_call(reach_kernel, grid=(1,), out_shape=(wide_f32, square, wide...  3.89 us
    ppermute x1, waiting for transfers between devices, body(): far = lax.ppermute(second, 'ctx', [(1, 3)])  3.65 us
  transfers between devices with their start and end apart: 30, of which 15 were waited for; matrix products, arithmetic and copies ran while one was open for 0% of the time, Pallas kernels for 13%

profile of v9, /device:TPU:123, one launch (start us, length us, event | category | flops | bytes accessed | tf_op | source)
XLA Modules:
  0.0 124.3 jit_solution(16814933203627595957)
XLA Ops:
  0.8 5.6 %shard_map.118 = (f32[256,256]{1,0:T(8,128)S(1)}, f32[256,256]{1,0:T(8,128)S(1)}, f32[2,256,128]{2,1,0:T(8,128)S(1)}, f32[2,256,256]{2,1,0:T(8,128)S(1)}, f32[2,...) custom-call(s32[5]{0:T(128)S(1)} %stack.23.pos_ref, ...), custom_call_target="tpu_custom_call" | custom-call | tf_op jit(solution)/shard_map/pallas_call | solution.py:446
  6.3 0.8 collective-permute-start.4
  7.1 1.3 %collective-permute-start = (f32[2,128,128]{2,1,0:T(8,128)S(1)}, f32[2,128,128]{2,1,0:T(8,128)S(1)}, u32[]{:S(2)}, u32[]{:S(2)}) collective-permute-start(f32[2,128,128]{2,1,0:T(8,128)S(1)} %get-tuple-element.54), channel_id=1, source_target_pairs={{0,4},{8,12},{1,5},{9,13},{2,6},{10,14},{3,7},{11,15},{16,20},{24,... | collective-permute-start | bytes 393224 | tf_op jit(solution)/shard_map/ppermute | solution.py:458
  8.4 1.3 %collective-permute-start.3 = (f32[2,128,128]{2,1,0:T(8,128)S(1)}, f32[2,128,128]{2,1,0:T(8,128)S(1)}, u32[]{:S(2)}, u32[]{:S(2)}) collective-permute-start(f32[2,128,128]{2,1,0:T(8,128)S(1)} %get-tuple-element.55.d_ref), channel_id=1, source_target_pairs={{8,12},{4,0},{9,13},{5,1},{10,14},{6,2},{11,15},{7,3},{24,28},{20,... | collective-permute-start | bytes 393224 | tf_op jit(solution)/shard_map/ppermute | solution.py:459
  9.7 3.9 %shard_map.119 = (f32[256,256]{1,0:T(8,128)S(1)}, f32[2,256,256]{2,1,0:T(8,128)S(1)}, f32[256,256]{1,0:T(8,128)S(1)}, f32[256,256]{1,0:T(8,128)S(1)}, f32[256,25...) custom-call(s32[5]{0:T(128)S(1)} %stack.23.pos_ref, f32[2]{0:T(128)S(1)} %copy-done.5, ...), custom_call_target="tpu_custom_call" | custom-call | tf_op jit(solution)/shard_map/pallas_call | solution.py:464
  14.3 1.4 %collective-permute-start.2 = (f32[2,128,128]{2,1,0:T(8,128)S(1)}, f32[2,128,128]{2,1,0:T(8,128)S(1)}, u32[]{:S(2)}, u32[]{:S(2)}) collective-permute-start(f32[2,128,128]{2,1,0:T(8,128)S(1)} %shard_map.120), channel_id=1, source_target_pairs={{4,12},{5,13},{6,14},{7,15},{20,28},{21,29},{22,30},{23,31},{36,44... | collective-permute-start | bytes 393224 | tf_op jit(solution)/shard_map/ppermute | solution.py:477
  15.7 0.7 collective-permute-start.1
  16.4 0.7 collective-permute-start.9
  17.1 0.7 collective-permute-start.8
  18.0 3.7 %collective-permute-done.2.far_ref = f32[2,128,128]{2,1,0:T(8,128)S(1)} collective-permute-done((f32[2,128,128]{2,1,0:T(8,128)S(1)}, f32[2,128,128]{2,1,0:T(8,128)S(1)}, u32[]{:S(2)}, u32[]{:S(2)}) %collective-permute-start.2) | collective-permute-done | bytes 131104 | tf_op jit(solution)/shard_map/ppermute | solution.py:477
  21.7 1.5 %shard_map.122 = (f32[2,128,128]{2,1,0:T(8,128)S(1)}, f32[256,256]{1,0:T(8,128)S(1)}, f32[2,128,128]{2,1,0:T(8,128)S(1)}, f32[2,128]{1,0:T(2,128)S(1)}) custom-call(s32[5]{0:T(128)S(1)} %stack.23.pos_ref, f32[2,128,128]{2,1,0:T(8,128)S(1)} %copy-done.2, f32[2,128,128]{2,1,0:T(8,128)S(1)} %collective-permute-done.w_ref.near_ref, ...), custom_call_target="tpu_custom_call" | custom-call | tf_op jit(solution)/shard_map/pallas_call | solution.py:480
  23.2 1.3 %collective-permute-start.7 = (f32[2,128,128]{2,1,0:T(8,128)S(1)}, f32[2,128,128]{2,1,0:T(8,128)S(1)}, u32[]{:S(2)}, u32[]{:S(2)}) collective-permute-start(f32[2,128,128]{2,1,0:T(8,128)S(1)} %get-tuple-element.63.p_ref), channel_id=1, source_target_pairs={{12,0},{13,1},{14,2},{15,3},{28,16},{29,17},{30,18},{31,19},{44,32... | collective-permute-start | bytes 393224 | tf_op jit(solution)/shard_map/ppermute | solution.py:486
  24.5 2.5 %collective-permute-start.6 = (f32[2,128,128]{2,1,0:T(8,128)S(1)}, f32[2,128,128]{2,1,0:T(8,128)S(1)}, u32[]{:S(2)}, u32[]{:S(2)}) collective-permute-start(f32[2,128,128]{2,1,0:T(8,128)S(1)} %get-tuple-element.63.p_ref), channel_id=1, source_target_pairs={{12,4},{8,0},{13,5},{9,1},{14,6},{10,2},{15,7},{11,3},{28,20},{24,... | collective-permute-start | bytes 393224 | tf_op jit(solution)/shard_map/ppermute | solution.py:485
  27.0 1.6 %collective-permute-start.5 = (f32[2,128,128]{2,1,0:T(8,128)S(1)}, f32[2,128,128]{2,1,0:T(8,128)S(1)}, u32[]{:S(2)}, u32[]{:S(2)}) collective-permute-start(f32[2,128,128]{2,1,0:T(8,128)S(1)} %get-tuple-element.63.p_ref), channel_id=1, source_target_pairs={{12,8},{8,4},{4,0},{13,9},{9,5},{5,1},{14,10},{10,6},{6,2},{15,11}... | collective-permute-start | bytes 393224 | tf_op jit(solution)/shard_map/ppermute | solution.py:484
  28.6 2.9 %shard_map.123 = (f32[256,256]{1,0:T(8,128)S(1)}, f32[256,256]{1,0:T(8,128)S(1)}, f32[256,256]{1,0:T(8,128)S(1)}, f32[256,256]{1,0:T(8,128)S(1)}, f32[2,256]{1,0:T(2,128)S(1)}) custom-call(f32[2]{0:T(128)S(1)} %copy-done.5, f32[1,2,256]{2,1,0:T(2,128)S(1)} %copy-done.4, f32[2,128,128]{2,1,0:T(8,128)S(1)} %get-tuple-element.64.w_ref, ...), custom_call_target="tpu_custom_call" | custom-call | tf_op jit(solution)/shard_map/pallas_call | solution.py:488
  31.5 2.5 %shard_map.124 = (f32[1024,256]{1,0:T(8,128)S(1)}, f32[1,2,256]{2,1,0:T(2,128)}) custom-call(s32[5]{0:T(128)S(1)} %stack.23.pos_ref, f32[2]{0:T(128)S(1)} %copy-done.5, f32[1,2,256]{2,1,0:T(2,128)S(1)} %copy-done.4, f32[2,128,128]{2,1,0:T(8,128)S(1)} %collective-permute-done.5.one_ref, f32[2,128,128]{2,1,0:T(8,128)S(1)} %collective-permute-done.6.two_ref, ...), custom_call_target="tpu_custom_call" | custom-call | tf_op jit(solution)/shard_map/pallas_call | solution.py:492
  34.1 2.2 %collective-permute-start.10 = (f32[1024,256]{1,0:T(8,128)S(1)}, f32[1024,256]{1,0:T(8,128)S(1)}, u32[]{:S(2)}, u32[]{:S(2)}) collective-permute-start(f32[1024,256]{1,0:T(8,128)S(1)} %get-tuple-element.79.all_ref.own_ref), channel_id=1, source_target_pairs={{0,16},{16,0},{32,48},{48,32},{64,80},{80,64},{96,112},{112,96},{1... | collective-permute-start | bytes 3145736 | tf_op jit(solution)/shard_map/ppermute | solution.py:385
  36.2 1.5 %shard_map.125 = (f32[256,512]{1,0:T(8,128)S(1)}, f32[256,512]{1,0:T(8,128)S(1)}, f32[256,512]{1,0:T(8,128)S(1)}, f32[256,512]{1,0:T(8,128)S(1)}) custom-call(s32[5]{0:T(128)S(1)} %stack.23.pos_ref, bf16[3,2048,256]{2,1,0:T(8,128)(2,1)S(1)} %copy-done, f32[1024,256]{1,0:T(8,128)S(1)} %get-tuple-element.79.all_ref.own_ref), custom_call_target="tpu_custom_call" | custom-call | tf_op jit(solution)/shard_map/pallas_call | solution.py:499
  38.5 1.5 %shard_map.126 = (f32[800,256]{1,0:T(8,128)S(1)}, f32[800,256]{1,0:T(8,128)S(1)}, f32[800,256]{1,0:T(8,128)S(1)}, f32[800,256]{1,0:T(8,128)S(1)}, f32[256,512]{1,0:T(8,128)S(1)}, /*index=5*/f32[256,512]{1,0:T(8,128)S(1)}) custom-call(s32[5]{0:T(128)S(1)} %stack.23.pos_ref, ...), custom_call_target="tpu_custom_call", output_to_operand_aliasing={{4}: (5, {}), {5}: (6, {})} | custom-call | tf_op jit(solution)/shard_map/pallas_call | solution.py:504
  40.0 1.3 %collective-permute-start.14 = (f32[800,256]{1,0:T(8,128)S(1)}, f32[800,256]{1,0:T(8,128)S(1)}, u32[]{:S(2)}, u32[]{:S(2)}) collective-permute-start(f32[800,256]{1,0:T(8,128)S(1)} %get-tuple-element.88), channel_id=1, source_target_pairs={{0,32},{4,36},{8,40},{12,44},{16,20},{20,24},{24,28},{28,16},{32,6... | collective-permute-start | bytes 2457608 | tf_op jit(solution)/shard_map/ppermute | solution.py:380
  41.3 1.1 collective-permute-start.15
  42.4 2.7 %collective-permute-start.16 = (f32[800,256]{1,0:T(8,128)S(1)}, f32[800,256]{1,0:T(8,128)S(1)}, u32[]{:S(2)}, u32[]{:S(2)}) collective-permute-start(f32[800,256]{1,0:T(8,128)S(1)} %get-tuple-element.90), channel_id=1, source_target_pairs={{0,64},{4,68},{8,72},{12,76},{16,24},{20,28},{24,16},{28,20},{32,9... | collective-permute-start | bytes 2457608 | tf_op jit(solution)/shard_map/ppermute | solution.py:380
  45.1 1.4 %collective-permute-start.11 = (f32[256,512]{1,0:T(8,128)S(1)}, f32[256,512]{1,0:T(8,128)S(1)}, u32[]{:S(2)}, u32[]{:S(2)}) collective-permute-start(f32[256,512]{1,0:T(8,128)S(1)} %get-tuple-element.84), channel_id=1, source_target_pairs={{0,2},{1,3},{2,0},{3,1},{4,6},{5,7},{6,4},{7,5},{8,10},{9,11},{10,... | collective-permute-start | bytes 1572872 | tf_op jit(solution)/shard_map/ppermute | solution.py:502
  46.5 5.1 %collective-permute-done.12.refs_0_ = f32[256,512]{1,0:T(8,128)S(1)} collective-permute-done((f32[256,512]{1,0:T(8,128)S(1)}, f32[256,512]{1,0:T(8,128)S(1)}, u32[]{:S(2)}, u32[]{:S(2)}) %collective-permute-start.12) | collective-permute-done | bytes 524320 | tf_op jit(solution)/shard_map/ppermute | solution.py:502
  51.6 0.5 collective-permute-start.13
  52.3 1.7 %collective-permute-done.15.ahead_ref = f32[800,256]{1,0:T(8,128)S(1)} collective-permute-done((f32[800,256]{1,0:T(8,128)S(1)}, f32[800,256]{1,0:T(8,128)S(1)}, u32[]{:S(2)}, u32[]{:S(2)}) %collective-permute-start.15) | collective-permute-done | bytes 819232 | tf_op jit(solution)/shard_map/ppermute | solution.py:380
  54.0 9.6 %collective-permute-done.16.far_ref = f32[800,256]{1,0:T(8,128)S(1)} collective-permute-done((f32[800,256]{1,0:T(8,128)S(1)}, f32[800,256]{1,0:T(8,128)S(1)}, u32[]{:S(2)}, u32[]{:S(2)}) %collective-permute-start.16) | collective-permute-done | bytes 819232 | tf_op jit(solution)/shard_map/ppermute | solution.py:380
  63.6 0.7 shard_map.127
  64.3 1.3 %collective-permute-start.17 = (f32[200,256]{1,0:T(8,128)S(1)}, f32[200,256]{1,0:T(8,128)S(1)}, u32[]{:S(2)}, u32[]{:S(2)}) collective-permute-start(f32[200,256]{1,0:T(8,128)S(1)} %get-tuple-element.92), channel_id=1, source_target_pairs={{0,4},{4,8},{8,12},{12,0},{16,48},{20,52},{24,56},{28,60},{32,36},... | collective-permute-start | bytes 614408 | tf_op jit(solution)/shard_map/ppermute | solution.py:380
  65.8 1.8 %collective-permute-start.19 = (f32[200,256]{1,0:T(8,128)S(1)}, f32[200,256]{1,0:T(8,128)S(1)}, u32[]{:S(2)}, u32[]{:S(2)}) collective-permute-start(f32[200,256]{1,0:T(8,128)S(1)} %get-tuple-element.94), channel_id=1, source_target_pairs={{0,8},{4,12},{8,0},{12,4},{16,80},{20,84},{24,88},{28,92},{32,40},... | collective-permute-start | bytes 614408 | tf_op jit(solution)/shard_map/ppermute | solution.py:380
  67.7 1.6 %collective-permute-done.17.back_ref = f32[200,256]{1,0:T(8,128)S(1)} collective-permute-done((f32[200,256]{1,0:T(8,128)S(1)}, f32[200,256]{1,0:T(8,128)S(1)}, u32[]{:S(2)}, u32[]{:S(2)}) %collective-permute-start.17) | collective-permute-done | bytes 204832 | tf_op jit(solution)/shard_map/ppermute | solution.py:380
  69.3 1.2 collective-permute-done.18.ahead_ref
  70.5 2.5 %collective-permute-done.19.far_ref = f32[200,256]{1,0:T(8,128)S(1)} collective-permute-done((f32[200,256]{1,0:T(8,128)S(1)}, f32[200,256]{1,0:T(8,128)S(1)}, u32[]{:S(2)}, u32[]{:S(2)}) %collective-permute-start.19) | collective-permute-done | bytes 204832 | tf_op jit(solution)/shard_map/ppermute | solution.py:380
  73.1 1.8 %collective-permute-start.22 = (f32[200,256]{1,0:T(8,128)S(1)}, f32[200,256]{1,0:T(8,128)S(1)}, u32[]{:S(2)}, u32[]{:S(2)}) collective-permute-start(f32[200,256]{1,0:T(8,128)S(1)} %shard_map.128.own_ref), channel_id=1, source_target_pairs={{0,8},{4,12},{8,0},{12,4},{16,80},{20,84},{24,88},{28,92},{32,40},... | collective-permute-start | bytes 614408 | tf_op jit(solution)/shard_map/ppermute | solution.py:380
  74.9 1.4 %collective-permute-start.20 = (f32[200,256]{1,0:T(8,128)S(1)}, f32[200,256]{1,0:T(8,128)S(1)}, u32[]{:S(2)}, u32[]{:S(2)}) collective-permute-start(f32[200,256]{1,0:T(8,128)S(1)} %shard_map.128.own_ref), channel_id=1, source_target_pairs={{0,12},{4,0},{8,4},{12,8},{16,112},{20,116},{24,120},{28,124},{32,... | collective-permute-start | bytes 614408 | tf_op jit(solution)/shard_map/ppermute | solution.py:380
  76.6 2.8 %collective-permute-done.22.far_ref = f32[200,256]{1,0:T(8,128)S(1)} collective-permute-done((f32[200,256]{1,0:T(8,128)S(1)}, f32[200,256]{1,0:T(8,128)S(1)}, u32[]{:S(2)}, u32[]{:S(2)}) %collective-permute-start.22) | collective-permute-done | bytes 204832 | tf_op jit(solution)/shard_map/ppermute | solution.py:380
  79.4 1.4 %collective-permute-done.21.back_ref = f32[200,256]{1,0:T(8,128)S(1)} collective-permute-done((f32[200,256]{1,0:T(8,128)S(1)}, f32[200,256]{1,0:T(8,128)S(1)}, u32[]{:S(2)}, u32[]{:S(2)}) %collective-permute-start.21) | collective-permute-done | bytes 204832 | tf_op jit(solution)/shard_map/ppermute | solution.py:380
  80.7 1.0 collective-permute-done.20.ahead_ref
  81.7 0.6 shard_map.129.refs_0_
  82.3 0.9 collective-permute-start.25
  83.2 1.3 %collective-permute-start.24 = (f32[800,256]{1,0:T(8,128)S(1)}, f32[800,256]{1,0:T(8,128)S(1)}, u32[]{:S(2)}, u32[]{:S(2)}) collective-permute-start(f32[800,256]{1,0:T(8,128)S(1)} %shard_map.129.refs_0_), channel_id=1, source_target_pairs={{0,32},{4,36},{8,40},{12,44},{16,20},{20,24},{24,28},{28,16},{32,6... | collective-permute-start | bytes 2457608 | tf_op jit(solution)/shard_map/ppermute | solution.py:380
  84.7 10.6 %collective-permute-done.25.refs_1_.refs_3_ = f32[800,256]{1,0:T(8,128)S(1)} collective-permute-done((f32[800,256]{1,0:T(8,128)S(1)}, f32[800,256]{1,0:T(8,128)S(1)}, u32[]{:S(2)}, u32[]{:S(2)}) %collective-permute-start.25) | collective-permute-done | bytes 819232 | tf_op jit(solution)/shard_map/ppermute | solution.py:380
  95.2 5.6 %collective-permute-start.29 = (f32[800,256]{1,0:T(8,128)S(1)}, f32[800,256]{1,0:T(8,128)S(1)}, u32[]{:S(2)}, u32[]{:S(2)}) collective-permute-start(f32[800,256]{1,0:T(8,128)S(1)} %collective-permute-done.25.refs_1_.refs_3_), channel_id=1, source_target_pairs={{0,16},{16,0},{32,48},{48,32},{64,80},{80,64},{96,112},{112,96},{1... | collective-permute-start | bytes 2457608 | tf_op jit(solution)/shard_map/ppermute | solution.py:385
  100.9 1.7 %shard_map.130 = (f32[3,2048,256]{2,1,0:T(8,128)}, f32[800,256]{1,0:T(8,128)S(1)}) custom-call(s32[5]{0:T(128)S(1)} %stack.23.pos_ref, f32[800,256]{1,0:T(8,128)S(1)} %shard_map.129.refs_0_, f32[800,256]{1,0:T(8,128)S(1)} %collective-permute-done.25.refs_1_.refs_3_), custom_call_target="tpu_custom_call" | custom-call | tf_op jit(solution)/shard_map/pallas_call | solution.py:524
  102.7 15.9 %collective-permute-start.28 = (f32[800,256]{1,0:T(8,128)S(1)}, f32[800,256]{1,0:T(8,128)S(1)}, u32[]{:S(2)}, u32[]{:S(2)}) collective-permute-start(f32[800,256]{1,0:T(8,128)S(1)} %collective-permute-done.24.refs_1_.refs_2_), channel_id=1, source_target_pairs={{0,16},{16,0},{32,48},{48,32},{64,80},{80,64},{96,112},{112,96},{1... | collective-permute-start | bytes 2457608 | tf_op jit(solution)/shard_map/ppermute | solution.py:385
  118.6 2.3 %shard_map.131.refs_8_ = f32[3,2048,256]{2,1,0:T(8,128)} custom-call(s32[5]{0:T(128)S(1)} %stack.23.pos_ref, f32[800,256]{1,0:T(8,128)S(1)} %collective-permute-done.23.refs_0_.refs_1_, f32[800,256]{1,0:T(8,128)S(1)} %collective-permute-done.24.refs_1_.refs_2_, ...), custom_call_target="tpu_custom_call", output_to_operand_aliasing={{}: (5, {})} | custom-call | tf_op jit(solution)/shard_map/pallas_call | solution.py:524
  120.9 0.8 collective-permute-done.27.refs_5_
  121.7 2.4 %shard_map.132 = (f32[3,2048,256]{2,1,0:T(8,128)}, f32[2,128,128]{2,1,0:T(8,128)}, f32[2,128]{1,0:T(2,128)}, f32[2]{0:T(128)}) custom-call(s32[5]{0:T(128)S(1)} %stack.23.pos_ref, f32[800,256]{1,0:T(8,128)S(1)} %shard_map.129.refs_0_, f32[800,256]{1,0:T(8,128)S(1)} %collective-permute-done.23.refs_0_.refs_1_, ...), custom_call_target="tpu_custom_call", output_to_operand_aliasing={{0}: (9, {})} | custom-call | tf_op jit(solution)/shard_map/pallas_call | solution.py:540
  (43 shorter events, 2.9 us)
Async XLA Ops:
  0.6 9.1 %copy-start.4 = (f32[1,2,256]{2,1,0:T(2,128)S(1)}, f32[1,2,256]{2,1,0:T(2,128)}, u32[]{:S(2)}) copy-start(f32[1,2,256]{2,1,0:T(2,128)} %gate_ref.7) | copy-start | bytes 6148
  0.6 9.0 %copy-start.5 = (f32[2]{0:T(128)S(1)}, f32[2]{0:T(128)}, u32[]{:S(2)}) copy-start(f32[2]{0:T(128)} %base_ref.7) | copy-start | bytes 28
  0.8 20.9 %copy-start.2 = (f32[2,128,128]{2,1,0:T(8,128)S(1)}, f32[2,128,128]{2,1,0:T(8,128)}, u32[]{:S(2)}) copy-start(f32[2,128,128]{2,1,0:T(8,128)} %init_ref.3) | copy-start | bytes 393220
  0.8 20.9 %copy-start.3 = (bf16[1,256,256]{2,1,0:T(8,128)(2,1)S(1)}, bf16[1,256,256]{2,1,0:T(8,128)(2,1)}, u32[]{:S(2)}) copy-start(bf16[1,256,256]{2,1,0:T(8,128)(2,1)} %up_ref.3) | copy-start | bytes 393220
  0.8 20.9 %copy-start.6 = (f32[2,128]{1,0:T(2,128)S(1)}, f32[2,128]{1,0:T(2,128)}, u32[]{:S(2)}) copy-start(f32[2,128]{1,0:T(2,128)} %gain_ref.1) | copy-start | bytes 3076
  6.3 10.7 %collective-permute-start.4 = (f32[256,1024]{1,0:T(8,128)S(1)}, f32[256,1024]{1,0:T(8,128)S(1)}, u32[]{:S(2)}, u32[]{:S(2)}) collective-permute-start(f32[256,1024]{1,0:T(8,128)S(1)} %get-tuple-element.62), channel_id=1, source_target_pairs={{0,16},{16,0},{32,48},{48,32},{64,80},{80,64},{96,112},{112,96},{1... | collective-permute-start | bytes 3145736 | tf_op jit(solution)/shard_map/ppermute | solution.py:385
  7.1 7.0 %collective-permute-start = (f32[2,128,128]{2,1,0:T(8,128)S(1)}, f32[2,128,128]{2,1,0:T(8,128)S(1)}, u32[]{:S(2)}, u32[]{:S(2)}) collective-permute-start(f32[2,128,128]{2,1,0:T(8,128)S(1)} %get-tuple-element.54), channel_id=1, source_target_pairs={{0,4},{8,12},{1,5},{9,13},{2,6},{10,14},{3,7},{11,15},{16,20},{24,... | collective-permute-start | bytes 393224 | tf_op jit(solution)/shard_map/ppermute | solution.py:458
  8.4 9.6 %collective-permute-start.3 = (f32[2,128,128]{2,1,0:T(8,128)S(1)}, f32[2,128,128]{2,1,0:T(8,128)S(1)}, u32[]{:S(2)}, u32[]{:S(2)}) collective-permute-start(f32[2,128,128]{2,1,0:T(8,128)S(1)} %get-tuple-element.55.d_ref), channel_id=1, source_target_pairs={{8,12},{4,0},{9,13},{5,1},{10,14},{6,2},{11,15},{7,3},{24,28},{20,... | collective-permute-start | bytes 393224 | tf_op jit(solution)/shard_map/ppermute | solution.py:459
  13.6 22.6 %copy-start = (bf16[3,2048,256]{2,1,0:T(8,128)(2,1)S(1)}, bf16[3,2048,256]{2,1,0:T(8,128)(2,1)}, u32[]{:S(2)}) copy-start(bf16[3,2048,256]{2,1,0:T(8,128)(2,1)} %w_ref.1) | copy-start | bytes 9437188
  14.3 7.3 %collective-permute-start.2 = (f32[2,128,128]{2,1,0:T(8,128)S(1)}, f32[2,128,128]{2,1,0:T(8,128)S(1)}, u32[]{:S(2)}, u32[]{:S(2)}) collective-permute-start(f32[2,128,128]{2,1,0:T(8,128)S(1)} %shard_map.120), channel_id=1, source_target_pairs={{4,12},{5,13},{6,14},{7,15},{20,28},{21,29},{22,30},{23,31},{36,44... | collective-permute-start | bytes 393224 | tf_op jit(solution)/shard_map/ppermute | solution.py:477
  15.7 5.9 %collective-permute-start.1 = (f32[2,128,128]{2,1,0:T(8,128)S(1)}, f32[2,128,128]{2,1,0:T(8,128)S(1)}, u32[]{:S(2)}, u32[]{:S(2)}) collective-permute-start(f32[2,128,128]{2,1,0:T(8,128)S(1)} %shard_map.120), channel_id=1, source_target_pairs={{4,8},{5,9},{6,10},{7,11},{20,24},{21,25},{22,26},{23,27},{36,40},... | collective-permute-start | bytes 393224 | tf_op jit(solution)/shard_map/ppermute | solution.py:476
  16.4 15.1 %collective-permute-start.9 = (f32[2,128,128]{2,1,0:T(8,128)S(1)}, f32[2,128,128]{2,1,0:T(8,128)S(1)}, u32[]{:S(2)}, u32[]{:S(2)}) collective-permute-start(f32[2,128,128]{2,1,0:T(8,128)S(1)} %get-tuple-element.55.d_ref), channel_id=1, source_target_pairs={{8,0},{9,1},{10,2},{11,3},{24,16},{25,17},{26,18},{27,19},{40,32},... | collective-permute-start | bytes 393224 | tf_op jit(solution)/shard_map/ppermute | solution.py:461
  17.1 14.4 %collective-permute-start.8 = (f32[2,128,128]{2,1,0:T(8,128)S(1)}, f32[2,128,128]{2,1,0:T(8,128)S(1)}, u32[]{:S(2)}, u32[]{:S(2)}) collective-permute-start(f32[2,128,128]{2,1,0:T(8,128)S(1)} %get-tuple-element.55.d_ref), channel_id=1, source_target_pairs={{8,4},{9,5},{10,6},{11,7},{24,20},{25,21},{26,22},{27,23},{40,36},... | collective-permute-start | bytes 393224 | tf_op jit(solution)/shard_map/ppermute | solution.py:460
  23.2 8.3 %collective-permute-start.7 = (f32[2,128,128]{2,1,0:T(8,128)S(1)}, f32[2,128,128]{2,1,0:T(8,128)S(1)}, u32[]{:S(2)}, u32[]{:S(2)}) collective-permute-start(f32[2,128,128]{2,1,0:T(8,128)S(1)} %get-tuple-element.63.p_ref), channel_id=1, source_target_pairs={{12,0},{13,1},{14,2},{15,3},{28,16},{29,17},{30,18},{31,19},{44,32... | collective-permute-start | bytes 393224 | tf_op jit(solution)/shard_map/ppermute | solution.py:486
  24.5 7.0 %collective-permute-start.6 = (f32[2,128,128]{2,1,0:T(8,128)S(1)}, f32[2,128,128]{2,1,0:T(8,128)S(1)}, u32[]{:S(2)}, u32[]{:S(2)}) collective-permute-start(f32[2,128,128]{2,1,0:T(8,128)S(1)} %get-tuple-element.63.p_ref), channel_id=1, source_target_pairs={{12,4},{8,0},{13,5},{9,1},{14,6},{10,2},{15,7},{11,3},{28,20},{24,... | collective-permute-start | bytes 393224 | tf_op jit(solution)/shard_map/ppermute | solution.py:485
  27.0 4.5 %collective-permute-start.5 = (f32[2,128,128]{2,1,0:T(8,128)S(1)}, f32[2,128,128]{2,1,0:T(8,128)S(1)}, u32[]{:S(2)}, u32[]{:S(2)}) collective-permute-start(f32[2,128,128]{2,1,0:T(8,128)S(1)} %get-tuple-element.63.p_ref), channel_id=1, source_target_pairs={{12,8},{8,4},{4,0},{13,9},{9,5},{5,1},{14,10},{10,6},{6,2},{15,11}... | collective-permute-start | bytes 393224 | tf_op jit(solution)/shard_map/ppermute | solution.py:484
  34.1 4.4 %collective-permute-start.10 = (f32[1024,256]{1,0:T(8,128)S(1)}, f32[1024,256]{1,0:T(8,128)S(1)}, u32[]{:S(2)}, u32[]{:S(2)}) collective-permute-start(f32[1024,256]{1,0:T(8,128)S(1)} %get-tuple-element.79.all_ref.own_ref), channel_id=1, source_target_pairs={{0,16},{16,0},{32,48},{48,32},{64,80},{80,64},{96,112},{112,96},{1... | collective-permute-start | bytes 3145736 | tf_op jit(solution)/shard_map/ppermute | solution.py:385
  37.8 13.8 %collective-permute-start.12 = (f32[256,512]{1,0:T(8,128)S(1)}, f32[256,512]{1,0:T(8,128)S(1)}, u32[]{:S(2)}, u32[]{:S(2)}) collective-permute-start(f32[256,512]{1,0:T(8,128)S(1)} %get-tuple-element.85), channel_id=1, source_target_pairs={{0,1},{1,2},{2,3},{3,0},{4,5},{5,6},{6,7},{7,4},{8,9},{9,10},{10,1... | collective-permute-start | bytes 1572872 | tf_op jit(solution)/shard_map/ppermute | solution.py:502
  40.0 12.3 %collective-permute-start.14 = (f32[800,256]{1,0:T(8,128)S(1)}, f32[800,256]{1,0:T(8,128)S(1)}, u32[]{:S(2)}, u32[]{:S(2)}) collective-permute-start(f32[800,256]{1,0:T(8,128)S(1)} %get-tuple-element.88), channel_id=1, source_target_pairs={{0,32},{4,36},{8,40},{12,44},{16,20},{20,24},{24,28},{28,16},{32,6... | collective-permute-start | bytes 2457608 | tf_op jit(solution)/shard_map/ppermute | solution.py:380
  41.3 12.7 %collective-permute-start.15 = (f32[800,256]{1,0:T(8,128)S(1)}, f32[800,256]{1,0:T(8,128)S(1)}, u32[]{:S(2)}, u32[]{:S(2)}) collective-permute-start(f32[800,256]{1,0:T(8,128)S(1)} %get-tuple-element.89), channel_id=1, source_target_pairs={{0,96},{4,100},{8,104},{12,108},{16,28},{20,16},{24,20},{28,24},{3... | collective-permute-start | bytes 2457608 | tf_op jit(solution)/shard_map/ppermute | solution.py:380
  42.4 21.2 %collective-permute-start.16 = (f32[800,256]{1,0:T(8,128)S(1)}, f32[800,256]{1,0:T(8,128)S(1)}, u32[]{:S(2)}, u32[]{:S(2)}) collective-permute-start(f32[800,256]{1,0:T(8,128)S(1)} %get-tuple-element.90), channel_id=1, source_target_pairs={{0,64},{4,68},{8,72},{12,76},{16,24},{20,28},{24,16},{28,20},{32,9... | collective-permute-start | bytes 2457608 | tf_op jit(solution)/shard_map/ppermute | solution.py:380
  45.1 31.2 %collective-permute-start.11 = (f32[256,512]{1,0:T(8,128)S(1)}, f32[256,512]{1,0:T(8,128)S(1)}, u32[]{:S(2)}, u32[]{:S(2)}) collective-permute-start(f32[256,512]{1,0:T(8,128)S(1)} %get-tuple-element.84), channel_id=1, source_target_pairs={{0,2},{1,3},{2,0},{3,1},{4,6},{5,7},{6,4},{7,5},{8,10},{9,11},{10,... | collective-permute-start | bytes 1572872 | tf_op jit(solution)/shard_map/ppermute | solution.py:502
  51.6 24.7 %collective-permute-start.13 = (f32[256,512]{1,0:T(8,128)S(1)}, f32[256,512]{1,0:T(8,128)S(1)}, u32[]{:S(2)}, u32[]{:S(2)}) collective-permute-start(f32[256,512]{1,0:T(8,128)S(1)} %get-tuple-element.86), channel_id=1, source_target_pairs={{0,3},{1,0},{2,1},{3,2},{4,7},{5,4},{6,5},{7,6},{8,11},{9,8},{10,9... | collective-permute-start | bytes 1572872 | tf_op jit(solution)/shard_map/ppermute | solution.py:502
  64.3 5.0 %collective-permute-start.17 = (f32[200,256]{1,0:T(8,128)S(1)}, f32[200,256]{1,0:T(8,128)S(1)}, u32[]{:S(2)}, u32[]{:S(2)}) collective-permute-start(f32[200,256]{1,0:T(8,128)S(1)} %get-tuple-element.92), channel_id=1, source_target_pairs={{0,4},{4,8},{8,12},{12,0},{16,48},{20,52},{24,56},{28,60},{32,36},... | collective-permute-start | bytes 614408 | tf_op jit(solution)/shard_map/ppermute | solution.py:380
  65.6 4.9 %collective-permute-start.18 = (f32[200,256]{1,0:T(8,128)S(1)}, f32[200,256]{1,0:T(8,128)S(1)}, u32[]{:S(2)}, u32[]{:S(2)}) collective-permute-start(f32[200,256]{1,0:T(8,128)S(1)} %get-tuple-element.93), channel_id=1, source_target_pairs={{0,12},{4,0},{8,4},{12,8},{16,112},{20,116},{24,120},{28,124},{32,... | collective-permute-start | bytes 614408 | tf_op jit(solution)/shard_map/ppermute | solution.py:380
  65.8 7.2 %collective-permute-start.19 = (f32[200,256]{1,0:T(8,128)S(1)}, f32[200,256]{1,0:T(8,128)S(1)}, u32[]{:S(2)}, u32[]{:S(2)}) collective-permute-start(f32[200,256]{1,0:T(8,128)S(1)} %get-tuple-element.94), channel_id=1, source_target_pairs={{0,8},{4,12},{8,0},{12,4},{16,80},{20,84},{24,88},{28,92},{32,40},... | collective-permute-start | bytes 614408 | tf_op jit(solution)/shard_map/ppermute | solution.py:380
  73.1 6.3 %collective-permute-start.22 = (f32[200,256]{1,0:T(8,128)S(1)}, f32[200,256]{1,0:T(8,128)S(1)}, u32[]{:S(2)}, u32[]{:S(2)}) collective-permute-start(f32[200,256]{1,0:T(8,128)S(1)} %shard_map.128.own_ref), channel_id=1, source_target_pairs={{0,8},{4,12},{8,0},{12,4},{16,80},{20,84},{24,88},{28,92},{32,40},... | collective-permute-start | bytes 614408 | tf_op jit(solution)/shard_map/ppermute | solution.py:380
  74.8 5.9 %collective-permute-start.21 = (f32[200,256]{1,0:T(8,128)S(1)}, f32[200,256]{1,0:T(8,128)S(1)}, u32[]{:S(2)}, u32[]{:S(2)}) collective-permute-start(f32[200,256]{1,0:T(8,128)S(1)} %shard_map.128.own_ref), channel_id=1, source_target_pairs={{0,4},{4,8},{8,12},{12,0},{16,48},{20,52},{24,56},{28,60},{32,36},... | collective-permute-start | bytes 614408 | tf_op jit(solution)/shard_map/ppermute | solution.py:380
  74.9 6.8 %collective-permute-start.20 = (f32[200,256]{1,0:T(8,128)S(1)}, f32[200,256]{1,0:T(8,128)S(1)}, u32[]{:S(2)}, u32[]{:S(2)}) collective-permute-start(f32[200,256]{1,0:T(8,128)S(1)} %shard_map.128.own_ref), channel_id=1, source_target_pairs={{0,12},{4,0},{8,4},{12,8},{16,112},{20,116},{24,120},{28,124},{32,... | collective-permute-start | bytes 614408 | tf_op jit(solution)/shard_map/ppermute | solution.py:380
  76.6 44.3 %copy-start.1 = (bf16[1,256,512]{2,1,0:T(8,128)(2,1)}, bf16[1,256,512]{2,1,0:T(8,128)(2,1)S(1)}, u32[]{:S(2)}) copy-start(bf16[1,256,512]{2,1,0:T(8,128)(2,1)S(1)} %fusion.refs_0_) | copy-start | bytes 786436
  82.3 12.9 %collective-permute-start.25 = (f32[800,256]{1,0:T(8,128)S(1)}, f32[800,256]{1,0:T(8,128)S(1)}, u32[]{:S(2)}, u32[]{:S(2)}) collective-permute-start(f32[800,256]{1,0:T(8,128)S(1)} %shard_map.129.refs_0_), channel_id=1, source_target_pairs={{0,64},{4,68},{8,72},{12,76},{16,24},{20,28},{24,16},{28,20},{32,9... | collective-permute-start | bytes 2457608 | tf_op jit(solution)/shard_map/ppermute | solution.py:380
  83.2 19.5 %collective-permute-start.24 = (f32[800,256]{1,0:T(8,128)S(1)}, f32[800,256]{1,0:T(8,128)S(1)}, u32[]{:S(2)}, u32[]{:S(2)}) collective-permute-start(f32[800,256]{1,0:T(8,128)S(1)} %shard_map.129.refs_0_), channel_id=1, source_target_pairs={{0,32},{4,36},{8,40},{12,44},{16,20},{20,24},{24,28},{28,16},{32,6... | collective-permute-start | bytes 2457608 | tf_op jit(solution)/shard_map/ppermute | solution.py:380
  84.5 34.1 %collective-permute-start.23 = (f32[800,256]{1,0:T(8,128)S(1)}, f32[800,256]{1,0:T(8,128)S(1)}, u32[]{:S(2)}, u32[]{:S(2)}) collective-permute-start(f32[800,256]{1,0:T(8,128)S(1)} %shard_map.129.refs_0_), channel_id=1, source_target_pairs={{0,96},{4,100},{8,104},{12,108},{16,28},{20,16},{24,20},{28,24},{3... | collective-permute-start | bytes 2457608 | tf_op jit(solution)/shard_map/ppermute | solution.py:380
  95.2 23.3 %collective-permute-start.29 = (f32[800,256]{1,0:T(8,128)S(1)}, f32[800,256]{1,0:T(8,128)S(1)}, u32[]{:S(2)}, u32[]{:S(2)}) collective-permute-start(f32[800,256]{1,0:T(8,128)S(1)} %collective-permute-done.25.refs_1_.refs_3_), channel_id=1, source_target_pairs={{0,16},{16,0},{32,48},{48,32},{64,80},{80,64},{96,112},{112,96},{1... | collective-permute-start | bytes 2457608 | tf_op jit(solution)/shard_map/ppermute | solution.py:385
  102.6 16.0 %collective-permute-start.26 = (f32[800,256]{1,0:T(8,128)S(1)}, f32[800,256]{1,0:T(8,128)S(1)}, u32[]{:S(2)}, u32[]{:S(2)}) collective-permute-start(f32[800,256]{1,0:T(8,128)S(1)} %get-tuple-element.95), channel_id=1, source_target_pairs={{0,16},{16,0},{32,48},{48,32},{64,80},{80,64},{96,112},{112,96},{1... | collective-permute-start | bytes 2457608 | tf_op jit(solution)/shard_map/ppermute | solution.py:385
  102.7 18.2 %collective-permute-start.28 = (f32[800,256]{1,0:T(8,128)S(1)}, f32[800,256]{1,0:T(8,128)S(1)}, u32[]{:S(2)}, u32[]{:S(2)}) collective-permute-start(f32[800,256]{1,0:T(8,128)S(1)} %collective-permute-done.24.refs_1_.refs_2_), channel_id=1, source_target_pairs={{0,16},{16,0},{32,48},{48,32},{64,80},{80,64},{96,112},{112,96},{1... | collective-permute-start | bytes 2457608 | tf_op jit(solution)/shard_map/ppermute | solution.py:385
  118.6 3.1 %collective-permute-start.27 = (f32[800,256]{1,0:T(8,128)S(1)}, f32[800,256]{1,0:T(8,128)S(1)}, u32[]{:S(2)}, u32[]{:S(2)}) collective-permute-start(f32[800,256]{1,0:T(8,128)S(1)} %collective-permute-done.23.refs_0_.refs_1_), channel_id=1, source_target_pairs={{0,16},{16,0},{32,48},{48,32},{64,80},{80,64},{96,112},{112,96},{1... | collective-permute-start | bytes 2457608 | tf_op jit(solution)/shard_map/ppermute | solution.py:385

commit v10 on v9

--- a/solution.py
+++ b/solution.py
@@ -12,8 +12,7 @@
 RING = 4
 TURNS = (0, 1, 3, 2)
 CHUNK = 256
-SLICE = CHUNK // RING
-PIECE = 32
+PIECE = 24
 EXTRA = 2 * RING * PIECE
 F32 = jnp.float32
 BF = jnp.bfloat16
@@ -288,31 +287,8 @@
         out_ref[...] = total + lax.dot_general(ds[2], w_ref[2, rows, :], NT, preferred_element_type=F32)
 
 
-def slice_rows(pos_ref, turn):
-    at = (pos_ref[2] + turn) & (RING - 1)
-    taken = [
-        (pl.ds(pl.multiple_of(m * CHUNK + at * SLICE, SLICE), SLICE), slice(m * SLICE, (m + 1) * SLICE))
-        for m in range(3)
-    ]
-    few = PIECE // RING
-    extra = pl.ds(pl.multiple_of(3 * CHUNK + at * few, few), few)
-    return taken + [(extra, slice(3 * SLICE, 3 * SLICE + few))]
-
-
-def split_kernel(pos_ref, own_ref, back_ref, ahead_ref, far_ref, *refs):
-    for turn, out_ref in zip(TURNS, refs[-RING:]):
-        for rows, to in slice_rows(pos_ref, turn):
-            out_ref[to, :] = (own_ref[rows, :] + far_ref[rows, :]) + (back_ref[rows, :] + ahead_ref[rows, :])
-
-
-def sum_kernel(own_ref, back_ref, ahead_ref, far_ref, out_ref):
-    out_ref[...] = (own_ref[...] + far_ref[...]) + (back_ref[...] + ahead_ref[...])
-
-
-def join_kernel(pos_ref, own_ref, ahead_ref, back_ref, far_ref, *refs):
-    for turn, part_ref in zip(TURNS, (own_ref, ahead_ref, back_ref, far_ref)):
-        for rows, to in slice_rows(pos_ref, turn):
-            refs[-1][rows, :] = part_ref[to, :]
+def sum_kernel(own_ref, back_ref, ahead_ref, far_ref, *refs):
+    refs[-1][...] = (own_ref[...] + far_ref[...]) + (back_ref[...] + ahead_ref[...])
 
 
 def place_kernel(pos_ref, *refs, which, passed):
@@ -501,20 +477,16 @@
     def along_head(terms, turn):
         return lax.ppermute(terms, "head", [(i, (i + turn) % RING) for i in range(RING)])
 
-    *chunks, near_two, far_quarter = whole(
+    *chunks, near_one, near_two = whole(
         product_kernel, (chunk,) * RING + (quarter,) * 2, [SM] + [VM] * 6, {5: RING, 6: RING + 1}
-    )(pos, tokt, other_tokt, grads, swap(grads), *quarters[2:])
+    )(pos, tokt, other_tokt, grads, swap(grads), *quarters[1:3])
     own, away = chunks[0], round_turn(chunks[1:], True)
-    from_back, from_ahead, from_far = along_head(quarters[1], 1), along_head(near_two, 3), along_head(far_quarter, 2)
-
-    piece = vmem(3 * SLICE + PIECE // RING, wide)
-    pieces = whole(split_kernel, (piece,) * RING, [SM] + [VM] * 4 + [anywhere])(pos, own, *away, from_back)
+    from_back, from_ahead, from_far = along_head(near_one, 1), along_head(near_two, 3), along_head(quarters[3], 2)
+
+    part_sum = whole(sum_kernel, chunk, [VM] * 4 + [anywhere] * 2)(own, *away, from_back, from_ahead)
     grad_tokens = ((quarters[0] + from_far) + (from_back + from_ahead)).astype(BF).reshape(1, n, -1)
-    own, away = pieces[0], pieces[1:]
-    part_sum = whole(sum_kernel, piece, [VM] * 4)(own, *round_turn(away, False))
-    from_back, from_ahead, from_far = round_turn([part_sum] * 3, False)
-    total = whole(join_kernel, chunk, [SM] + [VM] * 4 + [anywhere])(
-        pos, part_sum, from_ahead, from_back, from_far, grad_tokens
+    total = whole(sum_kernel, chunk, [VM] * 4 + [anywhere])(
+        part_sum, *round_turn([part_sum] * 3, False), grad_tokens
     )
     from_back, from_ahead, from_far = round_turn([total] * 3, True)
     out = shape(3, model, wide)

time: 125 us -> 117 us (0.936)
  the two profiles are of different devices: /device:TPU:123 before, /device:TPU:1 now
where the time goes in v10:
time: 117 us
  starting transfers between devices  44.7 us (38%)
  waiting for transfers between devices  44.1 us (38%)
  Pallas kernels  26.6 us (23%)
    ppermute x3, waiting for transfers between devices, along_head(): lax.ppermute(terms, 'head', [(i, (i + turn) % RING) for i in range(RING)])  20.7 us
    ppermute x9, waiting for transfers between devices, round_turn(): lax.ppermute(chunk, ('dp', 'ctx'), moves(first, turn))  18.3 us
    ppermute x9, starting transfers between devices, round_turn(): lax.ppermute(chunk, ('dp', 'ctx'), moves(first, turn))  14 us
    ppermute x6, starting transfers between devices, swap(): return lax.ppermute(value, 'dp', [(i, i ^ 1) for i in range(2 * RING)])  11.5 us
    ppermute x3, starting transfers between devices, along_head(): lax.ppermute(terms, 'head', [(i, (i + turn) % RING) for i in range(RING)])  7.36 us
    pallas_call x1, Pallas kernels, body(): pl.pallas_call(maps_kernel, grid=(1,), out_shape=(wide_f32, wide_f32, vme...  5.56 us
    pallas_call x2, Pallas kernels, place(): pl.pallas_call(functools.partial(place_kernel, which=which, passed=passed...  4.03 us
    pallas_call x1, Pallas kernels, body(): pl.pallas_call(reach_kernel, grid=(1,), out_shape=(wide_f32, square, wide...  3.89 us
  transfers between devices with their start and end apart: 27, of which 10 were waited for; matrix products, arithmetic and copies ran while one was open for 0% of the time, Pallas kernels for 12%

profile of v10, /device:TPU:1, one launch (start us, length us, event | category | flops | bytes accessed | tf_op | source)
XLA Modules:
  0.0 117.0 jit_solution(15775483091027735746)
XLA Ops:
  0.8 5.6 %shard_map.118 = (f32[256,256]{1,0:T(8,128)S(1)}, f32[256,256]{1,0:T(8,128)S(1)}, f32[2,256,128]{2,1,0:T(8,128)S(1)}, f32[2,256,256]{2,1,0:T(8,128)S(1)}, f32[2,...) custom-call(s32[5]{0:T(128)S(1)} %stack.23.pos_ref, ...), custom_call_target="tpu_custom_call" | custom-call | tf_op jit(solution)/shard_map/pallas_call | solution.py:422
  6.3 1.5 %collective-permute-start.4 = (f32[256,1024]{1,0:T(8,128)S(1)}, f32[256,1024]{1,0:T(8,128)S(1)}, u32[]{:S(2)}, u32[]{:S(2)}) collective-permute-start(f32[256,1024]{1,0:T(8,128)S(1)} %get-tuple-element.58), channel_id=1, source_target_pairs={{0,16},{16,0},{32,48},{48,32},{64,80},{80,64},{96,112},{112,96},{1... | collective-permute-start | bytes 3145736 | tf_op jit(solution)/shard_map/ppermute | solution.py:361
  7.8 3.3 %collective-permute-start = (f32[2,128,128]{2,1,0:T(8,128)S(1)}, f32[2,128,128]{2,1,0:T(8,128)S(1)}, u32[]{:S(2)}, u32[]{:S(2)}) collective-permute-start(f32[2,128,128]{2,1,0:T(8,128)S(1)} %get-tuple-element.50), channel_id=1, source_target_pairs={{0,4},{8,12},{1,5},{9,13},{2,6},{10,14},{3,7},{11,15},{16,20},{24,... | collective-permute-start | bytes 393224 | tf_op jit(solution)/shard_map/ppermute | solution.py:434
  11.1 1.3 %collective-permute-start.3 = (f32[2,128,128]{2,1,0:T(8,128)S(1)}, f32[2,128,128]{2,1,0:T(8,128)S(1)}, u32[]{:S(2)}, u32[]{:S(2)}) collective-permute-start(f32[2,128,128]{2,1,0:T(8,128)S(1)} %get-tuple-element.51.d_ref), channel_id=1, source_target_pairs={{8,12},{4,0},{9,13},{5,1},{10,14},{6,2},{11,15},{7,3},{24,28},{20,... | collective-permute-start | bytes 393224 | tf_op jit(solution)/shard_map/ppermute | solution.py:435
  12.4 3.9 %shard_map.119 = (f32[256,256]{1,0:T(8,128)S(1)}, f32[2,256,256]{2,1,0:T(8,128)S(1)}, f32[256,256]{1,0:T(8,128)S(1)}, f32[256,256]{1,0:T(8,128)S(1)}, f32[256,25...) custom-call(s32[5]{0:T(128)S(1)} %stack.23.pos_ref, f32[2]{0:T(128)S(1)} %copy-done.5, ...), custom_call_target="tpu_custom_call" | custom-call | tf_op jit(solution)/shard_map/pallas_call | solution.py:440
  16.4 0.2 shard_map.120
  16.6 0.8 collective-permute-start.2
  17.4 0.7 collective-permute-start.1
  18.1 1.3 %collective-permute-start.9 = (f32[2,128,128]{2,1,0:T(8,128)S(1)}, f32[2,128,128]{2,1,0:T(8,128)S(1)}, u32[]{:S(2)}, u32[]{:S(2)}) collective-permute-start(f32[2,128,128]{2,1,0:T(8,128)S(1)} %get-tuple-element.51.d_ref), channel_id=1, source_target_pairs={{8,0},{9,1},{10,2},{11,3},{24,16},{25,17},{26,18},{27,19},{40,32},... | collective-permute-start | bytes 393224 | tf_op jit(solution)/shard_map/ppermute | solution.py:437
  19.4 0.7 collective-permute-start.8
  20.0 0.2 shard_map.121.after_ref.other_tokt_ref
  20.3 1.5 %shard_map.122 = (f32[2,128,128]{2,1,0:T(8,128)S(1)}, f32[256,256]{1,0:T(8,128)S(1)}, f32[2,128,128]{2,1,0:T(8,128)S(1)}, f32[2,128]{1,0:T(2,128)S(1)}) custom-call(s32[5]{0:T(128)S(1)} %stack.23.pos_ref, f32[2,128,128]{2,1,0:T(8,128)S(1)} %copy-done.2, f32[2,128,128]{2,1,0:T(8,128)S(1)} %collective-permute-done.w_ref.near_ref, ...), custom_call_target="tpu_custom_call" | custom-call | tf_op jit(solution)/shard_map/pallas_call | solution.py:456
  21.9 1.3 %collective-permute-start.7 = (f32[2,128,128]{2,1,0:T(8,128)S(1)}, f32[2,128,128]{2,1,0:T(8,128)S(1)}, u32[]{:S(2)}, u32[]{:S(2)}) collective-permute-start(f32[2,128,128]{2,1,0:T(8,128)S(1)} %get-tuple-element.59.p_ref), channel_id=1, source_target_pairs={{12,0},{13,1},{14,2},{15,3},{28,16},{29,17},{30,18},{31,19},{44,32... | collective-permute-start | bytes 393224 | tf_op jit(solution)/shard_map/ppermute | solution.py:462
  23.2 1.3 %collective-permute-start.6 = (f32[2,128,128]{2,1,0:T(8,128)S(1)}, f32[2,128,128]{2,1,0:T(8,128)S(1)}, u32[]{:S(2)}, u32[]{:S(2)}) collective-permute-start(f32[2,128,128]{2,1,0:T(8,128)S(1)} %get-tuple-element.59.p_ref), channel_id=1, source_target_pairs={{12,4},{8,0},{13,5},{9,1},{14,6},{10,2},{15,7},{11,3},{28,20},{24,... | collective-permute-start | bytes 393224 | tf_op jit(solution)/shard_map/ppermute | solution.py:461
  24.5 1.3 %collective-permute-start.5 = (f32[2,128,128]{2,1,0:T(8,128)S(1)}, f32[2,128,128]{2,1,0:T(8,128)S(1)}, u32[]{:S(2)}, u32[]{:S(2)}) collective-permute-start(f32[2,128,128]{2,1,0:T(8,128)S(1)} %get-tuple-element.59.p_ref), channel_id=1, source_target_pairs={{12,8},{8,4},{4,0},{13,9},{9,5},{5,1},{14,10},{10,6},{6,2},{15,11}... | collective-permute-start | bytes 393224 | tf_op jit(solution)/shard_map/ppermute | solution.py:460
  25.8 2.9 %shard_map.123 = (f32[256,256]{1,0:T(8,128)S(1)}, f32[256,256]{1,0:T(8,128)S(1)}, f32[256,256]{1,0:T(8,128)S(1)}, f32[256,256]{1,0:T(8,128)S(1)}, f32[2,256]{1,0:T(2,128)S(1)}) custom-call(f32[2]{0:T(128)S(1)} %copy-done.5, f32[1,2,256]{2,1,0:T(2,128)S(1)} %copy-done.4, f32[2,128,128]{2,1,0:T(8,128)S(1)} %get-tuple-element.60.w_ref, ...), custom_call_target="tpu_custom_call" | custom-call | tf_op jit(solution)/shard_map/pallas_call | solution.py:464
  28.6 1.8 %collective-permute-done.7.three_ref = f32[2,128,128]{2,1,0:T(8,128)S(1)} collective-permute-done((f32[2,128,128]{2,1,0:T(8,128)S(1)}, f32[2,128,128]{2,1,0:T(8,128)S(1)}, u32[]{:S(2)}, u32[]{:S(2)}) %collective-permute-start.7) | collective-permute-done | bytes 131104 | tf_op jit(solution)/shard_map/ppermute | solution.py:462
  30.4 2.0 %collective-permute-done.6.two_ref = f32[2,128,128]{2,1,0:T(8,128)S(1)} collective-permute-done((f32[2,128,128]{2,1,0:T(8,128)S(1)}, f32[2,128,128]{2,1,0:T(8,128)S(1)}, u32[]{:S(2)}, u32[]{:S(2)}) %collective-permute-start.6) | collective-permute-done | bytes 131104 | tf_op jit(solution)/shard_map/ppermute | solution.py:461
  32.4 2.5 %shard_map.124 = (f32[960,256]{1,0:T(8,128)S(1)}, f32[1,2,256]{2,1,0:T(2,128)}) custom-call(s32[5]{0:T(128)S(1)} %stack.23.pos_ref, f32[2]{0:T(128)S(1)} %copy-done.5, f32[1,2,256]{2,1,0:T(2,128)S(1)} %copy-done.4, f32[2,128,128]{2,1,0:T(8,128)S(1)} %collective-permute-done.5.one_ref, f32[2,128,128]{2,1,0:T(8,128)S(1)} %collective-permute-done.6.two_ref, ...), custom_call_target="tpu_custom_call" | custom-call | tf_op jit(solution)/shard_map/pallas_call | solution.py:468
  34.9 3.4 %collective-permute-start.11 = (f32[960,256]{1,0:T(8,128)S(1)}, f32[960,256]{1,0:T(8,128)S(1)}, u32[]{:S(2)}, u32[]{:S(2)}) collective-permute-start(f32[960,256]{1,0:T(8,128)S(1)} %get-tuple-element.75.all_ref.own_ref), channel_id=1, source_target_pairs={{0,16},{16,0},{32,48},{48,32},{64,80},{80,64},{96,112},{112,96},{1... | collective-permute-start | bytes 2949128 | tf_op jit(solution)/shard_map/ppermute | solution.py:361
  38.3 1.5 %shard_map.125 = (f32[256,512]{1,0:T(8,128)S(1)}, f32[256,512]{1,0:T(8,128)S(1)}, f32[256,512]{1,0:T(8,128)S(1)}, f32[256,512]{1,0:T(8,128)S(1)}) custom-call(s32[5]{0:T(128)S(1)} %stack.23.pos_ref, bf16[3,2048,256]{2,1,0:T(8,128)(2,1)S(1)} %copy-done, f32[960,256]{1,0:T(8,128)S(1)} %get-tuple-element.75.all_ref.own_ref), custom_call_target="tpu_custom_call" | custom-call | tf_op jit(solution)/shard_map/pallas_call | solution.py:475
  39.9 0.6 collective-permute-done.11.other_ref
  40.5 1.5 %shard_map.126 = (f32[792,256]{1,0:T(8,128)S(1)}, f32[792,256]{1,0:T(8,128)S(1)}, f32[792,256]{1,0:T(8,128)S(1)}, f32[792,256]{1,0:T(8,128)S(1)}, f32[256,512]{1,0:T(8,128)S(1)}, /*index=5*/f32[256,512]{1,0:T(8,128)S(1)}) custom-call(s32[5]{0:T(128)S(1)} %stack.23.pos_ref, ...), custom_call_target="tpu_custom_call", output_to_operand_aliasing={{4}: (5, {}), {5}: (6, {})} | custom-call | tf_op jit(solution)/shard_map/pallas_call | solution.py:480
  42.0 2.8 %collective-permute-start.14 = (f32[792,256]{1,0:T(8,128)S(1)}, f32[792,256]{1,0:T(8,128)S(1)}, u32[]{:S(2)}, u32[]{:S(2)}) collective-permute-start(f32[792,256]{1,0:T(8,128)S(1)} %get-tuple-element.84), channel_id=1, source_target_pairs={{0,32},{4,36},{8,40},{12,44},{16,20},{20,24},{24,28},{28,16},{32,6... | collective-permute-start | bytes 2433032 | tf_op jit(solution)/shard_map/ppermute | solution.py:356
  45.0 2.2 %collective-permute-start.16 = (f32[792,256]{1,0:T(8,128)S(1)}, f32[792,256]{1,0:T(8,128)S(1)}, u32[]{:S(2)}, u32[]{:S(2)}) collective-permute-start(f32[792,256]{1,0:T(8,128)S(1)} %get-tuple-element.86), channel_id=1, source_target_pairs={{0,64},{4,68},{8,72},{12,76},{16,24},{20,28},{24,16},{28,20},{32,9... | collective-permute-start | bytes 2433032 | tf_op jit(solution)/shard_map/ppermute | solution.py:356
  47.1 1.6 %collective-permute-start.12 = (f32[256,512]{1,0:T(8,128)S(1)}, f32[256,512]{1,0:T(8,128)S(1)}, u32[]{:S(2)}, u32[]{:S(2)}) collective-permute-start(f32[256,512]{1,0:T(8,128)S(1)} %get-tuple-element.81), channel_id=1, source_target_pairs={{0,1},{1,2},{2,3},{3,0},{4,5},{5,6},{6,7},{7,4},{8,9},{9,10},{10,1... | collective-permute-start | bytes 1572872 | tf_op jit(solution)/shard_map/ppermute | solution.py:478
  48.8 2.1 %collective-permute-start.13 = (f32[256,512]{1,0:T(8,128)S(1)}, f32[256,512]{1,0:T(8,128)S(1)}, u32[]{:S(2)}, u32[]{:S(2)}) collective-permute-start(f32[256,512]{1,0:T(8,128)S(1)} %get-tuple-element.82), channel_id=1, source_target_pairs={{0,3},{1,0},{2,1},{3,2},{4,7},{5,4},{6,5},{7,6},{8,11},{9,8},{10,9... | collective-permute-start | bytes 1572872 | tf_op jit(solution)/shard_map/ppermute | solution.py:478
  50.9 11.8 %collective-permute-done.12.refs_0_ = f32[256,512]{1,0:T(8,128)S(1)} collective-permute-done((f32[256,512]{1,0:T(8,128)S(1)}, f32[256,512]{1,0:T(8,128)S(1)}, u32[]{:S(2)}, u32[]{:S(2)}) %collective-permute-start.12) | collective-permute-done | bytes 524320 | tf_op jit(solution)/shard_map/ppermute | solution.py:478
  62.7 1.6 %collective-permute-done.16.far_ref = f32[792,256]{1,0:T(8,128)S(1)} collective-permute-done((f32[792,256]{1,0:T(8,128)S(1)}, f32[792,256]{1,0:T(8,128)S(1)}, u32[]{:S(2)}, u32[]{:S(2)}) %collective-permute-start.16) | collective-permute-done | bytes 811040 | tf_op jit(solution)/shard_map/ppermute | solution.py:356
  64.3 0.2 shard_map.127.own_ref
  64.5 2.5 %collective-permute-start.19 = (f32[792,256]{1,0:T(8,128)S(1)}, f32[792,256]{1,0:T(8,128)S(1)}, u32[]{:S(2)}, u32[]{:S(2)}) collective-permute-start(f32[792,256]{1,0:T(8,128)S(1)} %shard_map.127.own_ref), channel_id=1, source_target_pairs={{0,8},{4,12},{8,0},{12,4},{16,80},{20,84},{24,88},{28,92},{32,40},... | collective-permute-start | bytes 2433032 | tf_op jit(solution)/shard_map/ppermute | solution.py:356
  67.0 0.9 collective-permute-start.18
  67.9 0.6 collective-permute-start.17
  68.5 3.6 %collective-permute-start.10 = (f32[256,512]{1,0:T(8,128)S(1)}, f32[256,512]{1,0:T(8,128)S(1)}, u32[]{:S(2)}, u32[]{:S(2)}) collective-permute-start(f32[256,512]{1,0:T(8,128)S(1)} %get-tuple-element.77), channel_id=1, source_target_pairs={{0,2},{1,3},{2,0},{3,1},{4,6},{5,7},{6,4},{7,5},{8,10},{9,11},{10,... | collective-permute-start | bytes 1572872 | tf_op jit(solution)/shard_map/ppermute | solution.py:478
  72.1 9.0 %collective-permute-done.10 = f32[256,512]{1,0:T(8,128)S(1)} collective-permute-done((f32[256,512]{1,0:T(8,128)S(1)}, f32[256,512]{1,0:T(8,128)S(1)}, u32[]{:S(2)}, u32[]{:S(2)}) %collective-permute-start.10) | collective-permute-done | bytes 524320 | tf_op jit(solution)/shard_map/ppermute | solution.py:478
  81.0 0.2 fusion.refs_0_
  81.3 5.0 %collective-permute-done.18.ahead_ref = f32[792,256]{1,0:T(8,128)S(1)} collective-permute-done((f32[792,256]{1,0:T(8,128)S(1)}, f32[792,256]{1,0:T(8,128)S(1)}, u32[]{:S(2)}, u32[]{:S(2)}) %collective-permute-start.18) | collective-permute-done | bytes 811040 | tf_op jit(solution)/shard_map/ppermute | solution.py:356
  86.5 2.2 %collective-permute-start.22 = (f32[792,256]{1,0:T(8,128)S(1)}, f32[792,256]{1,0:T(8,128)S(1)}, u32[]{:S(2)}, u32[]{:S(2)}) collective-permute-start(f32[792,256]{1,0:T(8,128)S(1)} %shard_map.128.refs_0_), channel_id=1, source_target_pairs={{0,64},{4,68},{8,72},{12,76},{16,24},{20,28},{24,16},{28,20},{32,9... | collective-permute-start | bytes 2433032 | tf_op jit(solution)/shard_map/ppermute | solution.py:356
  88.7 1.2 %collective-permute-start.21 = (f32[792,256]{1,0:T(8,128)S(1)}, f32[792,256]{1,0:T(8,128)S(1)}, u32[]{:S(2)}, u32[]{:S(2)}) collective-permute-start(f32[792,256]{1,0:T(8,128)S(1)} %shard_map.128.refs_0_), channel_id=1, source_target_pairs={{0,32},{4,36},{8,40},{12,44},{16,20},{20,24},{24,28},{28,16},{32,6... | collective-permute-start | bytes 2433032 | tf_op jit(solution)/shard_map/ppermute | solution.py:356
  89.9 1.5 %collective-permute-start.20 = (f32[792,256]{1,0:T(8,128)S(1)}, f32[792,256]{1,0:T(8,128)S(1)}, u32[]{:S(2)}, u32[]{:S(2)}) collective-permute-start(f32[792,256]{1,0:T(8,128)S(1)} %shard_map.128.refs_0_), channel_id=1, source_target_pairs={{0,96},{4,100},{8,104},{12,108},{16,28},{20,16},{24,20},{28,24},{3... | collective-permute-start | bytes 2433032 | tf_op jit(solution)/shard_map/ppermute | solution.py:356
  91.4 8.1 %collective-permute-done.22.refs_1_.refs_3_ = f32[792,256]{1,0:T(8,128)S(1)} collective-permute-done((f32[792,256]{1,0:T(8,128)S(1)}, f32[792,256]{1,0:T(8,128)S(1)}, u32[]{:S(2)}, u32[]{:S(2)}) %collective-permute-start.22) | collective-permute-done | bytes 811040 | tf_op jit(solution)/shard_map/ppermute | solution.py:356
  99.5 3.3 %collective-permute-start.26 = (f32[792,256]{1,0:T(8,128)S(1)}, f32[792,256]{1,0:T(8,128)S(1)}, u32[]{:S(2)}, u32[]{:S(2)}) collective-permute-start(f32[792,256]{1,0:T(8,128)S(1)} %collective-permute-done.22.refs_1_.refs_3_), channel_id=1, source_target_pairs={{0,16},{16,0},{32,48},{48,32},{64,80},{80,64},{96,112},{112,96},{1... | collective-permute-start | bytes 2433032 | tf_op jit(solution)/shard_map/ppermute | solution.py:361
  102.8 1.7 %shard_map.129 = (f32[3,2048,256]{2,1,0:T(8,128)}, f32[792,256]{1,0:T(8,128)S(1)}) custom-call(s32[5]{0:T(128)S(1)} %stack.23.pos_ref, f32[792,256]{1,0:T(8,128)S(1)} %shard_map.128.refs_0_, f32[792,256]{1,0:T(8,128)S(1)} %collective-permute-done.22.refs_1_.refs_3_), custom_call_target="tpu_custom_call" | custom-call | tf_op jit(solution)/shard_map/pallas_call | solution.py:496
  104.6 3.5 %collective-permute-done.21.refs_1_.refs_2_ = f32[792,256]{1,0:T(8,128)S(1)} collective-permute-done((f32[792,256]{1,0:T(8,128)S(1)}, f32[792,256]{1,0:T(8,128)S(1)}, u32[]{:S(2)}, u32[]{:S(2)}) %collective-permute-start.21) | collective-permute-done | bytes 811040 | tf_op jit(solution)/shard_map/ppermute | solution.py:356
  108.2 3.2 %collective-permute-start.25 = (f32[792,256]{1,0:T(8,128)S(1)}, f32[792,256]{1,0:T(8,128)S(1)}, u32[]{:S(2)}, u32[]{:S(2)}) collective-permute-start(f32[792,256]{1,0:T(8,128)S(1)} %collective-permute-done.21.refs_1_.refs_2_), channel_id=1, source_target_pairs={{0,16},{16,0},{32,48},{48,32},{64,80},{80,64},{96,112},{112,96},{1... | collective-permute-start | bytes 2433032 | tf_op jit(solution)/shard_map/ppermute | solution.py:361
  111.4 2.3 %shard_map.130.refs_8_ = f32[3,2048,256]{2,1,0:T(8,128)} custom-call(s32[5]{0:T(128)S(1)} %stack.23.pos_ref, f32[792,256]{1,0:T(8,128)S(1)} %collective-permute-done.20.refs_0_.refs_1_, f32[792,256]{1,0:T(8,128)S(1)} %collective-permute-done.21.refs_1_.refs_2_, ...), custom_call_target="tpu_custom_call", output_to_operand_aliasing={{}: (5, {})} | custom-call | tf_op jit(solution)/shard_map/pallas_call | solution.py:496
  113.7 0.8 collective-permute-done.24.refs_5_
  114.5 2.4 %shard_map.131 = (f32[3,2048,256]{2,1,0:T(8,128)}, f32[2,128,128]{2,1,0:T(8,128)}, f32[2,128]{1,0:T(2,128)}, f32[2]{0:T(128)}) custom-call(s32[5]{0:T(128)S(1)} %stack.23.pos_ref, f32[792,256]{1,0:T(8,128)S(1)} %shard_map.128.refs_0_, f32[792,256]{1,0:T(8,128)S(1)} %collective-permute-done.20.refs_0_.refs_1_, ...), custom_call_target="tpu_custom_call", output_to_operand_aliasing={{0}: (9, {})} | custom-call | tf_op jit(solution)/shard_map/pallas_call | solution.py:512
  (36 shorter events, 0.5 us)
Async XLA Ops:
  0.6 11.8 %copy-start.4 = (f32[1,2,256]{2,1,0:T(2,128)S(1)}, f32[1,2,256]{2,1,0:T(2,128)}, u32[]{:S(2)}) copy-start(f32[1,2,256]{2,1,0:T(2,128)} %gate_ref.7) | copy-start | bytes 6148
  0.6 11.8 %copy-start.5 = (f32[2]{0:T(128)S(1)}, f32[2]{0:T(128)}, u32[]{:S(2)}) copy-start(f32[2]{0:T(128)} %base_ref.7) | copy-start | bytes 28
  0.8 19.5 %copy-start.2 = (f32[2,128,128]{2,1,0:T(8,128)S(1)}, f32[2,128,128]{2,1,0:T(8,128)}, u32[]{:S(2)}) copy-start(f32[2,128,128]{2,1,0:T(8,128)} %init_ref.3) | copy-start | bytes 393220
  0.8 19.5 %copy-start.3 = (bf16[1,256,256]{2,1,0:T(8,128)(2,1)S(1)}, bf16[1,256,256]{2,1,0:T(8,128)(2,1)}, u32[]{:S(2)}) copy-start(bf16[1,256,256]{2,1,0:T(8,128)(2,1)} %up_ref.3) | copy-start | bytes 393220
  0.8 19.5 %copy-start.6 = (f32[2,128]{1,0:T(2,128)S(1)}, f32[2,128]{1,0:T(2,128)}, u32[]{:S(2)}) copy-start(f32[2,128]{1,0:T(2,128)} %gain_ref.1) | copy-start | bytes 3076
  6.3 13.0 %collective-permute-start.4 = (f32[256,1024]{1,0:T(8,128)S(1)}, f32[256,1024]{1,0:T(8,128)S(1)}, u32[]{:S(2)}, u32[]{:S(2)}) collective-permute-start(f32[256,1024]{1,0:T(8,128)S(1)} %get-tuple-element.58), channel_id=1, source_target_pairs={{0,16},{16,0},{32,48},{48,32},{64,80},{80,64},{96,112},{112,96},{1... | collective-permute-start | bytes 3145736 | tf_op jit(solution)/shard_map/ppermute | solution.py:361
  7.8 8.5 %collective-permute-start = (f32[2,128,128]{2,1,0:T(8,128)S(1)}, f32[2,128,128]{2,1,0:T(8,128)S(1)}, u32[]{:S(2)}, u32[]{:S(2)}) collective-permute-start(f32[2,128,128]{2,1,0:T(8,128)S(1)} %get-tuple-element.50), channel_id=1, source_target_pairs={{0,4},{8,12},{1,5},{9,13},{2,6},{10,14},{3,7},{11,15},{16,20},{24,... | collective-permute-start | bytes 393224 | tf_op jit(solution)/shard_map/ppermute | solution.py:434
  11.1 9.1 %collective-permute-start.3 = (f32[2,128,128]{2,1,0:T(8,128)S(1)}, f32[2,128,128]{2,1,0:T(8,128)S(1)}, u32[]{:S(2)}, u32[]{:S(2)}) collective-permute-start(f32[2,128,128]{2,1,0:T(8,128)S(1)} %get-tuple-element.51.d_ref), channel_id=1, source_target_pairs={{8,12},{4,0},{9,13},{5,1},{10,14},{6,2},{11,15},{7,3},{24,28},{20,... | collective-permute-start | bytes 393224 | tf_op jit(solution)/shard_map/ppermute | solution.py:435
  16.3 22.0 %copy-start = (bf16[3,2048,256]{2,1,0:T(8,128)(2,1)S(1)}, bf16[3,2048,256]{2,1,0:T(8,128)(2,1)}, u32[]{:S(2)}) copy-start(bf16[3,2048,256]{2,1,0:T(8,128)(2,1)} %w_ref.1) | copy-start | bytes 9437188
  16.6 3.7 %collective-permute-start.2 = (f32[2,128,128]{2,1,0:T(8,128)S(1)}, f32[2,128,128]{2,1,0:T(8,128)S(1)}, u32[]{:S(2)}, u32[]{:S(2)}) collective-permute-start(f32[2,128,128]{2,1,0:T(8,128)S(1)} %shard_map.120), channel_id=1, source_target_pairs={{4,12},{5,13},{6,14},{7,15},{20,28},{21,29},{22,30},{23,31},{36,44... | collective-permute-start | bytes 393224 | tf_op jit(solution)/shard_map/ppermute | solution.py:453
  17.4 2.9 %collective-permute-start.1 = (f32[2,128,128]{2,1,0:T(8,128)S(1)}, f32[2,128,128]{2,1,0:T(8,128)S(1)}, u32[]{:S(2)}, u32[]{:S(2)}) collective-permute-start(f32[2,128,128]{2,1,0:T(8,128)S(1)} %shard_map.120), channel_id=1, source_target_pairs={{4,8},{5,9},{6,10},{7,11},{20,24},{21,25},{22,26},{23,27},{36,40},... | collective-permute-start | bytes 393224 | tf_op jit(solution)/shard_map/ppermute | solution.py:452
  18.1 10.6 %collective-permute-start.9 = (f32[2,128,128]{2,1,0:T(8,128)S(1)}, f32[2,128,128]{2,1,0:T(8,128)S(1)}, u32[]{:S(2)}, u32[]{:S(2)}) collective-permute-start(f32[2,128,128]{2,1,0:T(8,128)S(1)} %get-tuple-element.51.d_ref), channel_id=1, source_target_pairs={{8,0},{9,1},{10,2},{11,3},{24,16},{25,17},{26,18},{27,19},{40,32},... | collective-permute-start | bytes 393224 | tf_op jit(solution)/shard_map/ppermute | solution.py:437
  19.4 9.3 %collective-permute-start.8 = (f32[2,128,128]{2,1,0:T(8,128)S(1)}, f32[2,128,128]{2,1,0:T(8,128)S(1)}, u32[]{:S(2)}, u32[]{:S(2)}) collective-permute-start(f32[2,128,128]{2,1,0:T(8,128)S(1)} %get-tuple-element.51.d_ref), channel_id=1, source_target_pairs={{8,4},{9,5},{10,6},{11,7},{24,20},{25,21},{26,22},{27,23},{40,36},... | collective-permute-start | bytes 393224 | tf_op jit(solution)/shard_map/ppermute | solution.py:436
  21.9 8.5 %collective-permute-start.7 = (f32[2,128,128]{2,1,0:T(8,128)S(1)}, f32[2,128,128]{2,1,0:T(8,128)S(1)}, u32[]{:S(2)}, u32[]{:S(2)}) collective-permute-start(f32[2,128,128]{2,1,0:T(8,128)S(1)} %get-tuple-element.59.p_ref), channel_id=1, source_target_pairs={{12,0},{13,1},{14,2},{15,3},{28,16},{29,17},{30,18},{31,19},{44,32... | collective-permute-start | bytes 393224 | tf_op jit(solution)/shard_map/ppermute | solution.py:462
  23.2 9.2 %collective-permute-start.6 = (f32[2,128,128]{2,1,0:T(8,128)S(1)}, f32[2,128,128]{2,1,0:T(8,128)S(1)}, u32[]{:S(2)}, u32[]{:S(2)}) collective-permute-start(f32[2,128,128]{2,1,0:T(8,128)S(1)} %get-tuple-element.59.p_ref), channel_id=1, source_target_pairs={{12,4},{8,0},{13,5},{9,1},{14,6},{10,2},{15,7},{11,3},{28,20},{24,... | collective-permute-start | bytes 393224 | tf_op jit(solution)/shard_map/ppermute | solution.py:461
  24.5 7.9 %collective-permute-start.5 = (f32[2,128,128]{2,1,0:T(8,128)S(1)}, f32[2,128,128]{2,1,0:T(8,128)S(1)}, u32[]{:S(2)}, u32[]{:S(2)}) collective-permute-start(f32[2,128,128]{2,1,0:T(8,128)S(1)} %get-tuple-element.59.p_ref), channel_id=1, source_target_pairs={{12,8},{8,4},{4,0},{13,9},{9,5},{5,1},{14,10},{10,6},{6,2},{15,11}... | collective-permute-start | bytes 393224 | tf_op jit(solution)/shard_map/ppermute | solution.py:460
  34.9 5.6 %collective-permute-start.11 = (f32[960,256]{1,0:T(8,128)S(1)}, f32[960,256]{1,0:T(8,128)S(1)}, u32[]{:S(2)}, u32[]{:S(2)}) collective-permute-start(f32[960,256]{1,0:T(8,128)S(1)} %get-tuple-element.75.all_ref.own_ref), channel_id=1, source_target_pairs={{0,16},{16,0},{32,48},{48,32},{64,80},{80,64},{96,112},{112,96},{1... | collective-permute-start | bytes 2949128 | tf_op jit(solution)/shard_map/ppermute | solution.py:361
  42.0 20.6 %collective-permute-start.14 = (f32[792,256]{1,0:T(8,128)S(1)}, f32[792,256]{1,0:T(8,128)S(1)}, u32[]{:S(2)}, u32[]{:S(2)}) collective-permute-start(f32[792,256]{1,0:T(8,128)S(1)} %get-tuple-element.84), channel_id=1, source_target_pairs={{0,32},{4,36},{8,40},{12,44},{16,20},{20,24},{24,28},{28,16},{32,6... | collective-permute-start | bytes 2433032 | tf_op jit(solution)/shard_map/ppermute | solution.py:356
  44.9 17.8 %collective-permute-start.15 = (f32[792,256]{1,0:T(8,128)S(1)}, f32[792,256]{1,0:T(8,128)S(1)}, u32[]{:S(2)}, u32[]{:S(2)}) collective-permute-start(f32[792,256]{1,0:T(8,128)S(1)} %get-tuple-element.85), channel_id=1, source_target_pairs={{0,96},{4,100},{8,104},{12,108},{16,28},{20,16},{24,20},{28,24},{3... | collective-permute-start | bytes 2433032 | tf_op jit(solution)/shard_map/ppermute | solution.py:356
  45.0 19.3 %collective-permute-start.16 = (f32[792,256]{1,0:T(8,128)S(1)}, f32[792,256]{1,0:T(8,128)S(1)}, u32[]{:S(2)}, u32[]{:S(2)}) collective-permute-start(f32[792,256]{1,0:T(8,128)S(1)} %get-tuple-element.86), channel_id=1, source_target_pairs={{0,64},{4,68},{8,72},{12,76},{16,24},{20,28},{24,16},{28,20},{32,9... | collective-permute-start | bytes 2433032 | tf_op jit(solution)/shard_map/ppermute | solution.py:356
  47.1 15.5 %collective-permute-start.12 = (f32[256,512]{1,0:T(8,128)S(1)}, f32[256,512]{1,0:T(8,128)S(1)}, u32[]{:S(2)}, u32[]{:S(2)}) collective-permute-start(f32[256,512]{1,0:T(8,128)S(1)} %get-tuple-element.81), channel_id=1, source_target_pairs={{0,1},{1,2},{2,3},{3,0},{4,5},{5,6},{6,7},{7,4},{8,9},{9,10},{10,1... | collective-permute-start | bytes 1572872 | tf_op jit(solution)/shard_map/ppermute | solution.py:478
  48.8 13.9 %collective-permute-start.13 = (f32[256,512]{1,0:T(8,128)S(1)}, f32[256,512]{1,0:T(8,128)S(1)}, u32[]{:S(2)}, u32[]{:S(2)}) collective-permute-start(f32[256,512]{1,0:T(8,128)S(1)} %get-tuple-element.82), channel_id=1, source_target_pairs={{0,3},{1,0},{2,1},{3,2},{4,7},{5,4},{6,5},{7,6},{8,11},{9,8},{10,9... | collective-permute-start | bytes 1572872 | tf_op jit(solution)/shard_map/ppermute | solution.py:478
  64.5 16.8 %collective-permute-start.19 = (f32[792,256]{1,0:T(8,128)S(1)}, f32[792,256]{1,0:T(8,128)S(1)}, u32[]{:S(2)}, u32[]{:S(2)}) collective-permute-start(f32[792,256]{1,0:T(8,128)S(1)} %shard_map.127.own_ref), channel_id=1, source_target_pairs={{0,8},{4,12},{8,0},{12,4},{16,80},{20,84},{24,88},{28,92},{32,40},... | collective-permute-start | bytes 2433032 | tf_op jit(solution)/shard_map/ppermute | solution.py:356
  67.0 19.3 %collective-permute-start.18 = (f32[792,256]{1,0:T(8,128)S(1)}, f32[792,256]{1,0:T(8,128)S(1)}, u32[]{:S(2)}, u32[]{:S(2)}) collective-permute-start(f32[792,256]{1,0:T(8,128)S(1)} %shard_map.127.own_ref), channel_id=1, source_target_pairs={{0,12},{4,0},{8,4},{12,8},{16,112},{20,116},{24,120},{28,124},{32,... | collective-permute-start | bytes 2433032 | tf_op jit(solution)/shard_map/ppermute | solution.py:356
  67.9 18.4 %collective-permute-start.17 = (f32[792,256]{1,0:T(8,128)S(1)}, f32[792,256]{1,0:T(8,128)S(1)}, u32[]{:S(2)}, u32[]{:S(2)}) collective-permute-start(f32[792,256]{1,0:T(8,128)S(1)} %shard_map.127.own_ref), channel_id=1, source_target_pairs={{0,4},{4,8},{8,12},{12,0},{16,48},{20,52},{24,56},{28,60},{32,36},... | collective-permute-start | bytes 2433032 | tf_op jit(solution)/shard_map/ppermute | solution.py:356
  68.5 12.6 %collective-permute-start.10 = (f32[256,512]{1,0:T(8,128)S(1)}, f32[256,512]{1,0:T(8,128)S(1)}, u32[]{:S(2)}, u32[]{:S(2)}) collective-permute-start(f32[256,512]{1,0:T(8,128)S(1)} %get-tuple-element.77), channel_id=1, source_target_pairs={{0,2},{1,3},{2,0},{3,1},{4,6},{5,7},{6,4},{7,5},{8,10},{9,11},{10,... | collective-permute-start | bytes 1572872 | tf_op jit(solution)/shard_map/ppermute | solution.py:478
  81.3 32.4 %copy-start.1 = (bf16[1,256,512]{2,1,0:T(8,128)(2,1)}, bf16[1,256,512]{2,1,0:T(8,128)(2,1)S(1)}, u32[]{:S(2)}) copy-start(bf16[1,256,512]{2,1,0:T(8,128)(2,1)S(1)} %fusion.refs_0_) | copy-start | bytes 786436
  86.5 13.0 %collective-permute-start.22 = (f32[792,256]{1,0:T(8,128)S(1)}, f32[792,256]{1,0:T(8,128)S(1)}, u32[]{:S(2)}, u32[]{:S(2)}) collective-permute-start(f32[792,256]{1,0:T(8,128)S(1)} %shard_map.128.refs_0_), channel_id=1, source_target_pairs={{0,64},{4,68},{8,72},{12,76},{16,24},{20,28},{24,16},{28,20},{32,9... | collective-permute-start | bytes 2433032 | tf_op jit(solution)/shard_map/ppermute | solution.py:356
  88.7 19.4 %collective-permute-start.21 = (f32[792,256]{1,0:T(8,128)S(1)}, f32[792,256]{1,0:T(8,128)S(1)}, u32[]{:S(2)}, u32[]{:S(2)}) collective-permute-start(f32[792,256]{1,0:T(8,128)S(1)} %shard_map.128.refs_0_), channel_id=1, source_target_pairs={{0,32},{4,36},{8,40},{12,44},{16,20},{20,24},{24,28},{28,16},{32,6... | collective-permute-start | bytes 2433032 | tf_op jit(solution)/shard_map/ppermute | solution.py:356
  89.9 21.5 %collective-permute-start.20 = (f32[792,256]{1,0:T(8,128)S(1)}, f32[792,256]{1,0:T(8,128)S(1)}, u32[]{:S(2)}, u32[]{:S(2)}) collective-permute-start(f32[792,256]{1,0:T(8,128)S(1)} %shard_map.128.refs_0_), channel_id=1, source_target_pairs={{0,96},{4,100},{8,104},{12,108},{16,28},{20,16},{24,20},{28,24},{3... | collective-permute-start | bytes 2433032 | tf_op jit(solution)/shard_map/ppermute | solution.py:356
  99.5 11.9 %collective-permute-start.26 = (f32[792,256]{1,0:T(8,128)S(1)}, f32[792,256]{1,0:T(8,128)S(1)}, u32[]{:S(2)}, u32[]{:S(2)}) collective-permute-start(f32[792,256]{1,0:T(8,128)S(1)} %collective-permute-done.22.refs_1_.refs_3_), channel_id=1, source_target_pairs={{0,16},{16,0},{32,48},{48,32},{64,80},{80,64},{96,112},{112,96},{1... | collective-permute-start | bytes 2433032 | tf_op jit(solution)/shard_map/ppermute | solution.py:361
  104.5 6.9 %collective-permute-start.23 = (f32[792,256]{1,0:T(8,128)S(1)}, f32[792,256]{1,0:T(8,128)S(1)}, u32[]{:S(2)}, u32[]{:S(2)}) collective-permute-start(f32[792,256]{1,0:T(8,128)S(1)} %get-tuple-element.87), channel_id=1, source_target_pairs={{0,16},{16,0},{32,48},{48,32},{64,80},{80,64},{96,112},{112,96},{1... | collective-permute-start | bytes 2433032 | tf_op jit(solution)/shard_map/ppermute | solution.py:361
  108.2 5.6 %collective-permute-start.25 = (f32[792,256]{1,0:T(8,128)S(1)}, f32[792,256]{1,0:T(8,128)S(1)}, u32[]{:S(2)}, u32[]{:S(2)}) collective-permute-start(f32[792,256]{1,0:T(8,128)S(1)} %collective-permute-done.21.refs_1_.refs_2_), channel_id=1, source_target_pairs={{0,16},{16,0},{32,48},{48,32},{64,80},{80,64},{96,112},{112,96},{1... | collective-permute-start | bytes 2433032 | tf_op jit(solution)/shard_map/ppermute | solution.py:361
  111.4 3.1 %collective-permute-start.24 = (f32[792,256]{1,0:T(8,128)S(1)}, f32[792,256]{1,0:T(8,128)S(1)}, u32[]{:S(2)}, u32[]{:S(2)}) collective-permute-start(f32[792,256]{1,0:T(8,128)S(1)} %collective-permute-done.20.refs_0_.refs_1_), channel_id=1, source_target_pairs={{0,16},{16,0},{32,48},{48,32},{64,80},{80,64},{96,112},{112,96},{1... | collective-permute-start | bytes 2433032 | tf_op jit(solution)/shard_map/ppermute | solution.py:361

commit v11 on v10

--- a/solution.py
+++ b/solution.py
@@ -13,6 +13,7 @@
 TURNS = (0, 1, 3, 2)
 CHUNK = 256
 PIECE = 24
+STEPS = 4
 EXTRA = 2 * RING * PIECE
 F32 = jnp.float32
 BF = jnp.bfloat16
@@ -78,40 +79,51 @@
 
 def maps_kernel(
     pos_ref, base_ref, tok_ref, wk_ref, wv_ref, gate_ref, init_ref,
-    k_ref, v_ref, ninv_ref, gram_ref, inv_ref, bt_ref, d_ref, send_ref, o_ref, half_ref,
+    k_ref, v_ref, ninv_ref, gram_ref, inv_ref, bt_ref, d_ref, send_ref, o_ref, half_ref, kacc_ref, vacc_ref,
 ):
-    half = tok_ref.shape[2] // 2
-    columns = pl.ds(pl.multiple_of((1 - pos_ref[0]) * half, half), half)
-    half_ref[...] = tok_ref[0, :, columns].astype(F32)
+    at = pl.program_id(0)
+    steps = pl.num_programs(0)
     tok = tok_ref[0]
-    kraw_all = jnp.dot(tok, wk_ref[0], preferred_element_type=F32).astype(BF).astype(F32)
-    v_all = jnp.dot(tok, wv_ref[0], preferred_element_type=F32).astype(BF).astype(F32)
-    n = kraw_all.shape[0]
-    i, j = places(n)
-    strict = (i // MB) > (j // MB)
-    heads = range(init_ref.shape[0])
-    kraws = [kraw_all[:, span(h)] for h in heads]
-    ninvs = [lax.rsqrt(jnp.sum(kraw * kraw, -1, keepdims=True) + 1e-06) for kraw in kraws]
-    ks = [kraw * ninv for kraw, ninv in zip(kraws, ninvs)]
-    kts = [k.T for k in ks]
-    es = [rates_of(base_ref, gate_ref, h)[1] for h in heads]
-    grams = [dot(k, kt, NN, 3) for k, kt in zip(ks, kts)]
-    inverses = unit_lower_inverses([jnp.where(strict, gram * e, 0.0) for gram, e in zip(grams, es)])
-    a, b = places(HS)
-    bts = [dot(kts[h] * es[h], inverses[h], NN, 3) for h in heads]
-    decays = [jnp.where(a == b, 1.0, 0.0) - dot(bts[h], ks[h], NN, 3) for h in heads]
-    offsets = [dot(bts[h], v_all[:, span(h)], NN, 3) for h in heads]
-    firsts = [dot(decays[h], init_ref[h], NN, 3) + offsets[h] for h in heads]
-    v_ref[...] = v_all
-    for h in heads:
-        send_ref[h] = jnp.where(pos_ref[4] == 0, firsts[h], offsets[h])
-        d_ref[h] = decays[h]
-        o_ref[h] = offsets[h]
-        k_ref[:, span(h)] = ks[h]
-        ninv_ref[h] = jnp.broadcast_to(ninvs[h], (n, HS))
-        gram_ref[h] = grams[h]
-        inv_ref[h] = inverses[h]
-        bt_ref[h] = bts[h]
+    width = tok.shape[1]
+    for acc_ref, weight_ref in ((kacc_ref, wk_ref), (vacc_ref, wv_ref)):
+        term = jnp.dot(tok, weight_ref[0], preferred_element_type=F32)
+        acc_ref[...] = jnp.where(at == 0, term, acc_ref[...] + term)
+
+    @pl.when((at // (steps // 2)) != pos_ref[0])
+    def _():
+        columns = pl.ds(pl.multiple_of((at % (steps // 2)) * width, width), width)
+        half_ref[:, columns] = tok.astype(F32)
+
+    @pl.when(at == steps - 1)
+    def _():
+        kraw_all = kacc_ref[...].astype(BF).astype(F32)
+        v_all = vacc_ref[...].astype(BF).astype(F32)
+        n = kraw_all.shape[0]
+        i, j = places(n)
+        strict = (i // MB) > (j // MB)
+        heads = range(init_ref.shape[0])
+        kraws = [kraw_all[:, span(h)] for h in heads]
+        ninvs = [lax.rsqrt(jnp.sum(kraw * kraw, -1, keepdims=True) + 1e-06) for kraw in kraws]
+        ks = [kraw * ninv for kraw, ninv in zip(kraws, ninvs)]
+        kts = [k.T for k in ks]
+        es = [rates_of(base_ref, gate_ref, h)[1] for h in heads]
+        grams = [dot(k, kt, NN, 3) for k, kt in zip(ks, kts)]
+        inverses = unit_lower_inverses([jnp.where(strict, gram * e, 0.0) for gram, e in zip(grams, es)])
+        a, b = places(HS)
+        bts = [dot(kts[h] * es[h], inverses[h], NN, 3) for h in heads]
+        decays = [jnp.where(a == b, 1.0, 0.0) - dot(bts[h], ks[h], NN, 3) for h in heads]
+        offsets = [dot(bts[h], v_all[:, span(h)], NN, 3) for h in heads]
+        firsts = [dot(decays[h], init_ref[h], NN, 3) + offsets[h] for h in heads]
+        v_ref[...] = v_all
+        for h in heads:
+            send_ref[h] = jnp.where(pos_ref[4] == 0, firsts[h], offsets[h])
+            d_ref[h] = decays[h]
+            o_ref[h] = offsets[h]
+            k_ref[:, span(h)] = ks[h]
+            ninv_ref[h] = jnp.broadcast_to(ninvs[h], (n, HS))
+            gram_ref[h] = grams[h]
+            inv_ref[h] = inverses[h]
+            bt_ref[h] = bts[h]
 
 
 def reach_kernel(
@@ -421,13 +433,19 @@
 
     k, v, ninv, gram, inv, bt, decay, send, offset, other_half = pl.pallas_call(
         maps_kernel,
-        grid=(1,),
+        grid=(STEPS,),
         out_shape=(
             wide_f32, wide_f32, vmem(heads, n, HS), square, square, vmem(heads, HS, n), small, small, small,
             vmem(n, half),
         ),
-        in_specs=[SM, SM, full(1, n, model), wspec(1), wspec(2), full(1, heads, n), full(heads, HS, HS)],
+        in_specs=[
+            SM, SM, pl.BlockSpec((1, n, model // STEPS), lambda i: (0, 0, i)),
+            pl.BlockSpec((1, model // STEPS, wide), lambda i: (1, i, 0)),
+            pl.BlockSpec((1, model // STEPS, wide), lambda i: (2, i, 0)),
+            full(1, heads, n), full(heads, HS, HS),
+        ],
         out_specs=(VM,) * 10,
+        scratch_shapes=[pltpu.VMEM((n, wide), F32)] * 2,
         compiler_params=PARAMS,
     )(pos, hbm(base_rates), tokens, proj_weights, proj_weights, hbm(gate_values), hbm(init_weight))
 

time: 117 us -> 118 us (level)
  no operation moved by 1% of the time
where the time goes in v11:
time: 118 us
  starting transfers between devices  44.7 us (38%)
  waiting for transfers between devices  44.2 us (37%)
  Pallas kernels  27.5 us (23%)
    ppermute x3, waiting for transfers between devices, along_head(): lax.ppermute(terms, 'head', [(i, (i + turn) % RING) for i in range(RING)])  20.7 us
    ppermute x9, waiting for transfers between devices, round_turn(): lax.ppermute(chunk, ('dp', 'ctx'), moves(first, turn))  18.3 us
    ppermute x9, starting transfers between devices, round_turn(): lax.ppermute(chunk, ('dp', 'ctx'), moves(first, turn))  14 us
    ppermute x6, starting transfers between devices, swap(): return lax.ppermute(value, 'dp', [(i, i ^ 1) for i in range(2 * RING)])  11.5 us
    ppermute x3, starting transfers between devices, along_head(): lax.ppermute(terms, 'head', [(i, (i + turn) % RING) for i in range(RING)])  7.36 us
    pallas_call x1, Pallas kernels, body(): pl.pallas_call(maps_kernel, grid=(STEPS,), out_shape=(wide_f32, wide_f32,...  6.45 us
    pallas_call x2, Pallas kernels, place(): pl.pallas_call(functools.partial(place_kernel, which=which, passed=passed...  4.03 us
    pallas_call x1, Pallas kernels, body(): pl.pallas_call(reach_kernel, grid=(1,), out_shape=(wide_f32, square, wide...  3.89 us
  transfers between devices with their start and end apart: 27, of which 10 were waited for; matrix products, arithmetic and copies ran while one was open for 0% of the time, Pallas kernels for 12%

profile of v11, /device:TPU:1, one launch (start us, length us, event | category | flops | bytes accessed | tf_op | source)
XLA Modules:
  0.0 117.9 jit_solution(16710606144315880209)
XLA Ops:
  0.8 6.4 %shard_map.118 = (f32[256,256]{1,0:T(8,128)S(1)}, f32[256,256]{1,0:T(8,128)S(1)}, f32[2,256,128]{2,1,0:T(8,128)S(1)}, f32[2,256,256]{2,1,0:T(8,128)S(1)}, f32[2,...) custom-call(s32[5]{0:T(128)S(1)} %stack.23.pos_ref, ...), custom_call_target="tpu_custom_call" | custom-call | tf_op jit(solution)/shard_map/pallas_call | solution.py:434
  7.2 1.5 %collective-permute-start.4 = (f32[256,1024]{1,0:T(8,128)S(1)}, f32[256,1024]{1,0:T(8,128)S(1)}, u32[]{:S(2)}, u32[]{:S(2)}) collective-permute-start(f32[256,1024]{1,0:T(8,128)S(1)} %get-tuple-element.58), channel_id=1, source_target_pairs={{0,16},{16,0},{32,48},{48,32},{64,80},{80,64},{96,112},{112,96},{1... | collective-permute-start | bytes 3145736 | tf_op jit(solution)/shard_map/ppermute | solution.py:373
  8.7 3.3 %collective-permute-start = (f32[2,128,128]{2,1,0:T(8,128)S(1)}, f32[2,128,128]{2,1,0:T(8,128)S(1)}, u32[]{:S(2)}, u32[]{:S(2)}) collective-permute-start(f32[2,128,128]{2,1,0:T(8,128)S(1)} %get-tuple-element.50), channel_id=1, source_target_pairs={{0,4},{8,12},{1,5},{9,13},{2,6},{10,14},{3,7},{11,15},{16,20},{24,... | collective-permute-start | bytes 393224 | tf_op jit(solution)/shard_map/ppermute | solution.py:452
  12.0 1.3 %collective-permute-start.3 = (f32[2,128,128]{2,1,0:T(8,128)S(1)}, f32[2,128,128]{2,1,0:T(8,128)S(1)}, u32[]{:S(2)}, u32[]{:S(2)}) collective-permute-start(f32[2,128,128]{2,1,0:T(8,128)S(1)} %get-tuple-element.51.d_ref), channel_id=1, source_target_pairs={{8,12},{4,0},{9,13},{5,1},{10,14},{6,2},{11,15},{7,3},{24,28},{20,... | collective-permute-start | bytes 393224 | tf_op jit(solution)/shard_map/ppermute | solution.py:453
  13.3 3.9 %shard_map.119 = (f32[256,256]{1,0:T(8,128)S(1)}, f32[2,256,256]{2,1,0:T(8,128)S(1)}, f32[256,256]{1,0:T(8,128)S(1)}, f32[256,256]{1,0:T(8,128)S(1)}, f32[256,25...) custom-call(s32[5]{0:T(128)S(1)} %stack.23.pos_ref, f32[2]{0:T(128)S(1)} %copy-done.5, ...), custom_call_target="tpu_custom_call" | custom-call | tf_op jit(solution)/shard_map/pallas_call | solution.py:458
  17.2 0.2 shard_map.120
  17.4 0.8 collective-permute-start.2
  18.2 0.7 collective-permute-start.1
  18.9 1.3 %collective-permute-start.9 = (f32[2,128,128]{2,1,0:T(8,128)S(1)}, f32[2,128,128]{2,1,0:T(8,128)S(1)}, u32[]{:S(2)}, u32[]{:S(2)}) collective-permute-start(f32[2,128,128]{2,1,0:T(8,128)S(1)} %get-tuple-element.51.d_ref), channel_id=1, source_target_pairs={{8,0},{9,1},{10,2},{11,3},{24,16},{25,17},{26,18},{27,19},{40,32},... | collective-permute-start | bytes 393224 | tf_op jit(solution)/shard_map/ppermute | solution.py:455
  20.2 0.7 collective-permute-start.8
  20.9 0.2 shard_map.121.after_ref.other_tokt_ref
  21.2 1.5 %shard_map.122 = (f32[2,128,128]{2,1,0:T(8,128)S(1)}, f32[256,256]{1,0:T(8,128)S(1)}, f32[2,128,128]{2,1,0:T(8,128)S(1)}, f32[2,128]{1,0:T(2,128)S(1)}) custom-call(s32[5]{0:T(128)S(1)} %stack.23.pos_ref, f32[2,128,128]{2,1,0:T(8,128)S(1)} %copy-done.2, f32[2,128,128]{2,1,0:T(8,128)S(1)} %collective-permute-done.w_ref.near_ref, ...), custom_call_target="tpu_custom_call" | custom-call | tf_op jit(solution)/shard_map/pallas_call | solution.py:474
  22.7 1.3 %collective-permute-start.7 = (f32[2,128,128]{2,1,0:T(8,128)S(1)}, f32[2,128,128]{2,1,0:T(8,128)S(1)}, u32[]{:S(2)}, u32[]{:S(2)}) collective-permute-start(f32[2,128,128]{2,1,0:T(8,128)S(1)} %get-tuple-element.59.p_ref), channel_id=1, source_target_pairs={{12,0},{13,1},{14,2},{15,3},{28,16},{29,17},{30,18},{31,19},{44,32... | collective-permute-start | bytes 393224 | tf_op jit(solution)/shard_map/ppermute | solution.py:480
  24.0 1.3 %collective-permute-start.6 = (f32[2,128,128]{2,1,0:T(8,128)S(1)}, f32[2,128,128]{2,1,0:T(8,128)S(1)}, u32[]{:S(2)}, u32[]{:S(2)}) collective-permute-start(f32[2,128,128]{2,1,0:T(8,128)S(1)} %get-tuple-element.59.p_ref), channel_id=1, source_target_pairs={{12,4},{8,0},{13,5},{9,1},{14,6},{10,2},{15,7},{11,3},{28,20},{24,... | collective-permute-start | bytes 393224 | tf_op jit(solution)/shard_map/ppermute | solution.py:479
  25.3 1.3 %collective-permute-start.5 = (f32[2,128,128]{2,1,0:T(8,128)S(1)}, f32[2,128,128]{2,1,0:T(8,128)S(1)}, u32[]{:S(2)}, u32[]{:S(2)}) collective-permute-start(f32[2,128,128]{2,1,0:T(8,128)S(1)} %get-tuple-element.59.p_ref), channel_id=1, source_target_pairs={{12,8},{8,4},{4,0},{13,9},{9,5},{5,1},{14,10},{10,6},{6,2},{15,11}... | collective-permute-start | bytes 393224 | tf_op jit(solution)/shard_map/ppermute | solution.py:478
  26.6 2.9 %shard_map.123 = (f32[256,256]{1,0:T(8,128)S(1)}, f32[256,256]{1,0:T(8,128)S(1)}, f32[256,256]{1,0:T(8,128)S(1)}, f32[256,256]{1,0:T(8,128)S(1)}, f32[2,256]{1,0:T(2,128)S(1)}) custom-call(f32[2]{0:T(128)S(1)} %copy-done.5, f32[1,2,256]{2,1,0:T(2,128)S(1)} %copy-done.4, f32[2,128,128]{2,1,0:T(8,128)S(1)} %get-tuple-element.60.w_ref, ...), custom_call_target="tpu_custom_call" | custom-call | tf_op jit(solution)/shard_map/pallas_call | solution.py:482
  29.5 1.7 %collective-permute-done.7.three_ref = f32[2,128,128]{2,1,0:T(8,128)S(1)} collective-permute-done((f32[2,128,128]{2,1,0:T(8,128)S(1)}, f32[2,128,128]{2,1,0:T(8,128)S(1)}, u32[]{:S(2)}, u32[]{:S(2)}) %collective-permute-start.7) | collective-permute-done | bytes 131104 | tf_op jit(solution)/shard_map/ppermute | solution.py:480
  31.2 2.0 %collective-permute-done.6.two_ref = f32[2,128,128]{2,1,0:T(8,128)S(1)} collective-permute-done((f32[2,128,128]{2,1,0:T(8,128)S(1)}, f32[2,128,128]{2,1,0:T(8,128)S(1)}, u32[]{:S(2)}, u32[]{:S(2)}) %collective-permute-start.6) | collective-permute-done | bytes 131104 | tf_op jit(solution)/shard_map/ppermute | solution.py:479
  33.3 2.5 %shard_map.124 = (f32[960,256]{1,0:T(8,128)S(1)}, f32[1,2,256]{2,1,0:T(2,128)}) custom-call(s32[5]{0:T(128)S(1)} %stack.23.pos_ref, f32[2]{0:T(128)S(1)} %copy-done.5, f32[1,2,256]{2,1,0:T(2,128)S(1)} %copy-done.4, f32[2,128,128]{2,1,0:T(8,128)S(1)} %collective-permute-done.5.one_ref, f32[2,128,128]{2,1,0:T(8,128)S(1)} %collective-permute-done.6.two_ref, ...), custom_call_target="tpu_custom_call" | custom-call | tf_op jit(solution)/shard_map/pallas_call | solution.py:486
  35.8 3.4 %collective-permute-start.11 = (f32[960,256]{1,0:T(8,128)S(1)}, f32[960,256]{1,0:T(8,128)S(1)}, u32[]{:S(2)}, u32[]{:S(2)}) collective-permute-start(f32[960,256]{1,0:T(8,128)S(1)} %get-tuple-element.75.all_ref.own_ref), channel_id=1, source_target_pairs={{0,16},{16,0},{32,48},{48,32},{64,80},{80,64},{96,112},{112,96},{1... | collective-permute-start | bytes 2949128 | tf_op jit(solution)/shard_map/ppermute | solution.py:373
  39.2 1.5 %shard_map.125 = (f32[256,512]{1,0:T(8,128)S(1)}, f32[256,512]{1,0:T(8,128)S(1)}, f32[256,512]{1,0:T(8,128)S(1)}, f32[256,512]{1,0:T(8,128)S(1)}) custom-call(s32[5]{0:T(128)S(1)} %stack.23.pos_ref, bf16[3,2048,256]{2,1,0:T(8,128)(2,1)S(1)} %copy-done, f32[960,256]{1,0:T(8,128)S(1)} %get-tuple-element.75.all_ref.own_ref), custom_call_target="tpu_custom_call" | custom-call | tf_op jit(solution)/shard_map/pallas_call | solution.py:493
  40.7 0.6 collective-permute-done.11.other_ref
  41.4 1.5 %shard_map.126 = (f32[792,256]{1,0:T(8,128)S(1)}, f32[792,256]{1,0:T(8,128)S(1)}, f32[792,256]{1,0:T(8,128)S(1)}, f32[792,256]{1,0:T(8,128)S(1)}, f32[256,512]{1,0:T(8,128)S(1)}, /*index=5*/f32[256,512]{1,0:T(8,128)S(1)}) custom-call(s32[5]{0:T(128)S(1)} %stack.23.pos_ref, ...), custom_call_target="tpu_custom_call", output_to_operand_aliasing={{4}: (5, {}), {5}: (6, {})} | custom-call | tf_op jit(solution)/shard_map/pallas_call | solution.py:498
  42.9 2.8 %collective-permute-start.14 = (f32[792,256]{1,0:T(8,128)S(1)}, f32[792,256]{1,0:T(8,128)S(1)}, u32[]{:S(2)}, u32[]{:S(2)}) collective-permute-start(f32[792,256]{1,0:T(8,128)S(1)} %get-tuple-element.84), channel_id=1, source_target_pairs={{0,32},{4,36},{8,40},{12,44},{16,20},{20,24},{24,28},{28,16},{32,6... | collective-permute-start | bytes 2433032 | tf_op jit(solution)/shard_map/ppermute | solution.py:368
  45.8 2.2 %collective-permute-start.16 = (f32[792,256]{1,0:T(8,128)S(1)}, f32[792,256]{1,0:T(8,128)S(1)}, u32[]{:S(2)}, u32[]{:S(2)}) collective-permute-start(f32[792,256]{1,0:T(8,128)S(1)} %get-tuple-element.86), channel_id=1, source_target_pairs={{0,64},{4,68},{8,72},{12,76},{16,24},{20,28},{24,16},{28,20},{32,9... | collective-permute-start | bytes 2433032 | tf_op jit(solution)/shard_map/ppermute | solution.py:368
  48.0 1.6 %collective-permute-start.12 = (f32[256,512]{1,0:T(8,128)S(1)}, f32[256,512]{1,0:T(8,128)S(1)}, u32[]{:S(2)}, u32[]{:S(2)}) collective-permute-start(f32[256,512]{1,0:T(8,128)S(1)} %get-tuple-element.81), channel_id=1, source_target_pairs={{0,1},{1,2},{2,3},{3,0},{4,5},{5,6},{6,7},{7,4},{8,9},{9,10},{10,1... | collective-permute-start | bytes 1572872 | tf_op jit(solution)/shard_map/ppermute | solution.py:496
  49.6 2.1 %collective-permute-start.13 = (f32[256,512]{1,0:T(8,128)S(1)}, f32[256,512]{1,0:T(8,128)S(1)}, u32[]{:S(2)}, u32[]{:S(2)}) collective-permute-start(f32[256,512]{1,0:T(8,128)S(1)} %get-tuple-element.82), channel_id=1, source_target_pairs={{0,3},{1,0},{2,1},{3,2},{4,7},{5,4},{6,5},{7,6},{8,11},{9,8},{10,9... | collective-permute-start | bytes 1572872 | tf_op jit(solution)/shard_map/ppermute | solution.py:496
  51.8 11.8 %collective-permute-done.12.refs_0_ = f32[256,512]{1,0:T(8,128)S(1)} collective-permute-done((f32[256,512]{1,0:T(8,128)S(1)}, f32[256,512]{1,0:T(8,128)S(1)}, u32[]{:S(2)}, u32[]{:S(2)}) %collective-permute-start.12) | collective-permute-done | bytes 524320 | tf_op jit(solution)/shard_map/ppermute | solution.py:496
  63.5 1.6 %collective-permute-done.16.far_ref = f32[792,256]{1,0:T(8,128)S(1)} collective-permute-done((f32[792,256]{1,0:T(8,128)S(1)}, f32[792,256]{1,0:T(8,128)S(1)}, u32[]{:S(2)}, u32[]{:S(2)}) %collective-permute-start.16) | collective-permute-done | bytes 811040 | tf_op jit(solution)/shard_map/ppermute | solution.py:368
  65.2 0.2 shard_map.127.own_ref
  65.4 2.5 %collective-permute-start.19 = (f32[792,256]{1,0:T(8,128)S(1)}, f32[792,256]{1,0:T(8,128)S(1)}, u32[]{:S(2)}, u32[]{:S(2)}) collective-permute-start(f32[792,256]{1,0:T(8,128)S(1)} %shard_map.127.own_ref), channel_id=1, source_target_pairs={{0,8},{4,12},{8,0},{12,4},{16,80},{20,84},{24,88},{28,92},{32,40},... | collective-permute-start | bytes 2433032 | tf_op jit(solution)/shard_map/ppermute | solution.py:368
  67.9 0.9 collective-permute-start.18
  68.7 0.6 collective-permute-start.17
  69.4 3.6 %collective-permute-start.10 = (f32[256,512]{1,0:T(8,128)S(1)}, f32[256,512]{1,0:T(8,128)S(1)}, u32[]{:S(2)}, u32[]{:S(2)}) collective-permute-start(f32[256,512]{1,0:T(8,128)S(1)} %get-tuple-element.77), channel_id=1, source_target_pairs={{0,2},{1,3},{2,0},{3,1},{4,6},{5,7},{6,4},{7,5},{8,10},{9,11},{10,... | collective-permute-start | bytes 1572872 | tf_op jit(solution)/shard_map/ppermute | solution.py:496
  73.0 9.0 %collective-permute-done.10 = f32[256,512]{1,0:T(8,128)S(1)} collective-permute-done((f32[256,512]{1,0:T(8,128)S(1)}, f32[256,512]{1,0:T(8,128)S(1)}, u32[]{:S(2)}, u32[]{:S(2)}) %collective-permute-start.10) | collective-permute-done | bytes 524320 | tf_op jit(solution)/shard_map/ppermute | solution.py:496
  81.9 0.2 fusion.refs_0_
  82.2 5.0 %collective-permute-done.18.ahead_ref = f32[792,256]{1,0:T(8,128)S(1)} collective-permute-done((f32[792,256]{1,0:T(8,128)S(1)}, f32[792,256]{1,0:T(8,128)S(1)}, u32[]{:S(2)}, u32[]{:S(2)}) %collective-permute-start.18) | collective-permute-done | bytes 811040 | tf_op jit(solution)/shard_map/ppermute | solution.py:368
  87.3 2.2 %collective-permute-start.22 = (f32[792,256]{1,0:T(8,128)S(1)}, f32[792,256]{1,0:T(8,128)S(1)}, u32[]{:S(2)}, u32[]{:S(2)}) collective-permute-start(f32[792,256]{1,0:T(8,128)S(1)} %shard_map.128.refs_0_), channel_id=1, source_target_pairs={{0,64},{4,68},{8,72},{12,76},{16,24},{20,28},{24,16},{28,20},{32,9... | collective-permute-start | bytes 2433032 | tf_op jit(solution)/shard_map/ppermute | solution.py:368
  89.6 1.2 collective-permute-start.21
  90.7 1.5 %collective-permute-start.20 = (f32[792,256]{1,0:T(8,128)S(1)}, f32[792,256]{1,0:T(8,128)S(1)}, u32[]{:S(2)}, u32[]{:S(2)}) collective-permute-start(f32[792,256]{1,0:T(8,128)S(1)} %shard_map.128.refs_0_), channel_id=1, source_target_pairs={{0,96},{4,100},{8,104},{12,108},{16,28},{20,16},{24,20},{28,24},{3... | collective-permute-start | bytes 2433032 | tf_op jit(solution)/shard_map/ppermute | solution.py:368
  92.3 8.1 %collective-permute-done.22.refs_1_.refs_3_ = f32[792,256]{1,0:T(8,128)S(1)} collective-permute-done((f32[792,256]{1,0:T(8,128)S(1)}, f32[792,256]{1,0:T(8,128)S(1)}, u32[]{:S(2)}, u32[]{:S(2)}) %collective-permute-start.22) | collective-permute-done | bytes 811040 | tf_op jit(solution)/shard_map/ppermute | solution.py:368
  100.4 3.3 %collective-permute-start.26 = (f32[792,256]{1,0:T(8,128)S(1)}, f32[792,256]{1,0:T(8,128)S(1)}, u32[]{:S(2)}, u32[]{:S(2)}) collective-permute-start(f32[792,256]{1,0:T(8,128)S(1)} %collective-permute-done.22.refs_1_.refs_3_), channel_id=1, source_target_pairs={{0,16},{16,0},{32,48},{48,32},{64,80},{80,64},{96,112},{112,96},{1... | collective-permute-start | bytes 2433032 | tf_op jit(solution)/shard_map/ppermute | solution.py:373
  103.6 1.7 %shard_map.129 = (f32[3,2048,256]{2,1,0:T(8,128)}, f32[792,256]{1,0:T(8,128)S(1)}) custom-call(s32[5]{0:T(128)S(1)} %stack.23.pos_ref, f32[792,256]{1,0:T(8,128)S(1)} %shard_map.128.refs_0_, f32[792,256]{1,0:T(8,128)S(1)} %collective-permute-done.22.refs_1_.refs_3_), custom_call_target="tpu_custom_call" | custom-call | tf_op jit(solution)/shard_map/pallas_call | solution.py:514
  105.5 3.5 %collective-permute-done.21.refs_1_.refs_2_ = f32[792,256]{1,0:T(8,128)S(1)} collective-permute-done((f32[792,256]{1,0:T(8,128)S(1)}, f32[792,256]{1,0:T(8,128)S(1)}, u32[]{:S(2)}, u32[]{:S(2)}) %collective-permute-start.21) | collective-permute-done | bytes 811040 | tf_op jit(solution)/shard_map/ppermute | solution.py:368
  109.0 3.2 %collective-permute-start.25 = (f32[792,256]{1,0:T(8,128)S(1)}, f32[792,256]{1,0:T(8,128)S(1)}, u32[]{:S(2)}, u32[]{:S(2)}) collective-permute-start(f32[792,256]{1,0:T(8,128)S(1)} %collective-permute-done.21.refs_1_.refs_2_), channel_id=1, source_target_pairs={{0,16},{16,0},{32,48},{48,32},{64,80},{80,64},{96,112},{112,96},{1... | collective-permute-start | bytes 2433032 | tf_op jit(solution)/shard_map/ppermute | solution.py:373
  112.3 2.3 %shard_map.130.refs_8_ = f32[3,2048,256]{2,1,0:T(8,128)} custom-call(s32[5]{0:T(128)S(1)} %stack.23.pos_ref, f32[792,256]{1,0:T(8,128)S(1)} %collective-permute-done.20.refs_0_.refs_1_, f32[792,256]{1,0:T(8,128)S(1)} %collective-permute-done.21.refs_1_.refs_2_, ...), custom_call_target="tpu_custom_call", output_to_operand_aliasing={{}: (5, {})} | custom-call | tf_op jit(solution)/shard_map/pallas_call | solution.py:514
  114.6 0.8 collective-permute-done.24.refs_5_
  115.3 2.4 %shard_map.131 = (f32[3,2048,256]{2,1,0:T(8,128)}, f32[2,128,128]{2,1,0:T(8,128)}, f32[2,128]{1,0:T(2,128)}, f32[2]{0:T(128)}) custom-call(s32[5]{0:T(128)S(1)} %stack.23.pos_ref, f32[792,256]{1,0:T(8,128)S(1)} %shard_map.128.refs_0_, f32[792,256]{1,0:T(8,128)S(1)} %collective-permute-done.20.refs_0_.refs_1_, ...), custom_call_target="tpu_custom_call", output_to_operand_aliasing={{0}: (9, {})} | custom-call | tf_op jit(solution)/shard_map/pallas_call | solution.py:530
  (36 shorter events, 0.5 us)
Async XLA Ops:
  0.6 12.7 %copy-start.4 = (f32[1,2,256]{2,1,0:T(2,128)S(1)}, f32[1,2,256]{2,1,0:T(2,128)}, u32[]{:S(2)}) copy-start(f32[1,2,256]{2,1,0:T(2,128)} %gate_ref.7) | copy-start | bytes 6148
  0.6 12.7 %copy-start.5 = (f32[2]{0:T(128)S(1)}, f32[2]{0:T(128)}, u32[]{:S(2)}) copy-start(f32[2]{0:T(128)} %base_ref.7) | copy-start | bytes 28
  0.8 20.4 %copy-start.2 = (f32[2,128,128]{2,1,0:T(8,128)S(1)}, f32[2,128,128]{2,1,0:T(8,128)}, u32[]{:S(2)}) copy-start(f32[2,128,128]{2,1,0:T(8,128)} %init_ref.3) | copy-start | bytes 393220
  0.8 20.4 %copy-start.3 = (bf16[1,256,256]{2,1,0:T(8,128)(2,1)S(1)}, bf16[1,256,256]{2,1,0:T(8,128)(2,1)}, u32[]{:S(2)}) copy-start(bf16[1,256,256]{2,1,0:T(8,128)(2,1)} %up_ref.3) | copy-start | bytes 393220
  0.8 20.4 %copy-start.6 = (f32[2,128]{1,0:T(2,128)S(1)}, f32[2,128]{1,0:T(2,128)}, u32[]{:S(2)}) copy-start(f32[2,128]{1,0:T(2,128)} %gain_ref.1) | copy-start | bytes 3076
  7.2 13.0 %collective-permute-start.4 = (f32[256,1024]{1,0:T(8,128)S(1)}, f32[256,1024]{1,0:T(8,128)S(1)}, u32[]{:S(2)}, u32[]{:S(2)}) collective-permute-start(f32[256,1024]{1,0:T(8,128)S(1)} %get-tuple-element.58), channel_id=1, source_target_pairs={{0,16},{16,0},{32,48},{48,32},{64,80},{80,64},{96,112},{112,96},{1... | collective-permute-start | bytes 3145736 | tf_op jit(solution)/shard_map/ppermute | solution.py:373
  8.7 8.5 %collective-permute-start = (f32[2,128,128]{2,1,0:T(8,128)S(1)}, f32[2,128,128]{2,1,0:T(8,128)S(1)}, u32[]{:S(2)}, u32[]{:S(2)}) collective-permute-start(f32[2,128,128]{2,1,0:T(8,128)S(1)} %get-tuple-element.50), channel_id=1, source_target_pairs={{0,4},{8,12},{1,5},{9,13},{2,6},{10,14},{3,7},{11,15},{16,20},{24,... | collective-permute-start | bytes 393224 | tf_op jit(solution)/shard_map/ppermute | solution.py:452
  12.0 9.1 %collective-permute-start.3 = (f32[2,128,128]{2,1,0:T(8,128)S(1)}, f32[2,128,128]{2,1,0:T(8,128)S(1)}, u32[]{:S(2)}, u32[]{:S(2)}) collective-permute-start(f32[2,128,128]{2,1,0:T(8,128)S(1)} %get-tuple-element.51.d_ref), channel_id=1, source_target_pairs={{8,12},{4,0},{9,13},{5,1},{10,14},{6,2},{11,15},{7,3},{24,28},{20,... | collective-permute-start | bytes 393224 | tf_op jit(solution)/shard_map/ppermute | solution.py:453
  17.2 22.0 %copy-start = (bf16[3,2048,256]{2,1,0:T(8,128)(2,1)S(1)}, bf16[3,2048,256]{2,1,0:T(8,128)(2,1)}, u32[]{:S(2)}) copy-start(bf16[3,2048,256]{2,1,0:T(8,128)(2,1)} %w_ref.1) | copy-start | bytes 9437188
  17.4 3.7 %collective-permute-start.2 = (f32[2,128,128]{2,1,0:T(8,128)S(1)}, f32[2,128,128]{2,1,0:T(8,128)S(1)}, u32[]{:S(2)}, u32[]{:S(2)}) collective-permute-start(f32[2,128,128]{2,1,0:T(8,128)S(1)} %shard_map.120), channel_id=1, source_target_pairs={{4,12},{5,13},{6,14},{7,15},{20,28},{21,29},{22,30},{23,31},{36,44... | collective-permute-start | bytes 393224 | tf_op jit(solution)/shard_map/ppermute | solution.py:471
  18.2 2.9 %collective-permute-start.1 = (f32[2,128,128]{2,1,0:T(8,128)S(1)}, f32[2,128,128]{2,1,0:T(8,128)S(1)}, u32[]{:S(2)}, u32[]{:S(2)}) collective-permute-start(f32[2,128,128]{2,1,0:T(8,128)S(1)} %shard_map.120), channel_id=1, source_target_pairs={{4,8},{5,9},{6,10},{7,11},{20,24},{21,25},{22,26},{23,27},{36,40},... | collective-permute-start | bytes 393224 | tf_op jit(solution)/shard_map/ppermute | solution.py:470
  18.9 10.6 %collective-permute-start.9 = (f32[2,128,128]{2,1,0:T(8,128)S(1)}, f32[2,128,128]{2,1,0:T(8,128)S(1)}, u32[]{:S(2)}, u32[]{:S(2)}) collective-permute-start(f32[2,128,128]{2,1,0:T(8,128)S(1)} %get-tuple-element.51.d_ref), channel_id=1, source_target_pairs={{8,0},{9,1},{10,2},{11,3},{24,16},{25,17},{26,18},{27,19},{40,32},... | collective-permute-start | bytes 393224 | tf_op jit(solution)/shard_map/ppermute | solution.py:455
  20.2 9.3 %collective-permute-start.8 = (f32[2,128,128]{2,1,0:T(8,128)S(1)}, f32[2,128,128]{2,1,0:T(8,128)S(1)}, u32[]{:S(2)}, u32[]{:S(2)}) collective-permute-start(f32[2,128,128]{2,1,0:T(8,128)S(1)} %get-tuple-element.51.d_ref), channel_id=1, source_target_pairs={{8,4},{9,5},{10,6},{11,7},{24,20},{25,21},{26,22},{27,23},{40,36},... | collective-permute-start | bytes 393224 | tf_op jit(solution)/shard_map/ppermute | solution.py:454
  22.7 8.5 %collective-permute-start.7 = (f32[2,128,128]{2,1,0:T(8,128)S(1)}, f32[2,128,128]{2,1,0:T(8,128)S(1)}, u32[]{:S(2)}, u32[]{:S(2)}) collective-permute-start(f32[2,128,128]{2,1,0:T(8,128)S(1)} %get-tuple-element.59.p_ref), channel_id=1, source_target_pairs={{12,0},{13,1},{14,2},{15,3},{28,16},{29,17},{30,18},{31,19},{44,32... | collective-permute-start | bytes 393224 | tf_op jit(solution)/shard_map/ppermute | solution.py:480
  24.0 9.2 %collective-permute-start.6 = (f32[2,128,128]{2,1,0:T(8,128)S(1)}, f32[2,128,128]{2,1,0:T(8,128)S(1)}, u32[]{:S(2)}, u32[]{:S(2)}) collective-permute-start(f32[2,128,128]{2,1,0:T(8,128)S(1)} %get-tuple-element.59.p_ref), channel_id=1, source_target_pairs={{12,4},{8,0},{13,5},{9,1},{14,6},{10,2},{15,7},{11,3},{28,20},{24,... | collective-permute-start | bytes 393224 | tf_op jit(solution)/shard_map/ppermute | solution.py:479
  25.3 7.9 %collective-permute-start.5 = (f32[2,128,128]{2,1,0:T(8,128)S(1)}, f32[2,128,128]{2,1,0:T(8,128)S(1)}, u32[]{:S(2)}, u32[]{:S(2)}) collective-permute-start(f32[2,128,128]{2,1,0:T(8,128)S(1)} %get-tuple-element.59.p_ref), channel_id=1, source_target_pairs={{12,8},{8,4},{4,0},{13,9},{9,5},{5,1},{14,10},{10,6},{6,2},{15,11}... | collective-permute-start | bytes 393224 | tf_op jit(solution)/shard_map/ppermute | solution.py:478
  35.8 5.6 %collective-permute-start.11 = (f32[960,256]{1,0:T(8,128)S(1)}, f32[960,256]{1,0:T(8,128)S(1)}, u32[]{:S(2)}, u32[]{:S(2)}) collective-permute-start(f32[960,256]{1,0:T(8,128)S(1)} %get-tuple-element.75.all_ref.own_ref), channel_id=1, source_target_pairs={{0,16},{16,0},{32,48},{48,32},{64,80},{80,64},{96,112},{112,96},{1... | collective-permute-start | bytes 2949128 | tf_op jit(solution)/shard_map/ppermute | solution.py:373
  42.9 20.6 %collective-permute-start.14 = (f32[792,256]{1,0:T(8,128)S(1)}, f32[792,256]{1,0:T(8,128)S(1)}, u32[]{:S(2)}, u32[]{:S(2)}) collective-permute-start(f32[792,256]{1,0:T(8,128)S(1)} %get-tuple-element.84), channel_id=1, source_target_pairs={{0,32},{4,36},{8,40},{12,44},{16,20},{20,24},{24,28},{28,16},{32,6... | collective-permute-start | bytes 2433032 | tf_op jit(solution)/shard_map/ppermute | solution.py:368
  45.7 17.8 %collective-permute-start.15 = (f32[792,256]{1,0:T(8,128)S(1)}, f32[792,256]{1,0:T(8,128)S(1)}, u32[]{:S(2)}, u32[]{:S(2)}) collective-permute-start(f32[792,256]{1,0:T(8,128)S(1)} %get-tuple-element.85), channel_id=1, source_target_pairs={{0,96},{4,100},{8,104},{12,108},{16,28},{20,16},{24,20},{28,24},{3... | collective-permute-start | bytes 2433032 | tf_op jit(solution)/shard_map/ppermute | solution.py:368
  45.8 19.3 %collective-permute-start.16 = (f32[792,256]{1,0:T(8,128)S(1)}, f32[792,256]{1,0:T(8,128)S(1)}, u32[]{:S(2)}, u32[]{:S(2)}) collective-permute-start(f32[792,256]{1,0:T(8,128)S(1)} %get-tuple-element.86), channel_id=1, source_target_pairs={{0,64},{4,68},{8,72},{12,76},{16,24},{20,28},{24,16},{28,20},{32,9... | collective-permute-start | bytes 2433032 | tf_op jit(solution)/shard_map/ppermute | solution.py:368
  48.0 15.5 %collective-permute-start.12 = (f32[256,512]{1,0:T(8,128)S(1)}, f32[256,512]{1,0:T(8,128)S(1)}, u32[]{:S(2)}, u32[]{:S(2)}) collective-permute-start(f32[256,512]{1,0:T(8,128)S(1)} %get-tuple-element.81), channel_id=1, source_target_pairs={{0,1},{1,2},{2,3},{3,0},{4,5},{5,6},{6,7},{7,4},{8,9},{9,10},{10,1... | collective-permute-start | bytes 1572872 | tf_op jit(solution)/shard_map/ppermute | solution.py:496
  49.6 13.9 %collective-permute-start.13 = (f32[256,512]{1,0:T(8,128)S(1)}, f32[256,512]{1,0:T(8,128)S(1)}, u32[]{:S(2)}, u32[]{:S(2)}) collective-permute-start(f32[256,512]{1,0:T(8,128)S(1)} %get-tuple-element.82), channel_id=1, source_target_pairs={{0,3},{1,0},{2,1},{3,2},{4,7},{5,4},{6,5},{7,6},{8,11},{9,8},{10,9... | collective-permute-start | bytes 1572872 | tf_op jit(solution)/shard_map/ppermute | solution.py:496
  65.4 16.8 %collective-permute-start.19 = (f32[792,256]{1,0:T(8,128)S(1)}, f32[792,256]{1,0:T(8,128)S(1)}, u32[]{:S(2)}, u32[]{:S(2)}) collective-permute-start(f32[792,256]{1,0:T(8,128)S(1)} %shard_map.127.own_ref), channel_id=1, source_target_pairs={{0,8},{4,12},{8,0},{12,4},{16,80},{20,84},{24,88},{28,92},{32,40},... | collective-permute-start | bytes 2433032 | tf_op jit(solution)/shard_map/ppermute | solution.py:368
  67.9 19.3 %collective-permute-start.18 = (f32[792,256]{1,0:T(8,128)S(1)}, f32[792,256]{1,0:T(8,128)S(1)}, u32[]{:S(2)}, u32[]{:S(2)}) collective-permute-start(f32[792,256]{1,0:T(8,128)S(1)} %shard_map.127.own_ref), channel_id=1, source_target_pairs={{0,12},{4,0},{8,4},{12,8},{16,112},{20,116},{24,120},{28,124},{32,... | collective-permute-start | bytes 2433032 | tf_op jit(solution)/shard_map/ppermute | solution.py:368
  68.7 18.4 %collective-permute-start.17 = (f32[792,256]{1,0:T(8,128)S(1)}, f32[792,256]{1,0:T(8,128)S(1)}, u32[]{:S(2)}, u32[]{:S(2)}) collective-permute-start(f32[792,256]{1,0:T(8,128)S(1)} %shard_map.127.own_ref), channel_id=1, source_target_pairs={{0,4},{4,8},{8,12},{12,0},{16,48},{20,52},{24,56},{28,60},{32,36},... | collective-permute-start | bytes 2433032 | tf_op jit(solution)/shard_map/ppermute | solution.py:368
  69.4 12.6 %collective-permute-start.10 = (f32[256,512]{1,0:T(8,128)S(1)}, f32[256,512]{1,0:T(8,128)S(1)}, u32[]{:S(2)}, u32[]{:S(2)}) collective-permute-start(f32[256,512]{1,0:T(8,128)S(1)} %get-tuple-element.77), channel_id=1, source_target_pairs={{0,2},{1,3},{2,0},{3,1},{4,6},{5,7},{6,4},{7,5},{8,10},{9,11},{10,... | collective-permute-start | bytes 1572872 | tf_op jit(solution)/shard_map/ppermute | solution.py:496
  82.1 32.4 %copy-start.1 = (bf16[1,256,512]{2,1,0:T(8,128)(2,1)}, bf16[1,256,512]{2,1,0:T(8,128)(2,1)S(1)}, u32[]{:S(2)}) copy-start(bf16[1,256,512]{2,1,0:T(8,128)(2,1)S(1)} %fusion.refs_0_) | copy-start | bytes 786436
  87.3 13.0 %collective-permute-start.22 = (f32[792,256]{1,0:T(8,128)S(1)}, f32[792,256]{1,0:T(8,128)S(1)}, u32[]{:S(2)}, u32[]{:S(2)}) collective-permute-start(f32[792,256]{1,0:T(8,128)S(1)} %shard_map.128.refs_0_), channel_id=1, source_target_pairs={{0,64},{4,68},{8,72},{12,76},{16,24},{20,28},{24,16},{28,20},{32,9... | collective-permute-start | bytes 2433032 | tf_op jit(solution)/shard_map/ppermute | solution.py:368
  89.6 19.4 %collective-permute-start.21 = (f32[792,256]{1,0:T(8,128)S(1)}, f32[792,256]{1,0:T(8,128)S(1)}, u32[]{:S(2)}, u32[]{:S(2)}) collective-permute-start(f32[792,256]{1,0:T(8,128)S(1)} %shard_map.128.refs_0_), channel_id=1, source_target_pairs={{0,32},{4,36},{8,40},{12,44},{16,20},{20,24},{24,28},{28,16},{32,6... | collective-permute-start | bytes 2433032 | tf_op jit(solution)/shard_map/ppermute | solution.py:368
  90.7 21.5 %collective-permute-start.20 = (f32[792,256]{1,0:T(8,128)S(1)}, f32[792,256]{1,0:T(8,128)S(1)}, u32[]{:S(2)}, u32[]{:S(2)}) collective-permute-start(f32[792,256]{1,0:T(8,128)S(1)} %shard_map.128.refs_0_), channel_id=1, source_target_pairs={{0,96},{4,100},{8,104},{12,108},{16,28},{20,16},{24,20},{28,24},{3... | collective-permute-start | bytes 2433032 | tf_op jit(solution)/shard_map/ppermute | solution.py:368
  100.4 11.9 %collective-permute-start.26 = (f32[792,256]{1,0:T(8,128)S(1)}, f32[792,256]{1,0:T(8,128)S(1)}, u32[]{:S(2)}, u32[]{:S(2)}) collective-permute-start(f32[792,256]{1,0:T(8,128)S(1)} %collective-permute-done.22.refs_1_.refs_3_), channel_id=1, source_target_pairs={{0,16},{16,0},{32,48},{48,32},{64,80},{80,64},{96,112},{112,96},{1... | collective-permute-start | bytes 2433032 | tf_op jit(solution)/shard_map/ppermute | solution.py:373
  105.4 6.9 %collective-permute-start.23 = (f32[792,256]{1,0:T(8,128)S(1)}, f32[792,256]{1,0:T(8,128)S(1)}, u32[]{:S(2)}, u32[]{:S(2)}) collective-permute-start(f32[792,256]{1,0:T(8,128)S(1)} %get-tuple-element.87), channel_id=1, source_target_pairs={{0,16},{16,0},{32,48},{48,32},{64,80},{80,64},{96,112},{112,96},{1... | collective-permute-start | bytes 2433032 | tf_op jit(solution)/shard_map/ppermute | solution.py:373
  109.0 5.6 %collective-permute-start.25 = (f32[792,256]{1,0:T(8,128)S(1)}, f32[792,256]{1,0:T(8,128)S(1)}, u32[]{:S(2)}, u32[]{:S(2)}) collective-permute-start(f32[792,256]{1,0:T(8,128)S(1)} %collective-permute-done.21.refs_1_.refs_2_), channel_id=1, source_target_pairs={{0,16},{16,0},{32,48},{48,32},{64,80},{80,64},{96,112},{112,96},{1... | collective-permute-start | bytes 2433032 | tf_op jit(solution)/shard_map/ppermute | solution.py:373
  112.2 3.1 %collective-permute-start.24 = (f32[792,256]{1,0:T(8,128)S(1)}, f32[792,256]{1,0:T(8,128)S(1)}, u32[]{:S(2)}, u32[]{:S(2)}) collective-permute-start(f32[792,256]{1,0:T(8,128)S(1)} %collective-permute-done.20.refs_0_.refs_1_), channel_id=1, source_target_pairs={{0,16},{16,0},{32,48},{48,32},{64,80},{80,64},{96,112},{112,96},{1... | collective-permute-start | bytes 2433032 | tf_op jit(solution)/shard_map/ppermute | solution.py:373

commit v12 on v10

--- a/solution.py
+++ b/solution.py
@@ -104,7 +104,7 @@
     firsts = [dot(decays[h], init_ref[h], NN, 3) + offsets[h] for h in heads]
     v_ref[...] = v_all
     for h in heads:
-        send_ref[h] = jnp.where(pos_ref[4] == 0, firsts[h], offsets[h])
+        send_ref[h] = jnp.where(pos_ref[4] == 0, firsts[h], decays[h])
         d_ref[h] = decays[h]
         o_ref[h] = offsets[h]
         k_ref[:, span(h)] = ks[h]
@@ -141,25 +141,19 @@
         zv_ref[:, span(h)] = dot(mix, rv, NN, 3)
 
 
-def step_kernel(d_ref, w_ref, o_ref, after_ref, out_ref):
-    del after_ref
-    for h in range(d_ref.shape[0]):
-        out_ref[h] = o_ref[h] + dot(d_ref[h], w_ref[h], NN, 3)
-
-
 def norm_kernel(
-    pos_ref, init_ref, near_ref, mid_ref, far_ref, rd_ref, qt_ref, zv_ref, up_ref, gain_ref, after_ref,
+    pos_ref, init_ref, map_one_ref, add_one_ref, map_two_ref, add_two_ref, map_three_ref, qt_ref, zv_ref, up_ref,
+    gain_ref, after_ref,
     w_ref, h_ref, p_ref, dgain_ref,
 ):
     del after_ref
     ctx = pos_ref[4]
     heads = range(init_ref.shape[0])
-    lasts = [dot(rd_ref[h], far_ref[h], NN, 3) + near_ref[h] for h in heads]
+    seconds = [dot(map_two_ref[h], map_three_ref[h], NN, 3) + add_two_ref[h] for h in heads]
+    seconds = [jnp.where(ctx == 3, seconds[h], map_two_ref[h]) for h in heads]
+    lasts = [dot(map_one_ref[h], seconds[h], NN, 3) + add_one_ref[h] for h in heads]
     starts = [
-        jnp.where(
-            ctx == 0, init_ref[h], jnp.where(ctx == 1, near_ref[h], jnp.where(ctx == 2, mid_ref[h], lasts[h]))
-        )
-        for h in heads
+        jnp.where(ctx == 0, init_ref[h], jnp.where(ctx == 1, map_one_ref[h], lasts[h])) for h in heads
     ]
     qts = [qt_ref[:, span(h)] for h in heads]
     zs = [dot(qts[h], starts[h], NN, 3) + zv_ref[:, span(h)] for h in heads]
@@ -211,7 +205,7 @@
 
 
 def keys_kernel(
-    pos_ref, base_ref, gate_ref, one_ref, two_ref, three_ref, rd_ref, rd_one_ref, rd_two_ref, p_ref, d_ref, w_ref, k_ref, ninv_ref,
+    pos_ref, base_ref, gate_ref, one_ref, two_ref, three_ref, rd_ref, rd_two_ref, p_ref, d_ref, w_ref, k_ref, ninv_ref,
     gram_ref, bt_ref, r_ref, x_ref, dk_ref, de_ref, dgain_ref, dq_ref,
     all_ref, gates_ref,
 ):
@@ -220,9 +214,8 @@
     i, j = places(n)
     strict = (i // MB) > (j // MB)
     heads = range(w_ref.shape[0])
-    steps = [jnp.where(ctx == 0, rd_ref[h], rd_one_ref[h]) for h in heads]
     inner = [two_ref[h] + dot(rd_two_ref[h], three_ref[h], TN, 3) for h in heads]
-    ends = [one_ref[h] + dot(steps[h], inner[h], TN, 3) for h in heads]
+    ends = [one_ref[h] + dot(rd_ref[h], inner[h], TN, 3) for h in heads]
     ks = [k_ref[:, span(h)] for h in heads]
     rs = [r_ref[:, span(h)] for h in heads]
     rates = [rates_of(base_ref, gate_ref, h) for h in heads]
@@ -431,9 +424,12 @@
         compiler_params=PARAMS,
     )(pos, hbm(base_rates), tokens, proj_weights, proj_weights, hbm(gate_values), hbm(init_weight))
 
-    near = lax.ppermute(send, "ctx", [(0, 1), (2, 3)])
-    moved = lax.ppermute(decay, "ctx", [(2, 3), (1, 0)])
-    moved_one = lax.ppermute(decay, "ctx", [(2, 1)])
+    map_one = lax.ppermute(send, "ctx", [(0, 1), (1, 2), (2, 3)])
+    add_one = lax.ppermute(offset, "ctx", [(1, 2), (2, 3)])
+    map_two = lax.ppermute(send, "ctx", [(0, 2), (1, 3)])
+    add_two = lax.ppermute(offset, "ctx", [(1, 3)])
+    map_three = lax.ppermute(send, "ctx", [(0, 3)])
+    moved = lax.ppermute(decay, "ctx", [(1, 0), (2, 1)])
     moved_two = lax.ppermute(decay, "ctx", [(2, 0)])
     got_half = swap(other_half)
 
@@ -446,16 +442,11 @@
         compiler_params=PARAMS,
     )(pos, base_rates, tokens, proj_weights, gate_values, k, v, inv)
 
-    second = whole(step_kernel, small, [VM] * 3 + [anywhere])(
-        decay, near, offset, qt
-    )
-    mid = lax.ppermute(second, "ctx", [(1, 2)])
-    far = lax.ppermute(second, "ctx", [(1, 3)])
     other_tokt = whole(turn_kernel, vmem(half, n, dtype=BF), [VM])(got_half)
 
     w, back, pulled, dgain = whole(
-        norm_kernel, (small, wide_f32, small, vmem(heads, HS)), [SM] + [VM] * 9 + [anywhere]
-    )(pos, init_weight, near, mid, far, moved, qt, zv, cotangent, out_gain, other_tokt)
+        norm_kernel, (small, wide_f32, small, vmem(heads, HS)), [SM] + [VM] * 10 + [anywhere]
+    )(pos, init_weight, map_one, add_one, map_two, add_two, map_three, qt, zv, cotangent, out_gain, other_tokt)
 
     back_one = lax.ppermute(pulled, "ctx", [(3, 2), (2, 1), (1, 0)])
     back_two = lax.ppermute(pulled, "ctx", [(3, 1), (2, 0)])
@@ -466,8 +457,8 @@
     )(base_rates, gate_values, w, back, cotangent, q, score, rv, y, k, inv)
 
     grads, grad_gates = whole(
-        keys_kernel, (vmem(3 * n + EXTRA, wide), shape(1, heads, n)), [SM, SM] + [VM] * 20
-    )(pos, base_rates, gate_values, back_one, back_two, back_three, moved, moved_one, moved_two, pulled, decay, w, k, ninv, gram, bt, r, x,
+        keys_kernel, (vmem(3 * n + EXTRA, wide), shape(1, heads, n)), [SM, SM] + [VM] * 19
+    )(pos, base_rates, gate_values, back_one, back_two, back_three, moved, moved_two, pulled, decay, w, k, ninv, gram, bt, r, x,
       dk, de, dgain, dq)
 
     chunk = vmem(3 * CHUNK + PIECE, wide)

time: 117 us -> 121 us (1.034)
  starting transfers between devices: 44.7 us -> 48.7 us
    ppermute x5 -> x6, starting transfers between devices: 6.71 us -> 12.4 us  [the longest x1 5.98 us: body(): map_three = lax.ppermute(send, 'ctx', [(0, 3)])]
    ppermute x1, waiting for transfers between devices: 2 us -> 0.01 us  [body(): back_two = lax.ppermute(pulled, 'ctx', [(3, 1), (2, 0)])]
    ppermute x6, starting transfers between devices: 11.5 us -> 9.53 us  [swap(): return lax.ppermute(value, 'dp', [(i, i ^ 1) for i in range(2 * RING)])]
    ppermute x1, waiting for transfers between devices: 1.76 us -> 3.59 us  [body(): back_three = lax.ppermute(pulled, 'ctx', [(3, 0)])]
  transfers between devices with their start and end apart: 27 -> 28, of which waited for: 10 -> 9; matrix products, arithmetic and copies ran while one was open for 0% -> 0% of each run, Pallas kernels for 12% -> 12%
where the time goes in v12:
time: 121 us
  starting transfers between devices  48.7 us (40%)
  waiting for transfers between devices  43.8 us (36%)
  Pallas kernels  26.8 us (22%)
    ppermute x3, waiting for transfers between devices, along_head(): lax.ppermute(terms, 'head', [(i, (i + turn) % RING) for i in range(RING)])  21 us
    ppermute x9, waiting for transfers between devices, round_turn(): lax.ppermute(chunk, ('dp', 'ctx'), moves(first, turn))  17.8 us
    ppermute x9, starting transfers between devices, round_turn(): lax.ppermute(chunk, ('dp', 'ctx'), moves(first, turn))  14.3 us
    ppermute x6, starting transfers between devices, swap(): return lax.ppermute(value, 'dp', [(i, i ^ 1) for i in range(2 * RING)])  9.53 us
    ppermute x3, starting transfers between devices, along_head(): lax.ppermute(terms, 'head', [(i, (i + turn) % RING) for i in range(RING)])  7.36 us
    ppermute x1, starting transfers between devices, body(): map_three = lax.ppermute(send, 'ctx', [(0, 3)])  5.98 us
    pallas_call x1, Pallas kernels, body(): pl.pallas_call(maps_kernel, grid=(1,), out_shape=(wide_f32, wide_f32, vme...  5.55 us
    pallas_call x1, Pallas kernels, body(): pl.pallas_call(reach_kernel, grid=(1,), out_shape=(wide_f32, square, wide...  4.03 us
  transfers between devices with their start and end apart: 28, of which 9 were waited for; matrix products, arithmetic and copies ran while one was open for 0% of the time, Pallas kernels for 12%

profile of v12, /device:TPU:1, one launch (start us, length us, event | category | flops | bytes accessed | tf_op | source)
XLA Modules:
  0.0 120.9 jit_solution(17548910238044376413)
XLA Ops:
  0.8 5.6 %shard_map.118 = (f32[256,256]{1,0:T(8,128)S(1)}, f32[256,256]{1,0:T(8,128)S(1)}, f32[2,256,128]{2,1,0:T(8,128)S(1)}, f32[2,256,256]{2,1,0:T(8,128)S(1)}, f32[2,...) custom-call(s32[5]{0:T(128)S(1)} %stack.23.pos_ref, ...), custom_call_target="tpu_custom_call" | custom-call | tf_op jit(solution)/shard_map/pallas_call | solution.py:415
  6.3 1.5 %collective-permute-start.5 = (f32[256,1024]{1,0:T(8,128)S(1)}, f32[256,1024]{1,0:T(8,128)S(1)}, u32[]{:S(2)}, u32[]{:S(2)}) collective-permute-start(f32[256,1024]{1,0:T(8,128)S(1)} %get-tuple-element.57), channel_id=1, source_target_pairs={{0,16},{16,0},{32,48},{48,32},{64,80},{80,64},{96,112},{112,96},{1... | collective-permute-start | bytes 3145736 | tf_op jit(solution)/shard_map/ppermute | solution.py:354
  7.8 0.7 collective-permute-start.3
  8.5 0.7 collective-permute-start.1
  9.2 6.0 %collective-permute-start.4 = (f32[2,128,128]{2,1,0:T(8,128)S(1)}, f32[2,128,128]{2,1,0:T(8,128)S(1)}, u32[]{:S(2)}, u32[]{:S(2)}) collective-permute-start(f32[2,128,128]{2,1,0:T(8,128)S(1)} %get-tuple-element.50), channel_id=1, source_target_pairs={{0,12},{1,13},{2,14},{3,15},{16,28},{17,29},{18,30},{19,31},{32,44... | collective-permute-start | bytes 393224 | tf_op jit(solution)/shard_map/ppermute | solution.py:431
  15.2 2.5 %collective-permute-start.2 = (f32[2,128,128]{2,1,0:T(8,128)S(1)}, f32[2,128,128]{2,1,0:T(8,128)S(1)}, u32[]{:S(2)}, u32[]{:S(2)}) collective-permute-start(f32[2,128,128]{2,1,0:T(8,128)S(1)} %get-tuple-element.50), channel_id=1, source_target_pairs={{0,8},{4,12},{1,9},{5,13},{2,10},{6,14},{3,11},{7,15},{16,24},{20,... | collective-permute-start | bytes 393224 | tf_op jit(solution)/shard_map/ppermute | solution.py:429
  17.6 1.3 %collective-permute-start = (f32[2,128,128]{2,1,0:T(8,128)S(1)}, f32[2,128,128]{2,1,0:T(8,128)S(1)}, u32[]{:S(2)}, u32[]{:S(2)}) collective-permute-start(f32[2,128,128]{2,1,0:T(8,128)S(1)} %get-tuple-element.50), channel_id=1, source_target_pairs={{0,4},{4,8},{8,12},{1,5},{5,9},{9,13},{2,6},{6,10},{10,14},{3,7},{... | collective-permute-start | bytes 393224 | tf_op jit(solution)/shard_map/ppermute | solution.py:427
  19.0 4.0 %shard_map.119 = (f32[256,256]{1,0:T(8,128)S(1)}, f32[2,256,256]{2,1,0:T(8,128)S(1)}, f32[256,256]{1,0:T(8,128)S(1)}, f32[256,256]{1,0:T(8,128)S(1)}, f32[256,25...) custom-call(s32[5]{0:T(128)S(1)} %stack.23.pos_ref, f32[2]{0:T(128)S(1)} %copy-done.5, ...), custom_call_target="tpu_custom_call" | custom-call | tf_op jit(solution)/shard_map/pallas_call | solution.py:436
  23.0 0.2 shard_map.120.after_ref.other_tokt_ref
  23.3 1.3 %collective-permute-start.10 = (f32[2,128,128]{2,1,0:T(8,128)S(1)}, f32[2,128,128]{2,1,0:T(8,128)S(1)}, u32[]{:S(2)}, u32[]{:S(2)}) collective-permute-start(f32[2,128,128]{2,1,0:T(8,128)S(1)} %get-tuple-element.59.d_ref), channel_id=1, source_target_pairs={{8,0},{9,1},{10,2},{11,3},{24,16},{25,17},{26,18},{27,19},{40,32},... | collective-permute-start | bytes 393224 | tf_op jit(solution)/shard_map/ppermute | solution.py:433
  24.6 1.3 %collective-permute-start.9 = (f32[2,128,128]{2,1,0:T(8,128)S(1)}, f32[2,128,128]{2,1,0:T(8,128)S(1)}, u32[]{:S(2)}, u32[]{:S(2)}) collective-permute-start(f32[2,128,128]{2,1,0:T(8,128)S(1)} %get-tuple-element.59.d_ref), channel_id=1, source_target_pairs={{4,0},{8,4},{5,1},{9,5},{6,2},{10,6},{7,3},{11,7},{20,16},{24,20},... | collective-permute-start | bytes 393224 | tf_op jit(solution)/shard_map/ppermute | solution.py:432
  25.9 1.7 %shard_map.121 = (f32[2,128,128]{2,1,0:T(8,128)S(1)}, f32[256,256]{1,0:T(8,128)S(1)}, f32[2,128,128]{2,1,0:T(8,128)S(1)}, f32[2,128]{1,0:T(2,128)S(1)}) custom-call(s32[5]{0:T(128)S(1)} %stack.23.pos_ref, f32[2,128,128]{2,1,0:T(8,128)S(1)} %copy-done.2, f32[2,128,128]{2,1,0:T(8,128)S(1)} %collective-permute-done.map_one_ref, ...), custom_call_target="tpu_custom_call" | custom-call | tf_op jit(solution)/shard_map/pallas_call | solution.py:447
  27.7 1.3 %collective-permute-start.8 = (f32[2,128,128]{2,1,0:T(8,128)S(1)}, f32[2,128,128]{2,1,0:T(8,128)S(1)}, u32[]{:S(2)}, u32[]{:S(2)}) collective-permute-start(f32[2,128,128]{2,1,0:T(8,128)S(1)} %get-tuple-element.58.p_ref), channel_id=1, source_target_pairs={{12,0},{13,1},{14,2},{15,3},{28,16},{29,17},{30,18},{31,19},{44,32... | collective-permute-start | bytes 393224 | tf_op jit(solution)/shard_map/ppermute | solution.py:453
  29.0 1.3 %collective-permute-start.7 = (f32[2,128,128]{2,1,0:T(8,128)S(1)}, f32[2,128,128]{2,1,0:T(8,128)S(1)}, u32[]{:S(2)}, u32[]{:S(2)}) collective-permute-start(f32[2,128,128]{2,1,0:T(8,128)S(1)} %get-tuple-element.58.p_ref), channel_id=1, source_target_pairs={{12,4},{8,0},{13,5},{9,1},{14,6},{10,2},{15,7},{11,3},{28,20},{24,... | collective-permute-start | bytes 393224 | tf_op jit(solution)/shard_map/ppermute | solution.py:452
  30.3 1.3 %collective-permute-start.6 = (f32[2,128,128]{2,1,0:T(8,128)S(1)}, f32[2,128,128]{2,1,0:T(8,128)S(1)}, u32[]{:S(2)}, u32[]{:S(2)}) collective-permute-start(f32[2,128,128]{2,1,0:T(8,128)S(1)} %get-tuple-element.58.p_ref), channel_id=1, source_target_pairs={{12,8},{8,4},{4,0},{13,9},{9,5},{5,1},{14,10},{10,6},{6,2},{15,11}... | collective-permute-start | bytes 393224 | tf_op jit(solution)/shard_map/ppermute | solution.py:451
  31.6 2.9 %shard_map.122 = (f32[256,256]{1,0:T(8,128)S(1)}, f32[256,256]{1,0:T(8,128)S(1)}, f32[256,256]{1,0:T(8,128)S(1)}, f32[256,256]{1,0:T(8,128)S(1)}, f32[2,256]{1,0:T(2,128)S(1)}) custom-call(f32[2]{0:T(128)S(1)} %copy-done.5, f32[1,2,256]{2,1,0:T(2,128)S(1)} %copy-done.4, f32[2,128,128]{2,1,0:T(8,128)S(1)} %get-tuple-element.60.w_ref, ...), custom_call_target="tpu_custom_call" | custom-call | tf_op jit(solution)/shard_map/pallas_call | solution.py:455
  34.5 3.6 %collective-permute-done.8.three_ref = f32[2,128,128]{2,1,0:T(8,128)S(1)} collective-permute-done((f32[2,128,128]{2,1,0:T(8,128)S(1)}, f32[2,128,128]{2,1,0:T(8,128)S(1)}, u32[]{:S(2)}, u32[]{:S(2)}) %collective-permute-start.8) | collective-permute-done | bytes 131104 | tf_op jit(solution)/shard_map/ppermute | solution.py:453
  38.1 2.5 %shard_map.123 = (f32[960,256]{1,0:T(8,128)S(1)}, f32[1,2,256]{2,1,0:T(2,128)}) custom-call(s32[5]{0:T(128)S(1)} %stack.23.pos_ref, f32[2]{0:T(128)S(1)} %copy-done.5, f32[1,2,256]{2,1,0:T(2,128)S(1)} %copy-done.4, f32[2,128,128]{2,1,0:T(8,128)S(1)} %collective-permute-done.6.one_ref, f32[2,128,128]{2,1,0:T(8,128)S(1)} %collective-permute-done.7.two_ref, ...), custom_call_target="tpu_custom_call" | custom-call | tf_op jit(solution)/shard_map/pallas_call | solution.py:459
  40.6 1.4 %collective-permute-start.12 = (f32[960,256]{1,0:T(8,128)S(1)}, f32[960,256]{1,0:T(8,128)S(1)}, u32[]{:S(2)}, u32[]{:S(2)}) collective-permute-start(f32[960,256]{1,0:T(8,128)S(1)} %get-tuple-element.75.all_ref.own_ref), channel_id=1, source_target_pairs={{0,16},{16,0},{32,48},{48,32},{64,80},{80,64},{96,112},{112,96},{1... | collective-permute-start | bytes 2949128 | tf_op jit(solution)/shard_map/ppermute | solution.py:354
  42.0 1.5 %shard_map.124 = (f32[256,512]{1,0:T(8,128)S(1)}, f32[256,512]{1,0:T(8,128)S(1)}, f32[256,512]{1,0:T(8,128)S(1)}, f32[256,512]{1,0:T(8,128)S(1)}) custom-call(s32[5]{0:T(128)S(1)} %stack.23.pos_ref, bf16[3,2048,256]{2,1,0:T(8,128)(2,1)S(1)} %copy-done, f32[960,256]{1,0:T(8,128)S(1)} %get-tuple-element.75.all_ref.own_ref), custom_call_target="tpu_custom_call" | custom-call | tf_op jit(solution)/shard_map/pallas_call | solution.py:466
  43.6 0.6 collective-permute-done.12.other_ref
  44.2 1.5 %shard_map.125 = (f32[792,256]{1,0:T(8,128)S(1)}, f32[792,256]{1,0:T(8,128)S(1)}, f32[792,256]{1,0:T(8,128)S(1)}, f32[792,256]{1,0:T(8,128)S(1)}, f32[256,512]{1,0:T(8,128)S(1)}, /*index=5*/f32[256,512]{1,0:T(8,128)S(1)}) custom-call(s32[5]{0:T(128)S(1)} %stack.23.pos_ref, ...), custom_call_target="tpu_custom_call", output_to_operand_aliasing={{4}: (5, {}), {5}: (6, {})} | custom-call | tf_op jit(solution)/shard_map/pallas_call | solution.py:471
  45.8 3.1 %collective-permute-start.15 = (f32[792,256]{1,0:T(8,128)S(1)}, f32[792,256]{1,0:T(8,128)S(1)}, u32[]{:S(2)}, u32[]{:S(2)}) collective-permute-start(f32[792,256]{1,0:T(8,128)S(1)} %get-tuple-element.84), channel_id=1, source_target_pairs={{0,32},{4,36},{8,40},{12,44},{16,20},{20,24},{24,28},{28,16},{32,6... | collective-permute-start | bytes 2433032 | tf_op jit(solution)/shard_map/ppermute | solution.py:349
  48.9 2.1 %collective-permute-start.17 = (f32[792,256]{1,0:T(8,128)S(1)}, f32[792,256]{1,0:T(8,128)S(1)}, u32[]{:S(2)}, u32[]{:S(2)}) collective-permute-start(f32[792,256]{1,0:T(8,128)S(1)} %get-tuple-element.86), channel_id=1, source_target_pairs={{0,64},{4,68},{8,72},{12,76},{16,24},{20,28},{24,16},{28,20},{32,9... | collective-permute-start | bytes 2433032 | tf_op jit(solution)/shard_map/ppermute | solution.py:349
  50.9 1.6 %collective-permute-start.13 = (f32[256,512]{1,0:T(8,128)S(1)}, f32[256,512]{1,0:T(8,128)S(1)}, u32[]{:S(2)}, u32[]{:S(2)}) collective-permute-start(f32[256,512]{1,0:T(8,128)S(1)} %get-tuple-element.81), channel_id=1, source_target_pairs={{0,1},{1,2},{2,3},{3,0},{4,5},{5,6},{6,7},{7,4},{8,9},{9,10},{10,1... | collective-permute-start | bytes 1572872 | tf_op jit(solution)/shard_map/ppermute | solution.py:469
  52.6 2.1 %collective-permute-start.14 = (f32[256,512]{1,0:T(8,128)S(1)}, f32[256,512]{1,0:T(8,128)S(1)}, u32[]{:S(2)}, u32[]{:S(2)}) collective-permute-start(f32[256,512]{1,0:T(8,128)S(1)} %get-tuple-element.82), channel_id=1, source_target_pairs={{0,3},{1,0},{2,1},{3,2},{4,7},{5,4},{6,5},{7,6},{8,11},{9,8},{10,9... | collective-permute-start | bytes 1572872 | tf_op jit(solution)/shard_map/ppermute | solution.py:469
  54.7 12.1 %collective-permute-done.13.refs_0_ = f32[256,512]{1,0:T(8,128)S(1)} collective-permute-done((f32[256,512]{1,0:T(8,128)S(1)}, f32[256,512]{1,0:T(8,128)S(1)}, u32[]{:S(2)}, u32[]{:S(2)}) %collective-permute-start.13) | collective-permute-done | bytes 524320 | tf_op jit(solution)/shard_map/ppermute | solution.py:469
  66.8 1.3 %collective-permute-done.17.far_ref = f32[792,256]{1,0:T(8,128)S(1)} collective-permute-done((f32[792,256]{1,0:T(8,128)S(1)}, f32[792,256]{1,0:T(8,128)S(1)}, u32[]{:S(2)}, u32[]{:S(2)}) %collective-permute-start.17) | collective-permute-done | bytes 811040 | tf_op jit(solution)/shard_map/ppermute | solution.py:349
  68.1 0.2 shard_map.126.own_ref
  68.3 2.5 %collective-permute-start.20 = (f32[792,256]{1,0:T(8,128)S(1)}, f32[792,256]{1,0:T(8,128)S(1)}, u32[]{:S(2)}, u32[]{:S(2)}) collective-permute-start(f32[792,256]{1,0:T(8,128)S(1)} %shard_map.126.own_ref), channel_id=1, source_target_pairs={{0,8},{4,12},{8,0},{12,4},{16,80},{20,84},{24,88},{28,92},{32,40},... | collective-permute-start | bytes 2433032 | tf_op jit(solution)/shard_map/ppermute | solution.py:349
  70.8 0.9 collective-permute-start.19
  71.7 0.6 collective-permute-start.18
  72.3 3.6 %collective-permute-start.11 = (f32[256,512]{1,0:T(8,128)S(1)}, f32[256,512]{1,0:T(8,128)S(1)}, u32[]{:S(2)}, u32[]{:S(2)}) collective-permute-start(f32[256,512]{1,0:T(8,128)S(1)} %get-tuple-element.77), channel_id=1, source_target_pairs={{0,2},{1,3},{2,0},{3,1},{4,6},{5,7},{6,4},{7,5},{8,10},{9,11},{10,... | collective-permute-start | bytes 1572872 | tf_op jit(solution)/shard_map/ppermute | solution.py:469
  75.9 8.9 %collective-permute-done.11 = f32[256,512]{1,0:T(8,128)S(1)} collective-permute-done((f32[256,512]{1,0:T(8,128)S(1)}, f32[256,512]{1,0:T(8,128)S(1)}, u32[]{:S(2)}, u32[]{:S(2)}) %collective-permute-start.11) | collective-permute-done | bytes 524320 | tf_op jit(solution)/shard_map/ppermute | solution.py:469
  84.8 0.2 fusion.refs_0_
  85.1 5.0 %collective-permute-done.19.ahead_ref = f32[792,256]{1,0:T(8,128)S(1)} collective-permute-done((f32[792,256]{1,0:T(8,128)S(1)}, f32[792,256]{1,0:T(8,128)S(1)}, u32[]{:S(2)}, u32[]{:S(2)}) %collective-permute-start.19) | collective-permute-done | bytes 811040 | tf_op jit(solution)/shard_map/ppermute | solution.py:349
  90.1 0.2 shard_map.127.refs_0_
  90.3 2.4 %collective-permute-start.23 = (f32[792,256]{1,0:T(8,128)S(1)}, f32[792,256]{1,0:T(8,128)S(1)}, u32[]{:S(2)}, u32[]{:S(2)}) collective-permute-start(f32[792,256]{1,0:T(8,128)S(1)} %shard_map.127.refs_0_), channel_id=1, source_target_pairs={{0,64},{4,68},{8,72},{12,76},{16,24},{20,28},{24,16},{28,20},{32,9... | collective-permute-start | bytes 2433032 | tf_op jit(solution)/shard_map/ppermute | solution.py:349
  92.7 1.2 collective-permute-start.22
  93.9 1.5 %collective-permute-start.21 = (f32[792,256]{1,0:T(8,128)S(1)}, f32[792,256]{1,0:T(8,128)S(1)}, u32[]{:S(2)}, u32[]{:S(2)}) collective-permute-start(f32[792,256]{1,0:T(8,128)S(1)} %shard_map.127.refs_0_), channel_id=1, source_target_pairs={{0,96},{4,100},{8,104},{12,108},{16,28},{20,16},{24,20},{28,24},{3... | collective-permute-start | bytes 2433032 | tf_op jit(solution)/shard_map/ppermute | solution.py:349
  95.4 7.9 %collective-permute-done.23.refs_1_.refs_3_ = f32[792,256]{1,0:T(8,128)S(1)} collective-permute-done((f32[792,256]{1,0:T(8,128)S(1)}, f32[792,256]{1,0:T(8,128)S(1)}, u32[]{:S(2)}, u32[]{:S(2)}) %collective-permute-start.23) | collective-permute-done | bytes 811040 | tf_op jit(solution)/shard_map/ppermute | solution.py:349
  103.3 3.3 %collective-permute-start.27 = (f32[792,256]{1,0:T(8,128)S(1)}, f32[792,256]{1,0:T(8,128)S(1)}, u32[]{:S(2)}, u32[]{:S(2)}) collective-permute-start(f32[792,256]{1,0:T(8,128)S(1)} %collective-permute-done.23.refs_1_.refs_3_), channel_id=1, source_target_pairs={{0,16},{16,0},{32,48},{48,32},{64,80},{80,64},{96,112},{112,96},{1... | collective-permute-start | bytes 2433032 | tf_op jit(solution)/shard_map/ppermute | solution.py:354
  106.6 1.7 %shard_map.128 = (f32[3,2048,256]{2,1,0:T(8,128)}, f32[792,256]{1,0:T(8,128)S(1)}) custom-call(s32[5]{0:T(128)S(1)} %stack.23.pos_ref, f32[792,256]{1,0:T(8,128)S(1)} %shard_map.127.refs_0_, f32[792,256]{1,0:T(8,128)S(1)} %collective-permute-done.23.refs_1_.refs_3_), custom_call_target="tpu_custom_call" | custom-call | tf_op jit(solution)/shard_map/pallas_call | solution.py:487
  108.4 3.5 %collective-permute-done.22.refs_1_.refs_2_ = f32[792,256]{1,0:T(8,128)S(1)} collective-permute-done((f32[792,256]{1,0:T(8,128)S(1)}, f32[792,256]{1,0:T(8,128)S(1)}, u32[]{:S(2)}, u32[]{:S(2)}) %collective-permute-start.22) | collective-permute-done | bytes 811040 | tf_op jit(solution)/shard_map/ppermute | solution.py:349
  112.0 3.2 %collective-permute-start.26 = (f32[792,256]{1,0:T(8,128)S(1)}, f32[792,256]{1,0:T(8,128)S(1)}, u32[]{:S(2)}, u32[]{:S(2)}) collective-permute-start(f32[792,256]{1,0:T(8,128)S(1)} %collective-permute-done.22.refs_1_.refs_2_), channel_id=1, source_target_pairs={{0,16},{16,0},{32,48},{48,32},{64,80},{80,64},{96,112},{112,96},{1... | collective-permute-start | bytes 2433032 | tf_op jit(solution)/shard_map/ppermute | solution.py:354
  115.2 2.3 %shard_map.129.refs_8_ = f32[3,2048,256]{2,1,0:T(8,128)} custom-call(s32[5]{0:T(128)S(1)} %stack.23.pos_ref, f32[792,256]{1,0:T(8,128)S(1)} %collective-permute-done.21.refs_0_.refs_1_, f32[792,256]{1,0:T(8,128)S(1)} %collective-permute-done.22.refs_1_.refs_2_, ...), custom_call_target="tpu_custom_call", output_to_operand_aliasing={{}: (5, {})} | custom-call | tf_op jit(solution)/shard_map/pallas_call | solution.py:487
  117.5 0.8 collective-permute-done.25.refs_5_
  118.3 2.4 %shard_map.130 = (f32[3,2048,256]{2,1,0:T(8,128)}, f32[2,128,128]{2,1,0:T(8,128)}, f32[2,128]{1,0:T(2,128)}, f32[2]{0:T(128)}) custom-call(s32[5]{0:T(128)S(1)} %stack.23.pos_ref, f32[792,256]{1,0:T(8,128)S(1)} %shard_map.127.refs_0_, f32[792,256]{1,0:T(8,128)S(1)} %collective-permute-done.21.refs_0_.refs_1_, ...), custom_call_target="tpu_custom_call", output_to_operand_aliasing={{0}: (9, {})} | custom-call | tf_op jit(solution)/shard_map/pallas_call | solution.py:503
  (37 shorter events, 0.3 us)
Async XLA Ops:
  0.6 18.3 %copy-start.4 = (f32[1,2,256]{2,1,0:T(2,128)S(1)}, f32[1,2,256]{2,1,0:T(2,128)}, u32[]{:S(2)}) copy-start(f32[1,2,256]{2,1,0:T(2,128)} %gate_ref.7) | copy-start | bytes 6148
  0.6 18.3 %copy-start.5 = (f32[2]{0:T(128)S(1)}, f32[2]{0:T(128)}, u32[]{:S(2)}) copy-start(f32[2]{0:T(128)} %base_ref.7) | copy-start | bytes 28
  0.8 25.1 %copy-start.2 = (f32[2,128,128]{2,1,0:T(8,128)S(1)}, f32[2,128,128]{2,1,0:T(8,128)}, u32[]{:S(2)}) copy-start(f32[2,128,128]{2,1,0:T(8,128)} %init_ref.3) | copy-start | bytes 393220
  0.8 25.1 %copy-start.3 = (bf16[1,256,256]{2,1,0:T(8,128)(2,1)S(1)}, bf16[1,256,256]{2,1,0:T(8,128)(2,1)}, u32[]{:S(2)}) copy-start(bf16[1,256,256]{2,1,0:T(8,128)(2,1)} %up_ref.3) | copy-start | bytes 393220
  0.8 25.2 %copy-start.6 = (f32[2,128]{1,0:T(2,128)S(1)}, f32[2,128]{1,0:T(2,128)}, u32[]{:S(2)}) copy-start(f32[2,128]{1,0:T(2,128)} %gain_ref.1) | copy-start | bytes 3076
  6.3 11.3 %collective-permute-start.5 = (f32[256,1024]{1,0:T(8,128)S(1)}, f32[256,1024]{1,0:T(8,128)S(1)}, u32[]{:S(2)}, u32[]{:S(2)}) collective-permute-start(f32[256,1024]{1,0:T(8,128)S(1)} %get-tuple-element.57), channel_id=1, source_target_pairs={{0,16},{16,0},{32,48},{48,32},{64,80},{80,64},{96,112},{112,96},{1... | collective-permute-start | bytes 3145736 | tf_op jit(solution)/shard_map/ppermute | solution.py:354
  7.8 15.4 %collective-permute-start.3 = (f32[2,128,128]{2,1,0:T(8,128)S(1)}, f32[2,128,128]{2,1,0:T(8,128)S(1)}, u32[]{:S(2)}, u32[]{:S(2)}) collective-permute-start(f32[2,128,128]{2,1,0:T(8,128)S(1)} %get-tuple-element.51), channel_id=1, source_target_pairs={{4,12},{5,13},{6,14},{7,15},{20,28},{21,29},{22,30},{23,31},{36,44... | collective-permute-start | bytes 393224 | tf_op jit(solution)/shard_map/ppermute | solution.py:430
  8.5 16.1 %collective-permute-start.1 = (f32[2,128,128]{2,1,0:T(8,128)S(1)}, f32[2,128,128]{2,1,0:T(8,128)S(1)}, u32[]{:S(2)}, u32[]{:S(2)}) collective-permute-start(f32[2,128,128]{2,1,0:T(8,128)S(1)} %get-tuple-element.51), channel_id=1, source_target_pairs={{4,8},{8,12},{5,9},{9,13},{6,10},{10,14},{7,11},{11,15},{20,24},{2... | collective-permute-start | bytes 393224 | tf_op jit(solution)/shard_map/ppermute | solution.py:428
  9.2 16.7 %collective-permute-start.4 = (f32[2,128,128]{2,1,0:T(8,128)S(1)}, f32[2,128,128]{2,1,0:T(8,128)S(1)}, u32[]{:S(2)}, u32[]{:S(2)}) collective-permute-start(f32[2,128,128]{2,1,0:T(8,128)S(1)} %get-tuple-element.50), channel_id=1, source_target_pairs={{0,12},{1,13},{2,14},{3,15},{16,28},{17,29},{18,30},{19,31},{32,44... | collective-permute-start | bytes 393224 | tf_op jit(solution)/shard_map/ppermute | solution.py:431
  15.2 10.7 %collective-permute-start.2 = (f32[2,128,128]{2,1,0:T(8,128)S(1)}, f32[2,128,128]{2,1,0:T(8,128)S(1)}, u32[]{:S(2)}, u32[]{:S(2)}) collective-permute-start(f32[2,128,128]{2,1,0:T(8,128)S(1)} %get-tuple-element.50), channel_id=1, source_target_pairs={{0,8},{4,12},{1,9},{5,13},{2,10},{6,14},{3,11},{7,15},{16,24},{20,... | collective-permute-start | bytes 393224 | tf_op jit(solution)/shard_map/ppermute | solution.py:429
  17.6 8.2 %collective-permute-start = (f32[2,128,128]{2,1,0:T(8,128)S(1)}, f32[2,128,128]{2,1,0:T(8,128)S(1)}, u32[]{:S(2)}, u32[]{:S(2)}) collective-permute-start(f32[2,128,128]{2,1,0:T(8,128)S(1)} %get-tuple-element.50), channel_id=1, source_target_pairs={{0,4},{4,8},{8,12},{1,5},{5,9},{9,13},{2,6},{6,10},{10,14},{3,7},{... | collective-permute-start | bytes 393224 | tf_op jit(solution)/shard_map/ppermute | solution.py:427
  19.0 23.1 %copy-start = (bf16[3,2048,256]{2,1,0:T(8,128)(2,1)S(1)}, bf16[3,2048,256]{2,1,0:T(8,128)(2,1)}, u32[]{:S(2)}) copy-start(bf16[3,2048,256]{2,1,0:T(8,128)(2,1)} %w_ref.1) | copy-start | bytes 9437188
  23.3 11.2 %collective-permute-start.10 = (f32[2,128,128]{2,1,0:T(8,128)S(1)}, f32[2,128,128]{2,1,0:T(8,128)S(1)}, u32[]{:S(2)}, u32[]{:S(2)}) collective-permute-start(f32[2,128,128]{2,1,0:T(8,128)S(1)} %get-tuple-element.59.d_ref), channel_id=1, source_target_pairs={{8,0},{9,1},{10,2},{11,3},{24,16},{25,17},{26,18},{27,19},{40,32},... | collective-permute-start | bytes 393224 | tf_op jit(solution)/shard_map/ppermute | solution.py:433
  24.6 9.9 %collective-permute-start.9 = (f32[2,128,128]{2,1,0:T(8,128)S(1)}, f32[2,128,128]{2,1,0:T(8,128)S(1)}, u32[]{:S(2)}, u32[]{:S(2)}) collective-permute-start(f32[2,128,128]{2,1,0:T(8,128)S(1)} %get-tuple-element.59.d_ref), channel_id=1, source_target_pairs={{4,0},{8,4},{5,1},{9,5},{6,2},{10,6},{7,3},{11,7},{20,16},{24,20},... | collective-permute-start | bytes 393224 | tf_op jit(solution)/shard_map/ppermute | solution.py:432
  27.7 10.4 %collective-permute-start.8 = (f32[2,128,128]{2,1,0:T(8,128)S(1)}, f32[2,128,128]{2,1,0:T(8,128)S(1)}, u32[]{:S(2)}, u32[]{:S(2)}) collective-permute-start(f32[2,128,128]{2,1,0:T(8,128)S(1)} %get-tuple-element.58.p_ref), channel_id=1, source_target_pairs={{12,0},{13,1},{14,2},{15,3},{28,16},{29,17},{30,18},{31,19},{44,32... | collective-permute-start | bytes 393224 | tf_op jit(solution)/shard_map/ppermute | solution.py:453
  29.0 9.1 %collective-permute-start.7 = (f32[2,128,128]{2,1,0:T(8,128)S(1)}, f32[2,128,128]{2,1,0:T(8,128)S(1)}, u32[]{:S(2)}, u32[]{:S(2)}) collective-permute-start(f32[2,128,128]{2,1,0:T(8,128)S(1)} %get-tuple-element.58.p_ref), channel_id=1, source_target_pairs={{12,4},{8,0},{13,5},{9,1},{14,6},{10,2},{15,7},{11,3},{28,20},{24,... | collective-permute-start | bytes 393224 | tf_op jit(solution)/shard_map/ppermute | solution.py:452
  30.3 7.8 %collective-permute-start.6 = (f32[2,128,128]{2,1,0:T(8,128)S(1)}, f32[2,128,128]{2,1,0:T(8,128)S(1)}, u32[]{:S(2)}, u32[]{:S(2)}) collective-permute-start(f32[2,128,128]{2,1,0:T(8,128)S(1)} %get-tuple-element.58.p_ref), channel_id=1, source_target_pairs={{12,8},{8,4},{4,0},{13,9},{9,5},{5,1},{14,10},{10,6},{6,2},{15,11}... | collective-permute-start | bytes 393224 | tf_op jit(solution)/shard_map/ppermute | solution.py:451
  40.6 3.6 %collective-permute-start.12 = (f32[960,256]{1,0:T(8,128)S(1)}, f32[960,256]{1,0:T(8,128)S(1)}, u32[]{:S(2)}, u32[]{:S(2)}) collective-permute-start(f32[960,256]{1,0:T(8,128)S(1)} %get-tuple-element.75.all_ref.own_ref), channel_id=1, source_target_pairs={{0,16},{16,0},{32,48},{48,32},{64,80},{80,64},{96,112},{112,96},{1... | collective-permute-start | bytes 2949128 | tf_op jit(solution)/shard_map/ppermute | solution.py:354
  45.8 21.0 %collective-permute-start.15 = (f32[792,256]{1,0:T(8,128)S(1)}, f32[792,256]{1,0:T(8,128)S(1)}, u32[]{:S(2)}, u32[]{:S(2)}) collective-permute-start(f32[792,256]{1,0:T(8,128)S(1)} %get-tuple-element.84), channel_id=1, source_target_pairs={{0,32},{4,36},{8,40},{12,44},{16,20},{20,24},{24,28},{28,16},{32,6... | collective-permute-start | bytes 2433032 | tf_op jit(solution)/shard_map/ppermute | solution.py:349
  48.9 17.9 %collective-permute-start.16 = (f32[792,256]{1,0:T(8,128)S(1)}, f32[792,256]{1,0:T(8,128)S(1)}, u32[]{:S(2)}, u32[]{:S(2)}) collective-permute-start(f32[792,256]{1,0:T(8,128)S(1)} %get-tuple-element.85), channel_id=1, source_target_pairs={{0,96},{4,100},{8,104},{12,108},{16,28},{20,16},{24,20},{28,24},{3... | collective-permute-start | bytes 2433032 | tf_op jit(solution)/shard_map/ppermute | solution.py:349
  48.9 19.2 %collective-permute-start.17 = (f32[792,256]{1,0:T(8,128)S(1)}, f32[792,256]{1,0:T(8,128)S(1)}, u32[]{:S(2)}, u32[]{:S(2)}) collective-permute-start(f32[792,256]{1,0:T(8,128)S(1)} %get-tuple-element.86), channel_id=1, source_target_pairs={{0,64},{4,68},{8,72},{12,76},{16,24},{20,28},{24,16},{28,20},{32,9... | collective-permute-start | bytes 2433032 | tf_op jit(solution)/shard_map/ppermute | solution.py:349
  50.9 15.8 %collective-permute-start.13 = (f32[256,512]{1,0:T(8,128)S(1)}, f32[256,512]{1,0:T(8,128)S(1)}, u32[]{:S(2)}, u32[]{:S(2)}) collective-permute-start(f32[256,512]{1,0:T(8,128)S(1)} %get-tuple-element.81), channel_id=1, source_target_pairs={{0,1},{1,2},{2,3},{3,0},{4,5},{5,6},{6,7},{7,4},{8,9},{9,10},{10,1... | collective-permute-start | bytes 1572872 | tf_op jit(solution)/shard_map/ppermute | solution.py:469
  52.6 14.2 %collective-permute-start.14 = (f32[256,512]{1,0:T(8,128)S(1)}, f32[256,512]{1,0:T(8,128)S(1)}, u32[]{:S(2)}, u32[]{:S(2)}) collective-permute-start(f32[256,512]{1,0:T(8,128)S(1)} %get-tuple-element.82), channel_id=1, source_target_pairs={{0,3},{1,0},{2,1},{3,2},{4,7},{5,4},{6,5},{7,6},{8,11},{9,8},{10,9... | collective-permute-start | bytes 1572872 | tf_op jit(solution)/shard_map/ppermute | solution.py:469
  68.3 16.8 %collective-permute-start.20 = (f32[792,256]{1,0:T(8,128)S(1)}, f32[792,256]{1,0:T(8,128)S(1)}, u32[]{:S(2)}, u32[]{:S(2)}) collective-permute-start(f32[792,256]{1,0:T(8,128)S(1)} %shard_map.126.own_ref), channel_id=1, source_target_pairs={{0,8},{4,12},{8,0},{12,4},{16,80},{20,84},{24,88},{28,92},{32,40},... | collective-permute-start | bytes 2433032 | tf_op jit(solution)/shard_map/ppermute | solution.py:349
  70.8 19.3 %collective-permute-start.19 = (f32[792,256]{1,0:T(8,128)S(1)}, f32[792,256]{1,0:T(8,128)S(1)}, u32[]{:S(2)}, u32[]{:S(2)}) collective-permute-start(f32[792,256]{1,0:T(8,128)S(1)} %shard_map.126.own_ref), channel_id=1, source_target_pairs={{0,12},{4,0},{8,4},{12,8},{16,112},{20,116},{24,120},{28,124},{32,... | collective-permute-start | bytes 2433032 | tf_op jit(solution)/shard_map/ppermute | solution.py:349
  71.7 18.4 %collective-permute-start.18 = (f32[792,256]{1,0:T(8,128)S(1)}, f32[792,256]{1,0:T(8,128)S(1)}, u32[]{:S(2)}, u32[]{:S(2)}) collective-permute-start(f32[792,256]{1,0:T(8,128)S(1)} %shard_map.126.own_ref), channel_id=1, source_target_pairs={{0,4},{4,8},{8,12},{12,0},{16,48},{20,52},{24,56},{28,60},{32,36},... | collective-permute-start | bytes 2433032 | tf_op jit(solution)/shard_map/ppermute | solution.py:349
  72.3 12.5 %collective-permute-start.11 = (f32[256,512]{1,0:T(8,128)S(1)}, f32[256,512]{1,0:T(8,128)S(1)}, u32[]{:S(2)}, u32[]{:S(2)}) collective-permute-start(f32[256,512]{1,0:T(8,128)S(1)} %get-tuple-element.77), channel_id=1, source_target_pairs={{0,2},{1,3},{2,0},{3,1},{4,6},{5,7},{6,4},{7,5},{8,10},{9,11},{10,... | collective-permute-start | bytes 1572872 | tf_op jit(solution)/shard_map/ppermute | solution.py:469
  85.0 32.5 %copy-start.1 = (bf16[1,256,512]{2,1,0:T(8,128)(2,1)}, bf16[1,256,512]{2,1,0:T(8,128)(2,1)S(1)}, u32[]{:S(2)}) copy-start(bf16[1,256,512]{2,1,0:T(8,128)(2,1)S(1)} %fusion.refs_0_) | copy-start | bytes 786436
  90.3 13.0 %collective-permute-start.23 = (f32[792,256]{1,0:T(8,128)S(1)}, f32[792,256]{1,0:T(8,128)S(1)}, u32[]{:S(2)}, u32[]{:S(2)}) collective-permute-start(f32[792,256]{1,0:T(8,128)S(1)} %shard_map.127.refs_0_), channel_id=1, source_target_pairs={{0,64},{4,68},{8,72},{12,76},{16,24},{20,28},{24,16},{28,20},{32,9... | collective-permute-start | bytes 2433032 | tf_op jit(solution)/shard_map/ppermute | solution.py:349
  92.7 19.2 %collective-permute-start.22 = (f32[792,256]{1,0:T(8,128)S(1)}, f32[792,256]{1,0:T(8,128)S(1)}, u32[]{:S(2)}, u32[]{:S(2)}) collective-permute-start(f32[792,256]{1,0:T(8,128)S(1)} %shard_map.127.refs_0_), channel_id=1, source_target_pairs={{0,32},{4,36},{8,40},{12,44},{16,20},{20,24},{24,28},{28,16},{32,6... | collective-permute-start | bytes 2433032 | tf_op jit(solution)/shard_map/ppermute | solution.py:349
  93.9 21.3 %collective-permute-start.21 = (f32[792,256]{1,0:T(8,128)S(1)}, f32[792,256]{1,0:T(8,128)S(1)}, u32[]{:S(2)}, u32[]{:S(2)}) collective-permute-start(f32[792,256]{1,0:T(8,128)S(1)} %shard_map.127.refs_0_), channel_id=1, source_target_pairs={{0,96},{4,100},{8,104},{12,108},{16,28},{20,16},{24,20},{28,24},{3... | collective-permute-start | bytes 2433032 | tf_op jit(solution)/shard_map/ppermute | solution.py:349
  103.3 11.9 %collective-permute-start.27 = (f32[792,256]{1,0:T(8,128)S(1)}, f32[792,256]{1,0:T(8,128)S(1)}, u32[]{:S(2)}, u32[]{:S(2)}) collective-permute-start(f32[792,256]{1,0:T(8,128)S(1)} %collective-permute-done.23.refs_1_.refs_3_), channel_id=1, source_target_pairs={{0,16},{16,0},{32,48},{48,32},{64,80},{80,64},{96,112},{112,96},{1... | collective-permute-start | bytes 2433032 | tf_op jit(solution)/shard_map/ppermute | solution.py:354
  108.3 6.9 %collective-permute-start.24 = (f32[792,256]{1,0:T(8,128)S(1)}, f32[792,256]{1,0:T(8,128)S(1)}, u32[]{:S(2)}, u32[]{:S(2)}) collective-permute-start(f32[792,256]{1,0:T(8,128)S(1)} %get-tuple-element.87), channel_id=1, source_target_pairs={{0,16},{16,0},{32,48},{48,32},{64,80},{80,64},{96,112},{112,96},{1... | collective-permute-start | bytes 2433032 | tf_op jit(solution)/shard_map/ppermute | solution.py:354
  112.0 5.6 %collective-permute-start.26 = (f32[792,256]{1,0:T(8,128)S(1)}, f32[792,256]{1,0:T(8,128)S(1)}, u32[]{:S(2)}, u32[]{:S(2)}) collective-permute-start(f32[792,256]{1,0:T(8,128)S(1)} %collective-permute-done.22.refs_1_.refs_2_), channel_id=1, source_target_pairs={{0,16},{16,0},{32,48},{48,32},{64,80},{80,64},{96,112},{112,96},{1... | collective-permute-start | bytes 2433032 | tf_op jit(solution)/shard_map/ppermute | solution.py:354
  115.2 3.1 %collective-permute-start.25 = (f32[792,256]{1,0:T(8,128)S(1)}, f32[792,256]{1,0:T(8,128)S(1)}, u32[]{:S(2)}, u32[]{:S(2)}) collective-permute-start(f32[792,256]{1,0:T(8,128)S(1)} %collective-permute-done.21.refs_0_.refs_1_), channel_id=1, source_target_pairs={{0,16},{16,0},{32,48},{48,32},{64,80},{80,64},{96,112},{112,96},{1... | collective-permute-start | bytes 2433032 | tf_op jit(solution)/shard_map/ppermute | solution.py:354

commit v13 on v10

--- a/solution.py
+++ b/solution.py
@@ -259,10 +259,11 @@
     out_ref[...] = other_ref[...].T.astype(BF)
 
 
-def product_kernel(pos_ref, tokt_ref, other_tokt_ref, own_ref, other_ref, *refs):
-    out_refs = refs[2 : 2 + RING]
+def product_kernel(pos_ref, tokt_ref, other_tokt_ref, own_ref, other_ref, *refs, turns, passed):
+    skipped = passed + 1 if passed else 0
+    out_refs = refs[skipped : skipped + len(turns)]
     n = tokt_ref.shape[1]
-    for turn, out_ref in zip(TURNS, out_refs):
+    for turn, out_ref in zip(turns, out_refs):
         at = (pos_ref[1] + turn) & (RING - 1)
         rows = pl.ds(pl.multiple_of(at * CHUNK, CHUNK), CHUNK)
         for m in range(3):
@@ -477,10 +478,15 @@
     def along_head(terms, turn):
         return lax.ppermute(terms, "head", [(i, (i + turn) % RING) for i in range(RING)])
 
-    *chunks, near_one, near_two = whole(
-        product_kernel, (chunk,) * RING + (quarter,) * 2, [SM] + [VM] * 6, {5: RING, 6: RING + 1}
-    )(pos, tokt, other_tokt, grads, swap(grads), *quarters[1:3])
-    own, away = chunks[0], round_turn(chunks[1:], True)
+    given = (pos, tokt, other_tokt, grads, swap(grads))
+    far_chunk = whole(
+        functools.partial(product_kernel, turns=(2,), passed=0), chunk, [SM] + [VM] * 4
+    )(*given)
+    own, one_chunk, three_chunk, near_one, near_two = whole(
+        functools.partial(product_kernel, turns=(0, 1, 3), passed=2),
+        (chunk,) * 3 + (quarter,) * 2, [SM] + [VM] * 6 + [anywhere], {5: 3, 6: 4},
+    )(*given, *quarters[1:3], far_chunk)
+    away = round_turn([one_chunk, three_chunk, far_chunk], True)
     from_back, from_ahead, from_far = along_head(near_one, 1), along_head(near_two, 3), along_head(quarters[3], 2)
 
     part_sum = whole(sum_kernel, chunk, [VM] * 4 + [anywhere] * 2)(own, *away, from_back, from_ahead)

time: 117 us -> 117 us (level)
  transfers between devices with their start and end apart: 27 -> 27, of which waited for: 10 -> 10; matrix products, arithmetic and copies ran while one was open for 0% -> 0% of each run, Pallas kernels for 12% -> 13%
where the time goes in v13:
time: 117 us
  starting transfers between devices  44.2 us (38%)
  waiting for transfers between devices  43.8 us (37%)
  Pallas kernels  27.4 us (23%)
  between operations  1.18 us (1%)
    ppermute x3, waiting for transfers between devices, along_head(): lax.ppermute(terms, 'head', [(i, (i + turn) % RING) for i in range(RING)])  21.3 us
    ppermute x9, waiting for transfers between devices, round_turn(): lax.ppermute(chunk, ('dp', 'ctx'), moves(first, turn))  17.4 us
    ppermute x9, starting transfers between devices, round_turn(): lax.ppermute(chunk, ('dp', 'ctx'), moves(first, turn))  14.2 us
    ppermute x6, starting transfers between devices, swap(): return lax.ppermute(value, 'dp', [(i, i ^ 1) for i in range(2 * RING)])  10.7 us
    ppermute x3, starting transfers between devices, along_head(): lax.ppermute(terms, 'head', [(i, (i + turn) % RING) for i in range(RING)])  7.35 us
    pallas_call x1, Pallas kernels, body(): pl.pallas_call(maps_kernel, grid=(1,), out_shape=(wide_f32, wide_f32, vme...  5.56 us
    pallas_call x2, Pallas kernels, place(): pl.pallas_call(functools.partial(place_kernel, which=which, passed=passed...  4.03 us
    pallas_call x1, Pallas kernels, body(): pl.pallas_call(reach_kernel, grid=(1,), out_shape=(wide_f32, square, wide...  3.89 us
  transfers between devices with their start and end apart: 27, of which 10 were waited for; matrix products, arithmetic and copies ran while one was open for 0% of the time, Pallas kernels for 13%

profile of v13, /device:TPU:1, one launch (start us, length us, event | category | flops | bytes accessed | tf_op | source)
XLA Modules:
  0.0 116.9 jit_solution(9048144656659110841)
XLA Ops:
  0.8 5.6 %shard_map.118 = (f32[256,256]{1,0:T(8,128)S(1)}, f32[256,256]{1,0:T(8,128)S(1)}, f32[2,256,128]{2,1,0:T(8,128)S(1)}, f32[2,256,256]{2,1,0:T(8,128)S(1)}, f32[2,...) custom-call(s32[5]{0:T(128)S(1)} %stack.23.pos_ref, ...), custom_call_target="tpu_custom_call" | custom-call | tf_op jit(solution)/shard_map/pallas_call | solution.py:423
  6.3 1.5 %collective-permute-start.4 = (f32[256,1024]{1,0:T(8,128)S(1)}, f32[256,1024]{1,0:T(8,128)S(1)}, u32[]{:S(2)}, u32[]{:S(2)}) collective-permute-start(f32[256,1024]{1,0:T(8,128)S(1)} %get-tuple-element.57), channel_id=1, source_target_pairs={{0,16},{16,0},{32,48},{48,32},{64,80},{80,64},{96,112},{112,96},{1... | collective-permute-start | bytes 3145736 | tf_op jit(solution)/shard_map/ppermute | solution.py:362
  7.8 3.3 %collective-permute-start = (f32[2,128,128]{2,1,0:T(8,128)S(1)}, f32[2,128,128]{2,1,0:T(8,128)S(1)}, u32[]{:S(2)}, u32[]{:S(2)}) collective-permute-start(f32[2,128,128]{2,1,0:T(8,128)S(1)} %get-tuple-element.49), channel_id=1, source_target_pairs={{0,4},{8,12},{1,5},{9,13},{2,6},{10,14},{3,7},{11,15},{16,20},{24,... | collective-permute-start | bytes 393224 | tf_op jit(solution)/shard_map/ppermute | solution.py:435
  11.1 1.3 %collective-permute-start.3 = (f32[2,128,128]{2,1,0:T(8,128)S(1)}, f32[2,128,128]{2,1,0:T(8,128)S(1)}, u32[]{:S(2)}, u32[]{:S(2)}) collective-permute-start(f32[2,128,128]{2,1,0:T(8,128)S(1)} %get-tuple-element.50.d_ref), channel_id=1, source_target_pairs={{8,12},{4,0},{9,13},{5,1},{10,14},{6,2},{11,15},{7,3},{24,28},{20,... | collective-permute-start | bytes 393224 | tf_op jit(solution)/shard_map/ppermute | solution.py:436
  12.4 3.9 %shard_map.119 = (f32[256,256]{1,0:T(8,128)S(1)}, f32[2,256,256]{2,1,0:T(8,128)S(1)}, f32[256,256]{1,0:T(8,128)S(1)}, f32[256,256]{1,0:T(8,128)S(1)}, f32[256,25...) custom-call(s32[5]{0:T(128)S(1)} %stack.23.pos_ref, f32[2]{0:T(128)S(1)} %copy-done.5, ...), custom_call_target="tpu_custom_call" | custom-call | tf_op jit(solution)/shard_map/pallas_call | solution.py:441
  16.4 0.2 shard_map.120
  16.6 0.8 collective-permute-start.2
  17.4 0.7 collective-permute-start.1
  18.1 1.3 %collective-permute-start.9 = (f32[2,128,128]{2,1,0:T(8,128)S(1)}, f32[2,128,128]{2,1,0:T(8,128)S(1)}, u32[]{:S(2)}, u32[]{:S(2)}) collective-permute-start(f32[2,128,128]{2,1,0:T(8,128)S(1)} %get-tuple-element.50.d_ref), channel_id=1, source_target_pairs={{8,0},{9,1},{10,2},{11,3},{24,16},{25,17},{26,18},{27,19},{40,32},... | collective-permute-start | bytes 393224 | tf_op jit(solution)/shard_map/ppermute | solution.py:438
  19.4 0.7 collective-permute-start.8
  20.0 0.2 shard_map.121.after_ref.other_tokt_ref
  20.3 1.5 %shard_map.122 = (f32[2,128,128]{2,1,0:T(8,128)S(1)}, f32[256,256]{1,0:T(8,128)S(1)}, f32[2,128,128]{2,1,0:T(8,128)S(1)}, f32[2,128]{1,0:T(2,128)S(1)}) custom-call(s32[5]{0:T(128)S(1)} %stack.23.pos_ref, f32[2,128,128]{2,1,0:T(8,128)S(1)} %copy-done.2, f32[2,128,128]{2,1,0:T(8,128)S(1)} %collective-permute-done.w_ref.near_ref, ...), custom_call_target="tpu_custom_call" | custom-call | tf_op jit(solution)/shard_map/pallas_call | solution.py:457
  21.9 1.3 %collective-permute-start.7 = (f32[2,128,128]{2,1,0:T(8,128)S(1)}, f32[2,128,128]{2,1,0:T(8,128)S(1)}, u32[]{:S(2)}, u32[]{:S(2)}) collective-permute-start(f32[2,128,128]{2,1,0:T(8,128)S(1)} %get-tuple-element.58.p_ref), channel_id=1, source_target_pairs={{12,0},{13,1},{14,2},{15,3},{28,16},{29,17},{30,18},{31,19},{44,32... | collective-permute-start | bytes 393224 | tf_op jit(solution)/shard_map/ppermute | solution.py:463
  23.2 1.3 %collective-permute-start.6 = (f32[2,128,128]{2,1,0:T(8,128)S(1)}, f32[2,128,128]{2,1,0:T(8,128)S(1)}, u32[]{:S(2)}, u32[]{:S(2)}) collective-permute-start(f32[2,128,128]{2,1,0:T(8,128)S(1)} %get-tuple-element.58.p_ref), channel_id=1, source_target_pairs={{12,4},{8,0},{13,5},{9,1},{14,6},{10,2},{15,7},{11,3},{28,20},{24,... | collective-permute-start | bytes 393224 | tf_op jit(solution)/shard_map/ppermute | solution.py:462
  24.5 1.3 %collective-permute-start.5 = (f32[2,128,128]{2,1,0:T(8,128)S(1)}, f32[2,128,128]{2,1,0:T(8,128)S(1)}, u32[]{:S(2)}, u32[]{:S(2)}) collective-permute-start(f32[2,128,128]{2,1,0:T(8,128)S(1)} %get-tuple-element.58.p_ref), channel_id=1, source_target_pairs={{12,8},{8,4},{4,0},{13,9},{9,5},{5,1},{14,10},{10,6},{6,2},{15,11}... | collective-permute-start | bytes 393224 | tf_op jit(solution)/shard_map/ppermute | solution.py:461
  25.8 2.9 %shard_map.123 = (f32[256,256]{1,0:T(8,128)S(1)}, f32[256,256]{1,0:T(8,128)S(1)}, f32[256,256]{1,0:T(8,128)S(1)}, f32[256,256]{1,0:T(8,128)S(1)}, f32[2,256]{1,0:T(2,128)S(1)}) custom-call(f32[2]{0:T(128)S(1)} %copy-done.5, f32[1,2,256]{2,1,0:T(2,128)S(1)} %copy-done.4, f32[2,128,128]{2,1,0:T(8,128)S(1)} %get-tuple-element.59.w_ref, ...), custom_call_target="tpu_custom_call" | custom-call | tf_op jit(solution)/shard_map/pallas_call | solution.py:465
  28.6 1.8 %collective-permute-done.7.three_ref = f32[2,128,128]{2,1,0:T(8,128)S(1)} collective-permute-done((f32[2,128,128]{2,1,0:T(8,128)S(1)}, f32[2,128,128]{2,1,0:T(8,128)S(1)}, u32[]{:S(2)}, u32[]{:S(2)}) %collective-permute-start.7) | collective-permute-done | bytes 131104 | tf_op jit(solution)/shard_map/ppermute | solution.py:463
  30.4 2.0 %collective-permute-done.6.two_ref = f32[2,128,128]{2,1,0:T(8,128)S(1)} collective-permute-done((f32[2,128,128]{2,1,0:T(8,128)S(1)}, f32[2,128,128]{2,1,0:T(8,128)S(1)}, u32[]{:S(2)}, u32[]{:S(2)}) %collective-permute-start.6) | collective-permute-done | bytes 131104 | tf_op jit(solution)/shard_map/ppermute | solution.py:462
  32.4 2.5 %shard_map.124 = (f32[960,256]{1,0:T(8,128)S(1)}, f32[1,2,256]{2,1,0:T(2,128)}) custom-call(s32[5]{0:T(128)S(1)} %stack.23.pos_ref, f32[2]{0:T(128)S(1)} %copy-done.5, f32[1,2,256]{2,1,0:T(2,128)S(1)} %copy-done.4, f32[2,128,128]{2,1,0:T(8,128)S(1)} %collective-permute-done.5.one_ref, f32[2,128,128]{2,1,0:T(8,128)S(1)} %collective-permute-done.6.two_ref, ...), custom_call_target="tpu_custom_call" | custom-call | tf_op jit(solution)/shard_map/pallas_call | solution.py:469
  34.9 3.4 %collective-permute-start.11 = (f32[960,256]{1,0:T(8,128)S(1)}, f32[960,256]{1,0:T(8,128)S(1)}, u32[]{:S(2)}, u32[]{:S(2)}) collective-permute-start(f32[960,256]{1,0:T(8,128)S(1)} %get-tuple-element.74.all_ref.own_ref), channel_id=1, source_target_pairs={{0,16},{16,0},{32,48},{48,32},{64,80},{80,64},{96,112},{112,96},{1... | collective-permute-start | bytes 2949128 | tf_op jit(solution)/shard_map/ppermute | solution.py:362
  38.3 1.6 %shard_map.125 = (f32[256,512]{1,0:T(8,128)S(1)}, f32[256,512]{1,0:T(8,128)S(1)}, f32[256,512]{1,0:T(8,128)S(1)}, f32[256,512]{1,0:T(8,128)S(1)}) custom-call(s32[5]{0:T(128)S(1)} %stack.23.pos_ref, bf16[3,2048,256]{2,1,0:T(8,128)(2,1)S(1)} %copy-done, f32[960,256]{1,0:T(8,128)S(1)} %get-tuple-element.74.all_ref.own_ref), custom_call_target="tpu_custom_call" | custom-call | tf_op jit(solution)/shard_map/pallas_call | solution.py:476
  39.9 0.6 collective-permute-done.11.other_ref
  40.5 0.9 shard_map.126.refs_2_
  41.4 3.6 %collective-permute-start.16 = (f32[792,256]{1,0:T(8,128)S(1)}, f32[792,256]{1,0:T(8,128)S(1)}, u32[]{:S(2)}, u32[]{:S(2)}) collective-permute-start(f32[792,256]{1,0:T(8,128)S(1)} %shard_map.126.refs_2_), channel_id=1, source_target_pairs={{0,64},{4,68},{8,72},{12,76},{16,24},{20,28},{24,16},{28,20},{32,9... | collective-permute-start | bytes 2433032 | tf_op jit(solution)/shard_map/ppermute | solution.py:357
  45.1 1.3 %shard_map.127 = (f32[792,256]{1,0:T(8,128)S(1)}, f32[792,256]{1,0:T(8,128)S(1)}, f32[792,256]{1,0:T(8,128)S(1)}, f32[256,512]{1,0:T(8,128)S(1)}, f32[256,512]{1,0:T(8,128)S(1)}) custom-call(s32[5]{0:T(128)S(1)} %stack.23.pos_ref, bf16[1024,256]{1,0:T(8,128)(2,1)S(1)} %get-tuple-element.77.tokt_ref, ...), custom_call_target="tpu_custom_call", output_to_operand_aliasing={{3}: (5, {}), {4}: (6, {})} | custom-call | tf_op jit(solution)/shard_map/pallas_call | solution.py:485
  46.5 2.7 %collective-permute-start.15 = (f32[792,256]{1,0:T(8,128)S(1)}, f32[792,256]{1,0:T(8,128)S(1)}, u32[]{:S(2)}, u32[]{:S(2)}) collective-permute-start(f32[792,256]{1,0:T(8,128)S(1)} %get-tuple-element.84), channel_id=1, source_target_pairs={{0,96},{4,100},{8,104},{12,108},{16,28},{20,16},{24,20},{28,24},{3... | collective-permute-start | bytes 2433032 | tf_op jit(solution)/shard_map/ppermute | solution.py:357
  49.1 1.6 %collective-permute-start.12 = (f32[256,512]{1,0:T(8,128)S(1)}, f32[256,512]{1,0:T(8,128)S(1)}, u32[]{:S(2)}, u32[]{:S(2)}) collective-permute-start(f32[256,512]{1,0:T(8,128)S(1)} %get-tuple-element.80), channel_id=1, source_target_pairs={{0,1},{1,2},{2,3},{3,0},{4,5},{5,6},{6,7},{7,4},{8,9},{9,10},{10,1... | collective-permute-start | bytes 1572872 | tf_op jit(solution)/shard_map/ppermute | solution.py:479
  50.8 2.1 %collective-permute-start.13 = (f32[256,512]{1,0:T(8,128)S(1)}, f32[256,512]{1,0:T(8,128)S(1)}, u32[]{:S(2)}, u32[]{:S(2)}) collective-permute-start(f32[256,512]{1,0:T(8,128)S(1)} %get-tuple-element.81), channel_id=1, source_target_pairs={{0,3},{1,0},{2,1},{3,2},{4,7},{5,4},{6,5},{7,6},{8,11},{9,8},{10,9... | collective-permute-start | bytes 1572872 | tf_op jit(solution)/shard_map/ppermute | solution.py:479
  52.9 11.7 %collective-permute-done.12.refs_0_ = f32[256,512]{1,0:T(8,128)S(1)} collective-permute-done((f32[256,512]{1,0:T(8,128)S(1)}, f32[256,512]{1,0:T(8,128)S(1)}, u32[]{:S(2)}, u32[]{:S(2)}) %collective-permute-start.12) | collective-permute-done | bytes 524320 | tf_op jit(solution)/shard_map/ppermute | solution.py:479
  64.7 0.2 shard_map.128.own_ref
  64.9 1.6 %collective-permute-start.19 = (f32[792,256]{1,0:T(8,128)S(1)}, f32[792,256]{1,0:T(8,128)S(1)}, u32[]{:S(2)}, u32[]{:S(2)}) collective-permute-start(f32[792,256]{1,0:T(8,128)S(1)} %shard_map.128.own_ref), channel_id=1, source_target_pairs={{0,8},{4,12},{8,0},{12,4},{16,80},{20,84},{24,88},{28,92},{32,40},... | collective-permute-start | bytes 2433032 | tf_op jit(solution)/shard_map/ppermute | solution.py:357
  66.4 1.4 %collective-permute-start.18 = (f32[792,256]{1,0:T(8,128)S(1)}, f32[792,256]{1,0:T(8,128)S(1)}, u32[]{:S(2)}, u32[]{:S(2)}) collective-permute-start(f32[792,256]{1,0:T(8,128)S(1)} %shard_map.128.own_ref), channel_id=1, source_target_pairs={{0,12},{4,0},{8,4},{12,8},{16,112},{20,116},{24,120},{28,124},{32,... | collective-permute-start | bytes 2433032 | tf_op jit(solution)/shard_map/ppermute | solution.py:357
  67.9 3.6 %collective-permute-start.10 = (f32[256,512]{1,0:T(8,128)S(1)}, f32[256,512]{1,0:T(8,128)S(1)}, u32[]{:S(2)}, u32[]{:S(2)}) collective-permute-start(f32[256,512]{1,0:T(8,128)S(1)} %get-tuple-element.76), channel_id=1, source_target_pairs={{0,2},{1,3},{2,0},{3,1},{4,6},{5,7},{6,4},{7,5},{8,10},{9,11},{10,... | collective-permute-start | bytes 1572872 | tf_op jit(solution)/shard_map/ppermute | solution.py:479
  71.5 9.5 %collective-permute-done.10 = f32[256,512]{1,0:T(8,128)S(1)} collective-permute-done((f32[256,512]{1,0:T(8,128)S(1)}, f32[256,512]{1,0:T(8,128)S(1)}, u32[]{:S(2)}, u32[]{:S(2)}) %collective-permute-start.10) | collective-permute-done | bytes 524320 | tf_op jit(solution)/shard_map/ppermute | solution.py:479
  81.0 0.2 fusion.refs_0_
  81.3 4.4 %collective-permute-done.18.ahead_ref = f32[792,256]{1,0:T(8,128)S(1)} collective-permute-done((f32[792,256]{1,0:T(8,128)S(1)}, f32[792,256]{1,0:T(8,128)S(1)}, u32[]{:S(2)}, u32[]{:S(2)}) %collective-permute-start.18) | collective-permute-done | bytes 811040 | tf_op jit(solution)/shard_map/ppermute | solution.py:357
  85.7 0.8 collective-permute-done.17.back_ref
  86.5 0.2 shard_map.129.refs_0_
  86.7 2.1 %collective-permute-start.22 = (f32[792,256]{1,0:T(8,128)S(1)}, f32[792,256]{1,0:T(8,128)S(1)}, u32[]{:S(2)}, u32[]{:S(2)}) collective-permute-start(f32[792,256]{1,0:T(8,128)S(1)} %shard_map.129.refs_0_), channel_id=1, source_target_pairs={{0,64},{4,68},{8,72},{12,76},{16,24},{20,28},{24,16},{28,20},{32,9... | collective-permute-start | bytes 2433032 | tf_op jit(solution)/shard_map/ppermute | solution.py:357
  88.9 2.7 %collective-permute-start.20 = (f32[792,256]{1,0:T(8,128)S(1)}, f32[792,256]{1,0:T(8,128)S(1)}, u32[]{:S(2)}, u32[]{:S(2)}) collective-permute-start(f32[792,256]{1,0:T(8,128)S(1)} %shard_map.129.refs_0_), channel_id=1, source_target_pairs={{0,96},{4,100},{8,104},{12,108},{16,28},{20,16},{24,20},{28,24},{3... | collective-permute-start | bytes 2433032 | tf_op jit(solution)/shard_map/ppermute | solution.py:357
  91.5 8.2 %collective-permute-done.22.refs_1_.refs_3_ = f32[792,256]{1,0:T(8,128)S(1)} collective-permute-done((f32[792,256]{1,0:T(8,128)S(1)}, f32[792,256]{1,0:T(8,128)S(1)}, u32[]{:S(2)}, u32[]{:S(2)}) %collective-permute-start.22) | collective-permute-done | bytes 811040 | tf_op jit(solution)/shard_map/ppermute | solution.py:357
  99.8 2.9 %collective-permute-start.26 = (f32[792,256]{1,0:T(8,128)S(1)}, f32[792,256]{1,0:T(8,128)S(1)}, u32[]{:S(2)}, u32[]{:S(2)}) collective-permute-start(f32[792,256]{1,0:T(8,128)S(1)} %collective-permute-done.22.refs_1_.refs_3_), channel_id=1, source_target_pairs={{0,16},{16,0},{32,48},{48,32},{64,80},{80,64},{96,112},{112,96},{1... | collective-permute-start | bytes 2433032 | tf_op jit(solution)/shard_map/ppermute | solution.py:362
  102.7 1.7 %shard_map.130 = (f32[3,2048,256]{2,1,0:T(8,128)}, f32[792,256]{1,0:T(8,128)S(1)}) custom-call(s32[5]{0:T(128)S(1)} %stack.23.pos_ref, f32[792,256]{1,0:T(8,128)S(1)} %shard_map.129.refs_0_, f32[792,256]{1,0:T(8,128)S(1)} %collective-permute-done.22.refs_1_.refs_3_), custom_call_target="tpu_custom_call" | custom-call | tf_op jit(solution)/shard_map/pallas_call | solution.py:502
  104.5 3.9 %collective-permute-done.21.refs_1_.refs_2_ = f32[792,256]{1,0:T(8,128)S(1)} collective-permute-done((f32[792,256]{1,0:T(8,128)S(1)}, f32[792,256]{1,0:T(8,128)S(1)}, u32[]{:S(2)}, u32[]{:S(2)}) %collective-permute-start.21) | collective-permute-done | bytes 811040 | tf_op jit(solution)/shard_map/ppermute | solution.py:357
  108.4 2.8 %collective-permute-start.25 = (f32[792,256]{1,0:T(8,128)S(1)}, f32[792,256]{1,0:T(8,128)S(1)}, u32[]{:S(2)}, u32[]{:S(2)}) collective-permute-start(f32[792,256]{1,0:T(8,128)S(1)} %collective-permute-done.21.refs_1_.refs_2_), channel_id=1, source_target_pairs={{0,16},{16,0},{32,48},{48,32},{64,80},{80,64},{96,112},{112,96},{1... | collective-permute-start | bytes 2433032 | tf_op jit(solution)/shard_map/ppermute | solution.py:362
  111.3 2.3 %shard_map.131.refs_8_ = f32[3,2048,256]{2,1,0:T(8,128)} custom-call(s32[5]{0:T(128)S(1)} %stack.23.pos_ref, f32[792,256]{1,0:T(8,128)S(1)} %collective-permute-done.20.refs_0_.refs_1_, f32[792,256]{1,0:T(8,128)S(1)} %collective-permute-done.21.refs_1_.refs_2_, ...), custom_call_target="tpu_custom_call", output_to_operand_aliasing={{}: (5, {})} | custom-call | tf_op jit(solution)/shard_map/pallas_call | solution.py:502
  113.6 0.8 collective-permute-done.24.refs_5_
  114.4 2.4 %shard_map.132 = (f32[3,2048,256]{2,1,0:T(8,128)}, f32[2,128,128]{2,1,0:T(8,128)}, f32[2,128]{1,0:T(2,128)}, f32[2]{0:T(128)}) custom-call(s32[5]{0:T(128)S(1)} %stack.23.pos_ref, f32[792,256]{1,0:T(8,128)S(1)} %shard_map.129.refs_0_, f32[792,256]{1,0:T(8,128)S(1)} %collective-permute-done.20.refs_0_.refs_1_, ...), custom_call_target="tpu_custom_call", output_to_operand_aliasing={{0}: (9, {})} | custom-call | tf_op jit(solution)/shard_map/pallas_call | solution.py:518
  (37 shorter events, 0.4 us)
Async XLA Ops:
  0.6 11.8 %copy-start.4 = (f32[1,2,256]{2,1,0:T(2,128)S(1)}, f32[1,2,256]{2,1,0:T(2,128)}, u32[]{:S(2)}) copy-start(f32[1,2,256]{2,1,0:T(2,128)} %gate_ref.7) | copy-start | bytes 6148
  0.6 11.8 %copy-start.5 = (f32[2]{0:T(128)S(1)}, f32[2]{0:T(128)}, u32[]{:S(2)}) copy-start(f32[2]{0:T(128)} %base_ref.7) | copy-start | bytes 28
  0.8 19.5 %copy-start.2 = (f32[2,128,128]{2,1,0:T(8,128)S(1)}, f32[2,128,128]{2,1,0:T(8,128)}, u32[]{:S(2)}) copy-start(f32[2,128,128]{2,1,0:T(8,128)} %init_ref.3) | copy-start | bytes 393220
  0.8 19.5 %copy-start.3 = (bf16[1,256,256]{2,1,0:T(8,128)(2,1)S(1)}, bf16[1,256,256]{2,1,0:T(8,128)(2,1)}, u32[]{:S(2)}) copy-start(bf16[1,256,256]{2,1,0:T(8,128)(2,1)} %up_ref.3) | copy-start | bytes 393220
  0.8 19.5 %copy-start.6 = (f32[2,128]{1,0:T(2,128)S(1)}, f32[2,128]{1,0:T(2,128)}, u32[]{:S(2)}) copy-start(f32[2,128]{1,0:T(2,128)} %gain_ref.1) | copy-start | bytes 3076
  6.3 13.0 %collective-permute-start.4 = (f32[256,1024]{1,0:T(8,128)S(1)}, f32[256,1024]{1,0:T(8,128)S(1)}, u32[]{:S(2)}, u32[]{:S(2)}) collective-permute-start(f32[256,1024]{1,0:T(8,128)S(1)} %get-tuple-element.57), channel_id=1, source_target_pairs={{0,16},{16,0},{32,48},{48,32},{64,80},{80,64},{96,112},{112,96},{1... | collective-permute-start | bytes 3145736 | tf_op jit(solution)/shard_map/ppermute | solution.py:362
  7.8 8.5 %collective-permute-start = (f32[2,128,128]{2,1,0:T(8,128)S(1)}, f32[2,128,128]{2,1,0:T(8,128)S(1)}, u32[]{:S(2)}, u32[]{:S(2)}) collective-permute-start(f32[2,128,128]{2,1,0:T(8,128)S(1)} %get-tuple-element.49), channel_id=1, source_target_pairs={{0,4},{8,12},{1,5},{9,13},{2,6},{10,14},{3,7},{11,15},{16,20},{24,... | collective-permute-start | bytes 393224 | tf_op jit(solution)/shard_map/ppermute | solution.py:435
  11.1 9.1 %collective-permute-start.3 = (f32[2,128,128]{2,1,0:T(8,128)S(1)}, f32[2,128,128]{2,1,0:T(8,128)S(1)}, u32[]{:S(2)}, u32[]{:S(2)}) collective-permute-start(f32[2,128,128]{2,1,0:T(8,128)S(1)} %get-tuple-element.50.d_ref), channel_id=1, source_target_pairs={{8,12},{4,0},{9,13},{5,1},{10,14},{6,2},{11,15},{7,3},{24,28},{20,... | collective-permute-start | bytes 393224 | tf_op jit(solution)/shard_map/ppermute | solution.py:436
  16.3 22.0 %copy-start = (bf16[3,2048,256]{2,1,0:T(8,128)(2,1)S(1)}, bf16[3,2048,256]{2,1,0:T(8,128)(2,1)}, u32[]{:S(2)}) copy-start(bf16[3,2048,256]{2,1,0:T(8,128)(2,1)} %w_ref.1) | copy-start | bytes 9437188
  16.6 3.7 %collective-permute-start.2 = (f32[2,128,128]{2,1,0:T(8,128)S(1)}, f32[2,128,128]{2,1,0:T(8,128)S(1)}, u32[]{:S(2)}, u32[]{:S(2)}) collective-permute-start(f32[2,128,128]{2,1,0:T(8,128)S(1)} %shard_map.120), channel_id=1, source_target_pairs={{4,12},{5,13},{6,14},{7,15},{20,28},{21,29},{22,30},{23,31},{36,44... | collective-permute-start | bytes 393224 | tf_op jit(solution)/shard_map/ppermute | solution.py:454
  17.4 2.9 %collective-permute-start.1 = (f32[2,128,128]{2,1,0:T(8,128)S(1)}, f32[2,128,128]{2,1,0:T(8,128)S(1)}, u32[]{:S(2)}, u32[]{:S(2)}) collective-permute-start(f32[2,128,128]{2,1,0:T(8,128)S(1)} %shard_map.120), channel_id=1, source_target_pairs={{4,8},{5,9},{6,10},{7,11},{20,24},{21,25},{22,26},{23,27},{36,40},... | collective-permute-start | bytes 393224 | tf_op jit(solution)/shard_map/ppermute | solution.py:453
  18.1 10.6 %collective-permute-start.9 = (f32[2,128,128]{2,1,0:T(8,128)S(1)}, f32[2,128,128]{2,1,0:T(8,128)S(1)}, u32[]{:S(2)}, u32[]{:S(2)}) collective-permute-start(f32[2,128,128]{2,1,0:T(8,128)S(1)} %get-tuple-element.50.d_ref), channel_id=1, source_target_pairs={{8,0},{9,1},{10,2},{11,3},{24,16},{25,17},{26,18},{27,19},{40,32},... | collective-permute-start | bytes 393224 | tf_op jit(solution)/shard_map/ppermute | solution.py:438
  19.4 9.3 %collective-permute-start.8 = (f32[2,128,128]{2,1,0:T(8,128)S(1)}, f32[2,128,128]{2,1,0:T(8,128)S(1)}, u32[]{:S(2)}, u32[]{:S(2)}) collective-permute-start(f32[2,128,128]{2,1,0:T(8,128)S(1)} %get-tuple-element.50.d_ref), channel_id=1, source_target_pairs={{8,4},{9,5},{10,6},{11,7},{24,20},{25,21},{26,22},{27,23},{40,36},... | collective-permute-start | bytes 393224 | tf_op jit(solution)/shard_map/ppermute | solution.py:437
  21.9 8.5 %collective-permute-start.7 = (f32[2,128,128]{2,1,0:T(8,128)S(1)}, f32[2,128,128]{2,1,0:T(8,128)S(1)}, u32[]{:S(2)}, u32[]{:S(2)}) collective-permute-start(f32[2,128,128]{2,1,0:T(8,128)S(1)} %get-tuple-element.58.p_ref), channel_id=1, source_target_pairs={{12,0},{13,1},{14,2},{15,3},{28,16},{29,17},{30,18},{31,19},{44,32... | collective-permute-start | bytes 393224 | tf_op jit(solution)/shard_map/ppermute | solution.py:463
  23.2 9.2 %collective-permute-start.6 = (f32[2,128,128]{2,1,0:T(8,128)S(1)}, f32[2,128,128]{2,1,0:T(8,128)S(1)}, u32[]{:S(2)}, u32[]{:S(2)}) collective-permute-start(f32[2,128,128]{2,1,0:T(8,128)S(1)} %get-tuple-element.58.p_ref), channel_id=1, source_target_pairs={{12,4},{8,0},{13,5},{9,1},{14,6},{10,2},{15,7},{11,3},{28,20},{24,... | collective-permute-start | bytes 393224 | tf_op jit(solution)/shard_map/ppermute | solution.py:462
  24.5 7.9 %collective-permute-start.5 = (f32[2,128,128]{2,1,0:T(8,128)S(1)}, f32[2,128,128]{2,1,0:T(8,128)S(1)}, u32[]{:S(2)}, u32[]{:S(2)}) collective-permute-start(f32[2,128,128]{2,1,0:T(8,128)S(1)} %get-tuple-element.58.p_ref), channel_id=1, source_target_pairs={{12,8},{8,4},{4,0},{13,9},{9,5},{5,1},{14,10},{10,6},{6,2},{15,11}... | collective-permute-start | bytes 393224 | tf_op jit(solution)/shard_map/ppermute | solution.py:461
  34.9 5.6 %collective-permute-start.11 = (f32[960,256]{1,0:T(8,128)S(1)}, f32[960,256]{1,0:T(8,128)S(1)}, u32[]{:S(2)}, u32[]{:S(2)}) collective-permute-start(f32[960,256]{1,0:T(8,128)S(1)} %get-tuple-element.74.all_ref.own_ref), channel_id=1, source_target_pairs={{0,16},{16,0},{32,48},{48,32},{64,80},{80,64},{96,112},{112,96},{1... | collective-permute-start | bytes 2949128 | tf_op jit(solution)/shard_map/ppermute | solution.py:362
  41.4 23.2 %collective-permute-start.16 = (f32[792,256]{1,0:T(8,128)S(1)}, f32[792,256]{1,0:T(8,128)S(1)}, u32[]{:S(2)}, u32[]{:S(2)}) collective-permute-start(f32[792,256]{1,0:T(8,128)S(1)} %shard_map.126.refs_2_), channel_id=1, source_target_pairs={{0,64},{4,68},{8,72},{12,76},{16,24},{20,28},{24,16},{28,20},{32,9... | collective-permute-start | bytes 2433032 | tf_op jit(solution)/shard_map/ppermute | solution.py:357
  46.4 18.3 %collective-permute-start.14 = (f32[792,256]{1,0:T(8,128)S(1)}, f32[792,256]{1,0:T(8,128)S(1)}, u32[]{:S(2)}, u32[]{:S(2)}) collective-permute-start(f32[792,256]{1,0:T(8,128)S(1)} %get-tuple-element.83), channel_id=1, source_target_pairs={{0,32},{4,36},{8,40},{12,44},{16,20},{20,24},{24,28},{28,16},{32,6... | collective-permute-start | bytes 2433032 | tf_op jit(solution)/shard_map/ppermute | solution.py:357
  46.5 18.2 %collective-permute-start.15 = (f32[792,256]{1,0:T(8,128)S(1)}, f32[792,256]{1,0:T(8,128)S(1)}, u32[]{:S(2)}, u32[]{:S(2)}) collective-permute-start(f32[792,256]{1,0:T(8,128)S(1)} %get-tuple-element.84), channel_id=1, source_target_pairs={{0,96},{4,100},{8,104},{12,108},{16,28},{20,16},{24,20},{28,24},{3... | collective-permute-start | bytes 2433032 | tf_op jit(solution)/shard_map/ppermute | solution.py:357
  49.1 15.5 %collective-permute-start.12 = (f32[256,512]{1,0:T(8,128)S(1)}, f32[256,512]{1,0:T(8,128)S(1)}, u32[]{:S(2)}, u32[]{:S(2)}) collective-permute-start(f32[256,512]{1,0:T(8,128)S(1)} %get-tuple-element.80), channel_id=1, source_target_pairs={{0,1},{1,2},{2,3},{3,0},{4,5},{5,6},{6,7},{7,4},{8,9},{9,10},{10,1... | collective-permute-start | bytes 1572872 | tf_op jit(solution)/shard_map/ppermute | solution.py:479
  50.8 13.9 %collective-permute-start.13 = (f32[256,512]{1,0:T(8,128)S(1)}, f32[256,512]{1,0:T(8,128)S(1)}, u32[]{:S(2)}, u32[]{:S(2)}) collective-permute-start(f32[256,512]{1,0:T(8,128)S(1)} %get-tuple-element.81), channel_id=1, source_target_pairs={{0,3},{1,0},{2,1},{3,2},{4,7},{5,4},{6,5},{7,6},{8,11},{9,8},{10,9... | collective-permute-start | bytes 1572872 | tf_op jit(solution)/shard_map/ppermute | solution.py:479
  64.9 16.4 %collective-permute-start.19 = (f32[792,256]{1,0:T(8,128)S(1)}, f32[792,256]{1,0:T(8,128)S(1)}, u32[]{:S(2)}, u32[]{:S(2)}) collective-permute-start(f32[792,256]{1,0:T(8,128)S(1)} %shard_map.128.own_ref), channel_id=1, source_target_pairs={{0,8},{4,12},{8,0},{12,4},{16,80},{20,84},{24,88},{28,92},{32,40},... | collective-permute-start | bytes 2433032 | tf_op jit(solution)/shard_map/ppermute | solution.py:357
  66.4 19.3 %collective-permute-start.18 = (f32[792,256]{1,0:T(8,128)S(1)}, f32[792,256]{1,0:T(8,128)S(1)}, u32[]{:S(2)}, u32[]{:S(2)}) collective-permute-start(f32[792,256]{1,0:T(8,128)S(1)} %shard_map.128.own_ref), channel_id=1, source_target_pairs={{0,12},{4,0},{8,4},{12,8},{16,112},{20,116},{24,120},{28,124},{32,... | collective-permute-start | bytes 2433032 | tf_op jit(solution)/shard_map/ppermute | solution.py:357
  67.8 18.7 %collective-permute-start.17 = (f32[792,256]{1,0:T(8,128)S(1)}, f32[792,256]{1,0:T(8,128)S(1)}, u32[]{:S(2)}, u32[]{:S(2)}) collective-permute-start(f32[792,256]{1,0:T(8,128)S(1)} %shard_map.128.own_ref), channel_id=1, source_target_pairs={{0,4},{4,8},{8,12},{12,0},{16,48},{20,52},{24,56},{28,60},{32,36},... | collective-permute-start | bytes 2433032 | tf_op jit(solution)/shard_map/ppermute | solution.py:357
  67.9 13.1 %collective-permute-start.10 = (f32[256,512]{1,0:T(8,128)S(1)}, f32[256,512]{1,0:T(8,128)S(1)}, u32[]{:S(2)}, u32[]{:S(2)}) collective-permute-start(f32[256,512]{1,0:T(8,128)S(1)} %get-tuple-element.76), channel_id=1, source_target_pairs={{0,2},{1,3},{2,0},{3,1},{4,6},{5,7},{6,4},{7,5},{8,10},{9,11},{10,... | collective-permute-start | bytes 1572872 | tf_op jit(solution)/shard_map/ppermute | solution.py:479
  81.3 32.3 %copy-start.1 = (bf16[1,256,512]{2,1,0:T(8,128)(2,1)}, bf16[1,256,512]{2,1,0:T(8,128)(2,1)S(1)}, u32[]{:S(2)}) copy-start(bf16[1,256,512]{2,1,0:T(8,128)(2,1)S(1)} %fusion.refs_0_) | copy-start | bytes 786436
  86.7 13.0 %collective-permute-start.22 = (f32[792,256]{1,0:T(8,128)S(1)}, f32[792,256]{1,0:T(8,128)S(1)}, u32[]{:S(2)}, u32[]{:S(2)}) collective-permute-start(f32[792,256]{1,0:T(8,128)S(1)} %shard_map.129.refs_0_), channel_id=1, source_target_pairs={{0,64},{4,68},{8,72},{12,76},{16,24},{20,28},{24,16},{28,20},{32,9... | collective-permute-start | bytes 2433032 | tf_op jit(solution)/shard_map/ppermute | solution.py:357
  88.9 19.5 %collective-permute-start.21 = (f32[792,256]{1,0:T(8,128)S(1)}, f32[792,256]{1,0:T(8,128)S(1)}, u32[]{:S(2)}, u32[]{:S(2)}) collective-permute-start(f32[792,256]{1,0:T(8,128)S(1)} %shard_map.129.refs_0_), channel_id=1, source_target_pairs={{0,32},{4,36},{8,40},{12,44},{16,20},{20,24},{24,28},{28,16},{32,6... | collective-permute-start | bytes 2433032 | tf_op jit(solution)/shard_map/ppermute | solution.py:357
  88.9 22.4 %collective-permute-start.20 = (f32[792,256]{1,0:T(8,128)S(1)}, f32[792,256]{1,0:T(8,128)S(1)}, u32[]{:S(2)}, u32[]{:S(2)}) collective-permute-start(f32[792,256]{1,0:T(8,128)S(1)} %shard_map.129.refs_0_), channel_id=1, source_target_pairs={{0,96},{4,100},{8,104},{12,108},{16,28},{20,16},{24,20},{28,24},{3... | collective-permute-start | bytes 2433032 | tf_op jit(solution)/shard_map/ppermute | solution.py:357
  99.8 11.5 %collective-permute-start.26 = (f32[792,256]{1,0:T(8,128)S(1)}, f32[792,256]{1,0:T(8,128)S(1)}, u32[]{:S(2)}, u32[]{:S(2)}) collective-permute-start(f32[792,256]{1,0:T(8,128)S(1)} %collective-permute-done.22.refs_1_.refs_3_), channel_id=1, source_target_pairs={{0,16},{16,0},{32,48},{48,32},{64,80},{80,64},{96,112},{112,96},{1... | collective-permute-start | bytes 2433032 | tf_op jit(solution)/shard_map/ppermute | solution.py:362
  104.4 6.9 %collective-permute-start.23 = (f32[792,256]{1,0:T(8,128)S(1)}, f32[792,256]{1,0:T(8,128)S(1)}, u32[]{:S(2)}, u32[]{:S(2)}) collective-permute-start(f32[792,256]{1,0:T(8,128)S(1)} %get-tuple-element.85), channel_id=1, source_target_pairs={{0,16},{16,0},{32,48},{48,32},{64,80},{80,64},{96,112},{112,96},{1... | collective-permute-start | bytes 2433032 | tf_op jit(solution)/shard_map/ppermute | solution.py:362
  108.4 5.2 %collective-permute-start.25 = (f32[792,256]{1,0:T(8,128)S(1)}, f32[792,256]{1,0:T(8,128)S(1)}, u32[]{:S(2)}, u32[]{:S(2)}) collective-permute-start(f32[792,256]{1,0:T(8,128)S(1)} %collective-permute-done.21.refs_1_.refs_2_), channel_id=1, source_target_pairs={{0,16},{16,0},{32,48},{48,32},{64,80},{80,64},{96,112},{112,96},{1... | collective-permute-start | bytes 2433032 | tf_op jit(solution)/shard_map/ppermute | solution.py:362
  111.3 3.1 %collective-permute-start.24 = (f32[792,256]{1,0:T(8,128)S(1)}, f32[792,256]{1,0:T(8,128)S(1)}, u32[]{:S(2)}, u32[]{:S(2)}) collective-permute-start(f32[792,256]{1,0:T(8,128)S(1)} %collective-permute-done.20.refs_0_.refs_1_), channel_id=1, source_target_pairs={{0,16},{16,0},{32,48},{48,32},{64,80},{80,64},{96,112},{112,96},{1... | collective-permute-start | bytes 2433032 | tf_op jit(solution)/shard_map/ppermute | solution.py:362

commit v14 on v13

--- a/solution.py
+++ b/solution.py
@@ -78,11 +78,8 @@
 
 def maps_kernel(
     pos_ref, base_ref, tok_ref, wk_ref, wv_ref, gate_ref, init_ref,
-    k_ref, v_ref, ninv_ref, gram_ref, inv_ref, bt_ref, d_ref, send_ref, o_ref, half_ref,
+    k_ref, v_ref, ninv_ref, gram_ref, inv_ref, bt_ref, d_ref, send_ref, o_ref,
 ):
-    half = tok_ref.shape[2] // 2
-    columns = pl.ds(pl.multiple_of((1 - pos_ref[0]) * half, half), half)
-    half_ref[...] = tok_ref[0, :, columns].astype(F32)
     tok = tok_ref[0]
     kraw_all = jnp.dot(tok, wk_ref[0], preferred_element_type=F32).astype(BF).astype(F32)
     v_all = jnp.dot(tok, wv_ref[0], preferred_element_type=F32).astype(BF).astype(F32)
@@ -116,11 +113,13 @@
 
 def reach_kernel(
     pos_ref, base_ref, tok_ref, wq_ref, gate_ref, k_ref, v_ref, inv_ref,
-    q_ref, score_ref, rv_ref, y_ref, qt_ref, zv_ref, tokt_ref,
+    q_ref, score_ref, rv_ref, y_ref, qt_ref, zv_ref, tokt_ref, half_ref,
 ):
     half = tok_ref.shape[2] // 2
     columns = pl.ds(pl.multiple_of(pos_ref[0] * half, half), half)
     tokt_ref[...] = tok_ref[0, :, columns].astype(F32).T.astype(BF)
+    columns = pl.ds(pl.multiple_of((1 - pos_ref[0]) * half, half), half)
+    half_ref[...] = tok_ref[0, :, columns].astype(F32)
     q_all = jnp.dot(tok_ref[0], wq_ref[0], preferred_element_type=F32).astype(BF).astype(F32)
     n = q_all.shape[0]
     i, j = places(n)
@@ -420,15 +419,14 @@
     proj_weights = hbm(proj_weights)
     anywhere = pl.BlockSpec(memory_space=pl.ANY)
 
-    k, v, ninv, gram, inv, bt, decay, send, offset, other_half = pl.pallas_call(
+    k, v, ninv, gram, inv, bt, decay, send, offset = pl.pallas_call(
         maps_kernel,
         grid=(1,),
         out_shape=(
             wide_f32, wide_f32, vmem(heads, n, HS), square, square, vmem(heads, HS, n), small, small, small,
-            vmem(n, half),
         ),
         in_specs=[SM, SM, full(1, n, model), wspec(1), wspec(2), full(1, heads, n), full(heads, HS, HS)],
-        out_specs=(VM,) * 10,
+        out_specs=(VM,) * 9,
         compiler_params=PARAMS,
     )(pos, hbm(base_rates), tokens, proj_weights, proj_weights, hbm(gate_values), hbm(init_weight))
 
@@ -436,14 +434,13 @@
     moved = lax.ppermute(decay, "ctx", [(2, 3), (1, 0)])
     moved_one = lax.ppermute(decay, "ctx", [(2, 1)])
     moved_two = lax.ppermute(decay, "ctx", [(2, 0)])
-    got_half = swap(other_half)
-
-    q, score, rv, y, qt, zv, tokt = pl.pallas_call(
+
+    q, score, rv, y, qt, zv, tokt, other_half = pl.pallas_call(
         reach_kernel,
         grid=(1,),
-        out_shape=(wide_f32, square, wide_f32, wide_f32, wide_f32, wide_f32, vmem(half, n, dtype=BF)),
+        out_shape=(wide_f32, square, wide_f32, wide_f32, wide_f32, wide_f32, vmem(half, n, dtype=BF), vmem(n, half)),
         in_specs=[SM, SM, full(1, n, model), wspec(0), full(1, heads, n), VM, VM, VM],
-        out_specs=(VM,) * 7,
+        out_specs=(VM,) * 8,
         compiler_params=PARAMS,
     )(pos, base_rates, tokens, proj_weights, gate_values, k, v, inv)
 
@@ -452,6 +449,7 @@
     )
     mid = lax.ppermute(second, "ctx", [(1, 2)])
     far = lax.ppermute(second, "ctx", [(1, 3)])
+    got_half = swap(other_half)
     other_tokt = whole(turn_kernel, vmem(half, n, dtype=BF), [VM])(got_half)
 
     w, back, pulled, dgain = whole(

time: 117 us -> 121 us (1.034)
  waiting for transfers between devices: 43.8 us -> 47.6 us
    ppermute x1, waiting for transfers between devices: 1.75 us -> 4.1 us  [body(): back_three = lax.ppermute(pulled, 'ctx', [(3, 0)])]
    ppermute x1, waiting for transfers between devices: 0.01 us -> 1.43 us  [body(): near = lax.ppermute(send, 'ctx', [(0, 1), (2, 3)])]
  transfers between devices with their start and end apart: 27 -> 27, of which waited for: 10 -> 11; matrix products, arithmetic and copies ran while one was open for 0% -> 0% of each run, Pallas kernels for 13% -> 10%
where the time goes in v14:
time: 121 us
  waiting for transfers between devices  47.6 us (39%)
  starting transfers between devices  44.2 us (37%)
  Pallas kernels  27.4 us (23%)
    ppermute x3, waiting for transfers between devices, along_head(): lax.ppermute(terms, 'head', [(i, (i + turn) % RING) for i in range(RING)])  21.3 us
    ppermute x9, waiting for transfers between devices, round_turn(): lax.ppermute(chunk, ('dp', 'ctx'), moves(first, turn))  17.4 us
    ppermute x9, starting transfers between devices, round_turn(): lax.ppermute(chunk, ('dp', 'ctx'), moves(first, turn))  14.2 us
    ppermute x6, starting transfers between devices, swap(): return lax.ppermute(value, 'dp', [(i, i ^ 1) for i in range(2 * RING)])  10.8 us
    ppermute x3, starting transfers between devices, along_head(): lax.ppermute(terms, 'head', [(i, (i + turn) % RING) for i in range(RING)])  7.36 us
    pallas_call x1, Pallas kernels, body(): pl.pallas_call(maps_kernel, grid=(1,), out_shape=(wide_f32, wide_f32, vme...  5.52 us
    ppermute x1, waiting for transfers between devices, body(): back_three = lax.ppermute(pulled, 'ctx', [(3, 0)])  4.1 us
    pallas_call x2, Pallas kernels, place(): pl.pallas_call(functools.partial(place_kernel, which=which, passed=passed...  4.03 us
  transfers between devices with their start and end apart: 27, of which 11 were waited for; matrix products, arithmetic and copies ran while one was open for 0% of the time, Pallas kernels for 10%

profile of v14, /device:TPU:1, one launch (start us, length us, event | category | flops | bytes accessed | tf_op | source)
XLA Modules:
  0.0 120.7 jit_solution(6894937029973902511)
XLA Ops:
  0.8 5.5 %shard_map.118 = (f32[256,256]{1,0:T(8,128)S(1)}, f32[256,256]{1,0:T(8,128)S(1)}, f32[2,256,128]{2,1,0:T(8,128)S(1)}, f32[2,256,256]{2,1,0:T(8,128)S(1)}, f32[2,...) custom-call(s32[5]{0:T(128)S(1)} %stack.23.pos_ref, ...), custom_call_target="tpu_custom_call" | custom-call | tf_op jit(solution)/shard_map/pallas_call | solution.py:422
  6.3 3.9 %shard_map.119 = (f32[256,256]{1,0:T(8,128)S(1)}, f32[2,256,256]{2,1,0:T(8,128)S(1)}, f32[256,256]{1,0:T(8,128)S(1)}, f32[256,256]{1,0:T(8,128)S(1)}, f32[256,25...) custom-call(s32[5]{0:T(128)S(1)} %stack.23.pos_ref, ...), custom_call_target="tpu_custom_call" | custom-call | tf_op jit(solution)/shard_map/pallas_call | solution.py:438
  10.3 1.5 %collective-permute-start.4 = (f32[256,1024]{1,0:T(8,128)S(1)}, f32[256,1024]{1,0:T(8,128)S(1)}, u32[]{:S(2)}, u32[]{:S(2)}) collective-permute-start(f32[256,1024]{1,0:T(8,128)S(1)} %get-tuple-element.57), channel_id=1, source_target_pairs={{0,16},{16,0},{32,48},{48,32},{64,80},{80,64},{96,112},{112,96},{1... | collective-permute-start | bytes 3145736 | tf_op jit(solution)/shard_map/ppermute | solution.py:361
  11.8 3.4 %collective-permute-start = (f32[2,128,128]{2,1,0:T(8,128)S(1)}, f32[2,128,128]{2,1,0:T(8,128)S(1)}, u32[]{:S(2)}, u32[]{:S(2)}) collective-permute-start(f32[2,128,128]{2,1,0:T(8,128)S(1)} %get-tuple-element.49), channel_id=1, source_target_pairs={{0,4},{8,12},{1,5},{9,13},{2,6},{10,14},{3,7},{11,15},{16,20},{24,... | collective-permute-start | bytes 393224 | tf_op jit(solution)/shard_map/ppermute | solution.py:433
  15.2 1.3 %collective-permute-start.3 = (f32[2,128,128]{2,1,0:T(8,128)S(1)}, f32[2,128,128]{2,1,0:T(8,128)S(1)}, u32[]{:S(2)}, u32[]{:S(2)}) collective-permute-start(f32[2,128,128]{2,1,0:T(8,128)S(1)} %get-tuple-element.50.d_ref), channel_id=1, source_target_pairs={{8,12},{4,0},{9,13},{5,1},{10,14},{6,2},{11,15},{7,3},{24,28},{20,... | collective-permute-start | bytes 393224 | tf_op jit(solution)/shard_map/ppermute | solution.py:434
  16.5 1.4 %collective-permute-done.w_ref.near_ref = f32[2,128,128]{2,1,0:T(8,128)S(1)} collective-permute-done((f32[2,128,128]{2,1,0:T(8,128)S(1)}, f32[2,128,128]{2,1,0:T(8,128)S(1)}, u32[]{:S(2)}, u32[]{:S(2)}) %collective-permute-start) | collective-permute-done | bytes 131104 | tf_op jit(solution)/shard_map/ppermute | solution.py:433
  18.1 0.7 collective-permute-start.2
  18.8 0.7 collective-permute-start.1
  19.5 1.3 %collective-permute-start.9 = (f32[2,128,128]{2,1,0:T(8,128)S(1)}, f32[2,128,128]{2,1,0:T(8,128)S(1)}, u32[]{:S(2)}, u32[]{:S(2)}) collective-permute-start(f32[2,128,128]{2,1,0:T(8,128)S(1)} %get-tuple-element.50.d_ref), channel_id=1, source_target_pairs={{8,0},{9,1},{10,2},{11,3},{24,16},{25,17},{26,18},{27,19},{40,32},... | collective-permute-start | bytes 393224 | tf_op jit(solution)/shard_map/ppermute | solution.py:436
  20.8 0.7 collective-permute-start.8
  21.4 0.2 shard_map.121.after_ref.other_tokt_ref
  21.7 1.5 %shard_map.122 = (f32[2,128,128]{2,1,0:T(8,128)S(1)}, f32[256,256]{1,0:T(8,128)S(1)}, f32[2,128,128]{2,1,0:T(8,128)S(1)}, f32[2,128]{1,0:T(2,128)S(1)}) custom-call(s32[5]{0:T(128)S(1)} %stack.23.pos_ref, f32[2,128,128]{2,1,0:T(8,128)S(1)} %copy-done.2, f32[2,128,128]{2,1,0:T(8,128)S(1)} %collective-permute-done.w_ref.near_ref, ...), custom_call_target="tpu_custom_call" | custom-call | tf_op jit(solution)/shard_map/pallas_call | solution.py:455
  23.3 1.3 %collective-permute-start.7 = (f32[2,128,128]{2,1,0:T(8,128)S(1)}, f32[2,128,128]{2,1,0:T(8,128)S(1)}, u32[]{:S(2)}, u32[]{:S(2)}) collective-permute-start(f32[2,128,128]{2,1,0:T(8,128)S(1)} %get-tuple-element.58.p_ref), channel_id=1, source_target_pairs={{12,0},{13,1},{14,2},{15,3},{28,16},{29,17},{30,18},{31,19},{44,32... | collective-permute-start | bytes 393224 | tf_op jit(solution)/shard_map/ppermute | solution.py:461
  24.6 1.3 %collective-permute-start.6 = (f32[2,128,128]{2,1,0:T(8,128)S(1)}, f32[2,128,128]{2,1,0:T(8,128)S(1)}, u32[]{:S(2)}, u32[]{:S(2)}) collective-permute-start(f32[2,128,128]{2,1,0:T(8,128)S(1)} %get-tuple-element.58.p_ref), channel_id=1, source_target_pairs={{12,4},{8,0},{13,5},{9,1},{14,6},{10,2},{15,7},{11,3},{28,20},{24,... | collective-permute-start | bytes 393224 | tf_op jit(solution)/shard_map/ppermute | solution.py:460
  25.9 1.3 %collective-permute-start.5 = (f32[2,128,128]{2,1,0:T(8,128)S(1)}, f32[2,128,128]{2,1,0:T(8,128)S(1)}, u32[]{:S(2)}, u32[]{:S(2)}) collective-permute-start(f32[2,128,128]{2,1,0:T(8,128)S(1)} %get-tuple-element.58.p_ref), channel_id=1, source_target_pairs={{12,8},{8,4},{4,0},{13,9},{9,5},{5,1},{14,10},{10,6},{6,2},{15,11}... | collective-permute-start | bytes 393224 | tf_op jit(solution)/shard_map/ppermute | solution.py:459
  27.2 2.9 %shard_map.123 = (f32[256,256]{1,0:T(8,128)S(1)}, f32[256,256]{1,0:T(8,128)S(1)}, f32[256,256]{1,0:T(8,128)S(1)}, f32[256,256]{1,0:T(8,128)S(1)}, f32[2,256]{1,0:T(2,128)S(1)}) custom-call(f32[2]{0:T(128)S(1)} %copy-done.5, f32[1,2,256]{2,1,0:T(2,128)S(1)} %copy-done.4, f32[2,128,128]{2,1,0:T(8,128)S(1)} %get-tuple-element.59.w_ref, ...), custom_call_target="tpu_custom_call" | custom-call | tf_op jit(solution)/shard_map/pallas_call | solution.py:463
  30.1 4.1 %collective-permute-done.7.three_ref = f32[2,128,128]{2,1,0:T(8,128)S(1)} collective-permute-done((f32[2,128,128]{2,1,0:T(8,128)S(1)}, f32[2,128,128]{2,1,0:T(8,128)S(1)}, u32[]{:S(2)}, u32[]{:S(2)}) %collective-permute-start.7) | collective-permute-done | bytes 131104 | tf_op jit(solution)/shard_map/ppermute | solution.py:461
  34.2 2.0 %collective-permute-done.6.two_ref = f32[2,128,128]{2,1,0:T(8,128)S(1)} collective-permute-done((f32[2,128,128]{2,1,0:T(8,128)S(1)}, f32[2,128,128]{2,1,0:T(8,128)S(1)}, u32[]{:S(2)}, u32[]{:S(2)}) %collective-permute-start.6) | collective-permute-done | bytes 131104 | tf_op jit(solution)/shard_map/ppermute | solution.py:460
  36.1 2.5 %shard_map.124 = (f32[960,256]{1,0:T(8,128)S(1)}, f32[1,2,256]{2,1,0:T(2,128)}) custom-call(s32[5]{0:T(128)S(1)} %stack.23.pos_ref, f32[2]{0:T(128)S(1)} %copy-done.5, f32[1,2,256]{2,1,0:T(2,128)S(1)} %copy-done.4, f32[2,128,128]{2,1,0:T(8,128)S(1)} %collective-permute-done.5.one_ref, f32[2,128,128]{2,1,0:T(8,128)S(1)} %collective-permute-done.6.two_ref, ...), custom_call_target="tpu_custom_call" | custom-call | tf_op jit(solution)/shard_map/pallas_call | solution.py:467
  38.6 3.5 %collective-permute-start.11 = (f32[960,256]{1,0:T(8,128)S(1)}, f32[960,256]{1,0:T(8,128)S(1)}, u32[]{:S(2)}, u32[]{:S(2)}) collective-permute-start(f32[960,256]{1,0:T(8,128)S(1)} %get-tuple-element.74.all_ref.own_ref), channel_id=1, source_target_pairs={{0,16},{16,0},{32,48},{48,32},{64,80},{80,64},{96,112},{112,96},{1... | collective-permute-start | bytes 2949128 | tf_op jit(solution)/shard_map/ppermute | solution.py:361
  42.1 1.5 %shard_map.125 = (f32[256,512]{1,0:T(8,128)S(1)}, f32[256,512]{1,0:T(8,128)S(1)}, f32[256,512]{1,0:T(8,128)S(1)}, f32[256,512]{1,0:T(8,128)S(1)}) custom-call(s32[5]{0:T(128)S(1)} %stack.23.pos_ref, bf16[3,2048,256]{2,1,0:T(8,128)(2,1)S(1)} %copy-done, f32[960,256]{1,0:T(8,128)S(1)} %get-tuple-element.74.all_ref.own_ref), custom_call_target="tpu_custom_call" | custom-call | tf_op jit(solution)/shard_map/pallas_call | solution.py:474
  43.6 0.6 collective-permute-done.11.other_ref
  44.3 0.9 shard_map.126.refs_2_
  45.2 3.6 %collective-permute-start.16 = (f32[792,256]{1,0:T(8,128)S(1)}, f32[792,256]{1,0:T(8,128)S(1)}, u32[]{:S(2)}, u32[]{:S(2)}) collective-permute-start(f32[792,256]{1,0:T(8,128)S(1)} %shard_map.126.refs_2_), channel_id=1, source_target_pairs={{0,64},{4,68},{8,72},{12,76},{16,24},{20,28},{24,16},{28,20},{32,9... | collective-permute-start | bytes 2433032 | tf_op jit(solution)/shard_map/ppermute | solution.py:356
  48.8 1.3 %shard_map.127 = (f32[792,256]{1,0:T(8,128)S(1)}, f32[792,256]{1,0:T(8,128)S(1)}, f32[792,256]{1,0:T(8,128)S(1)}, f32[256,512]{1,0:T(8,128)S(1)}, f32[256,512]{1,0:T(8,128)S(1)}) custom-call(s32[5]{0:T(128)S(1)} %stack.23.pos_ref, bf16[1024,256]{1,0:T(8,128)(2,1)S(1)} %get-tuple-element.77.tokt_ref, ...), custom_call_target="tpu_custom_call", output_to_operand_aliasing={{3}: (5, {}), {4}: (6, {})} | custom-call | tf_op jit(solution)/shard_map/pallas_call | solution.py:483
  50.2 2.7 %collective-permute-start.15 = (f32[792,256]{1,0:T(8,128)S(1)}, f32[792,256]{1,0:T(8,128)S(1)}, u32[]{:S(2)}, u32[]{:S(2)}) collective-permute-start(f32[792,256]{1,0:T(8,128)S(1)} %get-tuple-element.84), channel_id=1, source_target_pairs={{0,96},{4,100},{8,104},{12,108},{16,28},{20,16},{24,20},{28,24},{3... | collective-permute-start | bytes 2433032 | tf_op jit(solution)/shard_map/ppermute | solution.py:356
  52.9 1.6 %collective-permute-start.12 = (f32[256,512]{1,0:T(8,128)S(1)}, f32[256,512]{1,0:T(8,128)S(1)}, u32[]{:S(2)}, u32[]{:S(2)}) collective-permute-start(f32[256,512]{1,0:T(8,128)S(1)} %get-tuple-element.80), channel_id=1, source_target_pairs={{0,1},{1,2},{2,3},{3,0},{4,5},{5,6},{6,7},{7,4},{8,9},{9,10},{10,1... | collective-permute-start | bytes 1572872 | tf_op jit(solution)/shard_map/ppermute | solution.py:477
  54.5 2.1 %collective-permute-start.13 = (f32[256,512]{1,0:T(8,128)S(1)}, f32[256,512]{1,0:T(8,128)S(1)}, u32[]{:S(2)}, u32[]{:S(2)}) collective-permute-start(f32[256,512]{1,0:T(8,128)S(1)} %get-tuple-element.81), channel_id=1, source_target_pairs={{0,3},{1,0},{2,1},{3,2},{4,7},{5,4},{6,5},{7,6},{8,11},{9,8},{10,9... | collective-permute-start | bytes 1572872 | tf_op jit(solution)/shard_map/ppermute | solution.py:477
  56.7 11.7 %collective-permute-done.12.refs_0_ = f32[256,512]{1,0:T(8,128)S(1)} collective-permute-done((f32[256,512]{1,0:T(8,128)S(1)}, f32[256,512]{1,0:T(8,128)S(1)}, u32[]{:S(2)}, u32[]{:S(2)}) %collective-permute-start.12) | collective-permute-done | bytes 524320 | tf_op jit(solution)/shard_map/ppermute | solution.py:477
  68.4 0.2 shard_map.128.own_ref
  68.6 1.6 %collective-permute-start.19 = (f32[792,256]{1,0:T(8,128)S(1)}, f32[792,256]{1,0:T(8,128)S(1)}, u32[]{:S(2)}, u32[]{:S(2)}) collective-permute-start(f32[792,256]{1,0:T(8,128)S(1)} %shard_map.128.own_ref), channel_id=1, source_target_pairs={{0,8},{4,12},{8,0},{12,4},{16,80},{20,84},{24,88},{28,92},{32,40},... | collective-permute-start | bytes 2433032 | tf_op jit(solution)/shard_map/ppermute | solution.py:356
  70.2 1.4 %collective-permute-start.18 = (f32[792,256]{1,0:T(8,128)S(1)}, f32[792,256]{1,0:T(8,128)S(1)}, u32[]{:S(2)}, u32[]{:S(2)}) collective-permute-start(f32[792,256]{1,0:T(8,128)S(1)} %shard_map.128.own_ref), channel_id=1, source_target_pairs={{0,12},{4,0},{8,4},{12,8},{16,112},{20,116},{24,120},{28,124},{32,... | collective-permute-start | bytes 2433032 | tf_op jit(solution)/shard_map/ppermute | solution.py:356
  71.7 3.6 %collective-permute-start.10 = (f32[256,512]{1,0:T(8,128)S(1)}, f32[256,512]{1,0:T(8,128)S(1)}, u32[]{:S(2)}, u32[]{:S(2)}) collective-permute-start(f32[256,512]{1,0:T(8,128)S(1)} %get-tuple-element.76), channel_id=1, source_target_pairs={{0,2},{1,3},{2,0},{3,1},{4,6},{5,7},{6,4},{7,5},{8,10},{9,11},{10,... | collective-permute-start | bytes 1572872 | tf_op jit(solution)/shard_map/ppermute | solution.py:477
  75.3 9.5 %collective-permute-done.10 = f32[256,512]{1,0:T(8,128)S(1)} collective-permute-done((f32[256,512]{1,0:T(8,128)S(1)}, f32[256,512]{1,0:T(8,128)S(1)}, u32[]{:S(2)}, u32[]{:S(2)}) %collective-permute-start.10) | collective-permute-done | bytes 524320 | tf_op jit(solution)/shard_map/ppermute | solution.py:477
  84.8 0.2 fusion.refs_0_
  85.0 4.4 %collective-permute-done.18.ahead_ref = f32[792,256]{1,0:T(8,128)S(1)} collective-permute-done((f32[792,256]{1,0:T(8,128)S(1)}, f32[792,256]{1,0:T(8,128)S(1)}, u32[]{:S(2)}, u32[]{:S(2)}) %collective-permute-start.18) | collective-permute-done | bytes 811040 | tf_op jit(solution)/shard_map/ppermute | solution.py:356
  89.5 0.8 collective-permute-done.17.back_ref
  90.3 0.2 shard_map.129.refs_0_
  90.5 2.1 %collective-permute-start.22 = (f32[792,256]{1,0:T(8,128)S(1)}, f32[792,256]{1,0:T(8,128)S(1)}, u32[]{:S(2)}, u32[]{:S(2)}) collective-permute-start(f32[792,256]{1,0:T(8,128)S(1)} %shard_map.129.refs_0_), channel_id=1, source_target_pairs={{0,64},{4,68},{8,72},{12,76},{16,24},{20,28},{24,16},{28,20},{32,9... | collective-permute-start | bytes 2433032 | tf_op jit(solution)/shard_map/ppermute | solution.py:356
  92.6 2.7 %collective-permute-start.20 = (f32[792,256]{1,0:T(8,128)S(1)}, f32[792,256]{1,0:T(8,128)S(1)}, u32[]{:S(2)}, u32[]{:S(2)}) collective-permute-start(f32[792,256]{1,0:T(8,128)S(1)} %shard_map.129.refs_0_), channel_id=1, source_target_pairs={{0,96},{4,100},{8,104},{12,108},{16,28},{20,16},{24,20},{28,24},{3... | collective-permute-start | bytes 2433032 | tf_op jit(solution)/shard_map/ppermute | solution.py:356
  95.3 8.2 %collective-permute-done.22.refs_1_.refs_3_ = f32[792,256]{1,0:T(8,128)S(1)} collective-permute-done((f32[792,256]{1,0:T(8,128)S(1)}, f32[792,256]{1,0:T(8,128)S(1)}, u32[]{:S(2)}, u32[]{:S(2)}) %collective-permute-start.22) | collective-permute-done | bytes 811040 | tf_op jit(solution)/shard_map/ppermute | solution.py:356
  103.5 2.9 %collective-permute-start.26 = (f32[792,256]{1,0:T(8,128)S(1)}, f32[792,256]{1,0:T(8,128)S(1)}, u32[]{:S(2)}, u32[]{:S(2)}) collective-permute-start(f32[792,256]{1,0:T(8,128)S(1)} %collective-permute-done.22.refs_1_.refs_3_), channel_id=1, source_target_pairs={{0,16},{16,0},{32,48},{48,32},{64,80},{80,64},{96,112},{112,96},{1... | collective-permute-start | bytes 2433032 | tf_op jit(solution)/shard_map/ppermute | solution.py:361
  106.4 1.7 %shard_map.130 = (f32[3,2048,256]{2,1,0:T(8,128)}, f32[792,256]{1,0:T(8,128)S(1)}) custom-call(s32[5]{0:T(128)S(1)} %stack.23.pos_ref, f32[792,256]{1,0:T(8,128)S(1)} %shard_map.129.refs_0_, f32[792,256]{1,0:T(8,128)S(1)} %collective-permute-done.22.refs_1_.refs_3_), custom_call_target="tpu_custom_call" | custom-call | tf_op jit(solution)/shard_map/pallas_call | solution.py:500
  108.3 3.9 %collective-permute-done.21.refs_1_.refs_2_ = f32[792,256]{1,0:T(8,128)S(1)} collective-permute-done((f32[792,256]{1,0:T(8,128)S(1)}, f32[792,256]{1,0:T(8,128)S(1)}, u32[]{:S(2)}, u32[]{:S(2)}) %collective-permute-start.21) | collective-permute-done | bytes 811040 | tf_op jit(solution)/shard_map/ppermute | solution.py:356
  112.2 2.8 %collective-permute-start.25 = (f32[792,256]{1,0:T(8,128)S(1)}, f32[792,256]{1,0:T(8,128)S(1)}, u32[]{:S(2)}, u32[]{:S(2)}) collective-permute-start(f32[792,256]{1,0:T(8,128)S(1)} %collective-permute-done.21.refs_1_.refs_2_), channel_id=1, source_target_pairs={{0,16},{16,0},{32,48},{48,32},{64,80},{80,64},{96,112},{112,96},{1... | collective-permute-start | bytes 2433032 | tf_op jit(solution)/shard_map/ppermute | solution.py:361
  115.0 2.3 %shard_map.131.refs_8_ = f32[3,2048,256]{2,1,0:T(8,128)} custom-call(s32[5]{0:T(128)S(1)} %stack.23.pos_ref, f32[792,256]{1,0:T(8,128)S(1)} %collective-permute-done.20.refs_0_.refs_1_, f32[792,256]{1,0:T(8,128)S(1)} %collective-permute-done.21.refs_1_.refs_2_, ...), custom_call_target="tpu_custom_call", output_to_operand_aliasing={{}: (5, {})} | custom-call | tf_op jit(solution)/shard_map/pallas_call | solution.py:500
  117.4 0.8 collective-permute-done.24.refs_5_
  118.1 2.4 %shard_map.132 = (f32[3,2048,256]{2,1,0:T(8,128)}, f32[2,128,128]{2,1,0:T(8,128)}, f32[2,128]{1,0:T(2,128)}, f32[2]{0:T(128)}) custom-call(s32[5]{0:T(128)S(1)} %stack.23.pos_ref, f32[792,256]{1,0:T(8,128)S(1)} %shard_map.129.refs_0_, f32[792,256]{1,0:T(8,128)S(1)} %collective-permute-done.20.refs_0_.refs_1_, ...), custom_call_target="tpu_custom_call", output_to_operand_aliasing={{0}: (9, {})} | custom-call | tf_op jit(solution)/shard_map/pallas_call | solution.py:516
  (37 shorter events, 0.6 us)
Async XLA Ops:
  0.6 5.7 %copy-start.4 = (f32[1,2,256]{2,1,0:T(2,128)S(1)}, f32[1,2,256]{2,1,0:T(2,128)}, u32[]{:S(2)}) copy-start(f32[1,2,256]{2,1,0:T(2,128)} %gate_ref.7) | copy-start | bytes 6148
  0.6 5.7 %copy-start.5 = (f32[2]{0:T(128)S(1)}, f32[2]{0:T(128)}, u32[]{:S(2)}) copy-start(f32[2]{0:T(128)} %base_ref.7) | copy-start | bytes 28
  0.8 20.9 %copy-start.2 = (f32[2,128,128]{2,1,0:T(8,128)S(1)}, f32[2,128,128]{2,1,0:T(8,128)}, u32[]{:S(2)}) copy-start(f32[2,128,128]{2,1,0:T(8,128)} %init_ref.3) | copy-start | bytes 393220
  0.8 20.9 %copy-start.3 = (bf16[1,256,256]{2,1,0:T(8,128)(2,1)S(1)}, bf16[1,256,256]{2,1,0:T(8,128)(2,1)}, u32[]{:S(2)}) copy-start(bf16[1,256,256]{2,1,0:T(8,128)(2,1)} %up_ref.3) | copy-start | bytes 393220
  0.8 21.0 %copy-start.6 = (f32[2,128]{1,0:T(2,128)S(1)}, f32[2,128]{1,0:T(2,128)}, u32[]{:S(2)}) copy-start(f32[2,128]{1,0:T(2,128)} %gain_ref.1) | copy-start | bytes 3076
  10.2 31.8 %copy-start = (bf16[3,2048,256]{2,1,0:T(8,128)(2,1)S(1)}, bf16[3,2048,256]{2,1,0:T(8,128)(2,1)}, u32[]{:S(2)}) copy-start(bf16[3,2048,256]{2,1,0:T(8,128)(2,1)} %w_ref.1) | copy-start | bytes 9437188
  10.3 10.5 %collective-permute-start.4 = (f32[256,1024]{1,0:T(8,128)S(1)}, f32[256,1024]{1,0:T(8,128)S(1)}, u32[]{:S(2)}, u32[]{:S(2)}) collective-permute-start(f32[256,1024]{1,0:T(8,128)S(1)} %get-tuple-element.57), channel_id=1, source_target_pairs={{0,16},{16,0},{32,48},{48,32},{64,80},{80,64},{96,112},{112,96},{1... | collective-permute-start | bytes 3145736 | tf_op jit(solution)/shard_map/ppermute | solution.py:361
  11.8 6.1 %collective-permute-start = (f32[2,128,128]{2,1,0:T(8,128)S(1)}, f32[2,128,128]{2,1,0:T(8,128)S(1)}, u32[]{:S(2)}, u32[]{:S(2)}) collective-permute-start(f32[2,128,128]{2,1,0:T(8,128)S(1)} %get-tuple-element.49), channel_id=1, source_target_pairs={{0,4},{8,12},{1,5},{9,13},{2,6},{10,14},{3,7},{11,15},{16,20},{24,... | collective-permute-start | bytes 393224 | tf_op jit(solution)/shard_map/ppermute | solution.py:433
  15.2 6.5 %collective-permute-start.3 = (f32[2,128,128]{2,1,0:T(8,128)S(1)}, f32[2,128,128]{2,1,0:T(8,128)S(1)}, u32[]{:S(2)}, u32[]{:S(2)}) collective-permute-start(f32[2,128,128]{2,1,0:T(8,128)S(1)} %get-tuple-element.50.d_ref), channel_id=1, source_target_pairs={{8,12},{4,0},{9,13},{5,1},{10,14},{6,2},{11,15},{7,3},{24,28},{20,... | collective-permute-start | bytes 393224 | tf_op jit(solution)/shard_map/ppermute | solution.py:434
  18.1 3.6 %collective-permute-start.2 = (f32[2,128,128]{2,1,0:T(8,128)S(1)}, f32[2,128,128]{2,1,0:T(8,128)S(1)}, u32[]{:S(2)}, u32[]{:S(2)}) collective-permute-start(f32[2,128,128]{2,1,0:T(8,128)S(1)} %shard_map.120), channel_id=1, source_target_pairs={{4,12},{5,13},{6,14},{7,15},{20,28},{21,29},{22,30},{23,31},{36,44... | collective-permute-start | bytes 393224 | tf_op jit(solution)/shard_map/ppermute | solution.py:451
  18.8 2.9 %collective-permute-start.1 = (f32[2,128,128]{2,1,0:T(8,128)S(1)}, f32[2,128,128]{2,1,0:T(8,128)S(1)}, u32[]{:S(2)}, u32[]{:S(2)}) collective-permute-start(f32[2,128,128]{2,1,0:T(8,128)S(1)} %shard_map.120), channel_id=1, source_target_pairs={{4,8},{5,9},{6,10},{7,11},{20,24},{21,25},{22,26},{23,27},{36,40},... | collective-permute-start | bytes 393224 | tf_op jit(solution)/shard_map/ppermute | solution.py:450
  19.5 10.6 %collective-permute-start.9 = (f32[2,128,128]{2,1,0:T(8,128)S(1)}, f32[2,128,128]{2,1,0:T(8,128)S(1)}, u32[]{:S(2)}, u32[]{:S(2)}) collective-permute-start(f32[2,128,128]{2,1,0:T(8,128)S(1)} %get-tuple-element.50.d_ref), channel_id=1, source_target_pairs={{8,0},{9,1},{10,2},{11,3},{24,16},{25,17},{26,18},{27,19},{40,32},... | collective-permute-start | bytes 393224 | tf_op jit(solution)/shard_map/ppermute | solution.py:436
  20.8 9.3 %collective-permute-start.8 = (f32[2,128,128]{2,1,0:T(8,128)S(1)}, f32[2,128,128]{2,1,0:T(8,128)S(1)}, u32[]{:S(2)}, u32[]{:S(2)}) collective-permute-start(f32[2,128,128]{2,1,0:T(8,128)S(1)} %get-tuple-element.50.d_ref), channel_id=1, source_target_pairs={{8,4},{9,5},{10,6},{11,7},{24,20},{25,21},{26,22},{27,23},{40,36},... | collective-permute-start | bytes 393224 | tf_op jit(solution)/shard_map/ppermute | solution.py:435
  23.3 10.9 %collective-permute-start.7 = (f32[2,128,128]{2,1,0:T(8,128)S(1)}, f32[2,128,128]{2,1,0:T(8,128)S(1)}, u32[]{:S(2)}, u32[]{:S(2)}) collective-permute-start(f32[2,128,128]{2,1,0:T(8,128)S(1)} %get-tuple-element.58.p_ref), channel_id=1, source_target_pairs={{12,0},{13,1},{14,2},{15,3},{28,16},{29,17},{30,18},{31,19},{44,32... | collective-permute-start | bytes 393224 | tf_op jit(solution)/shard_map/ppermute | solution.py:461
  24.6 11.5 %collective-permute-start.6 = (f32[2,128,128]{2,1,0:T(8,128)S(1)}, f32[2,128,128]{2,1,0:T(8,128)S(1)}, u32[]{:S(2)}, u32[]{:S(2)}) collective-permute-start(f32[2,128,128]{2,1,0:T(8,128)S(1)} %get-tuple-element.58.p_ref), channel_id=1, source_target_pairs={{12,4},{8,0},{13,5},{9,1},{14,6},{10,2},{15,7},{11,3},{28,20},{24,... | collective-permute-start | bytes 393224 | tf_op jit(solution)/shard_map/ppermute | solution.py:460
  25.9 10.2 %collective-permute-start.5 = (f32[2,128,128]{2,1,0:T(8,128)S(1)}, f32[2,128,128]{2,1,0:T(8,128)S(1)}, u32[]{:S(2)}, u32[]{:S(2)}) collective-permute-start(f32[2,128,128]{2,1,0:T(8,128)S(1)} %get-tuple-element.58.p_ref), channel_id=1, source_target_pairs={{12,8},{8,4},{4,0},{13,9},{9,5},{5,1},{14,10},{10,6},{6,2},{15,11}... | collective-permute-start | bytes 393224 | tf_op jit(solution)/shard_map/ppermute | solution.py:459
  38.6 5.6 %collective-permute-start.11 = (f32[960,256]{1,0:T(8,128)S(1)}, f32[960,256]{1,0:T(8,128)S(1)}, u32[]{:S(2)}, u32[]{:S(2)}) collective-permute-start(f32[960,256]{1,0:T(8,128)S(1)} %get-tuple-element.74.all_ref.own_ref), channel_id=1, source_target_pairs={{0,16},{16,0},{32,48},{48,32},{64,80},{80,64},{96,112},{112,96},{1... | collective-permute-start | bytes 2949128 | tf_op jit(solution)/shard_map/ppermute | solution.py:361
  45.2 23.2 %collective-permute-start.16 = (f32[792,256]{1,0:T(8,128)S(1)}, f32[792,256]{1,0:T(8,128)S(1)}, u32[]{:S(2)}, u32[]{:S(2)}) collective-permute-start(f32[792,256]{1,0:T(8,128)S(1)} %shard_map.126.refs_2_), channel_id=1, source_target_pairs={{0,64},{4,68},{8,72},{12,76},{16,24},{20,28},{24,16},{28,20},{32,9... | collective-permute-start | bytes 2433032 | tf_op jit(solution)/shard_map/ppermute | solution.py:356
  50.1 18.3 %collective-permute-start.14 = (f32[792,256]{1,0:T(8,128)S(1)}, f32[792,256]{1,0:T(8,128)S(1)}, u32[]{:S(2)}, u32[]{:S(2)}) collective-permute-start(f32[792,256]{1,0:T(8,128)S(1)} %get-tuple-element.83), channel_id=1, source_target_pairs={{0,32},{4,36},{8,40},{12,44},{16,20},{20,24},{24,28},{28,16},{32,6... | collective-permute-start | bytes 2433032 | tf_op jit(solution)/shard_map/ppermute | solution.py:356
  50.2 18.2 %collective-permute-start.15 = (f32[792,256]{1,0:T(8,128)S(1)}, f32[792,256]{1,0:T(8,128)S(1)}, u32[]{:S(2)}, u32[]{:S(2)}) collective-permute-start(f32[792,256]{1,0:T(8,128)S(1)} %get-tuple-element.84), channel_id=1, source_target_pairs={{0,96},{4,100},{8,104},{12,108},{16,28},{20,16},{24,20},{28,24},{3... | collective-permute-start | bytes 2433032 | tf_op jit(solution)/shard_map/ppermute | solution.py:356
  52.9 15.5 %collective-permute-start.12 = (f32[256,512]{1,0:T(8,128)S(1)}, f32[256,512]{1,0:T(8,128)S(1)}, u32[]{:S(2)}, u32[]{:S(2)}) collective-permute-start(f32[256,512]{1,0:T(8,128)S(1)} %get-tuple-element.80), channel_id=1, source_target_pairs={{0,1},{1,2},{2,3},{3,0},{4,5},{5,6},{6,7},{7,4},{8,9},{9,10},{10,1... | collective-permute-start | bytes 1572872 | tf_op jit(solution)/shard_map/ppermute | solution.py:477
  54.5 13.9 %collective-permute-start.13 = (f32[256,512]{1,0:T(8,128)S(1)}, f32[256,512]{1,0:T(8,128)S(1)}, u32[]{:S(2)}, u32[]{:S(2)}) collective-permute-start(f32[256,512]{1,0:T(8,128)S(1)} %get-tuple-element.81), channel_id=1, source_target_pairs={{0,3},{1,0},{2,1},{3,2},{4,7},{5,4},{6,5},{7,6},{8,11},{9,8},{10,9... | collective-permute-start | bytes 1572872 | tf_op jit(solution)/shard_map/ppermute | solution.py:477
  68.6 16.4 %collective-permute-start.19 = (f32[792,256]{1,0:T(8,128)S(1)}, f32[792,256]{1,0:T(8,128)S(1)}, u32[]{:S(2)}, u32[]{:S(2)}) collective-permute-start(f32[792,256]{1,0:T(8,128)S(1)} %shard_map.128.own_ref), channel_id=1, source_target_pairs={{0,8},{4,12},{8,0},{12,4},{16,80},{20,84},{24,88},{28,92},{32,40},... | collective-permute-start | bytes 2433032 | tf_op jit(solution)/shard_map/ppermute | solution.py:356
  70.2 19.3 %collective-permute-start.18 = (f32[792,256]{1,0:T(8,128)S(1)}, f32[792,256]{1,0:T(8,128)S(1)}, u32[]{:S(2)}, u32[]{:S(2)}) collective-permute-start(f32[792,256]{1,0:T(8,128)S(1)} %shard_map.128.own_ref), channel_id=1, source_target_pairs={{0,12},{4,0},{8,4},{12,8},{16,112},{20,116},{24,120},{28,124},{32,... | collective-permute-start | bytes 2433032 | tf_op jit(solution)/shard_map/ppermute | solution.py:356
  71.6 18.7 %collective-permute-start.17 = (f32[792,256]{1,0:T(8,128)S(1)}, f32[792,256]{1,0:T(8,128)S(1)}, u32[]{:S(2)}, u32[]{:S(2)}) collective-permute-start(f32[792,256]{1,0:T(8,128)S(1)} %shard_map.128.own_ref), channel_id=1, source_target_pairs={{0,4},{4,8},{8,12},{12,0},{16,48},{20,52},{24,56},{28,60},{32,36},... | collective-permute-start | bytes 2433032 | tf_op jit(solution)/shard_map/ppermute | solution.py:356
  71.7 13.1 %collective-permute-start.10 = (f32[256,512]{1,0:T(8,128)S(1)}, f32[256,512]{1,0:T(8,128)S(1)}, u32[]{:S(2)}, u32[]{:S(2)}) collective-permute-start(f32[256,512]{1,0:T(8,128)S(1)} %get-tuple-element.76), channel_id=1, source_target_pairs={{0,2},{1,3},{2,0},{3,1},{4,6},{5,7},{6,4},{7,5},{8,10},{9,11},{10,... | collective-permute-start | bytes 1572872 | tf_op jit(solution)/shard_map/ppermute | solution.py:477
  85.0 32.3 %copy-start.1 = (bf16[1,256,512]{2,1,0:T(8,128)(2,1)}, bf16[1,256,512]{2,1,0:T(8,128)(2,1)S(1)}, u32[]{:S(2)}) copy-start(bf16[1,256,512]{2,1,0:T(8,128)(2,1)S(1)} %fusion.refs_0_) | copy-start | bytes 786436
  90.5 13.0 %collective-permute-start.22 = (f32[792,256]{1,0:T(8,128)S(1)}, f32[792,256]{1,0:T(8,128)S(1)}, u32[]{:S(2)}, u32[]{:S(2)}) collective-permute-start(f32[792,256]{1,0:T(8,128)S(1)} %shard_map.129.refs_0_), channel_id=1, source_target_pairs={{0,64},{4,68},{8,72},{12,76},{16,24},{20,28},{24,16},{28,20},{32,9... | collective-permute-start | bytes 2433032 | tf_op jit(solution)/shard_map/ppermute | solution.py:356
  92.6 19.6 %collective-permute-start.21 = (f32[792,256]{1,0:T(8,128)S(1)}, f32[792,256]{1,0:T(8,128)S(1)}, u32[]{:S(2)}, u32[]{:S(2)}) collective-permute-start(f32[792,256]{1,0:T(8,128)S(1)} %shard_map.129.refs_0_), channel_id=1, source_target_pairs={{0,32},{4,36},{8,40},{12,44},{16,20},{20,24},{24,28},{28,16},{32,6... | collective-permute-start | bytes 2433032 | tf_op jit(solution)/shard_map/ppermute | solution.py:356
  92.6 22.4 %collective-permute-start.20 = (f32[792,256]{1,0:T(8,128)S(1)}, f32[792,256]{1,0:T(8,128)S(1)}, u32[]{:S(2)}, u32[]{:S(2)}) collective-permute-start(f32[792,256]{1,0:T(8,128)S(1)} %shard_map.129.refs_0_), channel_id=1, source_target_pairs={{0,96},{4,100},{8,104},{12,108},{16,28},{20,16},{24,20},{28,24},{3... | collective-permute-start | bytes 2433032 | tf_op jit(solution)/shard_map/ppermute | solution.py:356
  103.5 11.5 %collective-permute-start.26 = (f32[792,256]{1,0:T(8,128)S(1)}, f32[792,256]{1,0:T(8,128)S(1)}, u32[]{:S(2)}, u32[]{:S(2)}) collective-permute-start(f32[792,256]{1,0:T(8,128)S(1)} %collective-permute-done.22.refs_1_.refs_3_), channel_id=1, source_target_pairs={{0,16},{16,0},{32,48},{48,32},{64,80},{80,64},{96,112},{112,96},{1... | collective-permute-start | bytes 2433032 | tf_op jit(solution)/shard_map/ppermute | solution.py:361
  108.2 6.9 %collective-permute-start.23 = (f32[792,256]{1,0:T(8,128)S(1)}, f32[792,256]{1,0:T(8,128)S(1)}, u32[]{:S(2)}, u32[]{:S(2)}) collective-permute-start(f32[792,256]{1,0:T(8,128)S(1)} %get-tuple-element.85), channel_id=1, source_target_pairs={{0,16},{16,0},{32,48},{48,32},{64,80},{80,64},{96,112},{112,96},{1... | collective-permute-start | bytes 2433032 | tf_op jit(solution)/shard_map/ppermute | solution.py:361
  112.2 5.2 %collective-permute-start.25 = (f32[792,256]{1,0:T(8,128)S(1)}, f32[792,256]{1,0:T(8,128)S(1)}, u32[]{:S(2)}, u32[]{:S(2)}) collective-permute-start(f32[792,256]{1,0:T(8,128)S(1)} %collective-permute-done.21.refs_1_.refs_2_), channel_id=1, source_target_pairs={{0,16},{16,0},{32,48},{48,32},{64,80},{80,64},{96,112},{112,96},{1... | collective-permute-start | bytes 2433032 | tf_op jit(solution)/shard_map/ppermute | solution.py:361
  115.0 3.1 %collective-permute-start.24 = (f32[792,256]{1,0:T(8,128)S(1)}, f32[792,256]{1,0:T(8,128)S(1)}, u32[]{:S(2)}, u32[]{:S(2)}) collective-permute-start(f32[792,256]{1,0:T(8,128)S(1)} %collective-permute-done.20.refs_0_.refs_1_), channel_id=1, source_target_pairs={{0,16},{16,0},{32,48},{48,32},{64,80},{80,64},{96,112},{112,96},{1... | collective-permute-start | bytes 2433032 | tf_op jit(solution)/shard_map/ppermute | solution.py:361
